TPU v7x, 512 devices: a whole 4x4x16 slice. The times are simulated.
512 devices in a mesh: rows: 32 (over x, z_hi, y), loop: 16 (over z_lo, core).
Axes of the slice: x: 4, y: 4, z: 16 (z_hi: 2, z_lo: 8; z = z_hi * 8 + z_lo), core: 2. Of those that a mesh axis runs over, the one named last changes fastest.
Arguments:
- integrals: float32 [2, 2, 8192, 8192], P(None, None, 'rows', 'loop'), may hold values from -6 to 6
- mask: int32 [2, 64, 64], P(None, 'rows', 'loop'), may hold values 0 or 1
- coeffs: float32 [8192, 640], P('loop'), may hold values from -0.0625 to 0.0625
Outputs:
- exchange: float32 [8192, 8192], P('rows', 'loop')
All inputs are finite; a program needn't handle non-finite values. No bound on the sum of `mask` on one device may be relied on, other than what follows from the above.
Results may differ from a plain program's by a relative error of at most 0.00009.
Values sent between devices are 32-bit elements; how exact they have to be, the bound alone decides.
No kernel may reach another device: no remote copies, remote signals or barrier semaphores. Data moves between devices by JAX's collectives and lax.ppermute only.
A program may use at most 64 MiB of HBM per device.

v0:
```python
import jax
import jax.numpy as jnp
from jax import lax
from jax.sharding import PartitionSpec as P

TILE = 128


def local(integrals, mask, coeffs):
    nslab, naux, mrows, lcols = integrals.shape
    blocks = mask.astype(jnp.float32)[:, None, :, None, :, None]
    shaped = integrals.reshape(nslab, naux, mrows // TILE, TILE, lcols // TILE, TILE)
    masked = (shaped * blocks).reshape(nslab * naux, mrows, lcols)
    norbit = coeffs.shape[1]
    loops = lax.axis_size("loop")
    row_count = lax.axis_size("rows")
    mine = norbit // loops
    ratio = row_count // loops
    depth = norbit * nslab * naux
    own_orbits = lax.psum_scatter(
        jnp.einsum("pml,li->ipm", masked, coeffs, precision=lax.Precision.HIGHEST),
        "loop",
        scatter_dimension=0,
        tiled=True,
    )
    row_full = lax.all_gather(own_orbits, "loop", axis=0, tiled=True)
    row_flat = row_full.reshape(depth, mrows)
    sub_rows = mrows // row_count
    split_rows = own_orbits.reshape(mine, nslab * naux, row_count, sub_rows)
    routed = lax.all_to_all(
        lax.all_to_all(split_rows, "rows", split_axis=2, concat_axis=2, tiled=True),
        "loop",
        split_axis=2,
        concat_axis=0,
        tiled=True,
    )
    piece = lax.all_gather(routed, "rows", axis=3, tiled=True)
    flat = piece.reshape(depth, ratio, piece.shape[3])
    tiles = jnp.einsum("dm,doc->moc", row_flat, flat, precision=lax.Precision.HIGHEST)
    total = tiles.reshape(mrows, lcols)
    scale = 1.0 / jnp.sqrt(jnp.float32(depth))
    return total * scale


def solution(mesh):
    in_specs = (P(None, None, "rows", "loop"), P(None, "rows", "loop"), P("loop", None))
    out_specs = P("rows", "loop")
    return jax.shard_map(local, mesh=mesh, in_specs=in_specs, out_specs=out_specs, check_vma=False)
```

profile of v0, /device:TPU:1, one launch (start us, length us, event | category | flops | bytes accessed | tf_op | source)
XLA Modules:
  0.0 561.5 jit_solution(16045904447721542678)
XLA Ops:
  6.5 0.8 convert_element_type.3
  7.3 1.7 mul.17
  9.0 2.1 mul.18
  11.1 2.1 bitcast_multiply_fusion
  13.2 6.7 %convolution_bitcast_fusion = f32[640,4,256]{0,2,1:T(8,128)} fusion(f32[4,256,512]{2,1,0:T(8,128)S(1)} %bitcast_multiply_fusion, f32[512,640]{1,0:T(8,128)S(1)} %copy-done), kind=kOutput, calls=%fused_computation.1 | convolution fusion | flops 4026531840 | bytes 6029312 | tf_op jit(solution)/shard_map/pml,li->ipm/dot_general | solution.py:21
  19.9 4.1 copy.13
  24.0 0.0 all-gather.3.cloned.1.call-start
  24.1 1.3 dynamic-slice
  26.0 210.0 %all-reduce.3.cloned.1.call-done = f32[640,4,256]{2,1,0:T(4,128)} async-done(((f32[640,4,256]{2,1,0:T(4,128)}), f32[640,4,256]{2,1,0:T(4,128)}) %all-reduce.3.cloned.1.call-update) | async-done | bytes 2621456
  236.0 1.6 constant_dynamic-slice_fusion
  237.6 0.0 all-gather.5.cloned.1.call-start
  237.7 1.1 copy.14
  238.8 0.1 copy_bitcast_fusion
  238.8 0.5 reshape.24
  239.3 26.7 %all_to_all.23 = f32[32,1,1280]{2,1,0:T(1,128)S(1)} all-to-all(f32[32,1,1280]{2,1,0:T(1,128)S(1)} %reshape.24), channel_id=1, replica_groups=mesh['rows'=32,'loop'=16] {'rows'}, dimensions={0} | all-to-all | bytes 327680 | tf_op jit(solution)/shard_map/all_to_all | solution.py:31
  266.0 0.6 broadcast.2
  266.6 1.0 reduce
  267.6 0.4 reshape.25
  268.1 0.4 reshape.26
  268.5 28.0 %all_to_all.24 = f32[16,1,2560]{2,1,0:T(1,128)S(1)} all-to-all(f32[16,1,2560]{2,1,0:T(1,128)S(1)} %reshape.26), channel_id=1, replica_groups=mesh['rows'=32,'loop'=16] {'loop'}, dimensions={0} | all-to-all | bytes 327680 | tf_op jit(solution)/shard_map/all_to_all | solution.py:30
  296.5 1.0 reduce.1
  297.5 0.4 reshape.27
  297.9 0.3 copy.17
  298.2 0.9 all_to_all.20
  299.1 0.0 all-gather.5.cloned.1.call-update
  299.1 41.1 %all-gather.3.cloned.1.call-done = f32[640,4,256]{2,1,0:T(4,128)} async-done(((f32[40,4,256]{2,1,0:T(4,128)}), f32[640,4,256]{2,1,0:T(4,128)}) %all-gather.3.cloned.1.call-update) | async-done | bytes 2621456 | tf_op jit(solution)/shard_map/all_gather | solution.py:26
  340.2 4.0 reshape.19
  344.2 193.0 %all-gather.5.cloned.1.call-done = f32[640,4,2,256]{0,3,2,1:T(8,128)} async-done(((f32[640,4,2,8]{0,3,2,1:T(8,128)}), f32[640,4,2,256]{0,3,2,1:T(8,128)}) %all-gather.5.cloned.1.call-update) | async-done | bytes 5242896 | tf_op jit(solution)/shard_map/all_gather | solution.py:37
  537.2 8.9 %copy.18 = f32[640,4,2,256]{3,2,1,0:T(2,128)} copy(f32[640,4,2,256]{0,3,2,1:T(8,128)} %all-gather.5.cloned.1.call-done) | data formatting | bytes 10485760 | tf_op jit(solution)/shard_map/all_gather | solution.py:37
  546.1 3.2 copy.20
  549.3 0.1 copy-done.1
  549.4 5.5 convolution_multiply_fusion
  (7 shorter events, 0.1 us)
Async XLA Ops:
  6.5 6.6 %copy-start = (f32[512,640]{1,0:T(8,128)S(1)}, f32[512,640]{1,0:T(8,128)}, u32[]{:S(2)}) copy-start(f32[512,640]{1,0:T(8,128)} %param.5) | copy-start | bytes 3932164
  6.5 229.4 %all-reduce.3.cloned.1.call-start = ((), (), s32[]{:S(2)}) async-start(), calls=%async_computation.4 | async-start | bytes 5242880
  24.0 316.2 %all-gather.3.cloned.1.call-start = ((), (), s32[]{:S(2)}) async-start(), calls=%async_computation.2 | async-start | bytes 2785280 | tf_op jit(solution)/shard_map/all_gather | solution.py:26
  237.6 299.6 %all-gather.5.cloned.1.call-start = ((), (), s32[]{:S(2)}) async-start(), calls=%async_computation.3 | async-start | bytes 5406720 | tf_op jit(solution)/shard_map/all_gather | solution.py:37
  546.1 3.3 copy-start.1
Sparse Core Ops, SparseCore 0:
  24.2 211.7 all-reduce.2
  238.1 102.0 all-gather.2
  344.6 192.5 all-gather.4
where the time goes:
time: 563 us; the launch traced here: 561 us
  waiting for transfers between devices  444 us (79%)
  blocking collectives  54.7 us (10%)
  local copies, waits for them, and re-layouts  31.6 us (6%)
  between operations  13.9 us (2%)
  matrix products  12.2 us (2%)
    unnamed x4, waiting for transfers between devices  210 us
    all_gather x1, waiting for transfers between devices, local(): piece = lax.all_gather(routed, 'rows', axis=3, tiled=True)  193 us
    all_gather x1, waiting for transfers between devices, local(): row_full = lax.all_gather(own_orbits, 'loop', axis=0, tiled=True)  41.1 us
    all_to_all x1, blocking collectives, local(): lax.all_to_all(lax.all_to_all(split_rows, 'rows', split_axis=2, concat_ax...  28 us
    all_to_all x1, blocking collectives, local(): lax.all_to_all(split_rows, 'rows', split_axis=2, concat_axis=2, tiled=True)  26.7 us
  transfers between devices with their start and end apart: 3, of which 3 were waited for; matrix products, arithmetic and copies ran while one was open for 2% of the time, Pallas kernels for 0%

commit v1 on v0

v1 whole, which is shorter than its diff:
```python
import jax
import jax.numpy as jnp
from jax import lax
from jax.experimental import pallas as pl
from jax.experimental.pallas import tpu as pltpu
from jax.sharding import Mesh, PartitionSpec as P

TILE = 128
VMEM = 48 * 1024 * 1024
HANDED = ((0, 3, 1, 2, 2, 1, 3, 0), (3, 0, 2, 1, 1, 2, 0, 3))
NT = (((1,), (1,)), ((), ()))


def halves(value):
    high = value.astype(jnp.bfloat16)
    return high, (value - high.astype(jnp.float32)).astype(jnp.bfloat16)


def half_kernel(slab_ref, mask_ref, a_ref, c_ref, o_ref, chigh, clow, ahigh, alow):
    @pl.when(pl.program_id(0) == 0)
    def _():
        chigh[...], clow[...] = halves(c_ref[...])

    slab = slab_ref[0]
    for i in range(a_ref.shape[2] // TILE):
        for j in range(a_ref.shape[3] // TILE):
            at = (pl.ds(i * TILE, TILE), pl.ds(j * TILE, TILE))
            kept = mask_ref[slab, i, j].astype(jnp.float32)
            ahigh[at], alow[at] = halves(a_ref[0, 0, at[0], at[1]] * kept)
    dot = lambda a, b: jnp.dot(a, b, preferred_element_type=jnp.float32)
    o_ref[0] = dot(ahigh[...], chigh[...]) + (dot(ahigh[...], clow[...]) + dot(alow[...], chigh[...]))


def half_of_slab(integrals, mask, coeffs, slab):
    nslab, naux, mrows, lcols = integrals.shape
    norbit = coeffs.shape[1]
    return pl.pallas_call(
        half_kernel,
        out_shape=jax.ShapeDtypeStruct((naux, mrows, norbit), jnp.float32),
        grid_spec=pltpu.PrefetchScalarGridSpec(
            num_scalar_prefetch=2,
            grid=(naux,),
            in_specs=[
                pl.BlockSpec((1, 1, mrows, lcols), lambda a, slab, mask: (slab[0], a, 0, 0)),
                pl.BlockSpec((lcols, norbit), lambda a, slab, mask: (0, 0)),
            ],
            out_specs=pl.BlockSpec((1, mrows, norbit), lambda a, slab, mask: (a, 0, 0)),
            scratch_shapes=[pltpu.VMEM((lcols, norbit), jnp.bfloat16)] * 2
            + [pltpu.VMEM((mrows, lcols), jnp.bfloat16)] * 2,
        ),
        compiler_params=pltpu.CompilerParams(vmem_limit_bytes=VMEM),
        cost_estimate=pl.CostEstimate(flops=6 * naux * mrows * lcols * norbit, bytes_accessed=4 * naux * mrows * (lcols + norbit) + 4 * lcols * norbit, transcendentals=0),
    )(slab.reshape(1), mask, integrals, coeffs)


def exchange_kernel(m_ref, n_ref, o_ref, mhigh, mlow, nhigh, nlow):
    planes, naux, rows, norbit = m_ref.shape
    parts, _, _, sub, _ = n_ref.shape
    per = parts // naux

    @pl.when(pl.program_id(0) == 0)
    def _():
        for a in range(naux):
            for z in range(planes):
                at = pl.ds(z * rows, rows)
                mhigh[a, at, :], mlow[a, at, :] = halves(m_ref[z, a])

    total = None
    for a in range(naux):
        for h in range(per):
            for z in range(planes):
                at = pl.ds(z * rows + h * sub, sub)
                nhigh[a, at, :], nlow[a, at, :] = halves(n_ref[a * per + h, 0, z])
        dot = lambda l, r: lax.dot_general(l[a], r[a], NT, preferred_element_type=jnp.float32)
        term = dot(mhigh, nhigh) + (dot(mhigh, nlow) + dot(mlow, nhigh))
        total = term if total is None else total + term
    o_ref[0] = total


def exchange_part(m, n):
    planes, naux, rows, norbit = m.shape
    parts, blocks, _, sub, _ = n.shape
    mrows = planes * rows
    return pl.pallas_call(
        exchange_kernel,
        out_shape=jax.ShapeDtypeStruct((blocks, mrows, mrows), jnp.float32),
        grid=(blocks,),
        in_specs=[
            pl.BlockSpec(m.shape, lambda y: (0, 0, 0, 0)),
            pl.BlockSpec((parts, 1, planes, sub, norbit), lambda y: (0, y, 0, 0, 0)),
        ],
        out_specs=pl.BlockSpec((1, mrows, mrows), lambda y: (y, 0, 0)),
        scratch_shapes=[pltpu.VMEM((naux, mrows, norbit), jnp.bfloat16)] * 4,
        compiler_params=pltpu.CompilerParams(vmem_limit_bytes=VMEM),
        cost_estimate=pl.CostEstimate(flops=6 * naux * blocks * mrows * mrows * norbit, bytes_accessed=4 * naux * mrows * norbit * (blocks + 1) + 4 * blocks * mrows * mrows, transcendentals=0),
    )(m, n)


def swap(value, axis, bit, size):
    return lax.ppermute(value, axis, [(i, i ^ bit) for i in range(size)])


def pick(value, index, axis):
    return lax.dynamic_index_in_dim(value, index, axis, keepdims=False)


def local(integrals, mask, coeffs):
    nslab, naux, mrows, lcols = integrals.shape
    norbit = coeffs.shape[1]
    core, zl, zh = lax.axis_index("core"), lax.axis_index("zl"), lax.axis_index("zh")
    rows = mrows // 8
    away = half_of_slab(integrals, mask, coeffs, 1 - core)
    kept = half_of_slab(integrals, mask, coeffs, core)
    part = kept + swap(away, "core", 1, 2)
    part = part.reshape(naux, 4, 2, rows, norbit)
    part = pick(part, zl & 1, 2) + swap(pick(part, 1 - (zl & 1), 2), "zl", 1, 8)
    part = part.reshape(naux, 2, 2, rows, norbit)
    bit = (zl >> 1) & 1
    part = pick(part, bit, 2) + swap(pick(part, 1 - bit, 2), "zl", 2, 8)
    bit = zl >> 2
    own = pick(part, bit, 1) + swap(pick(part, 1 - bit, 1), "zl", 4, 8)
    m = lax.all_gather(own, "zl")
    sub = rows // 2
    pieces = lax.all_to_all(own.reshape(2 * naux, sub, norbit), "x", split_axis=0, concat_axis=0)
    handed = jnp.stack([jnp.where(zh == 0, pieces[a], pieces[b]) for a, b in zip(*HANDED)])
    moved = lax.all_to_all(handed, "zl", split_axis=0, concat_axis=0)
    mirror = [(z, 15 - z) for z in range(16) if z % 2 == (z < 8)]
    passed = lax.ppermute(moved, ("zh", "zl"), mirror)
    mine = jnp.where(zh == (zl & 1), moved, passed)
    copies = jnp.broadcast_to(mine[None], (16,) + mine.shape)
    n = lax.all_to_all(copies, ("x", "y"), split_axis=0, concat_axis=0)
    n = n.reshape(4, 4, 8, sub, norbit)
    partial = exchange_part(m, n).reshape(2, 2, mrows, mrows)
    total = pick(partial, core, 0) + swap(pick(partial, 1 - core, 0), "core", 1, 2)
    total = jnp.swapaxes(total, 0, 1).reshape(mrows, lcols)
    return total * (1.0 / jnp.sqrt(jnp.float32(norbit * nslab * naux)))


def solution(mesh):
    fine = Mesh(mesh.devices.reshape(4, 2, 4, 8, 2), ("x", "zh", "y", "zl", "core"))
    r, c = ("x", "zh", "y"), ("zl", "core")
    in_specs = (P(None, None, r, c), P(None, r, c), P(c, None))
    return jax.shard_map(local, mesh=fine, in_specs=in_specs, out_specs=P(r, c), check_vma=False)
```

time: 563 us -> 238 us (0.42)
  waiting for transfers between devices: 444 us -> 140 us
  starting transfers between devices: 0.09 us -> 34.2 us
  blocking collectives: 54.7 us -> 23.2 us
  local copies, waits for them, and re-layouts: 31.6 us -> 9.13 us
  matrix products: 12.2 us -> 0 us
  Pallas kernels: 0 us -> 11 us
    unnamed x4 -> x1, waiting for transfers between devices: 210 us -> 0.68 us
    all_gather x2 -> x1, waiting for transfers between devices: 234 us -> 82.8 us  [local(): m = lax.all_gather(own, 'zl')]
    ppermute x0 -> x6, waiting for transfers between devices: none -> 51.8 us  [the longest x5 51.7 us: swap(): return lax.ppermute(value, axis, [(i, i ^ bit) for i in range(size)])]
    all_to_all x2 -> x1, blocking collectives: 54.7 us -> 23.2 us  [local(): moved = lax.all_to_all(handed, 'zl', split_axis=0, concat_axis=0)]
    ppermute x0 -> x6, starting transfers between devices: none -> 25.9 us  [the longest x5 25.2 us: swap(): return lax.ppermute(value, axis, [(i, i ^ bit) for i in range(size)])]
    dot_general x2 -> x0, matrix products: 12.2 us -> none  [the longest x1 6.69 us: local(): jnp.einsum('pml,li->ipm', masked, coeffs, precision=lax.Precision.HIGHEST)]
    pallas_call x0 -> x3, Pallas kernels: none -> 11 us  [the longest x2 5.64 us: half_of_slab(): pl.pallas_call(half_kernel, out_shape=jax.ShapeDtypeStruct((naux, mrows,...]
    all_gather x1 -> x0, local copies, waits for them, and re-layouts: 8.85 us -> none  [local(): piece = lax.all_gather(routed, 'rows', axis=3, tiled=True)]
  transfers between devices with their start and end apart: 3 -> 9, of which waited for: 3 -> 7; matrix products, arithmetic and copies ran while one was open for 2% -> 0% of each run, Pallas kernels for 0% -> 1%
where the time goes in v1:
time: 238 us; the launch traced here: 234 us
  waiting for transfers between devices  140 us (59%)
  starting transfers between devices  34.2 us (14%)
  blocking collectives  23.2 us (10%)
  between operations  13.7 us (6%)
  Pallas kernels  11 us (5%)
  local copies, waits for them, and re-layouts  9.13 us (4%)
  other arithmetic  2.4 us (1%)
    all_gather x1, waiting for transfers between devices, local(): m = lax.all_gather(own, 'zl')  82.8 us
    ppermute x5, waiting for transfers between devices, swap(): return lax.ppermute(value, axis, [(i, i ^ bit) for i in range(size)])  51.7 us
    ppermute x5, starting transfers between devices, swap(): return lax.ppermute(value, axis, [(i, i ^ bit) for i in range(size)])  25.2 us
    all_to_all x1, blocking collectives, local(): moved = lax.all_to_all(handed, 'zl', split_axis=0, concat_axis=0)  23.2 us
    pallas_call x2, Pallas kernels, half_of_slab(): pl.pallas_call(half_kernel, out_shape=jax.ShapeDtypeStruct((naux, mrows,...  5.64 us
    pallas_call x1, Pallas kernels, exchange_part(): pl.pallas_call(exchange_kernel, out_shape=jax.ShapeDtypeStruct((blocks, m...  5.33 us
    all_to_all x1, waiting for transfers between devices, local(): lax.all_to_all(own.reshape(2 * naux, sub, norbit), 'x', split_axis=0, con...  4.98 us
    all_to_all x1, starting transfers between devices, local(): n = lax.all_to_all(copies, ('x', 'y'), split_axis=0, concat_axis=0)  4.92 us
  transfers between devices with their start and end apart: 9, of which 7 were waited for; matrix products, arithmetic and copies ran while one was open for 0% of the time, Pallas kernels for 1%

profile of v1, /device:TPU:1, one launch (start us, length us, event | category | flops | bytes accessed | tf_op | source)
XLA Modules:
  0.0 233.8 jit_solution(12605879142209540410)
XLA Ops:
  6.5 1.6 copy-done
  8.1 1.3 copy-done.2
  9.4 0.7 copy-done.5
  10.1 3.2 %shard_map.38 = f32[2,256,640]{2,1,0:T(8,128)} custom-call(s32[1]{0:T(128)} %bitcast.1.slab_ref, s32[2,2,4]{2,1,0:T(2,128)S(1)} %copy-done.5, f32[2,2,256,512]{3,2,1,0:T(8,128)S(1)} %copy-done, f32[512,640]{1,0:T(8,128)S(1)} %copy-done.2), custom_call_target="tpu_custom_call" | custom-call | flops 1006632960 | bytes 3670016 | tf_op jit(solution)/shard_map/pallas_call | solution.py:37
  13.4 8.8 %collective-permute-start = (f32[2,256,640]{2,1,0:T(8,128)}, f32[2,256,640]{2,1,0:T(8,128)}, u32[]{:S(2)}, u32[]{:S(2)}) collective-permute-start(f32[2,256,640]{2,1,0:T(8,128)} %shard_map.38), channel_id=1, source_target_pairs={{0,1},{1,0},{2,3},{3,2},{4,5},{5,4},{6,7},{7,6},{8,9},{9,8},{10,11... | collective-permute-start | bytes 3932168 | tf_op jit(solution)/shard_map/ppermute | solution.py:100
  22.2 2.4 %shard_map.37 = f32[2,256,640]{2,1,0:T(8,128)S(1)} custom-call(s32[1]{0:T(128)} %bitcast.slab_ref, s32[2,2,4]{2,1,0:T(2,128)S(1)} %copy-done.6, f32[2,2,256,512]{3,2,1,0:T(8,128)S(1)} %copy-done.1, f32[512,640]{1,0:T(8,128)S(1)} %copy-done.3), custom_call_target="tpu_custom_call" | custom-call | flops 1006632960 | bytes 3670016 | tf_op jit(solution)/shard_map/pallas_call | solution.py:37
  24.6 0.5 collective-permute-done
  25.1 1.4 add.47
  26.6 0.1 dynamic-slice_bitcast_fusion
  26.7 1.9 collective-permute-start.1
  28.6 15.9 %collective-permute-done.1 = f32[2,4,32,640]{3,2,1,0:T(8,128)S(1)} collective-permute-done((f32[2,4,32,640]{3,2,1,0:T(8,128)S(1)}, f32[2,4,32,640]{3,2,1,0:T(8,128)S(1)}, u32[]{:S(2)}, u32[]{:S(2)}) %collective-permute-start.1) | collective-permute-done | bytes 655392 | tf_op jit(solution)/shard_map/ppermute | solution.py:100
  44.5 0.1 bitcast_add_fusion
  44.6 1.9 collective-permute-start.2
  46.5 17.5 %collective-permute-done.2 = f32[2,2,32,640]{3,2,1,0:T(8,128)S(1)} collective-permute-done((f32[2,2,32,640]{3,2,1,0:T(8,128)S(1)}, f32[2,2,32,640]{3,2,1,0:T(8,128)S(1)}, u32[]{:S(2)}, u32[]{:S(2)}) %collective-permute-start.2) | collective-permute-done | bytes 327712 | tf_op jit(solution)/shard_map/ppermute | solution.py:100
  64.1 3.5 %collective-permute-start.3 = (f32[2,32,640]{2,1,0:T(8,128)S(1)}, f32[2,32,640]{2,1,0:T(8,128)S(1)}, u32[]{:S(2)}, u32[]{:S(2)}) collective-permute-start(f32[2,32,640]{2,1,0:T(8,128)S(1)} %dynamic-slice_bitcast_fusion.3), channel_id=1, source_target_pairs={{0,8},{2,10},{4,12},{6,14},{8,0},{10,2},{12,4},{14,6},{1,9},{3,11}... | collective-permute-start | bytes 491528 | tf_op jit(solution)/shard_map/ppermute | solution.py:100
  67.6 16.3 %collective-permute-done.3 = f32[2,32,640]{2,1,0:T(8,128)S(1)} collective-permute-done((f32[2,32,640]{2,1,0:T(8,128)S(1)}, f32[2,32,640]{2,1,0:T(8,128)S(1)}, u32[]{:S(2)}, u32[]{:S(2)}) %collective-permute-start.3) | collective-permute-done | bytes 163872 | tf_op jit(solution)/shard_map/ppermute | solution.py:100
  83.9 0.7 bitcast_add_fusion.3
  84.6 3.3 %all-to-all-start = ((f32[4,16,640]{2,1,0:T(8,128)}), f32[4,16,640]{2,1,0:T(8,128)S(1)}, u32[]{:S(2)}, u32[]{:S(2)}) async-start(f32[4,16,640]{2,1,0:T(8,128)} %bitcast.11), calls=%async_computation | async-start | bytes 327680 | tf_op jit(solution)/shard_map/all_to_all | solution.py:124
  88.0 5.0 %all-to-all-done = f32[4,16,640]{2,1,0:T(8,128)S(1)} async-done(((f32[4,16,640]{2,1,0:T(8,128)}), f32[4,16,640]{2,1,0:T(8,128)S(1)}, u32[]{:S(2)}, u32[]{:S(2)}) %all-to-all-start) | async-done | bytes 163872 | tf_op jit(solution)/shard_map/all_to_all | solution.py:124
  93.1 23.2 %all_to_all.15 = f32[8,16,640]{2,1,0:T(8,128)S(1)} all-to-all(f32[8,16,640]{2,1,0:T(8,128)S(1)} %constant_dynamic-update-slice_fusion), channel_id=1, replica_groups=mesh['x'=4,'zh'=2,'y'=4,'zl'=8,'core'=2] {'zl'}, dimensions={0} | all-to-all | bytes 655360 | tf_op jit(solution)/shard_map/all_to_all | solution.py:126
  116.3 0.7 collective-permute-start.4
  117.0 2.9 %broadcast_in_dim.2 = f32[16,8,16,640]{3,2,1,0:T(8,128)} broadcast(f32[8,16,640]{2,1,0:T(8,128)S(1)} %broadcast_select_fusion), dimensions={1,2,3} | broadcast | bytes 5570560 | tf_op jit(solution)/shard_map/broadcast_in_dim | solution.py:130
  119.9 4.9 %all-to-all-start.2 = ((f32[16,8,16,640]{3,2,1,0:T(8,128)}), f32[16,8,16,640]{3,2,1,0:T(8,128)}, u32[]{:S(2)}, u32[]{:S(2)}) async-start(f32[16,8,16,640]{3,2,1,0:T(8,128)} %broadcast_in_dim.2), calls=%async_computation.2 | async-start | bytes 10485760 | tf_op jit(solution)/shard_map/all_to_all | solution.py:131
  124.9 0.7 all-gather.3.cloned.1.call-update
  125.6 82.8 %all-gather.3.cloned.1.call-done = f32[16,32,640]{2,1,0:T(8,128)} async-done(((f32[2,32,640]{2,1,0:T(8,128)}), f32[16,32,640]{2,1,0:T(8,128)}) %all-gather.3.cloned.1.call-update) | async-done | bytes 1310736 | tf_op jit(solution)/shard_map/all_gather | solution.py:122
  208.4 1.3 copy-done.4
  209.7 5.3 %shard_map.39 = f32[4,256,256]{2,1,0:T(8,128)S(1)} custom-call(f32[8,2,32,640]{3,2,1,0:T(8,128)S(1)} %bitcast.33, f32[4,4,8,16,640]{4,3,2,1,0:T(8,128)} %bitcast.12.n_ref), custom_call_target="tpu_custom_call" | custom-call | flops 2013265920 | bytes 7602176 | tf_op jit(solution)/shard_map/pallas_call | solution.py:84
  215.1 9.1 %collective-permute-start.5 = (f32[2,256,256]{2,1,0:T(8,128)S(1)}, f32[2,256,256]{2,1,0:T(8,128)S(1)}, u32[]{:S(2)}, u32[]{:S(2)}) collective-permute-start(f32[2,256,256]{2,1,0:T(8,128)S(1)} %dynamic-slice_bitcast_fusion.1), channel_id=1, source_target_pairs={{0,1},{1,0},{2,3},{3,2},{4,5},{5,4},{6,7},{7,6},{8,9},{9,8},{10,11... | collective-permute-start | bytes 1572872 | tf_op jit(solution)/shard_map/ppermute | solution.py:100
  224.2 1.5 collective-permute-done.5
  225.7 0.1 fusion.1
  225.8 0.2 copy.6
  226.0 1.0 copy.7
  (26 shorter events, 0.3 us)
Async XLA Ops:
  6.5 1.6 copy-start
  8.1 1.3 copy-start.2
  9.4 0.7 copy-start.5
  10.1 12.0 %copy-start.1 = (f32[2,2,256,512]{3,2,1,0:T(8,128)S(1)}, f32[2,2,256,512]{3,2,1,0:T(8,128)}, u32[]{:S(2)}) copy-start(f32[2,2,256,512]{3,2,1,0:T(8,128)} %a_ref.3) | copy-start | bytes 6291460
  10.1 12.1 %copy-start.3 = (f32[512,640]{1,0:T(8,128)S(1)}, f32[512,640]{1,0:T(8,128)}, u32[]{:S(2)}) copy-start(f32[512,640]{1,0:T(8,128)} %c_ref.3) | copy-start | bytes 3932164
  10.1 12.1 %copy-start.6 = (s32[2,2,4]{2,1,0:T(2,128)S(1)}, s32[2,2,4]{2,1,0:T(2,128)}, u32[]{:S(2)}) copy-start(s32[2,2,4]{2,1,0:T(2,128)} %mask_ref.3) | copy-start | bytes 196
  13.4 11.8 %collective-permute-start = (f32[2,256,640]{2,1,0:T(8,128)}, f32[2,256,640]{2,1,0:T(8,128)}, u32[]{:S(2)}, u32[]{:S(2)}) collective-permute-start(f32[2,256,640]{2,1,0:T(8,128)} %shard_map.38), channel_id=1, source_target_pairs={{0,1},{1,0},{2,3},{3,2},{4,5},{5,4},{6,7},{7,6},{8,9},{9,8},{10,11... | collective-permute-start | bytes 3932168 | tf_op jit(solution)/shard_map/ppermute | solution.py:100
  26.7 17.8 %collective-permute-start.1 = (f32[2,4,32,640]{3,2,1,0:T(8,128)S(1)}, f32[2,4,32,640]{3,2,1,0:T(8,128)S(1)}, u32[]{:S(2)}, u32[]{:S(2)}) collective-permute-start(f32[2,4,32,640]{3,2,1,0:T(8,128)S(1)} %dynamic-slice_bitcast_fusion), channel_id=1, source_target_pairs={{0,2},{2,0},{4,6},{6,4},{8,10},{10,8},{12,14},{14,12},{1,3},{3,1},... | collective-permute-start | bytes 1966088 | tf_op jit(solution)/shard_map/ppermute | solution.py:100
  44.6 19.4 %collective-permute-start.2 = (f32[2,2,32,640]{3,2,1,0:T(8,128)S(1)}, f32[2,2,32,640]{3,2,1,0:T(8,128)S(1)}, u32[]{:S(2)}, u32[]{:S(2)}) collective-permute-start(f32[2,2,32,640]{3,2,1,0:T(8,128)S(1)} %dynamic-slice_bitcast_fusion.2), channel_id=1, source_target_pairs={{0,4},{2,6},{4,0},{6,2},{8,12},{10,14},{12,8},{14,10},{1,5},{3,7},... | collective-permute-start | bytes 983048 | tf_op jit(solution)/shard_map/ppermute | solution.py:100
  64.1 19.9 %collective-permute-start.3 = (f32[2,32,640]{2,1,0:T(8,128)S(1)}, f32[2,32,640]{2,1,0:T(8,128)S(1)}, u32[]{:S(2)}, u32[]{:S(2)}) collective-permute-start(f32[2,32,640]{2,1,0:T(8,128)S(1)} %dynamic-slice_bitcast_fusion.3), channel_id=1, source_target_pairs={{0,8},{2,10},{4,12},{6,14},{8,0},{10,2},{12,4},{14,6},{1,9},{3,11}... | collective-permute-start | bytes 491528 | tf_op jit(solution)/shard_map/ppermute | solution.py:100
  84.6 8.3 %all-to-all-start = ((f32[4,16,640]{2,1,0:T(8,128)}), f32[4,16,640]{2,1,0:T(8,128)S(1)}, u32[]{:S(2)}, u32[]{:S(2)}) async-start(f32[4,16,640]{2,1,0:T(8,128)} %bitcast.11), calls=%async_computation | async-start | bytes 327680 | tf_op jit(solution)/shard_map/all_to_all | solution.py:124
  116.3 0.7 collective-permute-start.4
  119.9 88.5 %all-to-all-start.2 = ((f32[16,8,16,640]{3,2,1,0:T(8,128)}), f32[16,8,16,640]{3,2,1,0:T(8,128)}, u32[]{:S(2)}, u32[]{:S(2)}) async-start(f32[16,8,16,640]{3,2,1,0:T(8,128)} %broadcast_in_dim.2), calls=%async_computation.2 | async-start | bytes 10485760 | tf_op jit(solution)/shard_map/all_to_all | solution.py:131
  124.8 83.6 %all-gather.3.cloned.1.call-start = ((), (), s32[]{:S(2)}) async-start(), calls=%async_computation.3 | async-start | bytes 1474560 | tf_op jit(solution)/shard_map/all_gather | solution.py:122
  208.4 1.3 copy-start.4
  215.1 10.6 %collective-permute-start.5 = (f32[2,256,256]{2,1,0:T(8,128)S(1)}, f32[2,256,256]{2,1,0:T(8,128)S(1)}, u32[]{:S(2)}, u32[]{:S(2)}) collective-permute-start(f32[2,256,256]{2,1,0:T(8,128)S(1)} %dynamic-slice_bitcast_fusion.1), channel_id=1, source_target_pairs={{0,1},{1,0},{2,3},{3,2},{4,5},{5,4},{6,7},{7,6},{8,9},{9,8},{10,11... | collective-permute-start | bytes 1572872 | tf_op jit(solution)/shard_map/ppermute | solution.py:100
Sparse Core Ops, SparseCore 0:
  127.8 80.5 all-gather.2

commit v2 on v1

v2 whole, which is shorter than its diff:
```python
import jax
import jax.numpy as jnp
from jax import lax
from jax.experimental import pallas as pl
from jax.experimental.pallas import tpu as pltpu
from jax.sharding import Mesh, PartitionSpec as P

TILE = 128
VMEM = 60 * 1024 * 1024
NT = (((1,), (1,)), ((), ()))


def halves(value):
    high = value.astype(jnp.bfloat16)
    return high, (value - high.astype(jnp.float32)).astype(jnp.bfloat16)


def dot(a, b, dims=(((1,), (0,)), ((), ()))):
    return lax.dot_general(a, b, dims, preferred_element_type=jnp.float32)


def split_kernel(c_ref, high_ref, low_ref):
    high_ref[...], low_ref[...] = halves(c_ref[...])


def split(value):
    half = jax.ShapeDtypeStruct(value.shape, jnp.bfloat16)
    return pl.pallas_call(split_kernel, out_shape=(half, half))(value)


def half_kernel(slab_ref, mask_ref, a_ref, chigh_ref, clow_ref, o_ref, ahigh, alow):
    slab = slab_ref[0]
    for i in range(a_ref.shape[2] // TILE):
        for j in range(a_ref.shape[3] // TILE):
            at = (pl.ds(i * TILE, TILE), pl.ds(j * TILE, TILE))
            kept = mask_ref[slab, i, j].astype(jnp.float32)
            ahigh[at], alow[at] = halves(a_ref[0, 0, at[0], at[1]] * kept)
    chigh = chigh_ref[...]
    o_ref[...] = dot(ahigh[...], chigh) + (dot(ahigh[...], clow_ref[...]) + dot(alow[...], chigh))


def half_of(integrals, mask, chigh, clow, slab, aux):
    _, _, mrows, lcols = integrals.shape
    norbit = chigh.shape[1]
    return pl.pallas_call(
        half_kernel,
        out_shape=jax.ShapeDtypeStruct((mrows, norbit), jnp.float32),
        grid_spec=pltpu.PrefetchScalarGridSpec(
            num_scalar_prefetch=2,
            grid=(1,),
            in_specs=[
                pl.BlockSpec((1, 1, mrows, lcols), lambda g, slab, mask: (slab[0], aux, 0, 0)),
                pl.BlockSpec((lcols, norbit), lambda g, slab, mask: (0, 0)),
                pl.BlockSpec((lcols, norbit), lambda g, slab, mask: (0, 0)),
            ],
            out_specs=pl.BlockSpec((mrows, norbit), lambda g, slab, mask: (0, 0)),
            scratch_shapes=[pltpu.VMEM((mrows, lcols), jnp.bfloat16)] * 2,
        ),
        compiler_params=pltpu.CompilerParams(vmem_limit_bytes=VMEM),
        cost_estimate=pl.CostEstimate(flops=6 * mrows * lcols * norbit, bytes_accessed=4 * mrows * (lcols + norbit) + 4 * lcols * norbit, transcendentals=0),
    )(slab.reshape(1), mask, integrals, chigh, clow)


def exchange_kernel(place_ref, m_ref, n_ref, o_ref, mhigh, mlow, nhigh, nlow):
    planes, naux, rows, norbit = m_ref.shape
    parts, _, _, _, sub, _ = n_ref.shape
    per = parts // naux

    @pl.when(pl.program_id(0) == 0)
    def _():
        for z in range(planes):
            at = pl.ds(pl.multiple_of(place_ref[1 + z] * rows, rows), rows)
            for a in range(naux):
                mhigh[a, at, :], mlow[a, at, :] = halves(m_ref[z, a])

    total = None
    for a in range(naux):
        for h in range(per):
            for z in range(planes):
                at = pl.ds(z * rows + h * 2 * sub, 2 * sub)
                both = jnp.concatenate([n_ref[a * per + h, 0, k, z] for k in range(2)], axis=0)
                nhigh[a, at, :], nlow[a, at, :] = halves(both)
        term = dot(mhigh[a], nhigh[a], NT) + (dot(mhigh[a], nlow[a], NT) + dot(mlow[a], nhigh[a], NT))
        total = term if total is None else total + term
    o_ref[...] = total


def exchange_part(m, n, place):
    planes, naux, rows, norbit = m.shape
    parts, blocks, _, _, sub, _ = n.shape
    mrows = planes * rows
    mine = blocks // 2
    return pl.pallas_call(
        exchange_kernel,
        out_shape=jax.ShapeDtypeStruct((mrows, mine * mrows), jnp.float32),
        grid_spec=pltpu.PrefetchScalarGridSpec(
            num_scalar_prefetch=1,
            grid=(mine,),
            in_specs=[
                pl.BlockSpec(m.shape, lambda y, place: (0, 0, 0, 0)),
                pl.BlockSpec((parts, 1, 2, planes, sub, norbit), lambda y, place: (0, place[0] * mine + y, 0, 0, 0, 0)),
            ],
            out_specs=pl.BlockSpec((mrows, mrows), lambda y, place: (0, y)),
            scratch_shapes=[pltpu.VMEM((naux, mrows, norbit), jnp.bfloat16)] * 4,
        ),
        compiler_params=pltpu.CompilerParams(vmem_limit_bytes=VMEM),
        cost_estimate=pl.CostEstimate(flops=6 * naux * mine * mrows * mrows * norbit, bytes_accessed=4 * naux * mrows * norbit * (mine + 1) + 4 * mine * mrows * mrows, transcendentals=0),
    )(place, m, n)


def swap(value, axis, bit, size):
    return lax.ppermute(value, axis, [(i, i ^ bit) for i in range(size)])


def pick(value, index, axis):
    return lax.dynamic_index_in_dim(value, index, axis, keepdims=False)


def local(integrals, mask, coeffs):
    nslab, naux, mrows, lcols = integrals.shape
    norbit = coeffs.shape[1]
    core, zl, zh = lax.axis_index("core"), lax.axis_index("zl"), lax.axis_index("zh")
    rows = mrows // 8
    low, mid, top = zl & 1, (zl >> 1) & 1, zl >> 2
    chigh, clow = split(coeffs)
    chunks = range(naux)
    away = [half_of(integrals, mask, chigh, clow, 1 - core, a) for a in chunks]
    got = [swap(away[a], "core", 1, 2) for a in chunks]
    kept = [half_of(integrals, mask, chigh, clow, core, a) for a in chunks]
    part = [(kept[a].reshape(4, 2, rows, norbit), got[a].reshape(4, 2, rows, norbit)) for a in chunks]
    give = [pick(k, 1 - low, 1) + pick(g, 1 - low, 1) for k, g in part]
    keep = [pick(k, low, 1) + pick(g, low, 1) for k, g in part]
    part = [(k.reshape(2, 2, rows, norbit), swap(g, "zl", 1, 8).reshape(2, 2, rows, norbit)) for k, g in zip(keep, give)]
    give = [pick(k, 1 - mid, 1) + pick(g, 1 - mid, 1) for k, g in part]
    keep = [pick(k, mid, 1) + pick(g, mid, 1) for k, g in part]
    part = [(k, swap(g, "zl", 2, 8)) for k, g in zip(keep, give)]
    give = [pick(k, 1 - top, 0) + pick(g, 1 - top, 0) for k, g in part]
    keep = [pick(k, top, 0) + pick(g, top, 0) for k, g in part]
    own = jnp.stack([k + swap(g, "zl", 4, 8) for k, g in zip(keep, give)])
    sub = rows // 4
    pieces = lax.all_to_all(own.reshape(2 * naux, 2 * sub, norbit), "x", split_axis=0, concat_axis=0)
    pieces = pieces.reshape(4, 2, sub, norbit)
    handed = jnp.where(zh == 0, pieces, pieces[:, ::-1]).reshape(1, 8, sub, norbit)
    handed = jnp.broadcast_to(handed, (2, 8, sub, norbit)).reshape(16, sub, norbit)
    moved = lax.all_to_all(handed, ("zh", "zl"), split_axis=0, concat_axis=0).reshape(2, 8, sub, norbit)
    other = swap(pick(moved, 1 - low, 0), "zl", 1, 8)
    mine = jnp.stack([pick(moved, low, 0), other])
    copies = jnp.broadcast_to(mine[None], (16,) + mine.shape)
    n = lax.all_to_all(copies, ("x", "y"), split_axis=0, concat_axis=0)
    n = n.reshape(4, 4, 2, 8, sub, norbit)
    m = own[None]
    order = [0]
    for bit in (4, 2, 1):
        m = jnp.concatenate([m, swap(m, "zl", bit, 8)])
        order = order + [k ^ bit for k in order]
    planes = [zl ^ k for k in order]
    sent = exchange_part(m, n, jnp.stack([1 - core] + planes))
    held = exchange_part(m, n, jnp.stack([core] + planes))
    return (held + swap(sent, "core", 1, 2)) * (1.0 / jnp.sqrt(jnp.float32(norbit * nslab * naux)))


def solution(mesh):
    fine = Mesh(mesh.devices.reshape(4, 2, 4, 8, 2), ("x", "zh", "y", "zl", "core"))
    r, c = ("x", "zh", "y"), ("zl", "core")
    in_specs = (P(None, None, r, c), P(None, r, c), P(c, None))
    return jax.shard_map(local, mesh=fine, in_specs=in_specs, out_specs=P(r, c), check_vma=False)
```

time: 238 us -> 209 us (0.88); the launches traced: 234 us -> 207 us
  waiting for transfers between devices: 140 us -> 74.1 us
  starting transfers between devices: 34.2 us -> 69.4 us
  Pallas kernels: 11 us -> 27.4 us
  between operations: 13.7 us -> 0.22 us
  local copies, waits for them, and re-layouts: 9.13 us -> 4.3 us
  other arithmetic: 2.4 us -> 6.34 us
  blocking collectives: 23.2 us -> 25.6 us
    all_gather x1 -> x0, waiting for transfers between devices: 82.8 us -> none  [local(): m = lax.all_gather(own, 'zl')]
    ppermute x5 -> x13, starting transfers between devices: 25.2 us -> 61 us  [swap(): return lax.ppermute(value, axis, [(i, i ^ bit) for i in range(size)])]
    ppermute x5 -> x13, waiting for transfers between devices: 51.7 us -> 68.6 us  [swap(): return lax.ppermute(value, axis, [(i, i ^ bit) for i in range(size)])]
    pallas_call x3 -> x7, Pallas kernels: 11 us -> 27.4 us  [the longest x4 15.1 us: half_of(): pl.pallas_call(half_kernel, out_shape=jax.ShapeDtypeStruct((mrows, norbit...]
    unnamed x14 -> x0, local copies, waits for them, and re-layouts: 4.92 us -> none
  transfers between devices with their start and end apart: 9 -> 15, of which waited for: 7 -> 11; matrix products, arithmetic and copies ran while one was open for 0% -> 2% of each run, Pallas kernels for 1% -> 8%
where the time goes in v2:
time: 209 us; the launch traced here: 207 us
  waiting for transfers between devices  74.1 us (35%)
  starting transfers between devices  69.4 us (33%)
  Pallas kernels  27.4 us (13%)
  blocking collectives  25.6 us (12%)
  other arithmetic  6.34 us (3%)
  local copies, waits for them, and re-layouts  4.3 us (2%)
    ppermute x13, waiting for transfers between devices, swap(): return lax.ppermute(value, axis, [(i, i ^ bit) for i in range(size)])  68.6 us
    ppermute x13, starting transfers between devices, swap(): return lax.ppermute(value, axis, [(i, i ^ bit) for i in range(size)])  61 us
    all_to_all x1, blocking collectives, local(): lax.all_to_all(handed, ('zh', 'zl'), split_axis=0, concat_axis=0)  25.6 us
    pallas_call x4, Pallas kernels, half_of(): pl.pallas_call(half_kernel, out_shape=jax.ShapeDtypeStruct((mrows, norbit...  15.1 us
    pallas_call x2, Pallas kernels, exchange_part(): pl.pallas_call(exchange_kernel, out_shape=jax.ShapeDtypeStruct((mrows, mi...  9.84 us
    all_to_all x1, waiting for transfers between devices, local(): lax.all_to_all(own.reshape(2 * naux, 2 * sub, norbit), 'x', split_axis=0,...  5 us
    all_to_all x1, starting transfers between devices, local(): n = lax.all_to_all(copies, ('x', 'y'), split_axis=0, concat_axis=0)  4.91 us
  transfers between devices with their start and end apart: 15, of which 11 were waited for; matrix products, arithmetic and copies ran while one was open for 2% of the time, Pallas kernels for 8%

profile of v2, /device:TPU:1, one launch (start us, length us, event | category | flops | bytes accessed | tf_op | source)
XLA Modules:
  0.0 207.5 jit_solution(16942821721725112045)
XLA Ops:
  0.0 2.5 %shard_map.37 = (bf16[512,640]{1,0:T(8,128)(2,1)}, bf16[512,640]{1,0:T(8,128)(2,1)}) custom-call(f32[512,640]{1,0:T(8,128)} %c_ref.1), custom_call_target="tpu_custom_call" | custom-call | tf_op jit(solution)/shard_map/pallas_call | solution.py:28
  2.5 3.8 %shard_map.39 = f32[256,640]{1,0:T(8,128)} custom-call(s32[1]{0:T(128)} %bitcast.10.slab_ref, s32[2,2,4]{2,1,0:T(2,128)} %mask_ref.7, f32[2,2,256,512]{3,2,1,0:T(8,128)} %a_ref.7, bf16[512,640]{1,0:T(8,128)(2,1)} %get-tuple-element.7.chigh_ref, bf16[512,640]{1,0:T(8,128)(2,1)} %get-tuple-element.8.clow_ref), custom_call_target="tpu_custom_call" | custom-call | flops 503316480 | bytes 2490368 | tf_op jit(solution)/shard_map/pallas_call | solution.py:45
  6.3 8.8 %collective-permute-start = (f32[256,640]{1,0:T(8,128)}, f32[256,640]{1,0:T(8,128)S(1)}, u32[]{:S(2)}, u32[]{:S(2)}) collective-permute-start(f32[256,640]{1,0:T(8,128)} %shard_map.39), channel_id=1, source_target_pairs={{0,1},{1,0},{2,3},{3,2},{4,5},{5,4},{6,7},{7,6},{8,9},{9,8},{10,11... | collective-permute-start | bytes 1966088 | tf_op jit(solution)/shard_map/ppermute | solution.py:112
  15.0 3.8 %shard_map.41 = f32[256,640]{1,0:T(8,128)} custom-call(s32[1]{0:T(128)} %bitcast.10.slab_ref, s32[2,2,4]{2,1,0:T(2,128)} %mask_ref.7, f32[2,2,256,512]{3,2,1,0:T(8,128)} %a_ref.7, bf16[512,640]{1,0:T(8,128)(2,1)} %get-tuple-element.7.chigh_ref, bf16[512,640]{1,0:T(8,128)(2,1)} %get-tuple-element.8.clow_ref), custom_call_target="tpu_custom_call" | custom-call | flops 503316480 | bytes 2490368 | tf_op jit(solution)/shard_map/pallas_call | solution.py:45
  20.7 3.8 %shard_map.38 = f32[256,640]{1,0:T(8,128)} custom-call(s32[1]{0:T(128)} %bitcast.slab_ref, s32[2,2,4]{2,1,0:T(2,128)} %mask_ref.7, f32[2,2,256,512]{3,2,1,0:T(8,128)} %a_ref.7, bf16[512,640]{1,0:T(8,128)(2,1)} %get-tuple-element.7.chigh_ref, bf16[512,640]{1,0:T(8,128)(2,1)} %get-tuple-element.8.clow_ref), custom_call_target="tpu_custom_call" | custom-call | flops 503316480 | bytes 2490368 | tf_op jit(solution)/shard_map/pallas_call | solution.py:45
  25.7 1.9 collective-permute-start.1
  27.6 3.8 %shard_map.40 = f32[256,640]{1,0:T(8,128)} custom-call(s32[1]{0:T(128)} %bitcast.slab_ref, s32[2,2,4]{2,1,0:T(2,128)} %mask_ref.7, f32[2,2,256,512]{3,2,1,0:T(8,128)} %a_ref.7, bf16[512,640]{1,0:T(8,128)(2,1)} %get-tuple-element.7.chigh_ref, bf16[512,640]{1,0:T(8,128)(2,1)} %get-tuple-element.8.clow_ref), custom_call_target="tpu_custom_call" | custom-call | flops 503316480 | bytes 2490368 | tf_op jit(solution)/shard_map/pallas_call | solution.py:45
  32.5 3.4 %collective-permute-start.5 = (f32[4,32,640]{2,1,0:T(8,128)S(1)}, f32[4,32,640]{2,1,0:T(8,128)S(1)}, u32[]{:S(2)}, u32[]{:S(2)}) collective-permute-start(f32[4,32,640]{2,1,0:T(8,128)S(1)} %get-tuple-element.12), channel_id=1, source_target_pairs={{0,2},{2,0},{4,6},{6,4},{8,10},{10,8},{12,14},{14,12},{1,3},{3,1},... | collective-permute-start | bytes 983048 | tf_op jit(solution)/shard_map/ppermute | solution.py:112
  36.4 1.9 collective-permute-start.2
  38.3 6.5 %collective-permute-done.5 = f32[4,32,640]{2,1,0:T(8,128)S(1)} collective-permute-done((f32[4,32,640]{2,1,0:T(8,128)S(1)}, f32[4,32,640]{2,1,0:T(8,128)S(1)}, u32[]{:S(2)}, u32[]{:S(2)}) %collective-permute-start.5) | collective-permute-done | bytes 327712 | tf_op jit(solution)/shard_map/ppermute | solution.py:112
  44.9 1.9 collective-permute-start.6
  47.8 5.6 %collective-permute-start.3 = (f32[32,640]{1,0:T(8,128)S(1)}, f32[32,640]{1,0:T(8,128)S(1)}, u32[]{:S(2)}, u32[]{:S(2)}) collective-permute-start(f32[32,640]{1,0:T(8,128)S(1)} %fusion.6), channel_id=1, source_target_pairs={{0,8},{2,10},{4,12},{6,14},{8,0},{10,2},{12,4},{14,6},{1,9},{3,11}... | collective-permute-start | bytes 245768 | tf_op jit(solution)/shard_map/ppermute | solution.py:112
  53.5 2.3 %collective-permute-done.6 = f32[2,32,640]{2,1,0:T(8,128)S(1)} collective-permute-done((f32[2,32,640]{2,1,0:T(8,128)S(1)}, f32[2,32,640]{2,1,0:T(8,128)S(1)}, u32[]{:S(2)}, u32[]{:S(2)}) %collective-permute-start.6) | collective-permute-done | bytes 163872 | tf_op jit(solution)/shard_map/ppermute | solution.py:112
  55.8 8.7 %collective-permute-start.7 = (f32[32,640]{1,0:T(8,128)S(1)}, f32[32,640]{1,0:T(8,128)S(1)}, u32[]{:S(2)}, u32[]{:S(2)}) collective-permute-start(f32[32,640]{1,0:T(8,128)S(1)} %fusion.4), channel_id=1, source_target_pairs={{0,8},{2,10},{4,12},{6,14},{8,0},{10,2},{12,4},{14,6},{1,9},{3,11}... | collective-permute-start | bytes 245768 | tf_op jit(solution)/shard_map/ppermute | solution.py:112
  64.5 7.5 %collective-permute-done.7 = f32[32,640]{1,0:T(8,128)S(1)} collective-permute-done((f32[32,640]{1,0:T(8,128)S(1)}, f32[32,640]{1,0:T(8,128)S(1)}, u32[]{:S(2)}, u32[]{:S(2)}) %collective-permute-start.7) | collective-permute-done | bytes 81952 | tf_op jit(solution)/shard_map/ppermute | solution.py:112
  72.8 3.5 %all-to-all-start = ((f32[4,16,640]{2,1,0:T(8,128)}), f32[4,16,640]{2,1,0:T(8,128)S(1)}, u32[]{:S(2)}, u32[]{:S(2)}) async-start(f32[4,16,640]{2,1,0:T(8,128)} %bitcast.33), calls=%async_computation | async-start | bytes 327680 | tf_op jit(solution)/shard_map/all_to_all | solution.py:141
  76.3 5.0 %all-to-all-done = f32[4,16,640]{2,1,0:T(8,128)S(1)} async-done(((f32[4,16,640]{2,1,0:T(8,128)}), f32[4,16,640]{2,1,0:T(8,128)S(1)}, u32[]{:S(2)}, u32[]{:S(2)}) %all-to-all-start) | async-done | bytes 163872 | tf_op jit(solution)/shard_map/all_to_all | solution.py:141
  81.3 25.6 %all_to_all.15 = f32[16,8,640]{2,1,0:T(8,128)S(1)} all-to-all(f32[16,8,640]{2,1,0:T(8,128)S(1)} %bitcast.108), channel_id=1, replica_groups=mesh['x'=4,'zh'=2,'y'=4,'zl'=8,'core'=2] {'zh','zl'}, dimensions={0} | all-to-all | bytes 655360 | tf_op jit(solution)/shard_map/all_to_all | solution.py:145
  107.0 8.0 %collective-permute-start.11 = (f32[8,8,640]{2,1,0:T(8,128)S(1)}, f32[8,8,640]{2,1,0:T(8,128)S(1)}, u32[]{:S(2)}, u32[]{:S(2)}) collective-permute-start(f32[8,8,640]{2,1,0:T(8,128)S(1)} %get-tuple-element.14), channel_id=1, source_target_pairs={{0,2},{2,0},{4,6},{6,4},{8,10},{10,8},{12,14},{14,12},{1,3},{3,1},... | collective-permute-start | bytes 491528 | tf_op jit(solution)/shard_map/ppermute | solution.py:112
  115.0 2.7 %collective-permute-done.11 = f32[8,8,640]{2,1,0:T(8,128)S(1)} collective-permute-done((f32[8,8,640]{2,1,0:T(8,128)S(1)}, f32[8,8,640]{2,1,0:T(8,128)S(1)}, u32[]{:S(2)}, u32[]{:S(2)}) %collective-permute-start.11) | collective-permute-done | bytes 163872 | tf_op jit(solution)/shard_map/ppermute | solution.py:112
  117.7 3.0 %broadcast_in_dim.19 = f32[16,2,8,8,640]{4,3,2,1,0:T(8,128)} broadcast(f32[2,8,8,640]{3,2,1,0:T(8,128)S(1)} %pad_maximum_fusion.3), dimensions={1,2,3,4} | broadcast | bytes 5570560 | tf_op jit(solution)/shard_map/broadcast_in_dim | solution.py:148
  120.7 4.9 %all-to-all-start.2 = ((f32[16,2,8,8,640]{4,3,2,1,0:T(8,128)}), f32[16,2,8,8,640]{4,3,2,1,0:T(8,128)}, u32[]{:S(2)}, u32[]{:S(2)}) async-start(f32[16,2,8,8,640]{4,3,2,1,0:T(8,128)} %broadcast_in_dim.19), calls=%async_computation.2 | async-start | bytes 10485760 | tf_op jit(solution)/shard_map/all_to_all | solution.py:149
  125.6 4.8 %collective-permute-start.8 = (f32[1,2,32,640]{3,2,1,0:T(8,128)S(1)}, f32[1,2,32,640]{3,2,1,0:T(8,128)S(1)}, u32[]{:S(2)}, u32[]{:S(2)}) collective-permute-start(f32[1,2,32,640]{3,2,1,0:T(8,128)S(1)} %get-tuple-element.16), channel_id=1, source_target_pairs={{0,8},{2,10},{4,12},{6,14},{8,0},{10,2},{12,4},{14,6},{1,9},{3,11}... | collective-permute-start | bytes 491528 | tf_op jit(solution)/shard_map/ppermute | solution.py:112
  130.4 16.6 %collective-permute-done.8 = f32[1,2,32,640]{3,2,1,0:T(8,128)S(1)} collective-permute-done((f32[1,2,32,640]{3,2,1,0:T(8,128)S(1)}, f32[1,2,32,640]{3,2,1,0:T(8,128)S(1)}, u32[]{:S(2)}, u32[]{:S(2)}) %collective-permute-start.8) | collective-permute-done | bytes 163872 | tf_op jit(solution)/shard_map/ppermute | solution.py:112
  147.0 1.9 collective-permute-start.9
  148.9 16.1 %collective-permute-done.9 = f32[2,2,32,640]{3,2,1,0:T(8,128)S(1)} collective-permute-done((f32[2,2,32,640]{3,2,1,0:T(8,128)S(1)}, f32[2,2,32,640]{3,2,1,0:T(8,128)S(1)}, u32[]{:S(2)}, u32[]{:S(2)}) %collective-permute-start.9) | collective-permute-done | bytes 327712 | tf_op jit(solution)/shard_map/ppermute | solution.py:112
  165.1 1.9 collective-permute-start.10
  167.6 15.4 %collective-permute-done.10 = f32[4,2,32,640]{3,2,1,0:T(8,128)S(1)} collective-permute-done((f32[4,2,32,640]{3,2,1,0:T(8,128)S(1)}, f32[4,2,32,640]{3,2,1,0:T(8,128)S(1)}, u32[]{:S(2)}, u32[]{:S(2)}) %collective-permute-start.10) | collective-permute-done | bytes 655392 | tf_op jit(solution)/shard_map/ppermute | solution.py:112
  184.7 5.0 %shard_map.43 = f32[256,512]{1,0:T(8,128)} custom-call(s32[9]{0:T(128)} %stack.73.place_ref, f32[8,2,32,640]{3,2,1,0:T(8,128)} %pad_maximum_fusion.m_ref, f32[4,4,2,8,8,640]{5,4,3,2,1,0:T(8,128)} %bitcast.40.n_ref), custom_call_target="tpu_custom_call" | custom-call | flops 1006632960 | bytes 4456448 | tf_op jit(solution)/shard_map/pallas_call | solution.py:93
  189.7 10.3 %collective-permute-start.12 = (f32[256,512]{1,0:T(8,128)}, f32[256,512]{1,0:T(8,128)S(1)}, u32[]{:S(2)}, u32[]{:S(2)}) collective-permute-start(f32[256,512]{1,0:T(8,128)} %shard_map.43), channel_id=1, source_target_pairs={{0,1},{1,0},{2,3},{3,2},{4,5},{5,4},{6,7},{7,6},{8,9},{9,8},{10,11... | collective-permute-start | bytes 1572872 | tf_op jit(solution)/shard_map/ppermute | solution.py:112
  200.7 4.9 %shard_map.42 = f32[256,512]{1,0:T(8,128)} custom-call(s32[9]{0:T(128)} %stack.67.place_ref, f32[8,2,32,640]{3,2,1,0:T(8,128)} %pad_maximum_fusion.m_ref, f32[4,4,2,8,8,640]{5,4,3,2,1,0:T(8,128)} %bitcast.40.n_ref), custom_call_target="tpu_custom_call" | custom-call | flops 1006632960 | bytes 4456448 | tf_op jit(solution)/shard_map/pallas_call | solution.py:93
  205.5 1.9 add_multiply_fusion
  (28 shorter events, 9.6 us)
Async XLA Ops:
  6.3 18.3 %collective-permute-start = (f32[256,640]{1,0:T(8,128)}, f32[256,640]{1,0:T(8,128)S(1)}, u32[]{:S(2)}, u32[]{:S(2)}) collective-permute-start(f32[256,640]{1,0:T(8,128)} %shard_map.39), channel_id=1, source_target_pairs={{0,1},{1,0},{2,3},{3,2},{4,5},{5,4},{6,7},{7,6},{8,9},{9,8},{10,11... | collective-permute-start | bytes 1966088 | tf_op jit(solution)/shard_map/ppermute | solution.py:112
  18.8 12.6 %collective-permute-start.4 = (f32[256,640]{1,0:T(8,128)}, f32[256,640]{1,0:T(8,128)S(1)}, u32[]{:S(2)}, u32[]{:S(2)}) collective-permute-start(f32[256,640]{1,0:T(8,128)} %shard_map.41), channel_id=1, source_target_pairs={{0,1},{1,0},{2,3},{3,2},{4,5},{5,4},{6,7},{7,6},{8,9},{9,8},{10,11... | collective-permute-start | bytes 1966088 | tf_op jit(solution)/shard_map/ppermute | solution.py:112
  25.7 10.7 %collective-permute-start.1 = (f32[4,32,640]{2,1,0:T(8,128)S(1)}, f32[4,32,640]{2,1,0:T(8,128)S(1)}, u32[]{:S(2)}, u32[]{:S(2)}) collective-permute-start(f32[4,32,640]{2,1,0:T(8,128)S(1)} %get-tuple-element.10), channel_id=1, source_target_pairs={{0,2},{2,0},{4,6},{6,4},{8,10},{10,8},{12,14},{14,12},{1,3},{3,1},... | collective-permute-start | bytes 983048 | tf_op jit(solution)/shard_map/ppermute | solution.py:112
  32.5 12.3 %collective-permute-start.5 = (f32[4,32,640]{2,1,0:T(8,128)S(1)}, f32[4,32,640]{2,1,0:T(8,128)S(1)}, u32[]{:S(2)}, u32[]{:S(2)}) collective-permute-start(f32[4,32,640]{2,1,0:T(8,128)S(1)} %get-tuple-element.12), channel_id=1, source_target_pairs={{0,2},{2,0},{4,6},{6,4},{8,10},{10,8},{12,14},{14,12},{1,3},{3,1},... | collective-permute-start | bytes 983048 | tf_op jit(solution)/shard_map/ppermute | solution.py:112
  36.4 11.4 %collective-permute-start.2 = (f32[2,32,640]{2,1,0:T(8,128)S(1)}, f32[2,32,640]{2,1,0:T(8,128)S(1)}, u32[]{:S(2)}, u32[]{:S(2)}) collective-permute-start(f32[2,32,640]{2,1,0:T(8,128)S(1)} %fusion.3), channel_id=1, source_target_pairs={{0,4},{2,6},{4,0},{6,2},{8,12},{10,14},{12,8},{14,10},{1,5},{3,7},... | collective-permute-start | bytes 491528 | tf_op jit(solution)/shard_map/ppermute | solution.py:112
  44.9 10.9 %collective-permute-start.6 = (f32[2,32,640]{2,1,0:T(8,128)S(1)}, f32[2,32,640]{2,1,0:T(8,128)S(1)}, u32[]{:S(2)}, u32[]{:S(2)}) collective-permute-start(f32[2,32,640]{2,1,0:T(8,128)S(1)} %fusion.2), channel_id=1, source_target_pairs={{0,4},{2,6},{4,0},{6,2},{8,12},{10,14},{12,8},{14,10},{1,5},{3,7},... | collective-permute-start | bytes 491528 | tf_op jit(solution)/shard_map/ppermute | solution.py:112
  47.8 16.7 %collective-permute-start.3 = (f32[32,640]{1,0:T(8,128)S(1)}, f32[32,640]{1,0:T(8,128)S(1)}, u32[]{:S(2)}, u32[]{:S(2)}) collective-permute-start(f32[32,640]{1,0:T(8,128)S(1)} %fusion.6), channel_id=1, source_target_pairs={{0,8},{2,10},{4,12},{6,14},{8,0},{10,2},{12,4},{14,6},{1,9},{3,11}... | collective-permute-start | bytes 245768 | tf_op jit(solution)/shard_map/ppermute | solution.py:112
  55.8 16.3 %collective-permute-start.7 = (f32[32,640]{1,0:T(8,128)S(1)}, f32[32,640]{1,0:T(8,128)S(1)}, u32[]{:S(2)}, u32[]{:S(2)}) collective-permute-start(f32[32,640]{1,0:T(8,128)S(1)} %fusion.4), channel_id=1, source_target_pairs={{0,8},{2,10},{4,12},{6,14},{8,0},{10,2},{12,4},{14,6},{1,9},{3,11}... | collective-permute-start | bytes 245768 | tf_op jit(solution)/shard_map/ppermute | solution.py:112
  72.8 8.5 %all-to-all-start = ((f32[4,16,640]{2,1,0:T(8,128)}), f32[4,16,640]{2,1,0:T(8,128)S(1)}, u32[]{:S(2)}, u32[]{:S(2)}) async-start(f32[4,16,640]{2,1,0:T(8,128)} %bitcast.33), calls=%async_computation | async-start | bytes 327680 | tf_op jit(solution)/shard_map/all_to_all | solution.py:141
  107.0 10.8 %collective-permute-start.11 = (f32[8,8,640]{2,1,0:T(8,128)S(1)}, f32[8,8,640]{2,1,0:T(8,128)S(1)}, u32[]{:S(2)}, u32[]{:S(2)}) collective-permute-start(f32[8,8,640]{2,1,0:T(8,128)S(1)} %get-tuple-element.14), channel_id=1, source_target_pairs={{0,2},{2,0},{4,6},{6,4},{8,10},{10,8},{12,14},{14,12},{1,3},{3,1},... | collective-permute-start | bytes 491528 | tf_op jit(solution)/shard_map/ppermute | solution.py:112
  120.7 64.0 %all-to-all-start.2 = ((f32[16,2,8,8,640]{4,3,2,1,0:T(8,128)}), f32[16,2,8,8,640]{4,3,2,1,0:T(8,128)}, u32[]{:S(2)}, u32[]{:S(2)}) async-start(f32[16,2,8,8,640]{4,3,2,1,0:T(8,128)} %broadcast_in_dim.19), calls=%async_computation.2 | async-start | bytes 10485760 | tf_op jit(solution)/shard_map/all_to_all | solution.py:149
  125.6 21.3 %collective-permute-start.8 = (f32[1,2,32,640]{3,2,1,0:T(8,128)S(1)}, f32[1,2,32,640]{3,2,1,0:T(8,128)S(1)}, u32[]{:S(2)}, u32[]{:S(2)}) collective-permute-start(f32[1,2,32,640]{3,2,1,0:T(8,128)S(1)} %get-tuple-element.16), channel_id=1, source_target_pairs={{0,8},{2,10},{4,12},{6,14},{8,0},{10,2},{12,4},{14,6},{1,9},{3,11}... | collective-permute-start | bytes 491528 | tf_op jit(solution)/shard_map/ppermute | solution.py:112
  147.0 18.0 %collective-permute-start.9 = (f32[2,2,32,640]{3,2,1,0:T(8,128)S(1)}, f32[2,2,32,640]{3,2,1,0:T(8,128)S(1)}, u32[]{:S(2)}, u32[]{:S(2)}) collective-permute-start(f32[2,2,32,640]{3,2,1,0:T(8,128)S(1)} %pad_maximum_fusion.2), channel_id=1, source_target_pairs={{0,4},{2,6},{4,0},{6,2},{8,12},{10,14},{12,8},{14,10},{1,5},{3,7},... | collective-permute-start | bytes 983048 | tf_op jit(solution)/shard_map/ppermute | solution.py:112
  165.1 17.9 %collective-permute-start.10 = (f32[4,2,32,640]{3,2,1,0:T(8,128)S(1)}, f32[4,2,32,640]{3,2,1,0:T(8,128)S(1)}, u32[]{:S(2)}, u32[]{:S(2)}) collective-permute-start(f32[4,2,32,640]{3,2,1,0:T(8,128)S(1)} %pad_maximum_fusion.1), channel_id=1, source_target_pairs={{0,2},{2,0},{4,6},{6,4},{8,10},{10,8},{12,14},{14,12},{1,3},{3,1},... | collective-permute-start | bytes 1966088 | tf_op jit(solution)/shard_map/ppermute | solution.py:112
  189.7 15.9 %collective-permute-start.12 = (f32[256,512]{1,0:T(8,128)}, f32[256,512]{1,0:T(8,128)S(1)}, u32[]{:S(2)}, u32[]{:S(2)}) collective-permute-start(f32[256,512]{1,0:T(8,128)} %shard_map.43), channel_id=1, source_target_pairs={{0,1},{1,0},{2,3},{3,2},{4,5},{5,4},{6,7},{7,6},{8,9},{9,8},{10,11... | collective-permute-start | bytes 1572872 | tf_op jit(solution)/shard_map/ppermute | solution.py:112

commit v3 on v0

v3 whole, which is shorter than its diff:
```python
import jax
import jax.numpy as jnp
from jax import lax
from jax.experimental import pallas as pl
from jax.experimental.pallas import tpu as pltpu
from jax.sharding import Mesh, PartitionSpec as P

TILE = 128
VMEM = 60 * 1024 * 1024
NT = (((1,), (1,)), ((), ()))


def halves(value):
    high = value.astype(jnp.bfloat16)
    return high, (value - high.astype(jnp.float32)).astype(jnp.bfloat16)


def dot(a, b, dims=(((1,), (0,)), ((), ()))):
    return lax.dot_general(a, b, dims, preferred_element_type=jnp.float32)


def half_kernel(half_ref, mask_ref, a_ref, c_ref, *rest):
    *o_refs, chigh, clow, ahigh, alow = rest
    chunk = pl.program_id(0)
    parts, rows, lcols = a_ref.shape

    @pl.when(chunk == 0)
    def _():
        chigh[...], clow[...] = halves(c_ref[...])

    for p in range(parts):
        for j in range(lcols // TILE):
            at = (pl.ds(p * rows, rows), pl.ds(j * TILE, TILE))
            kept = mask_ref[p * mask_ref.shape[0] // parts, half_ref[0], j].astype(jnp.float32)
            ahigh[at], alow[at] = halves(a_ref[p, :, at[1]] * kept)
    total = dot(ahigh[...], chigh[...]) + (dot(ahigh[...], clow[...]) + dot(alow[...], chigh[...]))
    for k, o_ref in enumerate(o_refs):
        @pl.when(chunk == k)
        def _():
            o_ref[...] = total.reshape(o_ref.shape)


def half_of(integrals, mask, coeffs, half):
    parts, mrows, lcols = integrals.shape
    norbit = coeffs.shape[1]
    rows = mrows // 4
    return pl.pallas_call(
        half_kernel,
        out_shape=[jax.ShapeDtypeStruct((parts, rows, norbit), jnp.float32)] * 2,
        grid_spec=pltpu.PrefetchScalarGridSpec(
            num_scalar_prefetch=2,
            grid=(2,),
            in_specs=[
                pl.BlockSpec((parts, rows, lcols), lambda k, half, mask: (0, half[0] * 2 + k, 0)),
                pl.BlockSpec((lcols, norbit), lambda k, half, mask: (0, 0)),
            ],
            out_specs=[pl.BlockSpec((parts, rows, norbit), lambda k, half, mask: (0, 0, 0))] * 2,
            scratch_shapes=[pltpu.VMEM((lcols, norbit), jnp.bfloat16)] * 2
            + [pltpu.VMEM((parts * rows, lcols), jnp.bfloat16)] * 2,
        ),
        compiler_params=pltpu.CompilerParams(vmem_limit_bytes=VMEM),
        cost_estimate=pl.CostEstimate(flops=3 * parts * mrows * lcols * norbit, bytes_accessed=2 * parts * mrows * (lcols + norbit) + 4 * lcols * norbit, transcendentals=0),
    )(half.reshape(1), mask, integrals, coeffs)


def exchange_kernel(core_ref, mown_ref, moth_ref, nown_ref, noth_ref, o_ref, mhigh, mlow, nhigh, nlow):
    chunks, _, rows, norbit = mown_ref.shape
    blocks = nown_ref.shape[0]
    own = pl.multiple_of(core_ref[0] * chunks * rows, chunks * rows)
    oth = pl.multiple_of((1 - core_ref[0]) * chunks * rows, chunks * rows)

    @pl.when(pl.program_id(0) == 0)
    def _():
        for y in range(blocks):
            for k in range(chunks):
                for start, ref in ((own, nown_ref), (oth, noth_ref)):
                    at = pl.ds(start + (y * 2 * chunks + k) * rows, rows)
                    nhigh[at, :], nlow[at, :] = halves(ref[y, k])

    for k in range(chunks):
        for start, ref in ((own, mown_ref), (oth, moth_ref)):
            at = pl.ds(start + k * rows, rows)
            mhigh[at, :], mlow[at, :] = halves(ref[k, 0])
    o_ref[0] = dot(mhigh[...], nhigh[...], NT) + (dot(mhigh[...], nlow[...], NT) + dot(mlow[...], nhigh[...], NT))


def exchange_part(mown, moth, nown, noth, core):
    chunks, parts, rows, norbit = mown.shape
    blocks = nown.shape[0]
    mrows, ncols = 2 * chunks * rows, blocks * 2 * chunks * rows
    mspec = pl.BlockSpec((chunks, 1, rows, norbit), lambda x, core: (0, x, 0, 0))
    nspec = pl.BlockSpec(nown.shape, lambda x, core: (0, 0, 0, 0))
    return pl.pallas_call(
        exchange_kernel,
        out_shape=jax.ShapeDtypeStruct((parts, mrows, ncols), jnp.float32),
        grid_spec=pltpu.PrefetchScalarGridSpec(
            num_scalar_prefetch=1,
            grid=(parts,),
            in_specs=[mspec, mspec, nspec, nspec],
            out_specs=pl.BlockSpec((1, mrows, ncols), lambda x, core: (x, 0, 0)),
            scratch_shapes=[pltpu.VMEM((mrows, norbit), jnp.bfloat16)] * 2 + [pltpu.VMEM((ncols, norbit), jnp.bfloat16)] * 2,
        ),
        compiler_params=pltpu.CompilerParams(vmem_limit_bytes=VMEM),
        cost_estimate=pl.CostEstimate(flops=6 * parts * mrows * ncols * norbit, bytes_accessed=4 * norbit * (parts * mrows + ncols) + 4 * parts * mrows * ncols, transcendentals=0),
    )(core.reshape(1), mown, moth, nown, noth)


def swap(value, axis, bit, size):
    return lax.ppermute(value, axis, [(i, i ^ bit) for i in range(size)])


def pick(value, index, axis):
    return lax.dynamic_index_in_dim(value, index, axis, keepdims=False)


def join(own, got, bit, axis):
    return jnp.stack([jnp.where(bit == 0, own, got), jnp.where(bit == 0, got, own)], axis=axis)


def local(integrals, mask, coeffs):
    nslab, naux, mrows, lcols = integrals.shape
    norbit = coeffs.shape[1]
    core, zl, zh = lax.axis_index("core"), lax.axis_index("zl"), lax.axis_index("zh")
    low, mid = zl & 1, (zl >> 1) & 1
    parts = nslab * naux
    sub = mrows // 32
    chunks = (0, 1)
    integrals = integrals.reshape(parts, mrows, lcols)
    away = half_of(integrals, mask, coeffs, 1 - core)
    got = [swap(a, "core", 1, 2) for a in away]
    kept = half_of(integrals, mask, coeffs, core)
    part = [(v.reshape(parts, 2, 2, 2, sub, norbit), g.reshape(parts, 2, 2, 2, sub, norbit)) for v, g in zip(kept, got)]
    give = [pick(v, 1 - low, 3) + pick(g, 1 - low, 3) for v, g in part]
    keep = [pick(v, low, 3) + pick(g, low, 3) for v, g in part]
    part = [(v, swap(g, "zl", 1, 8)) for v, g in zip(keep, give)]
    give = [pick(v, 1 - mid, 2) + pick(g, 1 - mid, 2) for v, g in part]
    keep = [pick(v, mid, 2) + pick(g, mid, 2) for v, g in part]
    part = jnp.stack([v + swap(g, "zl", 2, 8) for v, g in zip(keep, give)], axis=1)
    part = lax.all_to_all(part, "x", split_axis=0, concat_axis=0)
    rows = []
    for k in chunks:
        m = part[:, k]
        m = m + swap(m, "zl", 4, 8)
        m = join(m, swap(m, "zl", 2, 8), mid, 2)
        m = join(m, swap(m, "zl", 1, 8), low, 3)
        rows.append(m.reshape(4, 8 * sub, norbit))
    mirror = [(z, 15 - z) for z in range(16) if z % 2 == (z < 8)]
    cols = []
    for m in rows:
        passed = lax.ppermute(pick(m, 3 - (zl >> 1), 0), ("zh", "zl"), mirror)
        cols.append(jnp.where(zh == low, pick(m, zl >> 1, 0), passed))
    cols = jnp.stack(cols)
    m = jnp.stack(rows)
    moth = swap(m, "core", 1, 2)
    n = lax.all_to_all(jnp.broadcast_to(cols[None], (4,) + cols.shape), "y", split_axis=0, concat_axis=0)
    n = n.reshape((2, 2) + cols.shape)
    nown, noth = pick(n, core, 0), swap(pick(n, 1 - core, 0), "core", 1, 2)
    partial = exchange_part(m, moth, nown, noth, core)
    partial = lax.all_to_all(partial, "x", split_axis=0, concat_axis=0)
    return jnp.sum(partial, axis=0) * (1.0 / jnp.sqrt(jnp.float32(norbit * parts)))


def solution(mesh):
    fine = Mesh(mesh.devices.reshape(4, 2, 4, 8, 2), ("x", "zh", "y", "zl", "core"))
    r, c = ("x", "zh", "y"), ("zl", "core")
    in_specs = (P(None, None, r, c), P(None, r, c), P(c, None))
    return jax.shard_map(local, mesh=fine, in_specs=in_specs, out_specs=P(r, c), check_vma=False)
```

time: 563 us -> 210 us (0.37)
  the two profiles are of different devices: /device:TPU:1 before, /device:TPU:32 now
where the time goes in v3:
time: 210 us
  starting transfers between devices  76.6 us (36%)
  waiting for transfers between devices  68 us (32%)
  blocking collectives  40.4 us (19%)
  Pallas kernels  16.7 us (8%)
  other arithmetic  4.31 us (2%)
  local copies, waits for them, and re-layouts  3.07 us (1%)
    ppermute x14, starting transfers between devices, swap(): return lax.ppermute(value, axis, [(i, i ^ bit) for i in range(size)])  54.9 us
    ppermute x14, waiting for transfers between devices, swap(): return lax.ppermute(value, axis, [(i, i ^ bit) for i in range(size)])  50.7 us
    all_to_all x1, blocking collectives, local(): partial = lax.all_to_all(partial, 'x', split_axis=0, concat_axis=0)  30.5 us
    ppermute x2, starting transfers between devices, local(): passed = lax.ppermute(pick(m, 3 - (zl >> 1), 0), ('zh', 'zl'), mirror)  17.2 us
    all_to_all x1, waiting for transfers between devices, local(): lax.all_to_all(jnp.broadcast_to(cols[None], (4,) + cols.shape), 'y', spli...  12.7 us
    pallas_call x2, Pallas kernels, half_of(): pl.pallas_call(half_kernel, out_shape=[jax.ShapeDtypeStruct((parts, rows,...  10.3 us
    all_to_all x1, blocking collectives, local(): part = lax.all_to_all(part, 'x', split_axis=0, concat_axis=0)  9.94 us
    pallas_call x1, Pallas kernels, exchange_part(): pl.pallas_call(exchange_kernel, out_shape=jax.ShapeDtypeStruct((parts, mr...  6.43 us
  transfers between devices with their start and end apart: 17, of which 11 were waited for; matrix products, arithmetic and copies ran while one was open for 1% of the time, Pallas kernels for 2%

profile of v3, /device:TPU:32, one launch (start us, length us, event | category | flops | bytes accessed | tf_op | source)
XLA Modules:
  0.0 209.5 jit_solution(10583456672360503735)
XLA Ops:
  0.0 5.2 %shard_map.38 = (f32[4,64,640]{2,1,0:T(8,128)}, f32[4,64,640]{2,1,0:T(8,128)}) custom-call(s32[1]{0:T(128)} %bitcast.3.half_ref, s32[2,2,4]{2,1,0:T(2,128)} %mask_ref.3, f32[4,256,512]{2,1,0:T(8,128)} %bitcast.115, f32[512,640]{1,0:T(8,128)} %c_ref.3), custom_call_target="tpu_custom_call" | custom-call | flops 1006632960 | bytes 3670016 | tf_op jit(solution)/shard_map/pallas_call | solution.py:47
  5.2 1.9 collective-permute-start
  7.1 2.4 %collective-permute-start.3 = (f32[4,64,640]{2,1,0:T(8,128)}, f32[4,64,640]{2,1,0:T(8,128)S(1)}, u32[]{:S(2)}, u32[]{:S(2)}) collective-permute-start(f32[4,64,640]{2,1,0:T(8,128)} %get-tuple-element.12), channel_id=1, source_target_pairs={{0,1},{1,0},{2,3},{3,2},{4,5},{5,4},{6,7},{7,6},{8,9},{9,8},{10,11... | collective-permute-start | bytes 1966088 | tf_op jit(solution)/shard_map/ppermute | solution.py:109
  9.5 5.2 %shard_map.37 = (f32[4,64,640]{2,1,0:T(8,128)}, f32[4,64,640]{2,1,0:T(8,128)}) custom-call(s32[1]{0:T(128)} %bitcast.half_ref.core_ref, s32[2,2,4]{2,1,0:T(2,128)} %mask_ref.3, f32[4,256,512]{2,1,0:T(8,128)} %bitcast.116, f32[512,640]{1,0:T(8,128)} %c_ref.3), custom_call_target="tpu_custom_call" | custom-call | flops 1006632960 | bytes 3670016 | tf_op jit(solution)/shard_map/pallas_call | solution.py:47
  16.2 7.4 %collective-permute-start.1 = (f32[4,2,2,8,640]{4,3,1,0,2:T(8,128)S(1)}, f32[4,2,2,8,640]{4,3,1,0,2:T(8,128)S(1)}, u32[]{:S(2)}, u32[]{:S(2)}) collective-permute-start(f32[4,2,2,8,640]{4,3,1,0,2:T(8,128)S(1)} %fusion.1), channel_id=1, source_target_pairs={{0,2},{2,0},{4,6},{6,4},{8,10},{10,8},{12,14},{14,12},{1,3},{3,1},... | collective-permute-start | bytes 983048 | tf_op jit(solution)/shard_map/ppermute | solution.py:109
  23.6 1.9 collective-permute-start.4
  25.5 6.5 %collective-permute-done.1 = f32[4,2,2,8,640]{4,3,1,0,2:T(8,128)S(1)} collective-permute-done((f32[4,2,2,8,640]{4,3,1,0,2:T(8,128)S(1)}, f32[4,2,2,8,640]{4,3,1,0,2:T(8,128)S(1)}, u32[]{:S(2)}, u32[]{:S(2)}) %collective-permute-start.1) | collective-permute-done | bytes 327712 | tf_op jit(solution)/shard_map/ppermute | solution.py:109
  32.1 1.9 collective-permute-start.2
  34.0 5.1 %collective-permute-done.4 = f32[4,2,2,8,640]{4,3,1,0,2:T(8,128)S(1)} collective-permute-done((f32[4,2,2,8,640]{4,3,1,0,2:T(8,128)S(1)}, f32[4,2,2,8,640]{4,3,1,0,2:T(8,128)S(1)}, u32[]{:S(2)}, u32[]{:S(2)}) %collective-permute-start.4) | collective-permute-done | bytes 327712 | tf_op jit(solution)/shard_map/ppermute | solution.py:109
  39.1 4.3 %collective-permute-start.5 = (f32[4,2,8,640]{3,2,1,0:T(8,128)S(1)}, f32[4,2,8,640]{3,2,1,0:T(8,128)S(1)}, u32[]{:S(2)}, u32[]{:S(2)}) collective-permute-start(f32[4,2,8,640]{3,2,1,0:T(8,128)S(1)} %fusion.4), channel_id=1, source_target_pairs={{0,4},{2,6},{4,0},{6,2},{8,12},{10,14},{12,8},{14,10},{1,5},{3,7},... | collective-permute-start | bytes 491528 | tf_op jit(solution)/shard_map/ppermute | solution.py:109
  43.5 4.8 %collective-permute-done.5 = f32[4,2,8,640]{3,2,1,0:T(8,128)S(1)} collective-permute-done((f32[4,2,8,640]{3,2,1,0:T(8,128)S(1)}, f32[4,2,8,640]{3,2,1,0:T(8,128)S(1)}, u32[]{:S(2)}, u32[]{:S(2)}) %collective-permute-start.5) | collective-permute-done | bytes 163872 | tf_op jit(solution)/shard_map/ppermute | solution.py:109
  48.3 9.9 %all_to_all.15 = f32[4,2,2,8,640]{4,3,2,1,0:T(8,128)S(1)} all-to-all(f32[4,2,2,8,640]{4,3,2,1,0:T(8,128)S(1)} %pad_maximum_fusion.3), channel_id=1, replica_groups=mesh['x'=4,'zh'=2,'y'=4,'zl'=8,'core'=2] {'x'}, dimensions={0} | all-to-all | bytes 655360 | tf_op jit(solution)/shard_map/all_to_all | solution.py:139
  58.3 9.1 %collective-permute-start.6 = (f32[4,2,8,640]{3,2,1,0:T(8,128)S(1)}, f32[4,2,8,640]{3,2,1,0:T(8,128)S(1)}, u32[]{:S(2)}, u32[]{:S(2)}) collective-permute-start(f32[4,2,8,640]{3,2,1,0:T(8,128)S(1)} %get-tuple-element.29), channel_id=1, source_target_pairs={{0,8},{2,10},{4,12},{6,14},{8,0},{10,2},{12,4},{14,6},{1,9},{3,11}... | collective-permute-start | bytes 491528 | tf_op jit(solution)/shard_map/ppermute | solution.py:109
  67.4 1.9 collective-permute-start.9
  69.3 16.6 %collective-permute-done.6 = f32[4,2,8,640]{3,2,1,0:T(8,128)S(1)} collective-permute-done((f32[4,2,8,640]{3,2,1,0:T(8,128)S(1)}, f32[4,2,8,640]{3,2,1,0:T(8,128)S(1)}, u32[]{:S(2)}, u32[]{:S(2)}) %collective-permute-start.6) | collective-permute-done | bytes 163872 | tf_op jit(solution)/shard_map/ppermute | solution.py:109
  85.9 2.3 %collective-permute-done.9 = f32[4,2,8,640]{3,2,1,0:T(8,128)S(1)} collective-permute-done((f32[4,2,8,640]{3,2,1,0:T(8,128)S(1)}, f32[4,2,8,640]{3,2,1,0:T(8,128)S(1)}, u32[]{:S(2)}, u32[]{:S(2)}) %collective-permute-start.9) | collective-permute-done | bytes 163872 | tf_op jit(solution)/shard_map/ppermute | solution.py:109
  88.2 10.4 %collective-permute-start.7 = (f32[4,2,8,640]{3,2,1,0:T(8,128)S(1)}, f32[4,2,8,640]{3,2,1,0:T(8,128)S(1)}, u32[]{:S(2)}, u32[]{:S(2)}) collective-permute-start(f32[4,2,8,640]{3,2,1,0:T(8,128)S(1)} %get-tuple-element.27), channel_id=1, source_target_pairs={{0,4},{2,6},{4,0},{6,2},{8,12},{10,14},{12,8},{14,10},{1,5},{3,7},... | collective-permute-start | bytes 491528 | tf_op jit(solution)/shard_map/ppermute | solution.py:109
  98.7 1.9 collective-permute-start.10
  100.6 8.4 %collective-permute-done.7 = f32[4,2,8,640]{3,2,1,0:T(8,128)S(1)} collective-permute-done((f32[4,2,8,640]{3,2,1,0:T(8,128)S(1)}, f32[4,2,8,640]{3,2,1,0:T(8,128)S(1)}, u32[]{:S(2)}, u32[]{:S(2)}) %collective-permute-start.7) | collective-permute-done | bytes 163872 | tf_op jit(solution)/shard_map/ppermute | solution.py:109
  109.0 4.5 %collective-permute-start.8 = (f32[4,2,2,8,640]{4,3,2,1,0:T(8,128)S(1)}, f32[4,2,2,8,640]{4,3,2,1,0:T(8,128)S(1)}, u32[]{:S(2)}, u32[]{:S(2)}) collective-permute-start(f32[4,2,2,8,640]{4,3,2,1,0:T(8,128)S(1)} %pad_maximum_fusion.4), channel_id=1, source_target_pairs={{0,2},{2,0},{4,6},{6,4},{8,10},{10,8},{12,14},{14,12},{1,3},{3,1},... | collective-permute-start | bytes 983048 | tf_op jit(solution)/shard_map/ppermute | solution.py:109
  113.6 3.3 %collective-permute-start.11 = (f32[4,2,2,8,640]{4,3,2,1,0:T(8,128)S(1)}, f32[4,2,2,8,640]{4,3,2,1,0:T(8,128)S(1)}, u32[]{:S(2)}, u32[]{:S(2)}) collective-permute-start(f32[4,2,2,8,640]{4,3,2,1,0:T(8,128)S(1)} %pad_maximum_fusion.5), channel_id=1, source_target_pairs={{0,2},{2,0},{4,6},{6,4},{8,10},{10,8},{12,14},{14,12},{1,3},{3,1},... | collective-permute-start | bytes 983048 | tf_op jit(solution)/shard_map/ppermute | solution.py:109
  117.0 5.1 %collective-permute-done.8 = f32[4,2,2,8,640]{4,3,2,1,0:T(8,128)S(1)} collective-permute-done((f32[4,2,2,8,640]{4,3,2,1,0:T(8,128)S(1)}, f32[4,2,2,8,640]{4,3,2,1,0:T(8,128)S(1)}, u32[]{:S(2)}, u32[]{:S(2)}) %collective-permute-start.8) | collective-permute-done | bytes 327712 | tf_op jit(solution)/shard_map/ppermute | solution.py:109
  122.2 7.5 %collective-permute-start.13 = (f32[64,640]{1,0:T(8,128)S(1)}, f32[64,640]{1,0:T(8,128)S(1)}, u32[]{:S(2)}, u32[]{:S(2)}) collective-permute-start(f32[64,640]{1,0:T(8,128)S(1)} %dynamic-slice_bitcast_fusion.3), channel_id=1, source_target_pairs={{2,76},{6,72},{10,68},{14,64},{64,14},{68,10},{72,6},{76,2},{3,77}... | collective-permute-start | bytes 491528 | tf_op jit(solution)/shard_map/ppermute | solution.py:150
  129.9 9.8 %collective-permute-start.14 = (f32[64,640]{1,0:T(8,128)S(1)}, f32[64,640]{1,0:T(8,128)S(1)}, u32[]{:S(2)}, u32[]{:S(2)}) collective-permute-start(f32[64,640]{1,0:T(8,128)S(1)} %dynamic-slice_bitcast_fusion.2), channel_id=1, source_target_pairs={{2,76},{6,72},{10,68},{14,64},{64,14},{68,10},{72,6},{76,2},{3,77}... | collective-permute-start | bytes 491528 | tf_op jit(solution)/shard_map/ppermute | solution.py:150
  139.7 2.9 %collective-permute-done.13 = f32[64,640]{1,0:T(8,128)S(1)} collective-permute-done((f32[64,640]{1,0:T(8,128)S(1)}, f32[64,640]{1,0:T(8,128)S(1)}, u32[]{:S(2)}, u32[]{:S(2)}) %collective-permute-start.13) | collective-permute-done | bytes 163872 | tf_op jit(solution)/shard_map/ppermute | solution.py:150
  145.6 4.4 %all-to-all-start.1 = ((f32[4,2,64,640]{3,2,1,0:T(8,128)}), f32[4,2,64,640]{3,2,1,0:T(8,128)S(1)}, u32[]{:S(2)}, u32[]{:S(2)}) async-start(f32[4,2,64,640]{3,2,1,0:T(8,128)} %broadcast_in_dim.2), calls=%async_computation.1 | async-start | bytes 2621440 | tf_op jit(solution)/shard_map/all_to_all | solution.py:155
  151.2 1.9 collective-permute-start.12
  153.1 12.7 %all-to-all-done.1 = f32[4,2,64,640]{3,2,1,0:T(8,128)S(1)} async-done(((f32[4,2,64,640]{3,2,1,0:T(8,128)}), f32[4,2,64,640]{3,2,1,0:T(8,128)S(1)}, u32[]{:S(2)}, u32[]{:S(2)}) %all-to-all-start.1) | async-done | bytes 1310752 | tf_op jit(solution)/shard_map/all_to_all | solution.py:155
  166.7 1.9 collective-permute-start.15
  168.6 2.0 collective-permute-done.15.noth_ref
  171.5 6.4 %shard_map.39 = f32[4,256,512]{2,1,0:T(8,128)} custom-call(s32[1]{0:T(128)} %bitcast.half_ref.core_ref, f32[2,4,64,640]{3,2,1,0:T(8,128)} %pad_maximum_fusion.mown_ref, f32[2,4,64,640]{3,2,1,0:T(8,128)} %copy-done, f32[2,2,64,640]{3,2,1,0:T(8,128)} %get-tuple-element.14.nown_ref, f32[2,2,64,640]{3,2,1,0:T(8,128)} %copy-done.1), custom_call_target="tpu_custom_call" | custom-call | flops 2013265920 | bytes 6029312 | tf_op jit(solution)/shard_map/pallas_call | solution.py:93
  177.9 30.5 %all_to_all.16 = f32[4,256,512]{2,1,0:T(8,128)S(1)} all-to-all(f32[4,256,512]{2,1,0:T(8,128)} %shard_map.39), channel_id=1, replica_groups=mesh['x'=4,'zh'=2,'y'=4,'zl'=8,'core'=2] {'x'}, dimensions={0} | all-to-all | bytes 4194304 | tf_op jit(solution)/shard_map/all_to_all | solution.py:159
  (40 shorter events, 9.1 us)
Async XLA Ops:
  5.2 9.5 %collective-permute-start = (f32[4,64,640]{2,1,0:T(8,128)}, f32[4,64,640]{2,1,0:T(8,128)S(1)}, u32[]{:S(2)}, u32[]{:S(2)}) collective-permute-start(f32[4,64,640]{2,1,0:T(8,128)} %get-tuple-element.10), channel_id=1, source_target_pairs={{0,1},{1,0},{2,3},{3,2},{4,5},{5,4},{6,7},{7,6},{8,9},{9,8},{10,11... | collective-permute-start | bytes 1966088 | tf_op jit(solution)/shard_map/ppermute | solution.py:109
  7.1 7.6 %collective-permute-start.3 = (f32[4,64,640]{2,1,0:T(8,128)}, f32[4,64,640]{2,1,0:T(8,128)S(1)}, u32[]{:S(2)}, u32[]{:S(2)}) collective-permute-start(f32[4,64,640]{2,1,0:T(8,128)} %get-tuple-element.12), channel_id=1, source_target_pairs={{0,1},{1,0},{2,3},{3,2},{4,5},{5,4},{6,7},{7,6},{8,9},{9,8},{10,11... | collective-permute-start | bytes 1966088 | tf_op jit(solution)/shard_map/ppermute | solution.py:109
  16.2 15.9 %collective-permute-start.1 = (f32[4,2,2,8,640]{4,3,1,0,2:T(8,128)S(1)}, f32[4,2,2,8,640]{4,3,1,0,2:T(8,128)S(1)}, u32[]{:S(2)}, u32[]{:S(2)}) collective-permute-start(f32[4,2,2,8,640]{4,3,1,0,2:T(8,128)S(1)} %fusion.1), channel_id=1, source_target_pairs={{0,2},{2,0},{4,6},{6,4},{8,10},{10,8},{12,14},{14,12},{1,3},{3,1},... | collective-permute-start | bytes 983048 | tf_op jit(solution)/shard_map/ppermute | solution.py:109
  23.6 15.5 %collective-permute-start.4 = (f32[4,2,2,8,640]{4,3,1,0,2:T(8,128)S(1)}, f32[4,2,2,8,640]{4,3,1,0,2:T(8,128)S(1)}, u32[]{:S(2)}, u32[]{:S(2)}) collective-permute-start(f32[4,2,2,8,640]{4,3,1,0,2:T(8,128)S(1)} %fusion), channel_id=1, source_target_pairs={{0,2},{2,0},{4,6},{6,4},{8,10},{10,8},{12,14},{14,12},{1,3},{3,1},... | collective-permute-start | bytes 983048 | tf_op jit(solution)/shard_map/ppermute | solution.py:109
  32.1 11.3 %collective-permute-start.2 = (f32[4,2,8,640]{3,2,1,0:T(8,128)S(1)}, f32[4,2,8,640]{3,2,1,0:T(8,128)S(1)}, u32[]{:S(2)}, u32[]{:S(2)}) collective-permute-start(f32[4,2,8,640]{3,2,1,0:T(8,128)S(1)} %fusion.6), channel_id=1, source_target_pairs={{0,4},{2,6},{4,0},{6,2},{8,12},{10,14},{12,8},{14,10},{1,5},{3,7},... | collective-permute-start | bytes 491528 | tf_op jit(solution)/shard_map/ppermute | solution.py:109
  39.1 9.2 %collective-permute-start.5 = (f32[4,2,8,640]{3,2,1,0:T(8,128)S(1)}, f32[4,2,8,640]{3,2,1,0:T(8,128)S(1)}, u32[]{:S(2)}, u32[]{:S(2)}) collective-permute-start(f32[4,2,8,640]{3,2,1,0:T(8,128)S(1)} %fusion.4), channel_id=1, source_target_pairs={{0,4},{2,6},{4,0},{6,2},{8,12},{10,14},{12,8},{14,10},{1,5},{3,7},... | collective-permute-start | bytes 491528 | tf_op jit(solution)/shard_map/ppermute | solution.py:109
  58.3 27.6 %collective-permute-start.6 = (f32[4,2,8,640]{3,2,1,0:T(8,128)S(1)}, f32[4,2,8,640]{3,2,1,0:T(8,128)S(1)}, u32[]{:S(2)}, u32[]{:S(2)}) collective-permute-start(f32[4,2,8,640]{3,2,1,0:T(8,128)S(1)} %get-tuple-element.29), channel_id=1, source_target_pairs={{0,8},{2,10},{4,12},{6,14},{8,0},{10,2},{12,4},{14,6},{1,9},{3,11}... | collective-permute-start | bytes 491528 | tf_op jit(solution)/shard_map/ppermute | solution.py:109
  67.4 20.7 %collective-permute-start.9 = (f32[4,2,8,640]{3,2,1,0:T(8,128)S(1)}, f32[4,2,8,640]{3,2,1,0:T(8,128)S(1)}, u32[]{:S(2)}, u32[]{:S(2)}) collective-permute-start(f32[4,2,8,640]{3,2,1,0:T(8,128)S(1)} %get-tuple-element.30), channel_id=1, source_target_pairs={{0,8},{2,10},{4,12},{6,14},{8,0},{10,2},{12,4},{14,6},{1,9},{3,11}... | collective-permute-start | bytes 491528 | tf_op jit(solution)/shard_map/ppermute | solution.py:109
  88.2 20.8 %collective-permute-start.7 = (f32[4,2,8,640]{3,2,1,0:T(8,128)S(1)}, f32[4,2,8,640]{3,2,1,0:T(8,128)S(1)}, u32[]{:S(2)}, u32[]{:S(2)}) collective-permute-start(f32[4,2,8,640]{3,2,1,0:T(8,128)S(1)} %get-tuple-element.27), channel_id=1, source_target_pairs={{0,4},{2,6},{4,0},{6,2},{8,12},{10,14},{12,8},{14,10},{1,5},{3,7},... | collective-permute-start | bytes 491528 | tf_op jit(solution)/shard_map/ppermute | solution.py:109
  98.7 14.9 %collective-permute-start.10 = (f32[4,2,8,640]{3,2,1,0:T(8,128)S(1)}, f32[4,2,8,640]{3,2,1,0:T(8,128)S(1)}, u32[]{:S(2)}, u32[]{:S(2)}) collective-permute-start(f32[4,2,8,640]{3,2,1,0:T(8,128)S(1)} %get-tuple-element.28), channel_id=1, source_target_pairs={{0,4},{2,6},{4,0},{6,2},{8,12},{10,14},{12,8},{14,10},{1,5},{3,7},... | collective-permute-start | bytes 491528 | tf_op jit(solution)/shard_map/ppermute | solution.py:109
  109.0 13.1 %collective-permute-start.8 = (f32[4,2,2,8,640]{4,3,2,1,0:T(8,128)S(1)}, f32[4,2,2,8,640]{4,3,2,1,0:T(8,128)S(1)}, u32[]{:S(2)}, u32[]{:S(2)}) collective-permute-start(f32[4,2,2,8,640]{4,3,2,1,0:T(8,128)S(1)} %pad_maximum_fusion.4), channel_id=1, source_target_pairs={{0,2},{2,0},{4,6},{6,4},{8,10},{10,8},{12,14},{14,12},{1,3},{3,1},... | collective-permute-start | bytes 983048 | tf_op jit(solution)/shard_map/ppermute | solution.py:109
  113.6 16.1 %collective-permute-start.11 = (f32[4,2,2,8,640]{4,3,2,1,0:T(8,128)S(1)}, f32[4,2,2,8,640]{4,3,2,1,0:T(8,128)S(1)}, u32[]{:S(2)}, u32[]{:S(2)}) collective-permute-start(f32[4,2,2,8,640]{4,3,2,1,0:T(8,128)S(1)} %pad_maximum_fusion.5), channel_id=1, source_target_pairs={{0,2},{2,0},{4,6},{6,4},{8,10},{10,8},{12,14},{14,12},{1,3},{3,1},... | collective-permute-start | bytes 983048 | tf_op jit(solution)/shard_map/ppermute | solution.py:109
  122.2 20.4 %collective-permute-start.13 = (f32[64,640]{1,0:T(8,128)S(1)}, f32[64,640]{1,0:T(8,128)S(1)}, u32[]{:S(2)}, u32[]{:S(2)}) collective-permute-start(f32[64,640]{1,0:T(8,128)S(1)} %dynamic-slice_bitcast_fusion.3), channel_id=1, source_target_pairs={{2,76},{6,72},{10,68},{14,64},{64,14},{68,10},{72,6},{76,2},{3,77}... | collective-permute-start | bytes 491528 | tf_op jit(solution)/shard_map/ppermute | solution.py:150
  129.9 14.4 %collective-permute-start.14 = (f32[64,640]{1,0:T(8,128)S(1)}, f32[64,640]{1,0:T(8,128)S(1)}, u32[]{:S(2)}, u32[]{:S(2)}) collective-permute-start(f32[64,640]{1,0:T(8,128)S(1)} %dynamic-slice_bitcast_fusion.2), channel_id=1, source_target_pairs={{2,76},{6,72},{10,68},{14,64},{64,14},{68,10},{72,6},{76,2},{3,77}... | collective-permute-start | bytes 491528 | tf_op jit(solution)/shard_map/ppermute | solution.py:150
  145.6 20.2 %all-to-all-start.1 = ((f32[4,2,64,640]{3,2,1,0:T(8,128)}), f32[4,2,64,640]{3,2,1,0:T(8,128)S(1)}, u32[]{:S(2)}, u32[]{:S(2)}) async-start(f32[4,2,64,640]{3,2,1,0:T(8,128)} %broadcast_in_dim.2), calls=%async_computation.1 | async-start | bytes 2621440 | tf_op jit(solution)/shard_map/all_to_all | solution.py:155
  151.2 17.4 %collective-permute-start.12 = (f32[2,4,64,640]{3,2,1,0:T(8,128)}, f32[2,4,64,640]{3,2,1,0:T(8,128)S(1)}, u32[]{:S(2)}, u32[]{:S(2)}) collective-permute-start(f32[2,4,64,640]{3,2,1,0:T(8,128)} %pad_maximum_fusion.mown_ref), channel_id=1, source_target_pairs={{0,1},{1,0},{2,3},{3,2},{4,5},{5,4},{6,7},{7,6},{8,9},{9,8},{10,11... | collective-permute-start | bytes 3932168 | tf_op jit(solution)/shard_map/ppermute | solution.py:109
  166.7 4.0 %collective-permute-start.15 = (f32[2,2,64,640]{3,2,1,0:T(8,128)S(1)}, f32[2,2,64,640]{3,2,1,0:T(8,128)S(1)}, u32[]{:S(2)}, u32[]{:S(2)}) collective-permute-start(f32[2,2,64,640]{3,2,1,0:T(8,128)S(1)} %get-tuple-element.13), channel_id=1, source_target_pairs={{0,1},{1,0},{2,3},{3,2},{4,5},{5,4},{6,7},{7,6},{8,9},{9,8},{10,11... | collective-permute-start | bytes 1966088 | tf_op jit(solution)/shard_map/ppermute | solution.py:109
  168.6 2.1 copy-start
  170.7 0.8 copy-start.1

commit v4 on v2

v4 whole, which is shorter than its diff:
```python
import jax
import jax.numpy as jnp
from jax import lax
from jax.experimental import pallas as pl
from jax.experimental.pallas import tpu as pltpu
from jax.sharding import Mesh, PartitionSpec as P

TILE = 128
VMEM = 60 * 1024 * 1024
NT = (((1,), (1,)), ((), ()))


def halves(value):
    high = value.astype(jnp.bfloat16)
    return high, (value - high.astype(jnp.float32)).astype(jnp.bfloat16)


def dot(a, b, dims=(((1,), (0,)), ((), ()))):
    return lax.dot_general(a, b, dims, preferred_element_type=jnp.float32)


def half_kernel(slab_ref, mask_ref, a_ref, c_ref, *rest):
    *o_refs, chigh, clow, ahigh, alow = rest
    aux = pl.program_id(0)

    @pl.when(aux == 0)
    def _():
        chigh[...], clow[...] = halves(c_ref[...])

    slab = slab_ref[0]
    for i in range(a_ref.shape[2] // TILE):
        for j in range(a_ref.shape[3] // TILE):
            at = (pl.ds(i * TILE, TILE), pl.ds(j * TILE, TILE))
            kept = mask_ref[slab, i, j].astype(jnp.float32)
            ahigh[at], alow[at] = halves(a_ref[0, 0, at[0], at[1]] * kept)
    total = dot(ahigh[...], chigh[...]) + (dot(ahigh[...], clow[...]) + dot(alow[...], chigh[...]))
    for k, o_ref in enumerate(o_refs):
        @pl.when(aux == k)
        def _():
            o_ref[...] = total


def half_of(integrals, mask, coeffs, slab):
    _, naux, mrows, lcols = integrals.shape
    norbit = coeffs.shape[1]
    return pl.pallas_call(
        half_kernel,
        out_shape=[jax.ShapeDtypeStruct((mrows, norbit), jnp.float32)] * naux,
        grid_spec=pltpu.PrefetchScalarGridSpec(
            num_scalar_prefetch=2,
            grid=(naux,),
            in_specs=[
                pl.BlockSpec((1, 1, mrows, lcols), lambda a, slab, mask: (slab[0], a, 0, 0)),
                pl.BlockSpec((lcols, norbit), lambda a, slab, mask: (0, 0)),
            ],
            out_specs=[pl.BlockSpec((mrows, norbit), lambda a, slab, mask: (0, 0))] * naux,
            scratch_shapes=[pltpu.VMEM((lcols, norbit), jnp.bfloat16)] * 2
            + [pltpu.VMEM((mrows, lcols), jnp.bfloat16)] * 2,
        ),
        compiler_params=pltpu.CompilerParams(vmem_limit_bytes=VMEM),
        cost_estimate=pl.CostEstimate(flops=6 * naux * mrows * lcols * norbit, bytes_accessed=4 * naux * mrows * (lcols + norbit) + 4 * lcols * norbit, transcendentals=0),
    )(slab.reshape(1), mask, integrals, coeffs)


def exchange_kernel(place_ref, m_ref, n_ref, sent_ref, held_ref, mhigh, mlow, nhigh, nlow):
    lanes, naux, tops, rows, norbit = m_ref.shape
    sub = n_ref.shape[5]
    step = pl.program_id(0)

    @pl.when(step == 0)
    def _():
        for lane in range(lanes):
            for top in range(tops):
                at = pl.ds(pl.multiple_of((top * lanes + place_ref[1 + lane]) * rows, rows), rows)
                for a in range(naux):
                    mhigh[a, at, :], mlow[a, at, :] = halves(m_ref[lane, a, top])

    total = None
    for a in range(naux):
        for h in range(2):
            for top in range(tops):
                for lane in range(lanes):
                    at = pl.ds((top * lanes + lane) * rows + h * 2 * sub, 2 * sub)
                    both = jnp.concatenate([n_ref[a * 2 + h, 0, k, lane, top] for k in range(2)], axis=0)
                    nhigh[a, at, :], nlow[a, at, :] = halves(both)
        term = dot(mhigh[a], nhigh[a], NT) + (dot(mhigh[a], nlow[a], NT) + dot(mlow[a], nhigh[a], NT))
        total = term if total is None else total + term

    @pl.when(step < 2)
    def _():
        sent_ref[...] = total

    @pl.when(step >= 2)
    def _():
        held_ref[...] = total


def exchange_part(m, n, place):
    lanes, naux, tops, rows, norbit = m.shape
    blocks = n.shape[1]
    mrows = lanes * tops * rows
    half = jax.ShapeDtypeStruct((mrows, blocks // 2 * mrows), jnp.float32)
    return pl.pallas_call(
        exchange_kernel,
        out_shape=(half, half),
        grid_spec=pltpu.PrefetchScalarGridSpec(
            num_scalar_prefetch=1,
            grid=(blocks,),
            in_specs=[
                pl.BlockSpec(m.shape, lambda g, place: (0,) * 5),
                pl.BlockSpec(n.shape[:1] + (1,) + n.shape[2:], lambda g, place: (0, (g + 2 * (1 - place[0])) % 4, 0, 0, 0, 0, 0)),
            ],
            out_specs=(
                pl.BlockSpec((mrows, mrows), lambda g, place: (0, jnp.minimum(g, 1))),
                pl.BlockSpec((mrows, mrows), lambda g, place: (0, jnp.maximum(g - 2, 0))),
            ),
            scratch_shapes=[pltpu.VMEM((naux, mrows, norbit), jnp.bfloat16)] * 4,
        ),
        compiler_params=pltpu.CompilerParams(vmem_limit_bytes=VMEM),
        cost_estimate=pl.CostEstimate(flops=6 * naux * blocks * mrows * mrows * norbit, bytes_accessed=4 * naux * mrows * norbit * (blocks + 1) + 4 * blocks * mrows * mrows, transcendentals=0),
    )(place, m, n)


def swap(value, axis, bit, size):
    return lax.ppermute(value, axis, [(i, i ^ bit) for i in range(size)])


def pick(value, index, axis):
    return lax.dynamic_index_in_dim(value, index, axis, keepdims=False)


def local(integrals, mask, coeffs):
    nslab, naux, mrows, lcols = integrals.shape
    norbit = coeffs.shape[1]
    core, zl, zh = lax.axis_index("core"), lax.axis_index("zl"), lax.axis_index("zh")
    rows, sub = mrows // 8, mrows // 32
    low, mid = zl & 1, (zl >> 1) & 1
    away = half_of(integrals, mask, coeffs, 1 - core)
    got = [swap(a, "core", 1, 2) for a in away]
    kept = half_of(integrals, mask, coeffs, core)
    part = [(k.reshape(4, 2, rows, norbit), g.reshape(4, 2, rows, norbit)) for k, g in zip(kept, got)]
    give = [pick(k, 1 - low, 1) + pick(g, 1 - low, 1) for k, g in part]
    keep = [pick(k, low, 1) + pick(g, low, 1) for k, g in part]
    part = [(k.reshape(2, 2, rows, norbit), swap(g, "zl", 1, 8).reshape(2, 2, rows, norbit)) for k, g in zip(keep, give)]
    give = [pick(k, 1 - mid, 1) + pick(g, 1 - mid, 1) for k, g in part]
    keep = [pick(k, mid, 1) + pick(g, mid, 1) for k, g in part]
    m = jnp.stack([k + swap(g, "zl", 2, 8) for k, g in zip(keep, give)])
    pieces = jnp.swapaxes(m.reshape(naux, 2, 2, 2 * sub, norbit), 1, 2).reshape(2 * naux, 2, 2 * sub, norbit)
    pieces = lax.all_to_all(pieces, "x", split_axis=0, concat_axis=0)
    pieces = jnp.swapaxes(pieces.reshape(4, 2, 2, sub, norbit), 1, 2)
    handed = jnp.where(zh == 0, pieces, pieces[:, ::-1]).reshape(1, 8, 2, sub, norbit)
    handed = jnp.broadcast_to(handed, (2, 8, 2, sub, norbit)).reshape(16, 2, sub, norbit)
    moved = lax.all_to_all(handed, ("zh", "zl"), split_axis=0, concat_axis=0).reshape(2, 2, 4, 2, sub, norbit)
    other = pick(moved, 1 - low, 0)
    other = swap(other[0] + other[1], "zl", 1, 8)
    moved = pick(moved, low, 0)
    mine = jnp.stack([moved[0] + moved[1], other])
    m, mine = lax.optimization_barrier((m, mine))
    copies = jnp.broadcast_to(mine[None], (16,) + mine.shape)
    n = lax.all_to_all(copies, ("x", "y"), split_axis=0, concat_axis=0)
    n = n.reshape((4, 4) + mine.shape)
    m = (m + swap(m, "zl", 4, 8))[None]
    order = [0]
    for bit in (2, 1):
        m = jnp.concatenate([m, swap(m, "zl", bit, 8)])
        order = order + [k ^ bit for k in order]
    sent, held = exchange_part(m, n, jnp.stack([core] + [(zl ^ k) & 3 for k in order]))
    return (held + swap(sent, "core", 1, 2)) * (1.0 / jnp.sqrt(jnp.float32(norbit * nslab * naux)))


def solution(mesh):
    fine = Mesh(mesh.devices.reshape(4, 2, 4, 8, 2), ("x", "zh", "y", "zl", "core"))
    r, c = ("x", "zh", "y"), ("zl", "core")
    in_specs = (P(None, None, r, c), P(None, r, c), P(c, None))
    return jax.shard_map(local, mesh=fine, in_specs=in_specs, out_specs=P(r, c), check_vma=False)
```

time: 209 us -> 211 us (level)
  the two profiles are of different devices: /device:TPU:1 before, /device:TPU:317 now
where the time goes in v4:
time: 211 us; the launch traced here: 210 us
  waiting for transfers between devices  119 us (56%)
  starting transfers between devices  62.6 us (30%)
  Pallas kernels  17.7 us (8%)
  other arithmetic  5.47 us (3%)
  local copies, waits for them, and re-layouts  4.49 us (2%)
    ppermute x11, waiting for transfers between devices, swap(): return lax.ppermute(value, axis, [(i, i ^ bit) for i in range(size)])  76.4 us
    ppermute x11, starting transfers between devices, swap(): return lax.ppermute(value, axis, [(i, i ^ bit) for i in range(size)])  37.6 us
    all_to_all x1, waiting for transfers between devices, local(): lax.all_to_all(handed, ('zh', 'zl'), split_axis=0, concat_axis=0)  29.7 us
    all_to_all x1, starting transfers between devices, local(): lax.all_to_all(handed, ('zh', 'zl'), split_axis=0, concat_axis=0)  13.2 us
    pallas_call x2, Pallas kernels, half_of(): pl.pallas_call(half_kernel, out_shape=[jax.ShapeDtypeStruct((mrows, norbi...  10.3 us
    all_to_all x1, waiting for transfers between devices, local(): n = lax.all_to_all(copies, ('x', 'y'), split_axis=0, concat_axis=0)  9.79 us
    all_to_all x1, starting transfers between devices, local(): n = lax.all_to_all(copies, ('x', 'y'), split_axis=0, concat_axis=0)  7.62 us
    pallas_call x1, Pallas kernels, exchange_part(): pl.pallas_call(exchange_kernel, out_shape=(half, half), grid_spec=pltpu.P...  7.37 us
  transfers between devices with their start and end apart: 14, of which 11 were waited for; matrix products, arithmetic and copies ran while one was open for 2% of the time, Pallas kernels for 2%

profile of v4, /device:TPU:317, one launch (start us, length us, event | category | flops | bytes accessed | tf_op | source)
XLA Modules:
  0.0 209.9 jit_solution(5178578831213931842)
XLA Ops:
  0.0 5.2 %shard_map.38 = (f32[256,640]{1,0:T(8,128)}, f32[256,640]{1,0:T(8,128)}) custom-call(s32[1]{0:T(128)} %bitcast.6.slab_ref, s32[2,2,4]{2,1,0:T(2,128)} %mask_ref.3, f32[2,2,256,512]{3,2,1,0:T(8,128)} %a_ref.3, f32[512,640]{1,0:T(8,128)} %c_ref.3), custom_call_target="tpu_custom_call" | custom-call | flops 1006632960 | bytes 3670016 | tf_op jit(solution)/shard_map/pallas_call | solution.py:46
  5.2 2.6 %collective-permute-start = (f32[256,640]{1,0:T(8,128)}, f32[256,640]{1,0:T(8,128)S(1)}, u32[]{:S(2)}, u32[]{:S(2)}) collective-permute-start(f32[256,640]{1,0:T(8,128)} %get-tuple-element.14), channel_id=1, source_target_pairs={{0,1},{1,0},{2,3},{3,2},{4,5},{5,4},{6,7},{7,6},{8,9},{9,8},{10,11... | collective-permute-start | bytes 1966088 | tf_op jit(solution)/shard_map/ppermute | solution.py:125
  7.7 1.9 collective-permute-start.3
  9.7 5.2 %shard_map.37 = (f32[256,640]{1,0:T(8,128)}, f32[256,640]{1,0:T(8,128)}) custom-call(s32[1]{0:T(128)} %bitcast.slab_ref, s32[2,2,4]{2,1,0:T(2,128)} %mask_ref.3, f32[2,2,256,512]{3,2,1,0:T(8,128)} %a_ref.3, f32[512,640]{1,0:T(8,128)} %c_ref.3), custom_call_target="tpu_custom_call" | custom-call | flops 1006632960 | bytes 3670016 | tf_op jit(solution)/shard_map/pallas_call | solution.py:46
  14.8 1.2 bitcast_add_fusion.3
  16.1 2.6 %collective-permute-start.1 = (f32[4,32,640]{2,1,0:T(8,128)S(1)}, f32[4,32,640]{2,1,0:T(8,128)S(1)}, u32[]{:S(2)}, u32[]{:S(2)}) collective-permute-start(f32[4,32,640]{2,1,0:T(8,128)S(1)} %get-tuple-element.22), channel_id=1, source_target_pairs={{0,2},{2,0},{4,6},{6,4},{8,10},{10,8},{12,14},{14,12},{1,3},{3,1},... | collective-permute-start | bytes 983048 | tf_op jit(solution)/shard_map/ppermute | solution.py:125
  18.8 2.7 %collective-permute-start.4 = (f32[4,32,640]{2,1,0:T(8,128)S(1)}, f32[4,32,640]{2,1,0:T(8,128)S(1)}, u32[]{:S(2)}, u32[]{:S(2)}) collective-permute-start(f32[4,32,640]{2,1,0:T(8,128)S(1)} %get-tuple-element.24), channel_id=1, source_target_pairs={{0,2},{2,0},{4,6},{6,4},{8,10},{10,8},{12,14},{14,12},{1,3},{3,1},... | collective-permute-start | bytes 983048 | tf_op jit(solution)/shard_map/ppermute | solution.py:125
  21.5 5.3 %collective-permute-done.1 = f32[4,32,640]{2,1,0:T(8,128)S(1)} collective-permute-done((f32[4,32,640]{2,1,0:T(8,128)S(1)}, f32[4,32,640]{2,1,0:T(8,128)S(1)}, u32[]{:S(2)}, u32[]{:S(2)}) %collective-permute-start.1) | collective-permute-done | bytes 327712 | tf_op jit(solution)/shard_map/ppermute | solution.py:125
  26.8 3.1 %collective-permute-start.2 = (f32[2,32,640]{2,1,0:T(8,128)S(1)}, f32[2,32,640]{2,1,0:T(8,128)S(1)}, u32[]{:S(2)}, u32[]{:S(2)}) collective-permute-start(f32[2,32,640]{2,1,0:T(8,128)S(1)} %fusion.10), channel_id=1, source_target_pairs={{0,4},{2,6},{4,0},{6,2},{8,12},{10,14},{12,8},{14,10},{1,5},{3,7},... | collective-permute-start | bytes 491528 | tf_op jit(solution)/shard_map/ppermute | solution.py:125
  29.9 4.2 %collective-permute-done.4 = f32[4,32,640]{2,1,0:T(8,128)S(1)} collective-permute-done((f32[4,32,640]{2,1,0:T(8,128)S(1)}, f32[4,32,640]{2,1,0:T(8,128)S(1)}, u32[]{:S(2)}, u32[]{:S(2)}) %collective-permute-start.4) | collective-permute-done | bytes 327712 | tf_op jit(solution)/shard_map/ppermute | solution.py:125
  34.0 5.1 %collective-permute-start.5 = (f32[2,32,640]{2,1,0:T(8,128)S(1)}, f32[2,32,640]{2,1,0:T(8,128)S(1)}, u32[]{:S(2)}, u32[]{:S(2)}) collective-permute-start(f32[2,32,640]{2,1,0:T(8,128)S(1)} %fusion.6), channel_id=1, source_target_pairs={{0,4},{2,6},{4,0},{6,2},{8,12},{10,14},{12,8},{14,10},{1,5},{3,7},... | collective-permute-start | bytes 491528 | tf_op jit(solution)/shard_map/ppermute | solution.py:125
  39.2 6.5 %collective-permute-done.5 = f32[2,32,640]{2,1,0:T(8,128)S(1)} collective-permute-done((f32[2,32,640]{2,1,0:T(8,128)S(1)}, f32[2,32,640]{2,1,0:T(8,128)S(1)}, u32[]{:S(2)}, u32[]{:S(2)}) %collective-permute-start.5) | collective-permute-done | bytes 163872 | tf_op jit(solution)/shard_map/ppermute | solution.py:125
  46.5 4.2 %all-to-all-start = ((f32[4,2,16,640]{3,2,1,0:T(8,128)}), f32[4,2,16,640]{3,2,1,0:T(8,128)S(1)}, u32[]{:S(2)}, u32[]{:S(2)}) async-start(f32[4,2,16,640]{3,2,1,0:T(8,128)} %bitcast.22), calls=%async_computation | async-start | bytes 655360 | tf_op jit(solution)/shard_map/all_to_all | solution.py:149
  50.8 3.6 %all-to-all-done = f32[4,2,16,640]{3,2,1,0:T(8,128)S(1)} async-done(((f32[4,2,16,640]{3,2,1,0:T(8,128)}), f32[4,2,16,640]{3,2,1,0:T(8,128)S(1)}, u32[]{:S(2)}, u32[]{:S(2)}) %all-to-all-start) | async-done | bytes 327712 | tf_op jit(solution)/shard_map/all_to_all | solution.py:149
  55.3 13.2 %all-to-all-start.1 = ((f32[16,2,8,640]{3,2,1,0:T(8,128)}), f32[16,2,8,640]{3,2,1,0:T(8,128)S(1)}, u32[]{:S(2)}, u32[]{:S(2)}) async-start(f32[16,2,8,640]{3,2,1,0:T(8,128)} %bitcast.27), calls=%async_computation.1 | async-start | bytes 1310720 | tf_op jit(solution)/shard_map/all_to_all | solution.py:153
  68.5 29.7 %all-to-all-done.1 = f32[16,2,8,640]{3,2,1,0:T(8,128)S(1)} async-done(((f32[16,2,8,640]{3,2,1,0:T(8,128)}), f32[16,2,8,640]{3,2,1,0:T(8,128)S(1)}, u32[]{:S(2)}, u32[]{:S(2)}) %all-to-all-start.1) | async-done | bytes 655392 | tf_op jit(solution)/shard_map/all_to_all | solution.py:153
  98.2 2.7 %collective-permute-start.6 = (f32[4,2,8,640]{3,2,1,0:T(8,128)S(1)}, f32[4,2,8,640]{3,2,1,0:T(8,128)S(1)}, u32[]{:S(2)}, u32[]{:S(2)}) collective-permute-start(f32[4,2,8,640]{3,2,1,0:T(8,128)S(1)} %get-tuple-element.26), channel_id=1, source_target_pairs={{0,2},{2,0},{4,6},{6,4},{8,10},{10,8},{12,14},{14,12},{1,3},{3,1},... | collective-permute-start | bytes 491528 | tf_op jit(solution)/shard_map/ppermute | solution.py:125
  100.9 3.8 %collective-permute-done.6 = f32[4,2,8,640]{3,2,1,0:T(8,128)S(1)} collective-permute-done((f32[4,2,8,640]{3,2,1,0:T(8,128)S(1)}, f32[4,2,8,640]{3,2,1,0:T(8,128)S(1)}, u32[]{:S(2)}, u32[]{:S(2)}) %collective-permute-start.6) | collective-permute-done | bytes 163872 | tf_op jit(solution)/shard_map/ppermute | solution.py:125
  104.8 3.0 %broadcast_in_dim.19 = f32[16,2,4,2,8,640]{5,4,3,2,1,0:T(8,128)} broadcast(f32[2,4,2,8,640]{4,3,2,1,0:T(8,128)S(1)} %pad_maximum_fusion.4), dimensions={1,2,3,4,5} | broadcast | bytes 5570560 | tf_op jit(solution)/shard_map/broadcast_in_dim | solution.py:159
  107.8 7.6 %all-to-all-start.2 = ((f32[16,2,4,2,8,640]{5,4,3,2,1,0:T(8,128)}), f32[16,2,4,2,8,640]{5,4,3,2,1,0:T(8,128)}, u32[]{:S(2)}, u32[]{:S(2)}) async-start(f32[16,2,4,2,8,640]{5,4,3,2,1,0:T(8,128)} %broadcast_in_dim.19), calls=%async_computation.2 | async-start | bytes 10485760 | tf_op jit(solution)/shard_map/all_to_all | solution.py:160
  115.4 1.9 collective-permute-start.7
  117.3 27.1 %collective-permute-done.7 = f32[2,2,32,640]{3,2,1,0:T(8,128)S(1)} collective-permute-done((f32[2,2,32,640]{3,2,1,0:T(8,128)S(1)}, f32[2,2,32,640]{3,2,1,0:T(8,128)S(1)}, u32[]{:S(2)}, u32[]{:S(2)}) %collective-permute-start.7) | collective-permute-done | bytes 327712 | tf_op jit(solution)/shard_map/ppermute | solution.py:125
  144.5 5.0 %collective-permute-start.8 = (f32[1,2,2,32,640]{4,3,2,1,0:T(8,128)S(1)}, f32[1,2,2,32,640]{4,3,2,1,0:T(8,128)S(1)}, u32[]{:S(2)}, u32[]{:S(2)}) collective-permute-start(f32[1,2,2,32,640]{4,3,2,1,0:T(8,128)S(1)} %add_bitcast_fusion), channel_id=1, source_target_pairs={{0,4},{2,6},{4,0},{6,2},{8,12},{10,14},{12,8},{14,10},{1,5},{3,7},... | collective-permute-start | bytes 983048 | tf_op jit(solution)/shard_map/ppermute | solution.py:125
  149.4 13.6 %collective-permute-done.8 = f32[1,2,2,32,640]{4,3,2,1,0:T(8,128)S(1)} collective-permute-done((f32[1,2,2,32,640]{4,3,2,1,0:T(8,128)S(1)}, f32[1,2,2,32,640]{4,3,2,1,0:T(8,128)S(1)}, u32[]{:S(2)}, u32[]{:S(2)}) %collective-permute-start.8) | collective-permute-done | bytes 327712 | tf_op jit(solution)/shard_map/ppermute | solution.py:125
  163.1 5.3 %collective-permute-start.9 = (f32[2,2,2,32,640]{4,3,2,1,0:T(8,128)S(1)}, f32[2,2,2,32,640]{4,3,2,1,0:T(8,128)S(1)}, u32[]{:S(2)}, u32[]{:S(2)}) collective-permute-start(f32[2,2,2,32,640]{4,3,2,1,0:T(8,128)S(1)} %pad_maximum_fusion.1), channel_id=1, source_target_pairs={{0,2},{2,0},{4,6},{6,4},{8,10},{10,8},{12,14},{14,12},{1,3},{3,1},... | collective-permute-start | bytes 1966088 | tf_op jit(solution)/shard_map/ppermute | solution.py:125
  169.0 14.2 %collective-permute-done.9 = f32[2,2,2,32,640]{4,3,2,1,0:T(8,128)S(1)} collective-permute-done((f32[2,2,2,32,640]{4,3,2,1,0:T(8,128)S(1)}, f32[2,2,2,32,640]{4,3,2,1,0:T(8,128)S(1)}, u32[]{:S(2)}, u32[]{:S(2)}) %collective-permute-start.9) | collective-permute-done | bytes 655392 | tf_op jit(solution)/shard_map/ppermute | solution.py:125
  183.1 1.2 pad_maximum_fusion.m_ref
  184.3 9.8 %all-to-all-done.2 = f32[16,2,4,2,8,640]{5,4,3,2,1,0:T(8,128)} async-done(((f32[16,2,4,2,8,640]{5,4,3,2,1,0:T(8,128)}), f32[16,2,4,2,8,640]{5,4,3,2,1,0:T(8,128)}, u32[]{:S(2)}, u32[]{:S(2)}) %all-to-all-start.2) | async-done | bytes 5242912 | tf_op jit(solution)/shard_map/all_to_all | solution.py:160
  194.1 7.4 %shard_map.39 = (f32[256,512]{1,0:T(8,128)}, f32[256,512]{1,0:T(8,128)}) custom-call(s32[5]{0:T(128)} %stack.39.place_ref, f32[4,2,2,32,640]{4,3,2,1,0:T(8,128)} %pad_maximum_fusion.m_ref, f32[4,4,2,4,2,8,640]{6,5,4,3,2,1,0:T(8,128)} %bitcast.33.n_ref), custom_call_target="tpu_custom_call" | custom-call | flops 2013265920 | bytes 7602176 | tf_op jit(solution)/shard_map/pallas_call | solution.py:103
  201.5 4.8 %collective-permute-start.10 = (f32[256,512]{1,0:T(8,128)}, f32[256,512]{1,0:T(8,128)S(1)}, u32[]{:S(2)}, u32[]{:S(2)}) collective-permute-start(f32[256,512]{1,0:T(8,128)} %get-tuple-element.20), channel_id=1, source_target_pairs={{0,1},{1,0},{2,3},{3,2},{4,5},{5,4},{6,7},{7,6},{8,9},{9,8},{10,11... | collective-permute-start | bytes 1572872 | tf_op jit(solution)/shard_map/ppermute | solution.py:125
  206.3 1.7 collective-permute-done.10
  208.0 1.9 add_multiply_fusion
  (21 shorter events, 2.7 us)
Async XLA Ops:
  5.2 9.7 %collective-permute-start = (f32[256,640]{1,0:T(8,128)}, f32[256,640]{1,0:T(8,128)S(1)}, u32[]{:S(2)}, u32[]{:S(2)}) collective-permute-start(f32[256,640]{1,0:T(8,128)} %get-tuple-element.14), channel_id=1, source_target_pairs={{0,1},{1,0},{2,3},{3,2},{4,5},{5,4},{6,7},{7,6},{8,9},{9,8},{10,11... | collective-permute-start | bytes 1966088 | tf_op jit(solution)/shard_map/ppermute | solution.py:125
  7.7 10.9 %collective-permute-start.3 = (f32[256,640]{1,0:T(8,128)}, f32[256,640]{1,0:T(8,128)S(1)}, u32[]{:S(2)}, u32[]{:S(2)}) collective-permute-start(f32[256,640]{1,0:T(8,128)} %get-tuple-element.16), channel_id=1, source_target_pairs={{0,1},{1,0},{2,3},{3,2},{4,5},{5,4},{6,7},{7,6},{8,9},{9,8},{10,11... | collective-permute-start | bytes 1966088 | tf_op jit(solution)/shard_map/ppermute | solution.py:125
  14.8 3.9 %copy-start = (f32[256,640]{1,0:T(8,128)S(1)}, f32[256,640]{1,0:T(8,128)}, u32[]{:S(2)}) copy-start(f32[256,640]{1,0:T(8,128)} %get-tuple-element.15) | copy-start | bytes 1966084
  16.1 10.7 %collective-permute-start.1 = (f32[4,32,640]{2,1,0:T(8,128)S(1)}, f32[4,32,640]{2,1,0:T(8,128)S(1)}, u32[]{:S(2)}, u32[]{:S(2)}) collective-permute-start(f32[4,32,640]{2,1,0:T(8,128)S(1)} %get-tuple-element.22), channel_id=1, source_target_pairs={{0,2},{2,0},{4,6},{6,4},{8,10},{10,8},{12,14},{14,12},{1,3},{3,1},... | collective-permute-start | bytes 983048 | tf_op jit(solution)/shard_map/ppermute | solution.py:125
  18.8 15.2 %collective-permute-start.4 = (f32[4,32,640]{2,1,0:T(8,128)S(1)}, f32[4,32,640]{2,1,0:T(8,128)S(1)}, u32[]{:S(2)}, u32[]{:S(2)}) collective-permute-start(f32[4,32,640]{2,1,0:T(8,128)S(1)} %get-tuple-element.24), channel_id=1, source_target_pairs={{0,2},{2,0},{4,6},{6,4},{8,10},{10,8},{12,14},{14,12},{1,3},{3,1},... | collective-permute-start | bytes 983048 | tf_op jit(solution)/shard_map/ppermute | solution.py:125
  26.8 12.4 %collective-permute-start.2 = (f32[2,32,640]{2,1,0:T(8,128)S(1)}, f32[2,32,640]{2,1,0:T(8,128)S(1)}, u32[]{:S(2)}, u32[]{:S(2)}) collective-permute-start(f32[2,32,640]{2,1,0:T(8,128)S(1)} %fusion.10), channel_id=1, source_target_pairs={{0,4},{2,6},{4,0},{6,2},{8,12},{10,14},{12,8},{14,10},{1,5},{3,7},... | collective-permute-start | bytes 491528 | tf_op jit(solution)/shard_map/ppermute | solution.py:125
  34.0 11.7 %collective-permute-start.5 = (f32[2,32,640]{2,1,0:T(8,128)S(1)}, f32[2,32,640]{2,1,0:T(8,128)S(1)}, u32[]{:S(2)}, u32[]{:S(2)}) collective-permute-start(f32[2,32,640]{2,1,0:T(8,128)S(1)} %fusion.6), channel_id=1, source_target_pairs={{0,4},{2,6},{4,0},{6,2},{8,12},{10,14},{12,8},{14,10},{1,5},{3,7},... | collective-permute-start | bytes 491528 | tf_op jit(solution)/shard_map/ppermute | solution.py:125
  46.5 7.9 %all-to-all-start = ((f32[4,2,16,640]{3,2,1,0:T(8,128)}), f32[4,2,16,640]{3,2,1,0:T(8,128)S(1)}, u32[]{:S(2)}, u32[]{:S(2)}) async-start(f32[4,2,16,640]{3,2,1,0:T(8,128)} %bitcast.22), calls=%async_computation | async-start | bytes 655360 | tf_op jit(solution)/shard_map/all_to_all | solution.py:149
  55.3 42.9 %all-to-all-start.1 = ((f32[16,2,8,640]{3,2,1,0:T(8,128)}), f32[16,2,8,640]{3,2,1,0:T(8,128)S(1)}, u32[]{:S(2)}, u32[]{:S(2)}) async-start(f32[16,2,8,640]{3,2,1,0:T(8,128)} %bitcast.27), calls=%async_computation.1 | async-start | bytes 1310720 | tf_op jit(solution)/shard_map/all_to_all | solution.py:153
  98.2 6.5 %collective-permute-start.6 = (f32[4,2,8,640]{3,2,1,0:T(8,128)S(1)}, f32[4,2,8,640]{3,2,1,0:T(8,128)S(1)}, u32[]{:S(2)}, u32[]{:S(2)}) collective-permute-start(f32[4,2,8,640]{3,2,1,0:T(8,128)S(1)} %get-tuple-element.26), channel_id=1, source_target_pairs={{0,2},{2,0},{4,6},{6,4},{8,10},{10,8},{12,14},{14,12},{1,3},{3,1},... | collective-permute-start | bytes 491528 | tf_op jit(solution)/shard_map/ppermute | solution.py:125
  107.8 86.3 %all-to-all-start.2 = ((f32[16,2,4,2,8,640]{5,4,3,2,1,0:T(8,128)}), f32[16,2,4,2,8,640]{5,4,3,2,1,0:T(8,128)}, u32[]{:S(2)}, u32[]{:S(2)}) async-start(f32[16,2,4,2,8,640]{5,4,3,2,1,0:T(8,128)} %broadcast_in_dim.19), calls=%async_computation.2 | async-start | bytes 10485760 | tf_op jit(solution)/shard_map/all_to_all | solution.py:160
  115.4 29.0 %collective-permute-start.7 = (f32[2,2,32,640]{3,2,1,0:T(8,128)S(1)}, f32[2,2,32,640]{3,2,1,0:T(8,128)S(1)}, u32[]{:S(2)}, u32[]{:S(2)}) collective-permute-start(f32[2,2,32,640]{3,2,1,0:T(8,128)S(1)} %pad_maximum_fusion.2), channel_id=1, source_target_pairs={{0,8},{2,10},{4,12},{6,14},{8,0},{10,2},{12,4},{14,6},{1,9},{3,11}... | collective-permute-start | bytes 983048 | tf_op jit(solution)/shard_map/ppermute | solution.py:125
  144.5 18.5 %collective-permute-start.8 = (f32[1,2,2,32,640]{4,3,2,1,0:T(8,128)S(1)}, f32[1,2,2,32,640]{4,3,2,1,0:T(8,128)S(1)}, u32[]{:S(2)}, u32[]{:S(2)}) collective-permute-start(f32[1,2,2,32,640]{4,3,2,1,0:T(8,128)S(1)} %add_bitcast_fusion), channel_id=1, source_target_pairs={{0,4},{2,6},{4,0},{6,2},{8,12},{10,14},{12,8},{14,10},{1,5},{3,7},... | collective-permute-start | bytes 983048 | tf_op jit(solution)/shard_map/ppermute | solution.py:125
  163.1 20.0 %collective-permute-start.9 = (f32[2,2,2,32,640]{4,3,2,1,0:T(8,128)S(1)}, f32[2,2,2,32,640]{4,3,2,1,0:T(8,128)S(1)}, u32[]{:S(2)}, u32[]{:S(2)}) collective-permute-start(f32[2,2,2,32,640]{4,3,2,1,0:T(8,128)S(1)} %pad_maximum_fusion.1), channel_id=1, source_target_pairs={{0,2},{2,0},{4,6},{6,4},{8,10},{10,8},{12,14},{14,12},{1,3},{3,1},... | collective-permute-start | bytes 1966088 | tf_op jit(solution)/shard_map/ppermute | solution.py:125
  201.5 6.5 %collective-permute-start.10 = (f32[256,512]{1,0:T(8,128)}, f32[256,512]{1,0:T(8,128)S(1)}, u32[]{:S(2)}, u32[]{:S(2)}) collective-permute-start(f32[256,512]{1,0:T(8,128)} %get-tuple-element.20), channel_id=1, source_target_pairs={{0,1},{1,0},{2,3},{3,2},{4,5},{5,4},{6,7},{7,6},{8,9},{9,8},{10,11... | collective-permute-start | bytes 1572872 | tf_op jit(solution)/shard_map/ppermute | solution.py:125

commit v5 on v3

v5 whole, which is shorter than its diff:
```python
import jax
import jax.numpy as jnp
from jax import lax
from jax.experimental import pallas as pl
from jax.experimental.pallas import tpu as pltpu
from jax.sharding import Mesh, PartitionSpec as P

TILE = 128
VMEM = 20 * 1024 * 1024
NT = (((1,), (1,)), ((), ()))


def halves(value):
    high = value.astype(jnp.bfloat16)
    return high, (value - high.astype(jnp.float32)).astype(jnp.bfloat16)


def dot(a, b, dims=(((1,), (0,)), ((), ()))):
    return lax.dot_general(a, b, dims, preferred_element_type=jnp.float32)


def half_kernel(half_ref, mask_ref, a_ref, c_ref, *rest):
    *o_refs, chigh, clow, ahigh, alow = rest
    chunk = pl.program_id(0)
    parts, bits, _, rows, lcols = a_ref.shape

    @pl.when(chunk == 0)
    def _():
        chigh[...], clow[...] = halves(c_ref[...])

    for p in range(parts):
        for b in range(bits):
            for j in range(lcols // TILE):
                at = (pl.ds((p * bits + b) * rows, rows), pl.ds(j * TILE, TILE))
                kept = mask_ref[p * mask_ref.shape[0] // parts, half_ref[0], j].astype(jnp.float32)
                ahigh[at], alow[at] = halves(a_ref[p, b, 0, :, at[1]] * kept)
    total = dot(ahigh[...], chigh[...]) + (dot(ahigh[...], clow[...]) + dot(alow[...], chigh[...]))
    for k, o_ref in enumerate(o_refs):
        @pl.when(chunk == k)
        def _():
            o_ref[...] = total.reshape(o_ref.shape)


def half_of(integrals, mask, coeffs, half):
    parts, mrows, lcols = integrals.shape
    norbit = coeffs.shape[1]
    rows = mrows // 8
    shape = (parts, 2, rows, norbit)
    return pl.pallas_call(
        half_kernel,
        out_shape=[jax.ShapeDtypeStruct(shape, jnp.float32)] * 2,
        grid_spec=pltpu.PrefetchScalarGridSpec(
            num_scalar_prefetch=2,
            grid=(2,),
            in_specs=[
                pl.BlockSpec((parts, 2, 1, rows, lcols), lambda k, half, mask: (0, half[0], k, 0, 0)),
                pl.BlockSpec((lcols, norbit), lambda k, half, mask: (0, 0)),
            ],
            out_specs=[pl.BlockSpec(shape, lambda k, half, mask: (0, 0, 0, 0))] * 2,
            scratch_shapes=[pltpu.VMEM((lcols, norbit), jnp.bfloat16)] * 2
            + [pltpu.VMEM((parts * 2 * rows, lcols), jnp.bfloat16)] * 2,
        ),
        compiler_params=pltpu.CompilerParams(vmem_limit_bytes=VMEM),
        cost_estimate=pl.CostEstimate(flops=3 * parts * mrows * lcols * norbit, bytes_accessed=2 * parts * mrows * (lcols + norbit) + 4 * lcols * norbit, transcendentals=0),
    )(half.reshape(1), mask, integrals.reshape(parts, 4, 2, rows, lcols), coeffs)


def exchange_kernel(core_ref, mown_ref, moth_ref, nown_ref, noth_ref, o_ref, mhigh, mlow, nhigh, nlow):
    count, rows, norbit = mown_ref.shape
    blocks, bits, nrows, _ = nown_ref.shape
    core = core_ref[0]
    both = ((core, mown_ref, nown_ref), (1 - core, moth_ref, noth_ref))

    @pl.when(pl.program_id(0) == 0)
    def _():
        for y in range(blocks):
            for c, _, ref in both:
                for b in range(bits):
                    at = pl.ds(pl.multiple_of(((y * 2 + c) * bits + b) * nrows, nrows), nrows)
                    nhigh[at, :], nlow[at, :] = halves(ref[y, b])

    for x in range(count):
        for c, ref, _ in both:
            at = pl.ds(pl.multiple_of((x * 2 + c) * rows, rows), rows)
            mhigh[at, :], mlow[at, :] = halves(ref[x])
    total = dot(mhigh[...], nhigh[...], NT) + (dot(mhigh[...], nlow[...], NT) + dot(mlow[...], nhigh[...], NT))
    o_ref[...] = total.reshape(o_ref.shape)


def exchange_part(mown, moth, nown, noth, core):
    parts, rows, norbit = mown.shape
    ncols = 2 * nown.shape[0] * nown.shape[1] * nown.shape[2]
    step = parts // 2
    mspec = pl.BlockSpec((step, rows, norbit), lambda x, core: (x, 0, 0))
    nspec = pl.BlockSpec(nown.shape, lambda x, core: (0, 0, 0, 0))
    return pl.pallas_call(
        exchange_kernel,
        out_shape=jax.ShapeDtypeStruct((parts, 2, rows, ncols), jnp.float32),
        grid_spec=pltpu.PrefetchScalarGridSpec(
            num_scalar_prefetch=1,
            grid=(2,),
            in_specs=[mspec, mspec, nspec, nspec],
            out_specs=pl.BlockSpec((step, 2, rows, ncols), lambda x, core: (x, 0, 0, 0)),
            scratch_shapes=[pltpu.VMEM((step * 2 * rows, norbit), jnp.bfloat16)] * 2 + [pltpu.VMEM((ncols, norbit), jnp.bfloat16)] * 2,
        ),
        compiler_params=pltpu.CompilerParams(vmem_limit_bytes=VMEM),
        cost_estimate=pl.CostEstimate(flops=12 * parts * rows * ncols * norbit, bytes_accessed=4 * norbit * (2 * parts * rows + ncols) + 8 * parts * rows * ncols, transcendentals=0),
    )(core.reshape(1), mown, moth, nown, noth)


def swap(value, axis, bit, size):
    return lax.ppermute(value, axis, [(i, i ^ bit) for i in range(size)])


def pick(value, index, axis):
    return lax.dynamic_index_in_dim(value, index, axis, keepdims=False)


def join(own, got, bit, axis):
    return jnp.stack([jnp.where(bit == 0, own, got), jnp.where(bit == 0, got, own)], axis=axis)


def to_x(value):
    return lax.all_to_all(value, "x", split_axis=0, concat_axis=0)


NEAR = [(z, (z + 8) % 16 if z % 2 == z // 8 else z ^ 1) for z in range(16)]
FAR = [(z, (z ^ 1) ^ 8) for z in range(16) if z % 2 != z // 8]


def local(integrals, mask, coeffs):
    nslab, naux, mrows, lcols = integrals.shape
    norbit = coeffs.shape[1]
    core, zl, zh = lax.axis_index("core"), lax.axis_index("zl"), lax.axis_index("zh")
    low, mid, top = zl & 1, (zl >> 1) & 1, zl >> 2
    parts, rows = nslab * naux, mrows // 8
    integrals = integrals.reshape(parts, mrows, lcols)
    away = half_of(integrals, mask, coeffs, 1 - core)
    got = [swap(a, "core", 1, 2) for a in away]
    kept = half_of(integrals, mask, coeffs, core)
    own = []
    for k, g in zip(kept, got):
        part = to_x(k + g)
        part = pick(part, low, 1) + swap(pick(part, 1 - low, 1), "zl", 1, 8)
        part = part.reshape(2, 2, rows, norbit)
        part = pick(part, mid, 1) + swap(pick(part, 1 - mid, 1), "zl", 2, 8)
        own.append(pick(part, top, 0) + swap(pick(part, 1 - top, 0), "zl", 4, 8))
    own = jnp.concatenate(own)
    near = lax.ppermute(own, ("zh", "zl"), NEAR)
    far = lax.ppermute(own, ("zh", "zl"), FAR)
    fits = zh == low
    cols = join(jnp.where(fits, own, near), jnp.where(fits, near, far), low, 0)
    n = lax.all_to_all(jnp.broadcast_to(cols[None], (4,) + cols.shape), "y", split_axis=0, concat_axis=0)
    n = n.reshape((2, 2) + cols.shape)
    nown, noth = pick(n, core, 0), swap(pick(n, 1 - core, 0), "core", 1, 2)
    m = join(own, swap(own, "zl", 4, 8), top, 0)
    m = join(m, swap(m, "zl", 2, 8), mid, 1).reshape(4, 2 * rows, norbit)
    tiles = []
    for m in (m, swap(m, "zl", 1, 8)):
        tile = exchange_part(m, swap(m, "core", 1, 2), nown, noth, core)
        tiles.append(jnp.sum(to_x(tile), axis=0))
    return join(*tiles, low, 1).reshape(mrows, lcols) * (1.0 / jnp.sqrt(jnp.float32(norbit * parts)))


def solution(mesh):
    fine = Mesh(mesh.devices.reshape(4, 2, 4, 8, 2), ("x", "zh", "y", "zl", "core"))
    r, c = ("x", "zh", "y"), ("zl", "core")
    in_specs = (P(None, None, r, c), P(None, r, c), P(c, None))
    return jax.shard_map(local, mesh=fine, in_specs=in_specs, out_specs=P(r, c), check_vma=False)
```

time: 210 us -> 195 us (0.929)
  the two profiles are of different devices: /device:TPU:32 before, /device:TPU:1 now
where the time goes in v5:
time: 195 us; the launch traced here: 194 us
  waiting for transfers between devices  97.5 us (50%)
  starting transfers between devices  76.2 us (39%)
  Pallas kernels  10.7 us (5%)
  local copies, waits for them, and re-layouts  4.99 us (3%)
  other arithmetic  4.54 us (2%)
    ppermute x14, waiting for transfers between devices, swap(): return lax.ppermute(value, axis, [(i, i ^ bit) for i in range(size)])  67.3 us
    ppermute x14, starting transfers between devices, swap(): return lax.ppermute(value, axis, [(i, i ^ bit) for i in range(size)])  45.2 us
    all_to_all x4, waiting for transfers between devices, to_x(): return lax.all_to_all(value, 'x', split_axis=0, concat_axis=0)  30.2 us
    all_to_all x4, starting transfers between devices, to_x(): return lax.all_to_all(value, 'x', split_axis=0, concat_axis=0)  14.7 us
    ppermute x1, starting transfers between devices, local(): near = lax.ppermute(own, ('zh', 'zl'), NEAR)  12.1 us
    pallas_call x2, Pallas kernels, exchange_part(): pl.pallas_call(exchange_kernel, out_shape=jax.ShapeDtypeStruct((parts, 2,...  5.51 us
    pallas_call x2, Pallas kernels, half_of(): pl.pallas_call(half_kernel, out_shape=[jax.ShapeDtypeStruct(shape, jnp.fl...  5.17 us
  transfers between devices with their start and end apart: 21, of which 9 were waited for; matrix products, arithmetic and copies ran while one was open for 2% of the time, Pallas kernels for 4%

profile of v5, /device:TPU:1, one launch (start us, length us, event | category | flops | bytes accessed | tf_op | source)
XLA Modules:
  0.0 194.4 jit_solution(5780453848435515873)
XLA Ops:
  3.6 2.6 %shard_map.38 = (f32[4,2,32,640]{3,2,1,0:T(8,128)S(1)}, f32[4,2,32,640]{3,2,1,0:T(8,128)S(1)}) custom-call(s32[1]{0:T(128)} %bitcast.2.half_ref, s32[2,2,4]{2,1,0:T(2,128)S(1)} %copy-done.3, f32[4,4,2,32,512]{4,3,2,1,0:T(8,128)S(1)} %bitcast.59, f32[512,640]{1,0:T(8,128)S(1)} %copy-done.2), custom_call_target="tpu_custom_call" | custom-call | flops 1006632960 | bytes 3670016 | tf_op jit(solution)/shard_map/pallas_call | solution.py:49
  6.2 8.8 %collective-permute-start.4 = (f32[4,2,32,640]{3,2,1,0:T(8,128)S(1)}, f32[4,2,32,640]{3,2,1,0:T(8,128)S(1)}, u32[]{:S(2)}, u32[]{:S(2)}) collective-permute-start(f32[4,2,32,640]{3,2,1,0:T(8,128)S(1)} %get-tuple-element.12), channel_id=1, source_target_pairs={{0,1},{1,0},{2,3},{3,2},{4,5},{5,4},{6,7},{7,6},{8,9},{9,8},{10,11... | collective-permute-start | bytes 1966088 | tf_op jit(solution)/shard_map/ppermute | solution.py:112
  15.0 1.9 collective-permute-start
  16.9 2.6 %shard_map.37 = (f32[4,2,32,640]{3,2,1,0:T(8,128)S(1)}, f32[4,2,32,640]{3,2,1,0:T(8,128)S(1)}) custom-call(s32[1]{0:T(128)} %bitcast.half_ref.core_ref, s32[2,2,4]{2,1,0:T(2,128)S(1)} %copy-done.4, f32[4,4,2,32,512]{4,3,2,1,0:T(8,128)S(1)} %bitcast.60, f32[512,640]{1,0:T(8,128)S(1)} %copy-done.2), custom_call_target="tpu_custom_call" | custom-call | flops 1006632960 | bytes 3670016 | tf_op jit(solution)/shard_map/pallas_call | solution.py:49
  20.4 3.5 %all-to-all-start.1 = ((f32[4,2,32,640]{3,2,1,0:T(8,128)}), f32[4,2,32,640]{3,2,1,0:T(8,128)S(1)}, u32[]{:S(2)}, u32[]{:S(2)}) async-start(f32[4,2,32,640]{3,2,1,0:T(8,128)} %add.72), calls=%async_computation.1 | async-start | bytes 1310720 | tf_op jit(solution)/shard_map/all_to_all | solution.py:124
  24.9 9.5 %all-to-all-done.1 = f32[4,2,32,640]{3,2,1,0:T(8,128)S(1)} async-done(((f32[4,2,32,640]{3,2,1,0:T(8,128)}), f32[4,2,32,640]{3,2,1,0:T(8,128)S(1)}, u32[]{:S(2)}, u32[]{:S(2)}) %all-to-all-start.1) | async-done | bytes 655392 | tf_op jit(solution)/shard_map/all_to_all | solution.py:124
  34.4 3.5 %all-to-all-start = ((f32[4,2,32,640]{3,2,1,0:T(8,128)}), f32[4,2,32,640]{3,2,1,0:T(8,128)S(1)}, u32[]{:S(2)}, u32[]{:S(2)}) async-start(f32[4,2,32,640]{3,2,1,0:T(8,128)} %add.62), calls=%async_computation | async-start | bytes 1310720 | tf_op jit(solution)/shard_map/all_to_all | solution.py:124
  37.9 1.9 collective-permute-start.5
  39.9 7.3 %all-to-all-done = f32[4,2,32,640]{3,2,1,0:T(8,128)S(1)} async-done(((f32[4,2,32,640]{3,2,1,0:T(8,128)}), f32[4,2,32,640]{3,2,1,0:T(8,128)S(1)}, u32[]{:S(2)}, u32[]{:S(2)}) %all-to-all-start) | async-done | bytes 655392 | tf_op jit(solution)/shard_map/all_to_all | solution.py:124
  47.1 1.9 collective-permute-start.1
  49.2 1.9 collective-permute-start.6
  51.1 6.2 %collective-permute-done.1 = f32[4,32,640]{2,1,0:T(8,128)S(1)} collective-permute-done((f32[4,32,640]{2,1,0:T(8,128)S(1)}, f32[4,32,640]{2,1,0:T(8,128)S(1)}, u32[]{:S(2)}, u32[]{:S(2)}) %collective-permute-start.1) | collective-permute-done | bytes 327712 | tf_op jit(solution)/shard_map/ppermute | solution.py:112
  57.4 1.9 collective-permute-start.2
  59.4 5.8 %collective-permute-start.7 = (f32[32,640]{1,0:T(8,128)S(1)}, f32[32,640]{1,0:T(8,128)S(1)}, u32[]{:S(2)}, u32[]{:S(2)}) collective-permute-start(f32[32,640]{1,0:T(8,128)S(1)} %dynamic-slice_bitcast_fusion.6), channel_id=1, source_target_pairs={{0,8},{2,10},{4,12},{6,14},{8,0},{10,2},{12,4},{14,6},{1,9},{3,11}... | collective-permute-start | bytes 245768 | tf_op jit(solution)/shard_map/ppermute | solution.py:112
  65.2 7.8 %collective-permute-start.3 = (f32[32,640]{1,0:T(8,128)S(1)}, f32[32,640]{1,0:T(8,128)S(1)}, u32[]{:S(2)}, u32[]{:S(2)}) collective-permute-start(f32[32,640]{1,0:T(8,128)S(1)} %dynamic-slice_bitcast_fusion.7), channel_id=1, source_target_pairs={{0,8},{2,10},{4,12},{6,14},{8,0},{10,2},{12,4},{14,6},{1,9},{3,11}... | collective-permute-start | bytes 245768 | tf_op jit(solution)/shard_map/ppermute | solution.py:112
  73.1 7.7 %collective-permute-done.3 = f32[32,640]{1,0:T(8,128)S(1)} collective-permute-done((f32[32,640]{1,0:T(8,128)S(1)}, f32[32,640]{1,0:T(8,128)S(1)}, u32[]{:S(2)}, u32[]{:S(2)}) %collective-permute-start.3) | collective-permute-done | bytes 81952 | tf_op jit(solution)/shard_map/ppermute | solution.py:112
  80.8 12.1 %collective-permute-start.11 = (f32[64,640]{1,0:T(8,128)S(1)}, f32[64,640]{1,0:T(8,128)S(1)}, u32[]{:S(2)}, u32[]{:S(2)}) collective-permute-start(f32[64,640]{1,0:T(8,128)S(1)} %pad_maximum_fusion.3), channel_id=1, source_target_pairs={{0,64},{2,0},{4,68},{6,4},{8,72},{10,8},{12,76},{14,12},{64,66},{6... | collective-permute-start | bytes 491528 | tf_op jit(solution)/shard_map/ppermute | solution.py:149
  93.6 1.9 collective-permute-start.8
  95.5 28.5 %collective-permute-done.8 = f32[64,640]{1,0:T(8,128)S(1)} collective-permute-done((f32[64,640]{1,0:T(8,128)S(1)}, f32[64,640]{1,0:T(8,128)S(1)}, u32[]{:S(2)}, u32[]{:S(2)}) %collective-permute-start.8) | collective-permute-done | bytes 163872 | tf_op jit(solution)/shard_map/ppermute | solution.py:112
  125.3 3.5 %all-to-all-start.2 = ((f32[4,2,64,640]{3,2,1,0:T(8,128)}), f32[4,2,64,640]{3,2,1,0:T(8,128)S(1)}, u32[]{:S(2)}, u32[]{:S(2)}) async-start(f32[4,2,64,640]{3,2,1,0:T(8,128)} %broadcast_in_dim.2), calls=%async_computation.2 | async-start | bytes 2621440 | tf_op jit(solution)/shard_map/all_to_all | solution.py:153
  128.9 1.9 collective-permute-start.9
  130.8 13.7 %collective-permute-done.9 = f32[2,64,640]{2,1,0:T(8,128)S(1)} collective-permute-done((f32[2,64,640]{2,1,0:T(8,128)S(1)}, f32[2,64,640]{2,1,0:T(8,128)S(1)}, u32[]{:S(2)}, u32[]{:S(2)}) %collective-permute-start.9) | collective-permute-done | bytes 327712 | tf_op jit(solution)/shard_map/ppermute | solution.py:112
  144.6 2.4 %collective-permute-start.10 = (f32[4,64,640]{2,1,0:T(8,128)S(1)}, f32[4,64,640]{2,1,0:T(8,128)S(1)}, u32[]{:S(2)}, u32[]{:S(2)}) collective-permute-start(f32[4,64,640]{2,1,0:T(8,128)S(1)} %bitcast.56), channel_id=1, source_target_pairs={{0,1},{1,0},{2,3},{3,2},{4,5},{5,4},{6,7},{7,6},{8,9},{9,8},{10,11... | collective-permute-start | bytes 1966088 | tf_op jit(solution)/shard_map/ppermute | solution.py:112
  147.2 2.5 %collective-permute-start.13 = (f32[2,2,64,640]{3,2,1,0:T(8,128)S(1)}, f32[2,2,64,640]{3,2,1,0:T(8,128)S(1)}, u32[]{:S(2)}, u32[]{:S(2)}) collective-permute-start(f32[2,2,64,640]{3,2,1,0:T(8,128)S(1)} %get-tuple-element.13), channel_id=1, source_target_pairs={{0,1},{1,0},{2,3},{3,2},{4,5},{5,4},{6,7},{7,6},{8,9},{9,8},{10,11... | collective-permute-start | bytes 1966088 | tf_op jit(solution)/shard_map/ppermute | solution.py:112
  149.7 1.9 collective-permute-start.14
  151.6 2.8 %shard_map.39 = f32[4,2,64,512]{3,2,1,0:T(8,128)} custom-call(s32[1]{0:T(128)} %bitcast.half_ref.core_ref, f32[4,64,640]{2,1,0:T(8,128)S(1)} %bitcast.58, f32[4,64,640]{2,1,0:T(8,128)S(1)} %collective-permute-done.10.moth_ref, f32[2,2,64,640]{3,2,1,0:T(8,128)S(1)} %get-tuple-element.14.nown_ref, f32[2,2,64,640]{3,2,1,0:T(8,128)S(1)} %collective-permute-done.13.noth_ref), custom_call_target="tpu_custom_call" | custom-call | flops 1006632960 | bytes 3670016 | tf_op jit(solution)/shard_map/pallas_call | solution.py:96
  154.4 4.2 %all-to-all-start.3 = ((f32[4,2,64,512]{3,2,1,0:T(8,128)}), f32[4,2,64,512]{3,2,1,0:T(8,128)}, u32[]{:S(2)}, u32[]{:S(2)}) async-start(f32[4,2,64,512]{3,2,1,0:T(8,128)} %shard_map.39), calls=%async_computation.3 | async-start | bytes 2097152 | tf_op jit(solution)/shard_map/all_to_all | solution.py:124
  158.6 9.4 %collective-permute-done.14.mown_ref = f32[4,64,640]{2,1,0:T(8,128)S(1)} collective-permute-done((f32[4,64,640]{2,1,0:T(8,128)S(1)}, f32[4,64,640]{2,1,0:T(8,128)S(1)}, u32[]{:S(2)}, u32[]{:S(2)}) %collective-permute-start.14) | collective-permute-done | bytes 655392 | tf_op jit(solution)/shard_map/ppermute | solution.py:112
  168.0 2.6 %collective-permute-start.15 = (f32[4,64,640]{2,1,0:T(8,128)S(1)}, f32[4,64,640]{2,1,0:T(8,128)S(1)}, u32[]{:S(2)}, u32[]{:S(2)}) collective-permute-start(f32[4,64,640]{2,1,0:T(8,128)S(1)} %collective-permute-done.14.mown_ref), channel_id=1, source_target_pairs={{0,1},{1,0},{2,3},{3,2},{4,5},{5,4},{6,7},{7,6},{8,9},{9,8},{10,11... | collective-permute-start | bytes 1966088 | tf_op jit(solution)/shard_map/ppermute | solution.py:112
  172.3 2.7 %shard_map.40 = f32[4,2,64,512]{3,2,1,0:T(8,128)} custom-call(s32[1]{0:T(128)} %bitcast.half_ref.core_ref, f32[4,64,640]{2,1,0:T(8,128)S(1)} %collective-permute-done.14.mown_ref, f32[4,64,640]{2,1,0:T(8,128)S(1)} %collective-permute-done.15.moth_ref, f32[2,2,64,640]{3,2,1,0:T(8,128)S(1)} %get-tuple-element.14.nown_ref, ...), custom_call_target="tpu_custom_call" | custom-call | flops 1006632960 | bytes 3670016 | tf_op jit(solution)/shard_map/pallas_call | solution.py:96
  175.1 3.5 %all-to-all-start.4 = ((f32[4,2,64,512]{3,2,1,0:T(8,128)}), f32[4,2,64,512]{3,2,1,0:T(8,128)S(1)}, u32[]{:S(2)}, u32[]{:S(2)}) async-start(f32[4,2,64,512]{3,2,1,0:T(8,128)} %shard_map.40), calls=%async_computation.4 | async-start | bytes 2097152 | tf_op jit(solution)/shard_map/all_to_all | solution.py:124
  179.9 13.5 %all-to-all-done.4 = f32[4,2,64,512]{3,2,1,0:T(8,128)S(1)} async-done(((f32[4,2,64,512]{3,2,1,0:T(8,128)}), f32[4,2,64,512]{3,2,1,0:T(8,128)S(1)}, u32[]{:S(2)}, u32[]{:S(2)}) %all-to-all-start.4) | async-done | bytes 1048608 | tf_op jit(solution)/shard_map/all_to_all | solution.py:124
  (50 shorter events, 11.9 us)
Async XLA Ops:
  0.0 1.6 copy-start
  1.6 1.3 copy-start.2
  2.9 0.7 copy-start.3
  3.6 13.3 %copy-start.1 = (f32[2,2,256,512]{3,2,1,0:T(8,128)S(1)}, f32[2,2,256,512]{3,2,1,0:T(8,128)}, u32[]{:S(2)}) copy-start(f32[2,2,256,512]{3,2,1,0:T(8,128)} %param.3) | copy-start | bytes 6291460
  3.6 13.3 %copy-start.4 = (s32[2,2,4]{2,1,0:T(2,128)S(1)}, s32[2,2,4]{2,1,0:T(2,128)}, u32[]{:S(2)}) copy-start(s32[2,2,4]{2,1,0:T(2,128)} %mask_ref.3) | copy-start | bytes 196
  6.2 13.3 %collective-permute-start.4 = (f32[4,2,32,640]{3,2,1,0:T(8,128)S(1)}, f32[4,2,32,640]{3,2,1,0:T(8,128)S(1)}, u32[]{:S(2)}, u32[]{:S(2)}) collective-permute-start(f32[4,2,32,640]{3,2,1,0:T(8,128)S(1)} %get-tuple-element.12), channel_id=1, source_target_pairs={{0,1},{1,0},{2,3},{3,2},{4,5},{5,4},{6,7},{7,6},{8,9},{9,8},{10,11... | collective-permute-start | bytes 1966088 | tf_op jit(solution)/shard_map/ppermute | solution.py:112
  15.0 9.0 %collective-permute-start = (f32[4,2,32,640]{3,2,1,0:T(8,128)S(1)}, f32[4,2,32,640]{3,2,1,0:T(8,128)S(1)}, u32[]{:S(2)}, u32[]{:S(2)}) collective-permute-start(f32[4,2,32,640]{3,2,1,0:T(8,128)S(1)} %get-tuple-element.10), channel_id=1, source_target_pairs={{0,1},{1,0},{2,3},{3,2},{4,5},{5,4},{6,7},{7,6},{8,9},{9,8},{10,11... | collective-permute-start | bytes 1966088 | tf_op jit(solution)/shard_map/ppermute | solution.py:112
  20.4 13.9 %all-to-all-start.1 = ((f32[4,2,32,640]{3,2,1,0:T(8,128)}), f32[4,2,32,640]{3,2,1,0:T(8,128)S(1)}, u32[]{:S(2)}, u32[]{:S(2)}) async-start(f32[4,2,32,640]{3,2,1,0:T(8,128)} %add.72), calls=%async_computation.1 | async-start | bytes 1310720 | tf_op jit(solution)/shard_map/all_to_all | solution.py:124
  34.4 12.7 %all-to-all-start = ((f32[4,2,32,640]{3,2,1,0:T(8,128)}), f32[4,2,32,640]{3,2,1,0:T(8,128)S(1)}, u32[]{:S(2)}, u32[]{:S(2)}) async-start(f32[4,2,32,640]{3,2,1,0:T(8,128)} %add.62), calls=%async_computation | async-start | bytes 1310720 | tf_op jit(solution)/shard_map/all_to_all | solution.py:124
  37.9 11.2 %collective-permute-start.5 = (f32[4,32,640]{2,1,0:T(8,128)S(1)}, f32[4,32,640]{2,1,0:T(8,128)S(1)}, u32[]{:S(2)}, u32[]{:S(2)}) collective-permute-start(f32[4,32,640]{2,1,0:T(8,128)S(1)} %dynamic-slice_bitcast_fusion.2), channel_id=1, source_target_pairs={{0,2},{2,0},{4,6},{6,4},{8,10},{10,8},{12,14},{14,12},{1,3},{3,1},... | collective-permute-start | bytes 983048 | tf_op jit(solution)/shard_map/ppermute | solution.py:112
  47.1 10.1 %collective-permute-start.1 = (f32[4,32,640]{2,1,0:T(8,128)S(1)}, f32[4,32,640]{2,1,0:T(8,128)S(1)}, u32[]{:S(2)}, u32[]{:S(2)}) collective-permute-start(f32[4,32,640]{2,1,0:T(8,128)S(1)} %dynamic-slice_bitcast_fusion.3), channel_id=1, source_target_pairs={{0,2},{2,0},{4,6},{6,4},{8,10},{10,8},{12,14},{14,12},{1,3},{3,1},... | collective-permute-start | bytes 983048 | tf_op jit(solution)/shard_map/ppermute | solution.py:112
  49.2 10.1 %collective-permute-start.6 = (f32[2,32,640]{2,1,0:T(8,128)S(1)}, f32[2,32,640]{2,1,0:T(8,128)S(1)}, u32[]{:S(2)}, u32[]{:S(2)}) collective-permute-start(f32[2,32,640]{2,1,0:T(8,128)S(1)} %dynamic-slice_bitcast_fusion.4), channel_id=1, source_target_pairs={{0,4},{2,6},{4,0},{6,2},{8,12},{10,14},{12,8},{14,10},{1,5},{3,7},... | collective-permute-start | bytes 491528 | tf_op jit(solution)/shard_map/ppermute | solution.py:112
  57.4 7.8 %collective-permute-start.2 = (f32[2,32,640]{2,1,0:T(8,128)S(1)}, f32[2,32,640]{2,1,0:T(8,128)S(1)}, u32[]{:S(2)}, u32[]{:S(2)}) collective-permute-start(f32[2,32,640]{2,1,0:T(8,128)S(1)} %dynamic-slice_bitcast_fusion.5), channel_id=1, source_target_pairs={{0,4},{2,6},{4,0},{6,2},{8,12},{10,14},{12,8},{14,10},{1,5},{3,7},... | collective-permute-start | bytes 491528 | tf_op jit(solution)/shard_map/ppermute | solution.py:112
  59.4 13.7 %collective-permute-start.7 = (f32[32,640]{1,0:T(8,128)S(1)}, f32[32,640]{1,0:T(8,128)S(1)}, u32[]{:S(2)}, u32[]{:S(2)}) collective-permute-start(f32[32,640]{1,0:T(8,128)S(1)} %dynamic-slice_bitcast_fusion.6), channel_id=1, source_target_pairs={{0,8},{2,10},{4,12},{6,14},{8,0},{10,2},{12,4},{14,6},{1,9},{3,11}... | collective-permute-start | bytes 245768 | tf_op jit(solution)/shard_map/ppermute | solution.py:112
  65.2 15.5 %collective-permute-start.3 = (f32[32,640]{1,0:T(8,128)S(1)}, f32[32,640]{1,0:T(8,128)S(1)}, u32[]{:S(2)}, u32[]{:S(2)}) collective-permute-start(f32[32,640]{1,0:T(8,128)S(1)} %dynamic-slice_bitcast_fusion.7), channel_id=1, source_target_pairs={{0,8},{2,10},{4,12},{6,14},{8,0},{10,2},{12,4},{14,6},{1,9},{3,11}... | collective-permute-start | bytes 245768 | tf_op jit(solution)/shard_map/ppermute | solution.py:112
  80.8 14.7 %collective-permute-start.11 = (f32[64,640]{1,0:T(8,128)S(1)}, f32[64,640]{1,0:T(8,128)S(1)}, u32[]{:S(2)}, u32[]{:S(2)}) collective-permute-start(f32[64,640]{1,0:T(8,128)S(1)} %pad_maximum_fusion.3), channel_id=1, source_target_pairs={{0,64},{2,0},{4,68},{6,4},{8,72},{10,8},{12,76},{14,12},{64,66},{6... | collective-permute-start | bytes 491528 | tf_op jit(solution)/shard_map/ppermute | solution.py:149
  92.9 2.6 %collective-permute-start.12 = (f32[64,640]{1,0:T(8,128)S(1)}, f32[64,640]{1,0:T(8,128)S(1)}, u32[]{:S(2)}, u32[]{:S(2)}) collective-permute-start(f32[64,640]{1,0:T(8,128)S(1)} %pad_maximum_fusion.3), channel_id=1, source_target_pairs={{2,64},{6,68},{10,72},{14,76},{64,2},{68,6},{72,10},{76,14},{3,65}... | collective-permute-start | bytes 491528 | tf_op jit(solution)/shard_map/ppermute | solution.py:150
  93.6 30.5 %collective-permute-start.8 = (f32[64,640]{1,0:T(8,128)S(1)}, f32[64,640]{1,0:T(8,128)S(1)}, u32[]{:S(2)}, u32[]{:S(2)}) collective-permute-start(f32[64,640]{1,0:T(8,128)S(1)} %pad_maximum_fusion.3), channel_id=1, source_target_pairs={{0,8},{2,10},{4,12},{6,14},{8,0},{10,2},{12,4},{14,6},{1,9},{3,11}... | collective-permute-start | bytes 491528 | tf_op jit(solution)/shard_map/ppermute | solution.py:112
  125.3 21.8 %all-to-all-start.2 = ((f32[4,2,64,640]{3,2,1,0:T(8,128)}), f32[4,2,64,640]{3,2,1,0:T(8,128)S(1)}, u32[]{:S(2)}, u32[]{:S(2)}) async-start(f32[4,2,64,640]{3,2,1,0:T(8,128)} %broadcast_in_dim.2), calls=%async_computation.2 | async-start | bytes 2621440 | tf_op jit(solution)/shard_map/all_to_all | solution.py:153
  128.9 15.7 %collective-permute-start.9 = (f32[2,64,640]{2,1,0:T(8,128)S(1)}, f32[2,64,640]{2,1,0:T(8,128)S(1)}, u32[]{:S(2)}, u32[]{:S(2)}) collective-permute-start(f32[2,64,640]{2,1,0:T(8,128)S(1)} %pad_maximum_fusion.1), channel_id=1, source_target_pairs={{0,4},{2,6},{4,0},{6,2},{8,12},{10,14},{12,8},{14,10},{1,5},{3,7},... | collective-permute-start | bytes 983048 | tf_op jit(solution)/shard_map/ppermute | solution.py:112
  144.6 7.0 %collective-permute-start.10 = (f32[4,64,640]{2,1,0:T(8,128)S(1)}, f32[4,64,640]{2,1,0:T(8,128)S(1)}, u32[]{:S(2)}, u32[]{:S(2)}) collective-permute-start(f32[4,64,640]{2,1,0:T(8,128)S(1)} %bitcast.56), channel_id=1, source_target_pairs={{0,1},{1,0},{2,3},{3,2},{4,5},{5,4},{6,7},{7,6},{8,9},{9,8},{10,11... | collective-permute-start | bytes 1966088 | tf_op jit(solution)/shard_map/ppermute | solution.py:112
  147.2 4.5 %collective-permute-start.13 = (f32[2,2,64,640]{3,2,1,0:T(8,128)S(1)}, f32[2,2,64,640]{3,2,1,0:T(8,128)S(1)}, u32[]{:S(2)}, u32[]{:S(2)}) collective-permute-start(f32[2,2,64,640]{3,2,1,0:T(8,128)S(1)} %get-tuple-element.13), channel_id=1, source_target_pairs={{0,1},{1,0},{2,3},{3,2},{4,5},{5,4},{6,7},{7,6},{8,9},{9,8},{10,11... | collective-permute-start | bytes 1966088 | tf_op jit(solution)/shard_map/ppermute | solution.py:112
  149.7 18.4 %collective-permute-start.14 = (f32[4,64,640]{2,1,0:T(8,128)S(1)}, f32[4,64,640]{2,1,0:T(8,128)S(1)}, u32[]{:S(2)}, u32[]{:S(2)}) collective-permute-start(f32[4,64,640]{2,1,0:T(8,128)S(1)} %bitcast.57), channel_id=1, source_target_pairs={{0,2},{2,0},{4,6},{6,4},{8,10},{10,8},{12,14},{14,12},{1,3},{3,1},... | collective-permute-start | bytes 1966088 | tf_op jit(solution)/shard_map/ppermute | solution.py:112
  154.4 20.7 %all-to-all-start.3 = ((f32[4,2,64,512]{3,2,1,0:T(8,128)}), f32[4,2,64,512]{3,2,1,0:T(8,128)}, u32[]{:S(2)}, u32[]{:S(2)}) async-start(f32[4,2,64,512]{3,2,1,0:T(8,128)} %shard_map.39), calls=%async_computation.3 | async-start | bytes 2097152 | tf_op jit(solution)/shard_map/all_to_all | solution.py:124
  168.0 4.3 %collective-permute-start.15 = (f32[4,64,640]{2,1,0:T(8,128)S(1)}, f32[4,64,640]{2,1,0:T(8,128)S(1)}, u32[]{:S(2)}, u32[]{:S(2)}) collective-permute-start(f32[4,64,640]{2,1,0:T(8,128)S(1)} %collective-permute-done.14.mown_ref), channel_id=1, source_target_pairs={{0,1},{1,0},{2,3},{3,2},{4,5},{5,4},{6,7},{7,6},{8,9},{9,8},{10,11... | collective-permute-start | bytes 1966088 | tf_op jit(solution)/shard_map/ppermute | solution.py:112
  175.1 18.3 %all-to-all-start.4 = ((f32[4,2,64,512]{3,2,1,0:T(8,128)}), f32[4,2,64,512]{3,2,1,0:T(8,128)S(1)}, u32[]{:S(2)}, u32[]{:S(2)}) async-start(f32[4,2,64,512]{3,2,1,0:T(8,128)} %shard_map.40), calls=%async_computation.4 | async-start | bytes 2097152 | tf_op jit(solution)/shard_map/all_to_all | solution.py:124

commit v6 on v5

--- a/solution.py
+++ b/solution.py
@@ -120,6 +120,10 @@
     return jnp.stack([jnp.where(bit == 0, own, got), jnp.where(bit == 0, got, own)], axis=axis)
 
 
+def after(value, other):
+    return lax.optimization_barrier((value, other))[0]
+
+
 def to_x(value):
     return lax.all_to_all(value, "x", split_axis=0, concat_axis=0)
 
@@ -138,11 +142,13 @@
     away = half_of(integrals, mask, coeffs, 1 - core)
     got = [swap(a, "core", 1, 2) for a in away]
     kept = half_of(integrals, mask, coeffs, core)
-    own = []
+    own, before = [], None
     for k, g in zip(kept, got):
-        part = to_x(k + g)
-        part = pick(part, low, 1) + swap(pick(part, 1 - low, 1), "zl", 1, 8)
-        part = part.reshape(2, 2, rows, norbit)
+        give = pick(k, 1 - low, 1) + pick(g, 1 - low, 1)
+        if before is not None:
+            give = after(give, before)
+        before = swap(give, "zl", 1, 8)
+        part = to_x(pick(k, low, 1) + pick(g, low, 1) + before).reshape(2, 2, rows, norbit)
         part = pick(part, mid, 1) + swap(pick(part, 1 - mid, 1), "zl", 2, 8)
         own.append(pick(part, top, 0) + swap(pick(part, 1 - top, 0), "zl", 4, 8))
     own = jnp.concatenate(own)
@@ -150,14 +156,15 @@
     far = lax.ppermute(own, ("zh", "zl"), FAR)
     fits = zh == low
     cols = join(jnp.where(fits, own, near), jnp.where(fits, near, far), low, 0)
-    n = lax.all_to_all(jnp.broadcast_to(cols[None], (4,) + cols.shape), "y", split_axis=0, concat_axis=0)
+    copies = jnp.broadcast_to(cols[None], (4,) + cols.shape)
+    n = lax.all_to_all(copies, "y", split_axis=0, concat_axis=0)
     n = n.reshape((2, 2) + cols.shape)
     nown, noth = pick(n, core, 0), swap(pick(n, 1 - core, 0), "core", 1, 2)
-    m = join(own, swap(own, "zl", 4, 8), top, 0)
+    m = join(own, after(swap(own, "zl", 4, 8), copies), top, 0)
     m = join(m, swap(m, "zl", 2, 8), mid, 1).reshape(4, 2 * rows, norbit)
     tiles = []
-    for m in (m, swap(m, "zl", 1, 8)):
-        tile = exchange_part(m, swap(m, "core", 1, 2), nown, noth, core)
+    for m, m_swap in ((m, after(m, nown)), (swap(m, "zl", 1, 8),) * 2):
+        tile = exchange_part(m, swap(m_swap, "core", 1, 2), nown, noth, core)
         tiles.append(jnp.sum(to_x(tile), axis=0))
     return join(*tiles, low, 1).reshape(mrows, lcols) * (1.0 / jnp.sqrt(jnp.float32(norbit * parts)))
 

time: 195 us -> 199 us (1.021)
  waiting for transfers between devices: 97.5 us -> 90.9 us
  starting transfers between devices: 76.2 us -> 80.7 us
  other arithmetic: 4.54 us -> 8.12 us
    all_to_all x4, waiting for transfers between devices: 30.2 us -> 20 us  [to_x(): return lax.all_to_all(value, 'x', split_axis=0, concat_axis=0)]
    all_to_all x4, starting transfers between devices: 14.7 us -> 20 us  [to_x(): return lax.all_to_all(value, 'x', split_axis=0, concat_axis=0)]
    ppermute x1, starting transfers between devices: 12.1 us -> 8.1 us  [local(): near = lax.ppermute(own, ('zh', 'zl'), NEAR)]
    ppermute x14, waiting for transfers between devices: 67.3 us -> 70.9 us  [swap(): return lax.ppermute(value, axis, [(i, i ^ bit) for i in range(size)])]
    add x4, other arithmetic: 1.96 us -> 5.53 us  [the longest x2 3.49 us: local(): pick(k, low, 1) + pick(g, low, 1) + before]
    ppermute x14, starting transfers between devices: 45.2 us -> 47.8 us  [swap(): return lax.ppermute(value, axis, [(i, i ^ bit) for i in range(size)])]
    unnamed x10 -> x12, local copies, waits for them, and re-layouts: 3.59 us -> 4.91 us
  transfers between devices with their start and end apart: 21 -> 21, of which waited for: 9 -> 13; matrix products, arithmetic and copies ran while one was open for 2% -> 4% of each run, Pallas kernels for 4% -> 4%
where the time goes in v6:
time: 199 us; the launch traced here: 198 us
  waiting for transfers between devices  90.9 us (46%)
  starting transfers between devices  80.7 us (41%)
  Pallas kernels  11.7 us (6%)
  other arithmetic  8.12 us (4%)
  local copies, waits for them, and re-layouts  6.23 us (3%)
    ppermute x14, waiting for transfers between devices, swap(): return lax.ppermute(value, axis, [(i, i ^ bit) for i in range(size)])  70.9 us
    ppermute x14, starting transfers between devices, swap(): return lax.ppermute(value, axis, [(i, i ^ bit) for i in range(size)])  47.8 us
    all_to_all x4, starting transfers between devices, to_x(): return lax.all_to_all(value, 'x', split_axis=0, concat_axis=0)  20 us
    all_to_all x4, waiting for transfers between devices, to_x(): return lax.all_to_all(value, 'x', split_axis=0, concat_axis=0)  20 us
    ppermute x1, starting transfers between devices, local(): near = lax.ppermute(own, ('zh', 'zl'), NEAR)  8.1 us
    pallas_call x2, Pallas kernels, half_of(): pl.pallas_call(half_kernel, out_shape=[jax.ShapeDtypeStruct(shape, jnp.fl...  6.21 us
    pallas_call x2, Pallas kernels, exchange_part(): pl.pallas_call(exchange_kernel, out_shape=jax.ShapeDtypeStruct((parts, 2,...  5.49 us
    unnamed x12, local copies, waits for them, and re-layouts  4.91 us
  transfers between devices with their start and end apart: 21, of which 13 were waited for; matrix products, arithmetic and copies ran while one was open for 4% of the time, Pallas kernels for 4%

profile of v6, /device:TPU:1, one launch (start us, length us, event | category | flops | bytes accessed | tf_op | source)
XLA Modules:
  0.0 198.1 jit_solution(9856883758076127359)
XLA Ops:
  3.6 3.6 %shard_map.38 = (f32[4,2,32,640]{3,2,1,0:T(8,128)}, f32[4,2,32,640]{3,2,1,0:T(8,128)}) custom-call(s32[1]{0:T(128)} %bitcast.2.half_ref, s32[2,2,4]{2,1,0:T(2,128)S(1)} %copy-done.4, f32[4,4,2,32,512]{4,3,2,1,0:T(8,128)S(1)} %bitcast.75, f32[512,640]{1,0:T(8,128)S(1)} %copy-done.2), custom_call_target="tpu_custom_call" | custom-call | flops 1006632960 | bytes 3670016 | tf_op jit(solution)/shard_map/pallas_call | solution.py:49
  7.2 8.8 %collective-permute-start = (f32[4,2,32,640]{3,2,1,0:T(8,128)}, f32[4,2,32,640]{3,2,1,0:T(8,128)}, u32[]{:S(2)}, u32[]{:S(2)}) collective-permute-start(f32[4,2,32,640]{3,2,1,0:T(8,128)} %get-tuple-element.13), channel_id=1, source_target_pairs={{0,1},{1,0},{2,3},{3,2},{4,5},{5,4},{6,7},{7,6},{8,9},{9,8},{10,11... | collective-permute-start | bytes 1966088 | tf_op jit(solution)/shard_map/ppermute | solution.py:112
  16.0 1.9 collective-permute-start.4
  19.3 2.6 %shard_map.37 = (f32[4,2,32,640]{3,2,1,0:T(8,128)S(1)}, f32[4,2,32,640]{3,2,1,0:T(8,128)S(1)}) custom-call(s32[1]{0:T(128)} %bitcast.half_ref.core_ref, s32[2,2,4]{2,1,0:T(2,128)S(1)} %copy-done.5, f32[4,4,2,32,512]{4,3,2,1,0:T(8,128)S(1)} %bitcast.76, f32[512,640]{1,0:T(8,128)S(1)} %copy-done.3), custom_call_target="tpu_custom_call" | custom-call | flops 1006632960 | bytes 3670016 | tf_op jit(solution)/shard_map/pallas_call | solution.py:49
  22.9 1.9 collective-permute-start.1
  25.9 7.7 %collective-permute-done.1 = f32[4,32,640]{2,1,0:T(8,128)S(1)} collective-permute-done((f32[4,32,640]{2,1,0:T(8,128)S(1)}, f32[4,32,640]{2,1,0:T(8,128)S(1)}, u32[]{:S(2)}, u32[]{:S(2)}) %collective-permute-start.1) | collective-permute-done | bytes 327712 | tf_op jit(solution)/shard_map/ppermute | solution.py:112
  33.6 2.2 %collective-permute-start.5 = (f32[4,32,640]{2,1,0:T(8,128)S(1)}, f32[4,32,640]{2,1,0:T(8,128)S(1)}, u32[]{:S(2)}, u32[]{:S(2)}) collective-permute-start(f32[4,32,640]{2,1,0:T(8,128)S(1)} %add_bitcast_fusion), channel_id=1, source_target_pairs={{0,2},{2,0},{4,6},{6,4},{8,10},{10,8},{12,14},{14,12},{1,3},{3,1},... | collective-permute-start | bytes 983048 | tf_op jit(solution)/shard_map/ppermute | solution.py:112
  37.6 3.5 %all-to-all-start = ((f32[4,32,640]{2,1,0:T(8,128)}), f32[4,32,640]{2,1,0:T(8,128)S(1)}, u32[]{:S(2)}, u32[]{:S(2)}) async-start(f32[4,32,640]{2,1,0:T(8,128)} %fusion.3), calls=%async_computation | async-start | bytes 655360 | tf_op jit(solution)/shard_map/all_to_all | solution.py:128
  41.0 2.3 %collective-permute-done.5 = f32[4,32,640]{2,1,0:T(8,128)S(1)} collective-permute-done((f32[4,32,640]{2,1,0:T(8,128)S(1)}, f32[4,32,640]{2,1,0:T(8,128)S(1)}, u32[]{:S(2)}, u32[]{:S(2)}) %collective-permute-start.5) | collective-permute-done | bytes 327712 | tf_op jit(solution)/shard_map/ppermute | solution.py:112
  46.9 3.5 %all-to-all-start.1 = ((f32[4,32,640]{2,1,0:T(8,128)}), f32[4,32,640]{2,1,0:T(8,128)S(1)}, u32[]{:S(2)}, u32[]{:S(2)}) async-start(f32[4,32,640]{2,1,0:T(8,128)} %fusion.1), calls=%async_computation.1 | async-start | bytes 655360 | tf_op jit(solution)/shard_map/all_to_all | solution.py:128
  50.4 1.9 collective-permute-start.2
  52.3 3.9 %all-to-all-done.1 = f32[4,32,640]{2,1,0:T(8,128)S(1)} async-done(((f32[4,32,640]{2,1,0:T(8,128)}), f32[4,32,640]{2,1,0:T(8,128)S(1)}, u32[]{:S(2)}, u32[]{:S(2)}) %all-to-all-start.1) | async-done | bytes 327712 | tf_op jit(solution)/shard_map/all_to_all | solution.py:128
  56.2 1.9 collective-permute-start.6
  60.0 7.4 %collective-permute-start.3 = (f32[32,640]{1,0:T(8,128)S(1)}, f32[32,640]{1,0:T(8,128)S(1)}, u32[]{:S(2)}, u32[]{:S(2)}) collective-permute-start(f32[32,640]{1,0:T(8,128)S(1)} %dynamic-slice_bitcast_fusion.5), channel_id=1, source_target_pairs={{0,8},{2,10},{4,12},{6,14},{8,0},{10,2},{12,4},{14,6},{1,9},{3,11}... | collective-permute-start | bytes 245768 | tf_op jit(solution)/shard_map/ppermute | solution.py:112
  67.5 7.9 %collective-permute-start.7 = (f32[32,640]{1,0:T(8,128)S(1)}, f32[32,640]{1,0:T(8,128)S(1)}, u32[]{:S(2)}, u32[]{:S(2)}) collective-permute-start(f32[32,640]{1,0:T(8,128)S(1)} %dynamic-slice_bitcast_fusion.4), channel_id=1, source_target_pairs={{0,8},{2,10},{4,12},{6,14},{8,0},{10,2},{12,4},{14,6},{1,9},{3,11}... | collective-permute-start | bytes 245768 | tf_op jit(solution)/shard_map/ppermute | solution.py:112
  75.5 9.8 %collective-permute-done.7 = f32[32,640]{1,0:T(8,128)S(1)} collective-permute-done((f32[32,640]{1,0:T(8,128)S(1)}, f32[32,640]{1,0:T(8,128)S(1)}, u32[]{:S(2)}, u32[]{:S(2)}) %collective-permute-start.7) | collective-permute-done | bytes 81952 | tf_op jit(solution)/shard_map/ppermute | solution.py:112
  85.3 8.1 %collective-permute-start.9 = (f32[64,640]{1,0:T(8,128)S(1)}, f32[64,640]{1,0:T(8,128)S(1)}, u32[]{:S(2)}, u32[]{:S(2)}) collective-permute-start(f32[64,640]{1,0:T(8,128)S(1)} %pad_maximum_fusion.3), channel_id=1, source_target_pairs={{0,64},{2,0},{4,68},{6,4},{8,72},{10,8},{12,76},{14,12},{64,66},{6... | collective-permute-start | bytes 491528 | tf_op jit(solution)/shard_map/ppermute | solution.py:155
  94.1 1.9 collective-permute-start.8
  97.3 4.2 %all-to-all-start.2 = ((f32[4,2,64,640]{3,2,1,0:T(8,128)}), f32[4,2,64,640]{3,2,1,0:T(8,128)S(1)}, u32[]{:S(2)}, u32[]{:S(2)}) async-start(f32[4,2,64,640]{3,2,1,0:T(8,128)} %broadcast_in_dim.2), calls=%async_computation.2 | async-start | bytes 2621440 | tf_op jit(solution)/shard_map/all_to_all | solution.py:160
  101.4 24.6 %collective-permute-done.8 = f32[64,640]{1,0:T(8,128)S(1)} collective-permute-done((f32[64,640]{1,0:T(8,128)S(1)}, f32[64,640]{1,0:T(8,128)S(1)}, u32[]{:S(2)}, u32[]{:S(2)}) %collective-permute-start.8) | collective-permute-done | bytes 163872 | tf_op jit(solution)/shard_map/ppermute | solution.py:112
  126.1 1.9 collective-permute-start.11
  128.0 17.0 %collective-permute-done.11 = f32[2,64,640]{2,1,0:T(8,128)S(1)} collective-permute-done((f32[2,64,640]{2,1,0:T(8,128)S(1)}, f32[2,64,640]{2,1,0:T(8,128)S(1)}, u32[]{:S(2)}, u32[]{:S(2)}) %collective-permute-start.11) | collective-permute-done | bytes 327712 | tf_op jit(solution)/shard_map/ppermute | solution.py:112
  145.2 2.9 %collective-permute-start.12 = (f32[4,64,640]{2,1,0:T(8,128)S(1)}, f32[4,64,640]{2,1,0:T(8,128)S(1)}, u32[]{:S(2)}, u32[]{:S(2)}) collective-permute-start(f32[4,64,640]{2,1,0:T(8,128)S(1)} %bitcast.72), channel_id=1, source_target_pairs={{0,1},{1,0},{2,3},{3,2},{4,5},{5,4},{6,7},{7,6},{8,9},{9,8},{10,11... | collective-permute-start | bytes 1966088 | tf_op jit(solution)/shard_map/ppermute | solution.py:112
  148.1 1.9 collective-permute-start.13
  150.1 1.9 collective-permute-start.14
  152.1 2.8 %shard_map.39 = f32[4,2,64,512]{3,2,1,0:T(8,128)} custom-call(s32[1]{0:T(128)} %bitcast.half_ref.core_ref, f32[4,64,640]{2,1,0:T(8,128)S(1)} %bitcast.74, f32[4,64,640]{2,1,0:T(8,128)S(1)} %collective-permute-done.12.moth_ref, f32[2,2,64,640]{3,2,1,0:T(8,128)S(1)} %get-tuple-element.20.nown_ref, f32[2,2,64,640]{3,2,1,0:T(8,128)S(1)} %collective-permute-done.13.noth_ref), custom_call_target="tpu_custom_call" | custom-call | flops 1006632960 | bytes 3670016 | tf_op jit(solution)/shard_map/pallas_call | solution.py:96
  154.9 7.1 %all-to-all-start.3 = ((f32[4,2,64,512]{3,2,1,0:T(8,128)}), f32[4,2,64,512]{3,2,1,0:T(8,128)}, u32[]{:S(2)}, u32[]{:S(2)}) async-start(f32[4,2,64,512]{3,2,1,0:T(8,128)} %shard_map.39), calls=%async_computation.3 | async-start | bytes 2097152 | tf_op jit(solution)/shard_map/all_to_all | solution.py:128
  162.0 5.9 %collective-permute-done.14.mown_ref = f32[4,64,640]{2,1,0:T(8,128)S(1)} collective-permute-done((f32[4,64,640]{2,1,0:T(8,128)S(1)}, f32[4,64,640]{2,1,0:T(8,128)S(1)}, u32[]{:S(2)}, u32[]{:S(2)}) %collective-permute-start.14) | collective-permute-done | bytes 655392 | tf_op jit(solution)/shard_map/ppermute | solution.py:112
  167.9 3.1 %collective-permute-start.15 = (f32[4,64,640]{2,1,0:T(8,128)S(1)}, f32[4,64,640]{2,1,0:T(8,128)S(1)}, u32[]{:S(2)}, u32[]{:S(2)}) collective-permute-start(f32[4,64,640]{2,1,0:T(8,128)S(1)} %collective-permute-done.14.mown_ref), channel_id=1, source_target_pairs={{0,1},{1,0},{2,3},{3,2},{4,5},{5,4},{6,7},{7,6},{8,9},{9,8},{10,11... | collective-permute-start | bytes 1966088 | tf_op jit(solution)/shard_map/ppermute | solution.py:112
  172.7 2.7 %shard_map.40 = f32[4,2,64,512]{3,2,1,0:T(8,128)} custom-call(s32[1]{0:T(128)} %bitcast.half_ref.core_ref, f32[4,64,640]{2,1,0:T(8,128)S(1)} %collective-permute-done.14.mown_ref, f32[4,64,640]{2,1,0:T(8,128)S(1)} %collective-permute-done.15.moth_ref, f32[2,2,64,640]{3,2,1,0:T(8,128)S(1)} %get-tuple-element.20.nown_ref, ...), custom_call_target="tpu_custom_call" | custom-call | flops 1006632960 | bytes 3670016 | tf_op jit(solution)/shard_map/pallas_call | solution.py:96
  176.5 6.0 %all-to-all-start.4 = ((f32[4,2,64,512]{3,2,1,0:T(8,128)}), f32[4,2,64,512]{3,2,1,0:T(8,128)S(1)}, u32[]{:S(2)}, u32[]{:S(2)}) async-start(f32[4,2,64,512]{3,2,1,0:T(8,128)} %shard_map.40), calls=%async_computation.4 | async-start | bytes 2097152 | tf_op jit(solution)/shard_map/all_to_all | solution.py:128
  183.9 13.2 %all-to-all-done.4 = f32[4,2,64,512]{3,2,1,0:T(8,128)S(1)} async-done(((f32[4,2,64,512]{3,2,1,0:T(8,128)}), f32[4,2,64,512]{3,2,1,0:T(8,128)S(1)}, u32[]{:S(2)}, u32[]{:S(2)}) %all-to-all-start.4) | async-done | bytes 1048608 | tf_op jit(solution)/shard_map/all_to_all | solution.py:128
  (51 shorter events, 21.6 us)
Async XLA Ops:
  0.0 1.6 copy-start
  1.6 1.3 copy-start.2
  2.9 0.7 copy-start.4
  3.6 14.4 %copy-start.1 = (f32[2,2,256,512]{3,2,1,0:T(8,128)S(1)}, f32[2,2,256,512]{3,2,1,0:T(8,128)}, u32[]{:S(2)}) copy-start(f32[2,2,256,512]{3,2,1,0:T(8,128)} %param.3) | copy-start | bytes 6291460
  3.6 14.4 %copy-start.5 = (s32[2,2,4]{2,1,0:T(2,128)S(1)}, s32[2,2,4]{2,1,0:T(2,128)}, u32[]{:S(2)}) copy-start(s32[2,2,4]{2,1,0:T(2,128)} %mask_ref.3) | copy-start | bytes 196
  7.2 14.6 %collective-permute-start = (f32[4,2,32,640]{3,2,1,0:T(8,128)}, f32[4,2,32,640]{3,2,1,0:T(8,128)}, u32[]{:S(2)}, u32[]{:S(2)}) collective-permute-start(f32[4,2,32,640]{3,2,1,0:T(8,128)} %get-tuple-element.13), channel_id=1, source_target_pairs={{0,1},{1,0},{2,3},{3,2},{4,5},{5,4},{6,7},{7,6},{8,9},{9,8},{10,11... | collective-permute-start | bytes 1966088 | tf_op jit(solution)/shard_map/ppermute | solution.py:112
  16.0 8.8 %collective-permute-start.4 = (f32[4,2,32,640]{3,2,1,0:T(8,128)}, f32[4,2,32,640]{3,2,1,0:T(8,128)}, u32[]{:S(2)}, u32[]{:S(2)}) collective-permute-start(f32[4,2,32,640]{3,2,1,0:T(8,128)} %get-tuple-element.15), channel_id=1, source_target_pairs={{0,1},{1,0},{2,3},{3,2},{4,5},{5,4},{6,7},{7,6},{8,9},{9,8},{10,11... | collective-permute-start | bytes 1966088 | tf_op jit(solution)/shard_map/ppermute | solution.py:112
  18.0 1.3 copy-start.3
  22.9 10.7 %collective-permute-start.1 = (f32[4,32,640]{2,1,0:T(8,128)S(1)}, f32[4,32,640]{2,1,0:T(8,128)S(1)}, u32[]{:S(2)}, u32[]{:S(2)}) collective-permute-start(f32[4,32,640]{2,1,0:T(8,128)S(1)} %add_bitcast_fusion.1), channel_id=1, source_target_pairs={{0,2},{2,0},{4,6},{6,4},{8,10},{10,8},{12,14},{14,12},{1,3},{3,1},... | collective-permute-start | bytes 983048 | tf_op jit(solution)/shard_map/ppermute | solution.py:112
  33.6 9.7 %collective-permute-start.5 = (f32[4,32,640]{2,1,0:T(8,128)S(1)}, f32[4,32,640]{2,1,0:T(8,128)S(1)}, u32[]{:S(2)}, u32[]{:S(2)}) collective-permute-start(f32[4,32,640]{2,1,0:T(8,128)S(1)} %add_bitcast_fusion), channel_id=1, source_target_pairs={{0,2},{2,0},{4,6},{6,4},{8,10},{10,8},{12,14},{14,12},{1,3},{3,1},... | collective-permute-start | bytes 983048 | tf_op jit(solution)/shard_map/ppermute | solution.py:112
  37.6 9.3 %all-to-all-start = ((f32[4,32,640]{2,1,0:T(8,128)}), f32[4,32,640]{2,1,0:T(8,128)S(1)}, u32[]{:S(2)}, u32[]{:S(2)}) async-start(f32[4,32,640]{2,1,0:T(8,128)} %fusion.3), calls=%async_computation | async-start | bytes 655360 | tf_op jit(solution)/shard_map/all_to_all | solution.py:128
  46.9 9.3 %all-to-all-start.1 = ((f32[4,32,640]{2,1,0:T(8,128)}), f32[4,32,640]{2,1,0:T(8,128)S(1)}, u32[]{:S(2)}, u32[]{:S(2)}) async-start(f32[4,32,640]{2,1,0:T(8,128)} %fusion.1), calls=%async_computation.1 | async-start | bytes 655360 | tf_op jit(solution)/shard_map/all_to_all | solution.py:128
  50.4 9.6 %collective-permute-start.2 = (f32[2,32,640]{2,1,0:T(8,128)S(1)}, f32[2,32,640]{2,1,0:T(8,128)S(1)}, u32[]{:S(2)}, u32[]{:S(2)}) collective-permute-start(f32[2,32,640]{2,1,0:T(8,128)S(1)} %dynamic-slice_bitcast_fusion.3), channel_id=1, source_target_pairs={{0,4},{2,6},{4,0},{6,2},{8,12},{10,14},{12,8},{14,10},{1,5},{3,7},... | collective-permute-start | bytes 491528 | tf_op jit(solution)/shard_map/ppermute | solution.py:112
  56.2 11.2 %collective-permute-start.6 = (f32[2,32,640]{2,1,0:T(8,128)S(1)}, f32[2,32,640]{2,1,0:T(8,128)S(1)}, u32[]{:S(2)}, u32[]{:S(2)}) collective-permute-start(f32[2,32,640]{2,1,0:T(8,128)S(1)} %dynamic-slice_bitcast_fusion.2), channel_id=1, source_target_pairs={{0,4},{2,6},{4,0},{6,2},{8,12},{10,14},{12,8},{14,10},{1,5},{3,7},... | collective-permute-start | bytes 491528 | tf_op jit(solution)/shard_map/ppermute | solution.py:112
  60.0 15.4 %collective-permute-start.3 = (f32[32,640]{1,0:T(8,128)S(1)}, f32[32,640]{1,0:T(8,128)S(1)}, u32[]{:S(2)}, u32[]{:S(2)}) collective-permute-start(f32[32,640]{1,0:T(8,128)S(1)} %dynamic-slice_bitcast_fusion.5), channel_id=1, source_target_pairs={{0,8},{2,10},{4,12},{6,14},{8,0},{10,2},{12,4},{14,6},{1,9},{3,11}... | collective-permute-start | bytes 245768 | tf_op jit(solution)/shard_map/ppermute | solution.py:112
  67.5 17.7 %collective-permute-start.7 = (f32[32,640]{1,0:T(8,128)S(1)}, f32[32,640]{1,0:T(8,128)S(1)}, u32[]{:S(2)}, u32[]{:S(2)}) collective-permute-start(f32[32,640]{1,0:T(8,128)S(1)} %dynamic-slice_bitcast_fusion.4), channel_id=1, source_target_pairs={{0,8},{2,10},{4,12},{6,14},{8,0},{10,2},{12,4},{14,6},{1,9},{3,11}... | collective-permute-start | bytes 245768 | tf_op jit(solution)/shard_map/ppermute | solution.py:112
  85.3 10.7 %collective-permute-start.9 = (f32[64,640]{1,0:T(8,128)S(1)}, f32[64,640]{1,0:T(8,128)S(1)}, u32[]{:S(2)}, u32[]{:S(2)}) collective-permute-start(f32[64,640]{1,0:T(8,128)S(1)} %pad_maximum_fusion.3), channel_id=1, source_target_pairs={{0,64},{2,0},{4,68},{6,4},{8,72},{10,8},{12,76},{14,12},{64,66},{6... | collective-permute-start | bytes 491528 | tf_op jit(solution)/shard_map/ppermute | solution.py:155
  93.4 2.6 %collective-permute-start.10 = (f32[64,640]{1,0:T(8,128)S(1)}, f32[64,640]{1,0:T(8,128)S(1)}, u32[]{:S(2)}, u32[]{:S(2)}) collective-permute-start(f32[64,640]{1,0:T(8,128)S(1)} %pad_maximum_fusion.3), channel_id=1, source_target_pairs={{2,64},{6,68},{10,72},{14,76},{64,2},{68,6},{72,10},{76,14},{3,65}... | collective-permute-start | bytes 491528 | tf_op jit(solution)/shard_map/ppermute | solution.py:156
  94.1 31.9 %collective-permute-start.8 = (f32[64,640]{1,0:T(8,128)S(1)}, f32[64,640]{1,0:T(8,128)S(1)}, u32[]{:S(2)}, u32[]{:S(2)}) collective-permute-start(f32[64,640]{1,0:T(8,128)S(1)} %pad_maximum_fusion.3), channel_id=1, source_target_pairs={{0,8},{2,10},{4,12},{6,14},{8,0},{10,2},{12,4},{14,6},{1,9},{3,11}... | collective-permute-start | bytes 491528 | tf_op jit(solution)/shard_map/ppermute | solution.py:112
  97.3 47.8 %all-to-all-start.2 = ((f32[4,2,64,640]{3,2,1,0:T(8,128)}), f32[4,2,64,640]{3,2,1,0:T(8,128)S(1)}, u32[]{:S(2)}, u32[]{:S(2)}) async-start(f32[4,2,64,640]{3,2,1,0:T(8,128)} %broadcast_in_dim.2), calls=%async_computation.2 | async-start | bytes 2621440 | tf_op jit(solution)/shard_map/all_to_all | solution.py:160
  126.1 18.9 %collective-permute-start.11 = (f32[2,64,640]{2,1,0:T(8,128)S(1)}, f32[2,64,640]{2,1,0:T(8,128)S(1)}, u32[]{:S(2)}, u32[]{:S(2)}) collective-permute-start(f32[2,64,640]{2,1,0:T(8,128)S(1)} %pad_maximum_fusion.2), channel_id=1, source_target_pairs={{0,4},{2,6},{4,0},{6,2},{8,12},{10,14},{12,8},{14,10},{1,5},{3,7},... | collective-permute-start | bytes 983048 | tf_op jit(solution)/shard_map/ppermute | solution.py:112
  145.2 6.8 %collective-permute-start.12 = (f32[4,64,640]{2,1,0:T(8,128)S(1)}, f32[4,64,640]{2,1,0:T(8,128)S(1)}, u32[]{:S(2)}, u32[]{:S(2)}) collective-permute-start(f32[4,64,640]{2,1,0:T(8,128)S(1)} %bitcast.72), channel_id=1, source_target_pairs={{0,1},{1,0},{2,3},{3,2},{4,5},{5,4},{6,7},{7,6},{8,9},{9,8},{10,11... | collective-permute-start | bytes 1966088 | tf_op jit(solution)/shard_map/ppermute | solution.py:112
  148.1 4.0 %collective-permute-start.13 = (f32[2,2,64,640]{3,2,1,0:T(8,128)S(1)}, f32[2,2,64,640]{3,2,1,0:T(8,128)S(1)}, u32[]{:S(2)}, u32[]{:S(2)}) collective-permute-start(f32[2,2,64,640]{3,2,1,0:T(8,128)S(1)} %get-tuple-element.19), channel_id=1, source_target_pairs={{0,1},{1,0},{2,3},{3,2},{4,5},{5,4},{6,7},{7,6},{8,9},{9,8},{10,11... | collective-permute-start | bytes 1966088 | tf_op jit(solution)/shard_map/ppermute | solution.py:112
  150.1 17.8 %collective-permute-start.14 = (f32[4,64,640]{2,1,0:T(8,128)S(1)}, f32[4,64,640]{2,1,0:T(8,128)S(1)}, u32[]{:S(2)}, u32[]{:S(2)}) collective-permute-start(f32[4,64,640]{2,1,0:T(8,128)S(1)} %bitcast.73), channel_id=1, source_target_pairs={{0,2},{2,0},{4,6},{6,4},{8,10},{10,8},{12,14},{14,12},{1,3},{3,1},... | collective-permute-start | bytes 1966088 | tf_op jit(solution)/shard_map/ppermute | solution.py:112
  154.9 21.6 %all-to-all-start.3 = ((f32[4,2,64,512]{3,2,1,0:T(8,128)}), f32[4,2,64,512]{3,2,1,0:T(8,128)}, u32[]{:S(2)}, u32[]{:S(2)}) async-start(f32[4,2,64,512]{3,2,1,0:T(8,128)} %shard_map.39), calls=%async_computation.3 | async-start | bytes 2097152 | tf_op jit(solution)/shard_map/all_to_all | solution.py:128
  167.9 4.9 %collective-permute-start.15 = (f32[4,64,640]{2,1,0:T(8,128)S(1)}, f32[4,64,640]{2,1,0:T(8,128)S(1)}, u32[]{:S(2)}, u32[]{:S(2)}) collective-permute-start(f32[4,64,640]{2,1,0:T(8,128)S(1)} %collective-permute-done.14.mown_ref), channel_id=1, source_target_pairs={{0,1},{1,0},{2,3},{3,2},{4,5},{5,4},{6,7},{7,6},{8,9},{9,8},{10,11... | collective-permute-start | bytes 1966088 | tf_op jit(solution)/shard_map/ppermute | solution.py:112
  176.5 20.6 %all-to-all-start.4 = ((f32[4,2,64,512]{3,2,1,0:T(8,128)}), f32[4,2,64,512]{3,2,1,0:T(8,128)S(1)}, u32[]{:S(2)}, u32[]{:S(2)}) async-start(f32[4,2,64,512]{3,2,1,0:T(8,128)} %shard_map.40), calls=%async_computation.4 | async-start | bytes 2097152 | tf_op jit(solution)/shard_map/all_to_all | solution.py:128

commit v7 on v6

--- a/solution.py
+++ b/solution.py
@@ -41,7 +41,7 @@
             o_ref[...] = total.reshape(o_ref.shape)
 
 
-def half_of(integrals, mask, coeffs, half):
+def half_of(integrals, mask, coeffs, half, vmem):
     parts, mrows, lcols = integrals.shape
     norbit = coeffs.shape[1]
     rows = mrows // 8
@@ -60,7 +60,7 @@
             scratch_shapes=[pltpu.VMEM((lcols, norbit), jnp.bfloat16)] * 2
             + [pltpu.VMEM((parts * 2 * rows, lcols), jnp.bfloat16)] * 2,
         ),
-        compiler_params=pltpu.CompilerParams(vmem_limit_bytes=VMEM),
+        compiler_params=pltpu.CompilerParams(vmem_limit_bytes=vmem),
         cost_estimate=pl.CostEstimate(flops=3 * parts * mrows * lcols * norbit, bytes_accessed=2 * parts * mrows * (lcols + norbit) + 4 * lcols * norbit, transcendentals=0),
     )(half.reshape(1), mask, integrals.reshape(parts, 4, 2, rows, lcols), coeffs)
 
@@ -139,28 +139,29 @@
     low, mid, top = zl & 1, (zl >> 1) & 1, zl >> 2
     parts, rows = nslab * naux, mrows // 8
     integrals = integrals.reshape(parts, mrows, lcols)
-    away = half_of(integrals, mask, coeffs, 1 - core)
+    away = half_of(integrals, mask, coeffs, 1 - core, 3 * VMEM)
     got = [swap(a, "core", 1, 2) for a in away]
-    kept = half_of(integrals, mask, coeffs, core)
+    kept = half_of(integrals, mask, coeffs, core, VMEM)
     own, before = [], None
     for k, g in zip(kept, got):
-        give = pick(k, 1 - low, 1) + pick(g, 1 - low, 1)
+        part = lax.optimization_barrier(k + g)
+        give = pick(part, 1 - low, 1)
         if before is not None:
             give = after(give, before)
         before = swap(give, "zl", 1, 8)
-        part = to_x(pick(k, low, 1) + pick(g, low, 1) + before).reshape(2, 2, rows, norbit)
+        part = to_x(pick(part, low, 1) + before).reshape(2, 2, rows, norbit)
         part = pick(part, mid, 1) + swap(pick(part, 1 - mid, 1), "zl", 2, 8)
         own.append(pick(part, top, 0) + swap(pick(part, 1 - top, 0), "zl", 4, 8))
     own = jnp.concatenate(own)
-    near = lax.ppermute(own, ("zh", "zl"), NEAR)
-    far = lax.ppermute(own, ("zh", "zl"), FAR)
+    m = join(own, swap(own, "zl", 4, 8), top, 0)
+    near = after(lax.ppermute(own, ("zh", "zl"), NEAR), m)
+    far = after(lax.ppermute(own, ("zh", "zl"), FAR), m)
     fits = zh == low
     cols = join(jnp.where(fits, own, near), jnp.where(fits, near, far), low, 0)
     copies = jnp.broadcast_to(cols[None], (4,) + cols.shape)
     n = lax.all_to_all(copies, "y", split_axis=0, concat_axis=0)
     n = n.reshape((2, 2) + cols.shape)
     nown, noth = pick(n, core, 0), swap(pick(n, 1 - core, 0), "core", 1, 2)
-    m = join(own, after(swap(own, "zl", 4, 8), copies), top, 0)
     m = join(m, swap(m, "zl", 2, 8), mid, 1).reshape(4, 2 * rows, norbit)
     tiles = []
     for m, m_swap in ((m, after(m, nown)), (swap(m, "zl", 1, 8),) * 2):

time: 199 us -> 200 us (level)
  the two profiles are of different devices: /device:TPU:1 before, /device:TPU:64 now
where the time goes in v7:
time: 200 us; the launch traced here: 199 us
  starting transfers between devices  112 us (56%)
  waiting for transfers between devices  64.3 us (32%)
  Pallas kernels  13.5 us (7%)
  other arithmetic  6.44 us (3%)
    ppermute x14, starting transfers between devices, swap(): return lax.ppermute(value, axis, [(i, i ^ bit) for i in range(size)])  78.4 us
    ppermute x14, waiting for transfers between devices, swap(): return lax.ppermute(value, axis, [(i, i ^ bit) for i in range(size)])  26.9 us
    all_to_all x4, waiting for transfers between devices, to_x(): return lax.all_to_all(value, 'x', split_axis=0, concat_axis=0)  24.7 us
    all_to_all x4, starting transfers between devices, to_x(): return lax.all_to_all(value, 'x', split_axis=0, concat_axis=0)  19.3 us
    ppermute x1, starting transfers between devices, local(): near = after(lax.ppermute(own, ('zh', 'zl'), NEAR), m)  9.11 us
    pallas_call x2, Pallas kernels, half_of(): pl.pallas_call(half_kernel, out_shape=[jax.ShapeDtypeStruct(shape, jnp.fl...  8.07 us
    ppermute x1, waiting for transfers between devices, local(): near = after(lax.ppermute(own, ('zh', 'zl'), NEAR), m)  8 us
    pallas_call x2, Pallas kernels, exchange_part(): pl.pallas_call(exchange_kernel, out_shape=jax.ShapeDtypeStruct((parts, 2,...  5.48 us
  transfers between devices with their start and end apart: 21, of which 13 were waited for; matrix products, arithmetic and copies ran while one was open for 3% of the time, Pallas kernels for 4%

profile of v7, /device:TPU:64, one launch (start us, length us, event | category | flops | bytes accessed | tf_op | source)
XLA Modules:
  0.0 198.5 jit_solution(13489251354526497048)
XLA Ops:
  0.0 5.5 %shard_map.38 = (f32[4,2,32,640]{3,2,1,0:T(8,128)}, f32[4,2,32,640]{3,2,1,0:T(8,128)}) custom-call(s32[1]{0:T(128)} %bitcast.2.half_ref, s32[2,2,4]{2,1,0:T(2,128)} %mask_ref.3, f32[4,4,2,32,512]{4,3,2,1,0:T(8,128)} %bitcast.59, f32[512,640]{1,0:T(8,128)} %c_ref.3), custom_call_target="tpu_custom_call" | custom-call | flops 1006632960 | bytes 3670016 | tf_op jit(solution)/shard_map/pallas_call | solution.py:49
  7.4 2.4 %collective-permute-start.4 = (f32[4,2,32,640]{3,2,1,0:T(8,128)}, f32[4,2,32,640]{3,2,1,0:T(8,128)}, u32[]{:S(2)}, u32[]{:S(2)}) collective-permute-start(f32[4,2,32,640]{3,2,1,0:T(8,128)} %get-tuple-element.16), channel_id=1, source_target_pairs={{0,1},{1,0},{2,3},{3,2},{4,5},{5,4},{6,7},{7,6},{8,9},{9,8},{10,11... | collective-permute-start | bytes 1966088 | tf_op jit(solution)/shard_map/ppermute | solution.py:112
  9.9 2.6 %shard_map.37 = (f32[4,2,32,640]{3,2,1,0:T(8,128)S(1)}, f32[4,2,32,640]{3,2,1,0:T(8,128)S(1)}) custom-call(s32[1]{0:T(128)} %bitcast.half_ref.core_ref, s32[2,2,4]{2,1,0:T(2,128)S(1)} %copy-done.2, f32[4,4,2,32,512]{4,3,2,1,0:T(8,128)S(1)} %bitcast.60, f32[512,640]{1,0:T(8,128)S(1)} %copy-done.1), custom_call_target="tpu_custom_call" | custom-call | flops 1006632960 | bytes 3670016 | tf_op jit(solution)/shard_map/pallas_call | solution.py:49
  13.7 3.8 %collective-permute-start.1 = (f32[4,32,640]{2,1,0:T(8,128)S(1)}, f32[4,32,640]{2,1,0:T(8,128)S(1)}, u32[]{:S(2)}, u32[]{:S(2)}) collective-permute-start(f32[4,32,640]{2,1,0:T(8,128)S(1)} %dynamic-slice_bitcast_fusion.3), channel_id=1, source_target_pairs={{0,2},{2,0},{4,6},{6,4},{8,10},{10,8},{12,14},{14,12},{1,3},{3,1},... | collective-permute-start | bytes 983048 | tf_op jit(solution)/shard_map/ppermute | solution.py:112
  18.7 6.7 %collective-permute-done.1 = f32[4,32,640]{2,1,0:T(8,128)S(1)} collective-permute-done((f32[4,32,640]{2,1,0:T(8,128)S(1)}, f32[4,32,640]{2,1,0:T(8,128)S(1)}, u32[]{:S(2)}, u32[]{:S(2)}) %collective-permute-start.1) | collective-permute-done | bytes 327712 | tf_op jit(solution)/shard_map/ppermute | solution.py:112
  25.4 3.6 %collective-permute-start.5 = (f32[4,32,640]{2,1,0:T(8,128)S(1)}, f32[4,32,640]{2,1,0:T(8,128)S(1)}, u32[]{:S(2)}, u32[]{:S(2)}) collective-permute-start(f32[4,32,640]{2,1,0:T(8,128)S(1)} %dynamic-slice_bitcast_fusion.2), channel_id=1, source_target_pairs={{0,2},{2,0},{4,6},{6,4},{8,10},{10,8},{12,14},{14,12},{1,3},{3,1},... | collective-permute-start | bytes 983048 | tf_op jit(solution)/shard_map/ppermute | solution.py:112
  29.8 4.3 %all-to-all-start = ((f32[4,32,640]{2,1,0:T(8,128)}), f32[4,32,640]{2,1,0:T(8,128)S(1)}, u32[]{:S(2)}, u32[]{:S(2)}) async-start(f32[4,32,640]{2,1,0:T(8,128)} %bitcast_add_fusion.1), calls=%async_computation | async-start | bytes 655360 | tf_op jit(solution)/shard_map/all_to_all | solution.py:128
  34.1 2.2 %collective-permute-done.5 = f32[4,32,640]{2,1,0:T(8,128)S(1)} collective-permute-done((f32[4,32,640]{2,1,0:T(8,128)S(1)}, f32[4,32,640]{2,1,0:T(8,128)S(1)}, u32[]{:S(2)}, u32[]{:S(2)}) %collective-permute-start.5) | collective-permute-done | bytes 327712 | tf_op jit(solution)/shard_map/ppermute | solution.py:112
  37.0 4.1 %all-to-all-done = f32[4,32,640]{2,1,0:T(8,128)S(1)} async-done(((f32[4,32,640]{2,1,0:T(8,128)}), f32[4,32,640]{2,1,0:T(8,128)S(1)}, u32[]{:S(2)}, u32[]{:S(2)}) %all-to-all-start) | async-done | bytes 327712 | tf_op jit(solution)/shard_map/all_to_all | solution.py:128
  41.1 3.5 %all-to-all-start.1 = ((f32[4,32,640]{2,1,0:T(8,128)}), f32[4,32,640]{2,1,0:T(8,128)S(1)}, u32[]{:S(2)}, u32[]{:S(2)}) async-start(f32[4,32,640]{2,1,0:T(8,128)} %bitcast_add_fusion), calls=%async_computation.1 | async-start | bytes 655360 | tf_op jit(solution)/shard_map/all_to_all | solution.py:128
  44.6 4.4 %collective-permute-start.2 = (f32[2,32,640]{2,1,0:T(8,128)S(1)}, f32[2,32,640]{2,1,0:T(8,128)S(1)}, u32[]{:S(2)}, u32[]{:S(2)}) collective-permute-start(f32[2,32,640]{2,1,0:T(8,128)S(1)} %dynamic-slice_bitcast_fusion.5), channel_id=1, source_target_pairs={{0,4},{2,6},{4,0},{6,2},{8,12},{10,14},{12,8},{14,10},{1,5},{3,7},... | collective-permute-start | bytes 491528 | tf_op jit(solution)/shard_map/ppermute | solution.py:112
  49.1 2.5 %all-to-all-done.1 = f32[4,32,640]{2,1,0:T(8,128)S(1)} async-done(((f32[4,32,640]{2,1,0:T(8,128)}), f32[4,32,640]{2,1,0:T(8,128)S(1)}, u32[]{:S(2)}, u32[]{:S(2)}) %all-to-all-start.1) | async-done | bytes 327712 | tf_op jit(solution)/shard_map/all_to_all | solution.py:128
  51.6 4.4 %collective-permute-start.6 = (f32[2,32,640]{2,1,0:T(8,128)S(1)}, f32[2,32,640]{2,1,0:T(8,128)S(1)}, u32[]{:S(2)}, u32[]{:S(2)}) collective-permute-start(f32[2,32,640]{2,1,0:T(8,128)S(1)} %dynamic-slice_bitcast_fusion.4), channel_id=1, source_target_pairs={{0,4},{2,6},{4,0},{6,2},{8,12},{10,14},{12,8},{14,10},{1,5},{3,7},... | collective-permute-start | bytes 491528 | tf_op jit(solution)/shard_map/ppermute | solution.py:112
  57.1 6.2 %collective-permute-start.3 = (f32[32,640]{1,0:T(8,128)S(1)}, f32[32,640]{1,0:T(8,128)S(1)}, u32[]{:S(2)}, u32[]{:S(2)}) collective-permute-start(f32[32,640]{1,0:T(8,128)S(1)} %dynamic-slice_bitcast_fusion.7), channel_id=1, source_target_pairs={{0,8},{2,10},{4,12},{6,14},{8,0},{10,2},{12,4},{14,6},{1,9},{3,11}... | collective-permute-start | bytes 245768 | tf_op jit(solution)/shard_map/ppermute | solution.py:112
  63.3 7.5 %collective-permute-start.7 = (f32[32,640]{1,0:T(8,128)S(1)}, f32[32,640]{1,0:T(8,128)S(1)}, u32[]{:S(2)}, u32[]{:S(2)}) collective-permute-start(f32[32,640]{1,0:T(8,128)S(1)} %dynamic-slice_bitcast_fusion.6), channel_id=1, source_target_pairs={{0,8},{2,10},{4,12},{6,14},{8,0},{10,2},{12,4},{14,6},{1,9},{3,11}... | collective-permute-start | bytes 245768 | tf_op jit(solution)/shard_map/ppermute | solution.py:112
  70.9 2.8 %collective-permute-done.7 = f32[32,640]{1,0:T(8,128)S(1)} collective-permute-done((f32[32,640]{1,0:T(8,128)S(1)}, f32[32,640]{1,0:T(8,128)S(1)}, u32[]{:S(2)}, u32[]{:S(2)}) %collective-permute-start.7) | collective-permute-done | bytes 81952 | tf_op jit(solution)/shard_map/ppermute | solution.py:112
  73.8 7.4 %collective-permute-start.8 = (f32[64,640]{1,0:T(8,128)S(1)}, f32[64,640]{1,0:T(8,128)S(1)}, u32[]{:S(2)}, u32[]{:S(2)}) collective-permute-start(f32[64,640]{1,0:T(8,128)S(1)} %pad_maximum_fusion.3), channel_id=1, source_target_pairs={{0,8},{2,10},{4,12},{6,14},{8,0},{10,2},{12,4},{14,6},{1,9},{3,11}... | collective-permute-start | bytes 491528 | tf_op jit(solution)/shard_map/ppermute | solution.py:112
  81.2 9.1 %collective-permute-start.10 = (f32[64,640]{1,0:T(8,128)S(1)}, f32[64,640]{1,0:T(8,128)S(1)}, u32[]{:S(2)}, u32[]{:S(2)}) collective-permute-start(f32[64,640]{1,0:T(8,128)S(1)} %pad_maximum_fusion.3), channel_id=1, source_target_pairs={{0,64},{2,0},{4,68},{6,4},{8,72},{10,8},{12,76},{14,12},{64,66},{6... | collective-permute-start | bytes 491528 | tf_op jit(solution)/shard_map/ppermute | solution.py:157
  91.1 8.0 %collective-permute-done.10 = f32[64,640]{1,0:T(8,128)S(1)} collective-permute-done((f32[64,640]{1,0:T(8,128)S(1)}, f32[64,640]{1,0:T(8,128)S(1)}, u32[]{:S(2)}, u32[]{:S(2)}) %collective-permute-start.10) | collective-permute-done | bytes 163872 | tf_op jit(solution)/shard_map/ppermute | solution.py:157
  100.3 4.9 %all-to-all-start.2 = ((f32[4,2,64,640]{3,2,1,0:T(8,128)}), f32[4,2,64,640]{3,2,1,0:T(8,128)S(1)}, u32[]{:S(2)}, u32[]{:S(2)}) async-start(f32[4,2,64,640]{3,2,1,0:T(8,128)} %broadcast_in_dim.2), calls=%async_computation.2 | async-start | bytes 2621440 | tf_op jit(solution)/shard_map/all_to_all | solution.py:162
  105.2 4.2 %collective-permute-start.9 = (f32[2,64,640]{2,1,0:T(8,128)S(1)}, f32[2,64,640]{2,1,0:T(8,128)S(1)}, u32[]{:S(2)}, u32[]{:S(2)}) collective-permute-start(f32[2,64,640]{2,1,0:T(8,128)S(1)} %pad_maximum_fusion.1), channel_id=1, source_target_pairs={{0,4},{2,6},{4,0},{6,2},{8,12},{10,14},{12,8},{14,10},{1,5},{3,7},... | collective-permute-start | bytes 983048 | tf_op jit(solution)/shard_map/ppermute | solution.py:112
  109.5 7.9 %collective-permute-done.9 = f32[2,64,640]{2,1,0:T(8,128)S(1)} collective-permute-done((f32[2,64,640]{2,1,0:T(8,128)S(1)}, f32[2,64,640]{2,1,0:T(8,128)S(1)}, u32[]{:S(2)}, u32[]{:S(2)}) %collective-permute-start.9) | collective-permute-done | bytes 327712 | tf_op jit(solution)/shard_map/ppermute | solution.py:112
  117.4 4.6 %all-to-all-done.2 = f32[4,2,64,640]{3,2,1,0:T(8,128)S(1)} async-done(((f32[4,2,64,640]{3,2,1,0:T(8,128)}), f32[4,2,64,640]{3,2,1,0:T(8,128)S(1)}, u32[]{:S(2)}, u32[]{:S(2)}) %all-to-all-start.2) | async-done | bytes 1310752 | tf_op jit(solution)/shard_map/all_to_all | solution.py:162
  124.1 2.4 %collective-permute-start.13 = (f32[2,2,64,640]{3,2,1,0:T(8,128)S(1)}, f32[2,2,64,640]{3,2,1,0:T(8,128)S(1)}, u32[]{:S(2)}, u32[]{:S(2)}) collective-permute-start(f32[2,2,64,640]{3,2,1,0:T(8,128)S(1)} %get-tuple-element.21), channel_id=1, source_target_pairs={{0,1},{1,0},{2,3},{3,2},{4,5},{5,4},{6,7},{7,6},{8,9},{9,8},{10,11... | collective-permute-start | bytes 1966088 | tf_op jit(solution)/shard_map/ppermute | solution.py:112
  126.5 26.2 %collective-permute-start.14 = (f32[4,64,640]{2,1,0:T(8,128)S(1)}, f32[4,64,640]{2,1,0:T(8,128)S(1)}, u32[]{:S(2)}, u32[]{:S(2)}) collective-permute-start(f32[4,64,640]{2,1,0:T(8,128)S(1)} %bitcast.57), channel_id=1, source_target_pairs={{0,2},{2,0},{4,6},{6,4},{8,10},{10,8},{12,14},{14,12},{1,3},{3,1},... | collective-permute-start | bytes 1966088 | tf_op jit(solution)/shard_map/ppermute | solution.py:112
  152.8 2.8 %shard_map.39 = f32[4,2,64,512]{3,2,1,0:T(8,128)} custom-call(s32[1]{0:T(128)} %bitcast.half_ref.core_ref, f32[4,64,640]{2,1,0:T(8,128)S(1)} %bitcast.58, f32[4,64,640]{2,1,0:T(8,128)S(1)} %collective-permute-done.12.moth_ref, f32[2,2,64,640]{3,2,1,0:T(8,128)S(1)} %get-tuple-element.22.nown_ref, f32[2,2,64,640]{3,2,1,0:T(8,128)S(1)} %collective-permute-done.13.noth_ref), custom_call_target="tpu_custom_call" | custom-call | flops 1006632960 | bytes 3670016 | tf_op jit(solution)/shard_map/pallas_call | solution.py:96
  155.5 7.8 %all-to-all-start.3 = ((f32[4,2,64,512]{3,2,1,0:T(8,128)}), f32[4,2,64,512]{3,2,1,0:T(8,128)}, u32[]{:S(2)}, u32[]{:S(2)}) async-start(f32[4,2,64,512]{3,2,1,0:T(8,128)} %shard_map.39), calls=%async_computation.3 | async-start | bytes 2097152 | tf_op jit(solution)/shard_map/all_to_all | solution.py:128
  163.3 4.3 %collective-permute-done.14.mown_ref = f32[4,64,640]{2,1,0:T(8,128)S(1)} collective-permute-done((f32[4,64,640]{2,1,0:T(8,128)S(1)}, f32[4,64,640]{2,1,0:T(8,128)S(1)}, u32[]{:S(2)}, u32[]{:S(2)}) %collective-permute-start.14) | collective-permute-done | bytes 655392 | tf_op jit(solution)/shard_map/ppermute | solution.py:112
  171.6 2.7 %shard_map.40 = f32[4,2,64,512]{3,2,1,0:T(8,128)} custom-call(s32[1]{0:T(128)} %bitcast.half_ref.core_ref, f32[4,64,640]{2,1,0:T(8,128)S(1)} %collective-permute-done.14.mown_ref, f32[4,64,640]{2,1,0:T(8,128)S(1)} %collective-permute-done.15.moth_ref, f32[2,2,64,640]{3,2,1,0:T(8,128)S(1)} %get-tuple-element.22.nown_ref, ...), custom_call_target="tpu_custom_call" | custom-call | flops 1006632960 | bytes 3670016 | tf_op jit(solution)/shard_map/pallas_call | solution.py:96
  174.3 4.1 %all-to-all-done.3 = f32[4,2,64,512]{3,2,1,0:T(8,128)} async-done(((f32[4,2,64,512]{3,2,1,0:T(8,128)}), f32[4,2,64,512]{3,2,1,0:T(8,128)}, u32[]{:S(2)}, u32[]{:S(2)}) %all-to-all-start.3) | async-done | bytes 1048608 | tf_op jit(solution)/shard_map/all_to_all | solution.py:128
  178.4 3.7 %all-to-all-start.4 = ((f32[4,2,64,512]{3,2,1,0:T(8,128)}), f32[4,2,64,512]{3,2,1,0:T(8,128)S(1)}, u32[]{:S(2)}, u32[]{:S(2)}) async-start(f32[4,2,64,512]{3,2,1,0:T(8,128)} %shard_map.40), calls=%async_computation.4 | async-start | bytes 2097152 | tf_op jit(solution)/shard_map/all_to_all | solution.py:128
  183.5 14.1 %all-to-all-done.4 = f32[4,2,64,512]{3,2,1,0:T(8,128)S(1)} async-done(((f32[4,2,64,512]{3,2,1,0:T(8,128)}), f32[4,2,64,512]{3,2,1,0:T(8,128)S(1)}, u32[]{:S(2)}, u32[]{:S(2)}) %all-to-all-start.4) | async-done | bytes 1048608 | tf_op jit(solution)/shard_map/all_to_all | solution.py:128
  (47 shorter events, 17.4 us)
Async XLA Ops:
  0.0 9.8 %copy-start = (f32[2,2,256,512]{3,2,1,0:T(8,128)S(1)}, f32[2,2,256,512]{3,2,1,0:T(8,128)}, u32[]{:S(2)}) copy-start(f32[2,2,256,512]{3,2,1,0:T(8,128)} %param.3) | copy-start | bytes 6291460
  0.0 9.9 %copy-start.1 = (f32[512,640]{1,0:T(8,128)S(1)}, f32[512,640]{1,0:T(8,128)}, u32[]{:S(2)}) copy-start(f32[512,640]{1,0:T(8,128)} %c_ref.3) | copy-start | bytes 3932164
  0.0 9.9 %copy-start.2 = (s32[2,2,4]{2,1,0:T(2,128)S(1)}, s32[2,2,4]{2,1,0:T(2,128)}, u32[]{:S(2)}) copy-start(s32[2,2,4]{2,1,0:T(2,128)} %mask_ref.3) | copy-start | bytes 196
  5.5 7.0 %collective-permute-start = (f32[4,2,32,640]{3,2,1,0:T(8,128)}, f32[4,2,32,640]{3,2,1,0:T(8,128)}, u32[]{:S(2)}, u32[]{:S(2)}) collective-permute-start(f32[4,2,32,640]{3,2,1,0:T(8,128)} %get-tuple-element.14), channel_id=1, source_target_pairs={{0,1},{1,0},{2,3},{3,2},{4,5},{5,4},{6,7},{7,6},{8,9},{9,8},{10,11... | collective-permute-start | bytes 1966088 | tf_op jit(solution)/shard_map/ppermute | solution.py:112
  7.4 10.1 %collective-permute-start.4 = (f32[4,2,32,640]{3,2,1,0:T(8,128)}, f32[4,2,32,640]{3,2,1,0:T(8,128)}, u32[]{:S(2)}, u32[]{:S(2)}) collective-permute-start(f32[4,2,32,640]{3,2,1,0:T(8,128)} %get-tuple-element.16), channel_id=1, source_target_pairs={{0,1},{1,0},{2,3},{3,2},{4,5},{5,4},{6,7},{7,6},{8,9},{9,8},{10,11... | collective-permute-start | bytes 1966088 | tf_op jit(solution)/shard_map/ppermute | solution.py:112
  13.7 11.7 %collective-permute-start.1 = (f32[4,32,640]{2,1,0:T(8,128)S(1)}, f32[4,32,640]{2,1,0:T(8,128)S(1)}, u32[]{:S(2)}, u32[]{:S(2)}) collective-permute-start(f32[4,32,640]{2,1,0:T(8,128)S(1)} %dynamic-slice_bitcast_fusion.3), channel_id=1, source_target_pairs={{0,2},{2,0},{4,6},{6,4},{8,10},{10,8},{12,14},{14,12},{1,3},{3,1},... | collective-permute-start | bytes 983048 | tf_op jit(solution)/shard_map/ppermute | solution.py:112
  25.4 10.9 %collective-permute-start.5 = (f32[4,32,640]{2,1,0:T(8,128)S(1)}, f32[4,32,640]{2,1,0:T(8,128)S(1)}, u32[]{:S(2)}, u32[]{:S(2)}) collective-permute-start(f32[4,32,640]{2,1,0:T(8,128)S(1)} %dynamic-slice_bitcast_fusion.2), channel_id=1, source_target_pairs={{0,2},{2,0},{4,6},{6,4},{8,10},{10,8},{12,14},{14,12},{1,3},{3,1},... | collective-permute-start | bytes 983048 | tf_op jit(solution)/shard_map/ppermute | solution.py:112
  29.8 11.3 %all-to-all-start = ((f32[4,32,640]{2,1,0:T(8,128)}), f32[4,32,640]{2,1,0:T(8,128)S(1)}, u32[]{:S(2)}, u32[]{:S(2)}) async-start(f32[4,32,640]{2,1,0:T(8,128)} %bitcast_add_fusion.1), calls=%async_computation | async-start | bytes 655360 | tf_op jit(solution)/shard_map/all_to_all | solution.py:128
  41.1 10.5 %all-to-all-start.1 = ((f32[4,32,640]{2,1,0:T(8,128)}), f32[4,32,640]{2,1,0:T(8,128)S(1)}, u32[]{:S(2)}, u32[]{:S(2)}) async-start(f32[4,32,640]{2,1,0:T(8,128)} %bitcast_add_fusion), calls=%async_computation.1 | async-start | bytes 655360 | tf_op jit(solution)/shard_map/all_to_all | solution.py:128
  44.6 12.4 %collective-permute-start.2 = (f32[2,32,640]{2,1,0:T(8,128)S(1)}, f32[2,32,640]{2,1,0:T(8,128)S(1)}, u32[]{:S(2)}, u32[]{:S(2)}) collective-permute-start(f32[2,32,640]{2,1,0:T(8,128)S(1)} %dynamic-slice_bitcast_fusion.5), channel_id=1, source_target_pairs={{0,4},{2,6},{4,0},{6,2},{8,12},{10,14},{12,8},{14,10},{1,5},{3,7},... | collective-permute-start | bytes 491528 | tf_op jit(solution)/shard_map/ppermute | solution.py:112
  51.6 11.7 %collective-permute-start.6 = (f32[2,32,640]{2,1,0:T(8,128)S(1)}, f32[2,32,640]{2,1,0:T(8,128)S(1)}, u32[]{:S(2)}, u32[]{:S(2)}) collective-permute-start(f32[2,32,640]{2,1,0:T(8,128)S(1)} %dynamic-slice_bitcast_fusion.4), channel_id=1, source_target_pairs={{0,4},{2,6},{4,0},{6,2},{8,12},{10,14},{12,8},{14,10},{1,5},{3,7},... | collective-permute-start | bytes 491528 | tf_op jit(solution)/shard_map/ppermute | solution.py:112
  57.1 13.8 %collective-permute-start.3 = (f32[32,640]{1,0:T(8,128)S(1)}, f32[32,640]{1,0:T(8,128)S(1)}, u32[]{:S(2)}, u32[]{:S(2)}) collective-permute-start(f32[32,640]{1,0:T(8,128)S(1)} %dynamic-slice_bitcast_fusion.7), channel_id=1, source_target_pairs={{0,8},{2,10},{4,12},{6,14},{8,0},{10,2},{12,4},{14,6},{1,9},{3,11}... | collective-permute-start | bytes 245768 | tf_op jit(solution)/shard_map/ppermute | solution.py:112
  63.3 10.4 %collective-permute-start.7 = (f32[32,640]{1,0:T(8,128)S(1)}, f32[32,640]{1,0:T(8,128)S(1)}, u32[]{:S(2)}, u32[]{:S(2)}) collective-permute-start(f32[32,640]{1,0:T(8,128)S(1)} %dynamic-slice_bitcast_fusion.6), channel_id=1, source_target_pairs={{0,8},{2,10},{4,12},{6,14},{8,0},{10,2},{12,4},{14,6},{1,9},{3,11}... | collective-permute-start | bytes 245768 | tf_op jit(solution)/shard_map/ppermute | solution.py:112
  73.8 17.2 %collective-permute-start.8 = (f32[64,640]{1,0:T(8,128)S(1)}, f32[64,640]{1,0:T(8,128)S(1)}, u32[]{:S(2)}, u32[]{:S(2)}) collective-permute-start(f32[64,640]{1,0:T(8,128)S(1)} %pad_maximum_fusion.3), channel_id=1, source_target_pairs={{0,8},{2,10},{4,12},{6,14},{8,0},{10,2},{12,4},{14,6},{1,9},{3,11}... | collective-permute-start | bytes 491528 | tf_op jit(solution)/shard_map/ppermute | solution.py:112
  81.2 17.9 %collective-permute-start.10 = (f32[64,640]{1,0:T(8,128)S(1)}, f32[64,640]{1,0:T(8,128)S(1)}, u32[]{:S(2)}, u32[]{:S(2)}) collective-permute-start(f32[64,640]{1,0:T(8,128)S(1)} %pad_maximum_fusion.3), channel_id=1, source_target_pairs={{0,64},{2,0},{4,68},{6,4},{8,72},{10,8},{12,76},{14,12},{64,66},{6... | collective-permute-start | bytes 491528 | tf_op jit(solution)/shard_map/ppermute | solution.py:157
  90.3 8.8 %collective-permute-start.11 = (f32[64,640]{1,0:T(8,128)S(1)}, f32[64,640]{1,0:T(8,128)S(1)}, u32[]{:S(2)}, u32[]{:S(2)}) collective-permute-start(f32[64,640]{1,0:T(8,128)S(1)} %pad_maximum_fusion.3), channel_id=1, source_target_pairs={{2,64},{6,68},{10,72},{14,76},{64,2},{68,6},{72,10},{76,14},{3,65}... | collective-permute-start | bytes 491528 | tf_op jit(solution)/shard_map/ppermute | solution.py:158
  100.3 21.8 %all-to-all-start.2 = ((f32[4,2,64,640]{3,2,1,0:T(8,128)}), f32[4,2,64,640]{3,2,1,0:T(8,128)S(1)}, u32[]{:S(2)}, u32[]{:S(2)}) async-start(f32[4,2,64,640]{3,2,1,0:T(8,128)} %broadcast_in_dim.2), calls=%async_computation.2 | async-start | bytes 2621440 | tf_op jit(solution)/shard_map/all_to_all | solution.py:162
  105.2 12.1 %collective-permute-start.9 = (f32[2,64,640]{2,1,0:T(8,128)S(1)}, f32[2,64,640]{2,1,0:T(8,128)S(1)}, u32[]{:S(2)}, u32[]{:S(2)}) collective-permute-start(f32[2,64,640]{2,1,0:T(8,128)S(1)} %pad_maximum_fusion.1), channel_id=1, source_target_pairs={{0,4},{2,6},{4,0},{6,2},{8,12},{10,14},{12,8},{14,10},{1,5},{3,7},... | collective-permute-start | bytes 983048 | tf_op jit(solution)/shard_map/ppermute | solution.py:112
  122.2 30.6 %collective-permute-start.12 = (f32[4,64,640]{2,1,0:T(8,128)S(1)}, f32[4,64,640]{2,1,0:T(8,128)S(1)}, u32[]{:S(2)}, u32[]{:S(2)}) collective-permute-start(f32[4,64,640]{2,1,0:T(8,128)S(1)} %bitcast.56), channel_id=1, source_target_pairs={{0,1},{1,0},{2,3},{3,2},{4,5},{5,4},{6,7},{7,6},{8,9},{9,8},{10,11... | collective-permute-start | bytes 1966088 | tf_op jit(solution)/shard_map/ppermute | solution.py:112
  124.1 28.6 %collective-permute-start.13 = (f32[2,2,64,640]{3,2,1,0:T(8,128)S(1)}, f32[2,2,64,640]{3,2,1,0:T(8,128)S(1)}, u32[]{:S(2)}, u32[]{:S(2)}) collective-permute-start(f32[2,2,64,640]{3,2,1,0:T(8,128)S(1)} %get-tuple-element.21), channel_id=1, source_target_pairs={{0,1},{1,0},{2,3},{3,2},{4,5},{5,4},{6,7},{7,6},{8,9},{9,8},{10,11... | collective-permute-start | bytes 1966088 | tf_op jit(solution)/shard_map/ppermute | solution.py:112
  126.5 41.1 %collective-permute-start.14 = (f32[4,64,640]{2,1,0:T(8,128)S(1)}, f32[4,64,640]{2,1,0:T(8,128)S(1)}, u32[]{:S(2)}, u32[]{:S(2)}) collective-permute-start(f32[4,64,640]{2,1,0:T(8,128)S(1)} %bitcast.57), channel_id=1, source_target_pairs={{0,2},{2,0},{4,6},{6,4},{8,10},{10,8},{12,14},{14,12},{1,3},{3,1},... | collective-permute-start | bytes 1966088 | tf_op jit(solution)/shard_map/ppermute | solution.py:112
  155.5 22.9 %all-to-all-start.3 = ((f32[4,2,64,512]{3,2,1,0:T(8,128)}), f32[4,2,64,512]{3,2,1,0:T(8,128)}, u32[]{:S(2)}, u32[]{:S(2)}) async-start(f32[4,2,64,512]{3,2,1,0:T(8,128)} %shard_map.39), calls=%async_computation.3 | async-start | bytes 2097152 | tf_op jit(solution)/shard_map/all_to_all | solution.py:128
  167.6 4.0 %collective-permute-start.15 = (f32[4,64,640]{2,1,0:T(8,128)S(1)}, f32[4,64,640]{2,1,0:T(8,128)S(1)}, u32[]{:S(2)}, u32[]{:S(2)}) collective-permute-start(f32[4,64,640]{2,1,0:T(8,128)S(1)} %collective-permute-done.14.mown_ref), channel_id=1, source_target_pairs={{0,1},{1,0},{2,3},{3,2},{4,5},{5,4},{6,7},{7,6},{8,9},{9,8},{10,11... | collective-permute-start | bytes 1966088 | tf_op jit(solution)/shard_map/ppermute | solution.py:112
  178.4 19.1 %all-to-all-start.4 = ((f32[4,2,64,512]{3,2,1,0:T(8,128)}), f32[4,2,64,512]{3,2,1,0:T(8,128)S(1)}, u32[]{:S(2)}, u32[]{:S(2)}) async-start(f32[4,2,64,512]{3,2,1,0:T(8,128)} %shard_map.40), calls=%async_computation.4 | async-start | bytes 2097152 | tf_op jit(solution)/shard_map/all_to_all | solution.py:128

commit v8 on v7

--- a/solution.py
+++ b/solution.py
@@ -128,8 +128,13 @@
     return lax.all_to_all(value, "x", split_axis=0, concat_axis=0)
 
 
-NEAR = [(z, (z + 8) % 16 if z % 2 == z // 8 else z ^ 1) for z in range(16)]
-FAR = [(z, (z ^ 1) ^ 8) for z in range(16) if z % 2 != z // 8]
+def column_planes(z):
+    half, x = z // 8, (z % 8 >> 1) ^ 1
+    return half * 8 + 2 * x + half, (1 - half) * 8 + 2 * x + half
+
+
+FIRST = [(z, column_planes(z)[z % 2]) for z in range(16)]
+SECOND = [(z, column_planes(z)[1 - z % 2]) for z in range(16)]
 
 
 def local(integrals, mask, coeffs):
@@ -150,19 +155,18 @@
             give = after(give, before)
         before = swap(give, "zl", 1, 8)
         part = to_x(pick(part, low, 1) + before).reshape(2, 2, rows, norbit)
-        part = pick(part, mid, 1) + swap(pick(part, 1 - mid, 1), "zl", 2, 8)
+        part = pick(part, 1 - mid, 1) + swap(pick(part, mid, 1), "zl", 2, 8)
         own.append(pick(part, top, 0) + swap(pick(part, 1 - top, 0), "zl", 4, 8))
     own = jnp.concatenate(own)
     m = join(own, swap(own, "zl", 4, 8), top, 0)
-    near = after(lax.ppermute(own, ("zh", "zl"), NEAR), m)
-    far = after(lax.ppermute(own, ("zh", "zl"), FAR), m)
-    fits = zh == low
-    cols = join(jnp.where(fits, own, near), jnp.where(fits, near, far), low, 0)
+    first = after(lax.ppermute(own, ("zh", "zl"), FIRST), m)
+    second = after(lax.ppermute(own, ("zh", "zl"), SECOND), m)
+    cols = join(first, second, jnp.where(zh == low, 0, 1), 0)
     copies = jnp.broadcast_to(cols[None], (4,) + cols.shape)
     n = lax.all_to_all(copies, "y", split_axis=0, concat_axis=0)
     n = n.reshape((2, 2) + cols.shape)
     nown, noth = pick(n, core, 0), swap(pick(n, 1 - core, 0), "core", 1, 2)
-    m = join(m, swap(m, "zl", 2, 8), mid, 1).reshape(4, 2 * rows, norbit)
+    m = join(m, swap(m, "zl", 2, 8), 1 - mid, 1).reshape(4, 2 * rows, norbit)
     tiles = []
     for m, m_swap in ((m, after(m, nown)), (swap(m, "zl", 1, 8),) * 2):
         tile = exchange_part(m, swap(m_swap, "core", 1, 2), nown, noth, core)

time: 200 us -> 189 us (0.945)
  the two profiles are of different devices: /device:TPU:64 before, /device:TPU:1 now
where the time goes in v8:
time: 189 us; the launch traced here: 188 us
  starting transfers between devices  92.2 us (49%)
  waiting for transfers between devices  74.3 us (39%)
  Pallas kernels  13.6 us (7%)
  other arithmetic  6.42 us (3%)
    ppermute x14, starting transfers between devices, swap(): return lax.ppermute(value, axis, [(i, i ^ bit) for i in range(size)])  65.2 us
    ppermute x14, waiting for transfers between devices, swap(): return lax.ppermute(value, axis, [(i, i ^ bit) for i in range(size)])  48.8 us
    all_to_all x4, waiting for transfers between devices, to_x(): return lax.all_to_all(value, 'x', split_axis=0, concat_axis=0)  18.7 us
    all_to_all x4, starting transfers between devices, to_x(): return lax.all_to_all(value, 'x', split_axis=0, concat_axis=0)  15 us
    pallas_call x2, Pallas kernels, half_of(): pl.pallas_call(half_kernel, out_shape=[jax.ShapeDtypeStruct(shape, jnp.fl...  8.07 us
    ppermute x1, starting transfers between devices, local(): second = after(lax.ppermute(own, ('zh', 'zl'), SECOND), m)  6.57 us
    pallas_call x2, Pallas kernels, exchange_part(): pl.pallas_call(exchange_kernel, out_shape=jax.ShapeDtypeStruct((parts, 2,...  5.48 us
    ppermute x1, waiting for transfers between devices, local(): second = after(lax.ppermute(own, ('zh', 'zl'), SECOND), m)  5.09 us
  transfers between devices with their start and end apart: 21, of which 13 were waited for; matrix products, arithmetic and copies ran while one was open for 3% of the time, Pallas kernels for 4%

profile of v8, /device:TPU:1, one launch (start us, length us, event | category | flops | bytes accessed | tf_op | source)
XLA Modules:
  0.0 188.4 jit_solution(11216554531499234207)
XLA Ops:
  0.0 5.5 %shard_map.38 = (f32[4,2,32,640]{3,2,1,0:T(8,128)}, f32[4,2,32,640]{3,2,1,0:T(8,128)}) custom-call(s32[1]{0:T(128)} %bitcast.2.half_ref, s32[2,2,4]{2,1,0:T(2,128)} %mask_ref.3, f32[4,4,2,32,512]{4,3,2,1,0:T(8,128)} %bitcast.59, f32[512,640]{1,0:T(8,128)} %c_ref.3), custom_call_target="tpu_custom_call" | custom-call | flops 1006632960 | bytes 3670016 | tf_op jit(solution)/shard_map/pallas_call | solution.py:49
  5.5 8.8 %collective-permute-start = (f32[4,2,32,640]{3,2,1,0:T(8,128)}, f32[4,2,32,640]{3,2,1,0:T(8,128)}, u32[]{:S(2)}, u32[]{:S(2)}) collective-permute-start(f32[4,2,32,640]{3,2,1,0:T(8,128)} %get-tuple-element.14), channel_id=1, source_target_pairs={{0,1},{1,0},{2,3},{3,2},{4,5},{5,4},{6,7},{7,6},{8,9},{9,8},{10,11... | collective-permute-start | bytes 1966088 | tf_op jit(solution)/shard_map/ppermute | solution.py:112
  14.3 1.9 %collective-permute-start.4 = (f32[4,2,32,640]{3,2,1,0:T(8,128)}, f32[4,2,32,640]{3,2,1,0:T(8,128)}, u32[]{:S(2)}, u32[]{:S(2)}) collective-permute-start(f32[4,2,32,640]{3,2,1,0:T(8,128)} %get-tuple-element.16), channel_id=1, source_target_pairs={{0,1},{1,0},{2,3},{3,2},{4,5},{5,4},{6,7},{7,6},{8,9},{9,8},{10,11... | collective-permute-start | bytes 1966088 | tf_op jit(solution)/shard_map/ppermute | solution.py:112
  16.3 2.6 %shard_map.37 = (f32[4,2,32,640]{3,2,1,0:T(8,128)S(1)}, f32[4,2,32,640]{3,2,1,0:T(8,128)S(1)}) custom-call(s32[1]{0:T(128)} %bitcast.half_ref.core_ref, s32[2,2,4]{2,1,0:T(2,128)S(1)} %copy-done.2, f32[4,4,2,32,512]{4,3,2,1,0:T(8,128)S(1)} %bitcast.60, f32[512,640]{1,0:T(8,128)S(1)} %copy-done.1), custom_call_target="tpu_custom_call" | custom-call | flops 1006632960 | bytes 3670016 | tf_op jit(solution)/shard_map/pallas_call | solution.py:49
  20.1 1.9 %collective-permute-start.1 = (f32[4,32,640]{2,1,0:T(8,128)S(1)}, f32[4,32,640]{2,1,0:T(8,128)S(1)}, u32[]{:S(2)}, u32[]{:S(2)}) collective-permute-start(f32[4,32,640]{2,1,0:T(8,128)S(1)} %dynamic-slice_bitcast_fusion.3), channel_id=1, source_target_pairs={{0,2},{2,0},{4,6},{6,4},{8,10},{10,8},{12,14},{14,12},{1,3},{3,1},... | collective-permute-start | bytes 983048 | tf_op jit(solution)/shard_map/ppermute | solution.py:112
  23.2 7.5 %collective-permute-done.1 = f32[4,32,640]{2,1,0:T(8,128)S(1)} collective-permute-done((f32[4,32,640]{2,1,0:T(8,128)S(1)}, f32[4,32,640]{2,1,0:T(8,128)S(1)}, u32[]{:S(2)}, u32[]{:S(2)}) %collective-permute-start.1) | collective-permute-done | bytes 327712 | tf_op jit(solution)/shard_map/ppermute | solution.py:112
  30.7 2.2 %collective-permute-start.5 = (f32[4,32,640]{2,1,0:T(8,128)S(1)}, f32[4,32,640]{2,1,0:T(8,128)S(1)}, u32[]{:S(2)}, u32[]{:S(2)}) collective-permute-start(f32[4,32,640]{2,1,0:T(8,128)S(1)} %dynamic-slice_bitcast_fusion.2), channel_id=1, source_target_pairs={{0,2},{2,0},{4,6},{6,4},{8,10},{10,8},{12,14},{14,12},{1,3},{3,1},... | collective-permute-start | bytes 983048 | tf_op jit(solution)/shard_map/ppermute | solution.py:112
  33.7 3.5 %all-to-all-start = ((f32[4,32,640]{2,1,0:T(8,128)}), f32[4,32,640]{2,1,0:T(8,128)S(1)}, u32[]{:S(2)}, u32[]{:S(2)}) async-start(f32[4,32,640]{2,1,0:T(8,128)} %bitcast_add_fusion.1), calls=%async_computation | async-start | bytes 655360 | tf_op jit(solution)/shard_map/all_to_all | solution.py:128
  37.2 3.3 %collective-permute-done.5 = f32[4,32,640]{2,1,0:T(8,128)S(1)} collective-permute-done((f32[4,32,640]{2,1,0:T(8,128)S(1)}, f32[4,32,640]{2,1,0:T(8,128)S(1)}, u32[]{:S(2)}, u32[]{:S(2)}) %collective-permute-start.5) | collective-permute-done | bytes 327712 | tf_op jit(solution)/shard_map/ppermute | solution.py:112
  43.1 3.5 %all-to-all-start.1 = ((f32[4,32,640]{2,1,0:T(8,128)}), f32[4,32,640]{2,1,0:T(8,128)S(1)}, u32[]{:S(2)}, u32[]{:S(2)}) async-start(f32[4,32,640]{2,1,0:T(8,128)} %bitcast_add_fusion), calls=%async_computation.1 | async-start | bytes 655360 | tf_op jit(solution)/shard_map/all_to_all | solution.py:128
  46.6 1.9 %collective-permute-start.2 = (f32[2,32,640]{2,1,0:T(8,128)S(1)}, f32[2,32,640]{2,1,0:T(8,128)S(1)}, u32[]{:S(2)}, u32[]{:S(2)}) collective-permute-start(f32[2,32,640]{2,1,0:T(8,128)S(1)} %dynamic-slice_bitcast_fusion.5), channel_id=1, source_target_pairs={{0,4},{2,6},{4,0},{6,2},{8,12},{10,14},{12,8},{14,10},{1,5},{3,7},... | collective-permute-start | bytes 491528 | tf_op jit(solution)/shard_map/ppermute | solution.py:112
  48.5 3.9 %all-to-all-done.1 = f32[4,32,640]{2,1,0:T(8,128)S(1)} async-done(((f32[4,32,640]{2,1,0:T(8,128)}), f32[4,32,640]{2,1,0:T(8,128)S(1)}, u32[]{:S(2)}, u32[]{:S(2)}) %all-to-all-start.1) | async-done | bytes 327712 | tf_op jit(solution)/shard_map/all_to_all | solution.py:128
  52.4 1.9 %collective-permute-start.6 = (f32[2,32,640]{2,1,0:T(8,128)S(1)}, f32[2,32,640]{2,1,0:T(8,128)S(1)}, u32[]{:S(2)}, u32[]{:S(2)}) collective-permute-start(f32[2,32,640]{2,1,0:T(8,128)S(1)} %dynamic-slice_bitcast_fusion.4), channel_id=1, source_target_pairs={{0,4},{2,6},{4,0},{6,2},{8,12},{10,14},{12,8},{14,10},{1,5},{3,7},... | collective-permute-start | bytes 491528 | tf_op jit(solution)/shard_map/ppermute | solution.py:112
  56.2 7.4 %collective-permute-start.3 = (f32[32,640]{1,0:T(8,128)S(1)}, f32[32,640]{1,0:T(8,128)S(1)}, u32[]{:S(2)}, u32[]{:S(2)}) collective-permute-start(f32[32,640]{1,0:T(8,128)S(1)} %dynamic-slice_bitcast_fusion.7), channel_id=1, source_target_pairs={{0,8},{2,10},{4,12},{6,14},{8,0},{10,2},{12,4},{14,6},{1,9},{3,11}... | collective-permute-start | bytes 245768 | tf_op jit(solution)/shard_map/ppermute | solution.py:112
  63.6 7.9 %collective-permute-start.7 = (f32[32,640]{1,0:T(8,128)S(1)}, f32[32,640]{1,0:T(8,128)S(1)}, u32[]{:S(2)}, u32[]{:S(2)}) collective-permute-start(f32[32,640]{1,0:T(8,128)S(1)} %dynamic-slice_bitcast_fusion.6), channel_id=1, source_target_pairs={{0,8},{2,10},{4,12},{6,14},{8,0},{10,2},{12,4},{14,6},{1,9},{3,11}... | collective-permute-start | bytes 245768 | tf_op jit(solution)/shard_map/ppermute | solution.py:112
  71.6 9.8 %collective-permute-done.7 = f32[32,640]{1,0:T(8,128)S(1)} collective-permute-done((f32[32,640]{1,0:T(8,128)S(1)}, f32[32,640]{1,0:T(8,128)S(1)}, u32[]{:S(2)}, u32[]{:S(2)}) %collective-permute-start.7) | collective-permute-done | bytes 81952 | tf_op jit(solution)/shard_map/ppermute | solution.py:112
  81.4 1.9 %collective-permute-start.8 = (f32[64,640]{1,0:T(8,128)S(1)}, f32[64,640]{1,0:T(8,128)S(1)}, u32[]{:S(2)}, u32[]{:S(2)}) collective-permute-start(f32[64,640]{1,0:T(8,128)S(1)} %pad_maximum_fusion.3), channel_id=1, source_target_pairs={{0,8},{2,10},{4,12},{6,14},{8,0},{10,2},{12,4},{14,6},{1,9},{3,11}... | collective-permute-start | bytes 491528 | tf_op jit(solution)/shard_map/ppermute | solution.py:112
  85.3 6.6 %collective-permute-start.11 = (f32[64,640]{1,0:T(8,128)S(1)}, f32[64,640]{1,0:T(8,128)S(1)}, u32[]{:S(2)}, u32[]{:S(2)}) collective-permute-start(f32[64,640]{1,0:T(8,128)S(1)} %pad_maximum_fusion.3), channel_id=1, source_target_pairs={{0,68},{2,4},{4,64},{6,0},{8,76},{10,12},{12,72},{14,8},{64,6},{66... | collective-permute-start | bytes 491528 | tf_op jit(solution)/shard_map/ppermute | solution.py:163
  91.9 5.6 %collective-permute-done.8 = f32[64,640]{1,0:T(8,128)S(1)} collective-permute-done((f32[64,640]{1,0:T(8,128)S(1)}, f32[64,640]{1,0:T(8,128)S(1)}, u32[]{:S(2)}, u32[]{:S(2)}) %collective-permute-start.8) | collective-permute-done | bytes 163872 | tf_op jit(solution)/shard_map/ppermute | solution.py:112
  97.5 5.1 %collective-permute-done.11 = f32[64,640]{1,0:T(8,128)S(1)} collective-permute-done((f32[64,640]{1,0:T(8,128)S(1)}, f32[64,640]{1,0:T(8,128)S(1)}, u32[]{:S(2)}, u32[]{:S(2)}) %collective-permute-start.11) | collective-permute-done | bytes 163872 | tf_op jit(solution)/shard_map/ppermute | solution.py:163
  103.8 3.5 %all-to-all-start.2 = ((f32[4,2,64,640]{3,2,1,0:T(8,128)}), f32[4,2,64,640]{3,2,1,0:T(8,128)S(1)}, u32[]{:S(2)}, u32[]{:S(2)}) async-start(f32[4,2,64,640]{3,2,1,0:T(8,128)} %broadcast_in_dim.2), calls=%async_computation.2 | async-start | bytes 2621440 | tf_op jit(solution)/shard_map/all_to_all | solution.py:166
  107.4 2.3 %collective-permute-start.9 = (f32[2,64,640]{2,1,0:T(8,128)S(1)}, f32[2,64,640]{2,1,0:T(8,128)S(1)}, u32[]{:S(2)}, u32[]{:S(2)}) collective-permute-start(f32[2,64,640]{2,1,0:T(8,128)S(1)} %pad_maximum_fusion.1), channel_id=1, source_target_pairs={{0,4},{2,6},{4,0},{6,2},{8,12},{10,14},{12,8},{14,10},{1,5},{3,7},... | collective-permute-start | bytes 983048 | tf_op jit(solution)/shard_map/ppermute | solution.py:112
  109.7 11.3 %collective-permute-done.9 = f32[2,64,640]{2,1,0:T(8,128)S(1)} collective-permute-done((f32[2,64,640]{2,1,0:T(8,128)S(1)}, f32[2,64,640]{2,1,0:T(8,128)S(1)}, u32[]{:S(2)}, u32[]{:S(2)}) %collective-permute-start.9) | collective-permute-done | bytes 327712 | tf_op jit(solution)/shard_map/ppermute | solution.py:112
  123.0 5.2 %collective-permute-start.12 = (f32[4,64,640]{2,1,0:T(8,128)S(1)}, f32[4,64,640]{2,1,0:T(8,128)S(1)}, u32[]{:S(2)}, u32[]{:S(2)}) collective-permute-start(f32[4,64,640]{2,1,0:T(8,128)S(1)} %bitcast.56), channel_id=1, source_target_pairs={{0,1},{1,0},{2,3},{3,2},{4,5},{5,4},{6,7},{7,6},{8,9},{9,8},{10,11... | collective-permute-start | bytes 1966088 | tf_op jit(solution)/shard_map/ppermute | solution.py:112
  130.2 17.0 %collective-permute-start.14 = (f32[4,64,640]{2,1,0:T(8,128)S(1)}, f32[4,64,640]{2,1,0:T(8,128)S(1)}, u32[]{:S(2)}, u32[]{:S(2)}) collective-permute-start(f32[4,64,640]{2,1,0:T(8,128)S(1)} %bitcast.57), channel_id=1, source_target_pairs={{0,2},{2,0},{4,6},{6,4},{8,10},{10,8},{12,14},{14,12},{1,3},{3,1},... | collective-permute-start | bytes 1966088 | tf_op jit(solution)/shard_map/ppermute | solution.py:112
  147.2 2.8 %shard_map.39 = f32[4,2,64,512]{3,2,1,0:T(8,128)} custom-call(s32[1]{0:T(128)} %bitcast.half_ref.core_ref, f32[4,64,640]{2,1,0:T(8,128)S(1)} %bitcast.58, f32[4,64,640]{2,1,0:T(8,128)S(1)} %collective-permute-done.12.moth_ref, f32[2,2,64,640]{3,2,1,0:T(8,128)S(1)} %get-tuple-element.22.nown_ref, f32[2,2,64,640]{3,2,1,0:T(8,128)S(1)} %collective-permute-done.13.noth_ref), custom_call_target="tpu_custom_call" | custom-call | flops 1006632960 | bytes 3670016 | tf_op jit(solution)/shard_map/pallas_call | solution.py:96
  150.0 4.2 %all-to-all-start.3 = ((f32[4,2,64,512]{3,2,1,0:T(8,128)}), f32[4,2,64,512]{3,2,1,0:T(8,128)}, u32[]{:S(2)}, u32[]{:S(2)}) async-start(f32[4,2,64,512]{3,2,1,0:T(8,128)} %shard_map.39), calls=%async_computation.3 | async-start | bytes 2097152 | tf_op jit(solution)/shard_map/all_to_all | solution.py:128
  154.3 7.7 %collective-permute-done.14.mown_ref = f32[4,64,640]{2,1,0:T(8,128)S(1)} collective-permute-done((f32[4,64,640]{2,1,0:T(8,128)S(1)}, f32[4,64,640]{2,1,0:T(8,128)S(1)}, u32[]{:S(2)}, u32[]{:S(2)}) %collective-permute-start.14) | collective-permute-done | bytes 655392 | tf_op jit(solution)/shard_map/ppermute | solution.py:112
  162.0 2.8 %collective-permute-start.15 = (f32[4,64,640]{2,1,0:T(8,128)S(1)}, f32[4,64,640]{2,1,0:T(8,128)S(1)}, u32[]{:S(2)}, u32[]{:S(2)}) collective-permute-start(f32[4,64,640]{2,1,0:T(8,128)S(1)} %collective-permute-done.14.mown_ref), channel_id=1, source_target_pairs={{0,1},{1,0},{2,3},{3,2},{4,5},{5,4},{6,7},{7,6},{8,9},{9,8},{10,11... | collective-permute-start | bytes 1966088 | tf_op jit(solution)/shard_map/ppermute | solution.py:112
  166.5 2.7 %shard_map.40 = f32[4,2,64,512]{3,2,1,0:T(8,128)} custom-call(s32[1]{0:T(128)} %bitcast.half_ref.core_ref, f32[4,64,640]{2,1,0:T(8,128)S(1)} %collective-permute-done.14.mown_ref, f32[4,64,640]{2,1,0:T(8,128)S(1)} %collective-permute-done.15.moth_ref, f32[2,2,64,640]{3,2,1,0:T(8,128)S(1)} %get-tuple-element.22.nown_ref, ...), custom_call_target="tpu_custom_call" | custom-call | flops 1006632960 | bytes 3670016 | tf_op jit(solution)/shard_map/pallas_call | solution.py:96
  169.2 3.8 %all-to-all-start.4 = ((f32[4,2,64,512]{3,2,1,0:T(8,128)}), f32[4,2,64,512]{3,2,1,0:T(8,128)S(1)}, u32[]{:S(2)}, u32[]{:S(2)}) async-start(f32[4,2,64,512]{3,2,1,0:T(8,128)} %shard_map.40), calls=%async_computation.4 | async-start | bytes 2097152 | tf_op jit(solution)/shard_map/all_to_all | solution.py:128
  174.4 13.0 %all-to-all-done.4 = f32[4,2,64,512]{3,2,1,0:T(8,128)S(1)} async-done(((f32[4,2,64,512]{3,2,1,0:T(8,128)}), f32[4,2,64,512]{3,2,1,0:T(8,128)S(1)}, u32[]{:S(2)}, u32[]{:S(2)}) %all-to-all-start.4) | async-done | bytes 1048608 | tf_op jit(solution)/shard_map/all_to_all | solution.py:128
  (47 shorter events, 18.8 us)
Async XLA Ops:
  0.0 16.2 %copy-start = (f32[2,2,256,512]{3,2,1,0:T(8,128)S(1)}, f32[2,2,256,512]{3,2,1,0:T(8,128)}, u32[]{:S(2)}) copy-start(f32[2,2,256,512]{3,2,1,0:T(8,128)} %param.3) | copy-start | bytes 6291460
  0.0 16.2 %copy-start.1 = (f32[512,640]{1,0:T(8,128)S(1)}, f32[512,640]{1,0:T(8,128)}, u32[]{:S(2)}) copy-start(f32[512,640]{1,0:T(8,128)} %c_ref.3) | copy-start | bytes 3932164
  0.0 16.2 %copy-start.2 = (s32[2,2,4]{2,1,0:T(2,128)S(1)}, s32[2,2,4]{2,1,0:T(2,128)}, u32[]{:S(2)}) copy-start(s32[2,2,4]{2,1,0:T(2,128)} %mask_ref.3) | copy-start | bytes 196
  5.5 13.3 %collective-permute-start = (f32[4,2,32,640]{3,2,1,0:T(8,128)}, f32[4,2,32,640]{3,2,1,0:T(8,128)}, u32[]{:S(2)}, u32[]{:S(2)}) collective-permute-start(f32[4,2,32,640]{3,2,1,0:T(8,128)} %get-tuple-element.14), channel_id=1, source_target_pairs={{0,1},{1,0},{2,3},{3,2},{4,5},{5,4},{6,7},{7,6},{8,9},{9,8},{10,11... | collective-permute-start | bytes 1966088 | tf_op jit(solution)/shard_map/ppermute | solution.py:112
  14.3 7.7 %collective-permute-start.4 = (f32[4,2,32,640]{3,2,1,0:T(8,128)}, f32[4,2,32,640]{3,2,1,0:T(8,128)}, u32[]{:S(2)}, u32[]{:S(2)}) collective-permute-start(f32[4,2,32,640]{3,2,1,0:T(8,128)} %get-tuple-element.16), channel_id=1, source_target_pairs={{0,1},{1,0},{2,3},{3,2},{4,5},{5,4},{6,7},{7,6},{8,9},{9,8},{10,11... | collective-permute-start | bytes 1966088 | tf_op jit(solution)/shard_map/ppermute | solution.py:112
  20.1 10.7 %collective-permute-start.1 = (f32[4,32,640]{2,1,0:T(8,128)S(1)}, f32[4,32,640]{2,1,0:T(8,128)S(1)}, u32[]{:S(2)}, u32[]{:S(2)}) collective-permute-start(f32[4,32,640]{2,1,0:T(8,128)S(1)} %dynamic-slice_bitcast_fusion.3), channel_id=1, source_target_pairs={{0,2},{2,0},{4,6},{6,4},{8,10},{10,8},{12,14},{14,12},{1,3},{3,1},... | collective-permute-start | bytes 983048 | tf_op jit(solution)/shard_map/ppermute | solution.py:112
  30.7 9.7 %collective-permute-start.5 = (f32[4,32,640]{2,1,0:T(8,128)S(1)}, f32[4,32,640]{2,1,0:T(8,128)S(1)}, u32[]{:S(2)}, u32[]{:S(2)}) collective-permute-start(f32[4,32,640]{2,1,0:T(8,128)S(1)} %dynamic-slice_bitcast_fusion.2), channel_id=1, source_target_pairs={{0,2},{2,0},{4,6},{6,4},{8,10},{10,8},{12,14},{14,12},{1,3},{3,1},... | collective-permute-start | bytes 983048 | tf_op jit(solution)/shard_map/ppermute | solution.py:112
  33.7 9.3 %all-to-all-start = ((f32[4,32,640]{2,1,0:T(8,128)}), f32[4,32,640]{2,1,0:T(8,128)S(1)}, u32[]{:S(2)}, u32[]{:S(2)}) async-start(f32[4,32,640]{2,1,0:T(8,128)} %bitcast_add_fusion.1), calls=%async_computation | async-start | bytes 655360 | tf_op jit(solution)/shard_map/all_to_all | solution.py:128
  43.1 9.3 %all-to-all-start.1 = ((f32[4,32,640]{2,1,0:T(8,128)}), f32[4,32,640]{2,1,0:T(8,128)S(1)}, u32[]{:S(2)}, u32[]{:S(2)}) async-start(f32[4,32,640]{2,1,0:T(8,128)} %bitcast_add_fusion), calls=%async_computation.1 | async-start | bytes 655360 | tf_op jit(solution)/shard_map/all_to_all | solution.py:128
  46.6 9.6 %collective-permute-start.2 = (f32[2,32,640]{2,1,0:T(8,128)S(1)}, f32[2,32,640]{2,1,0:T(8,128)S(1)}, u32[]{:S(2)}, u32[]{:S(2)}) collective-permute-start(f32[2,32,640]{2,1,0:T(8,128)S(1)} %dynamic-slice_bitcast_fusion.5), channel_id=1, source_target_pairs={{0,4},{2,6},{4,0},{6,2},{8,12},{10,14},{12,8},{14,10},{1,5},{3,7},... | collective-permute-start | bytes 491528 | tf_op jit(solution)/shard_map/ppermute | solution.py:112
  52.4 11.2 %collective-permute-start.6 = (f32[2,32,640]{2,1,0:T(8,128)S(1)}, f32[2,32,640]{2,1,0:T(8,128)S(1)}, u32[]{:S(2)}, u32[]{:S(2)}) collective-permute-start(f32[2,32,640]{2,1,0:T(8,128)S(1)} %dynamic-slice_bitcast_fusion.4), channel_id=1, source_target_pairs={{0,4},{2,6},{4,0},{6,2},{8,12},{10,14},{12,8},{14,10},{1,5},{3,7},... | collective-permute-start | bytes 491528 | tf_op jit(solution)/shard_map/ppermute | solution.py:112
  56.2 15.4 %collective-permute-start.3 = (f32[32,640]{1,0:T(8,128)S(1)}, f32[32,640]{1,0:T(8,128)S(1)}, u32[]{:S(2)}, u32[]{:S(2)}) collective-permute-start(f32[32,640]{1,0:T(8,128)S(1)} %dynamic-slice_bitcast_fusion.7), channel_id=1, source_target_pairs={{0,8},{2,10},{4,12},{6,14},{8,0},{10,2},{12,4},{14,6},{1,9},{3,11}... | collective-permute-start | bytes 245768 | tf_op jit(solution)/shard_map/ppermute | solution.py:112
  63.6 17.7 %collective-permute-start.7 = (f32[32,640]{1,0:T(8,128)S(1)}, f32[32,640]{1,0:T(8,128)S(1)}, u32[]{:S(2)}, u32[]{:S(2)}) collective-permute-start(f32[32,640]{1,0:T(8,128)S(1)} %dynamic-slice_bitcast_fusion.6), channel_id=1, source_target_pairs={{0,8},{2,10},{4,12},{6,14},{8,0},{10,2},{12,4},{14,6},{1,9},{3,11}... | collective-permute-start | bytes 245768 | tf_op jit(solution)/shard_map/ppermute | solution.py:112
  81.4 16.0 %collective-permute-start.8 = (f32[64,640]{1,0:T(8,128)S(1)}, f32[64,640]{1,0:T(8,128)S(1)}, u32[]{:S(2)}, u32[]{:S(2)}) collective-permute-start(f32[64,640]{1,0:T(8,128)S(1)} %pad_maximum_fusion.3), channel_id=1, source_target_pairs={{0,8},{2,10},{4,12},{6,14},{8,0},{10,2},{12,4},{14,6},{1,9},{3,11}... | collective-permute-start | bytes 491528 | tf_op jit(solution)/shard_map/ppermute | solution.py:112
  83.4 14.1 %collective-permute-start.10 = (f32[64,640]{1,0:T(8,128)S(1)}, f32[64,640]{1,0:T(8,128)S(1)}, u32[]{:S(2)}, u32[]{:S(2)}) collective-permute-start(f32[64,640]{1,0:T(8,128)S(1)} %pad_maximum_fusion.3), channel_id=1, source_target_pairs={{0,4},{2,68},{4,0},{6,64},{8,12},{10,76},{12,8},{14,72},{64,70},{6... | collective-permute-start | bytes 491528 | tf_op jit(solution)/shard_map/ppermute | solution.py:162
  85.3 17.3 %collective-permute-start.11 = (f32[64,640]{1,0:T(8,128)S(1)}, f32[64,640]{1,0:T(8,128)S(1)}, u32[]{:S(2)}, u32[]{:S(2)}) collective-permute-start(f32[64,640]{1,0:T(8,128)S(1)} %pad_maximum_fusion.3), channel_id=1, source_target_pairs={{0,68},{2,4},{4,64},{6,0},{8,76},{10,12},{12,72},{14,8},{64,6},{66... | collective-permute-start | bytes 491528 | tf_op jit(solution)/shard_map/ppermute | solution.py:163
  103.8 19.1 %all-to-all-start.2 = ((f32[4,2,64,640]{3,2,1,0:T(8,128)}), f32[4,2,64,640]{3,2,1,0:T(8,128)S(1)}, u32[]{:S(2)}, u32[]{:S(2)}) async-start(f32[4,2,64,640]{3,2,1,0:T(8,128)} %broadcast_in_dim.2), calls=%async_computation.2 | async-start | bytes 2621440 | tf_op jit(solution)/shard_map/all_to_all | solution.py:166
  107.4 13.6 %collective-permute-start.9 = (f32[2,64,640]{2,1,0:T(8,128)S(1)}, f32[2,64,640]{2,1,0:T(8,128)S(1)}, u32[]{:S(2)}, u32[]{:S(2)}) collective-permute-start(f32[2,64,640]{2,1,0:T(8,128)S(1)} %pad_maximum_fusion.1), channel_id=1, source_target_pairs={{0,4},{2,6},{4,0},{6,2},{8,12},{10,14},{12,8},{14,10},{1,5},{3,7},... | collective-permute-start | bytes 983048 | tf_op jit(solution)/shard_map/ppermute | solution.py:112
  123.0 24.2 %collective-permute-start.12 = (f32[4,64,640]{2,1,0:T(8,128)S(1)}, f32[4,64,640]{2,1,0:T(8,128)S(1)}, u32[]{:S(2)}, u32[]{:S(2)}) collective-permute-start(f32[4,64,640]{2,1,0:T(8,128)S(1)} %bitcast.56), channel_id=1, source_target_pairs={{0,1},{1,0},{2,3},{3,2},{4,5},{5,4},{6,7},{7,6},{8,9},{9,8},{10,11... | collective-permute-start | bytes 1966088 | tf_op jit(solution)/shard_map/ppermute | solution.py:112
  128.2 19.0 %collective-permute-start.13 = (f32[2,2,64,640]{3,2,1,0:T(8,128)S(1)}, f32[2,2,64,640]{3,2,1,0:T(8,128)S(1)}, u32[]{:S(2)}, u32[]{:S(2)}) collective-permute-start(f32[2,2,64,640]{3,2,1,0:T(8,128)S(1)} %get-tuple-element.21), channel_id=1, source_target_pairs={{0,1},{1,0},{2,3},{3,2},{4,5},{5,4},{6,7},{7,6},{8,9},{9,8},{10,11... | collective-permute-start | bytes 1966088 | tf_op jit(solution)/shard_map/ppermute | solution.py:112
  130.2 31.8 %collective-permute-start.14 = (f32[4,64,640]{2,1,0:T(8,128)S(1)}, f32[4,64,640]{2,1,0:T(8,128)S(1)}, u32[]{:S(2)}, u32[]{:S(2)}) collective-permute-start(f32[4,64,640]{2,1,0:T(8,128)S(1)} %bitcast.57), channel_id=1, source_target_pairs={{0,2},{2,0},{4,6},{6,4},{8,10},{10,8},{12,14},{14,12},{1,3},{3,1},... | collective-permute-start | bytes 1966088 | tf_op jit(solution)/shard_map/ppermute | solution.py:112
  150.0 19.2 %all-to-all-start.3 = ((f32[4,2,64,512]{3,2,1,0:T(8,128)}), f32[4,2,64,512]{3,2,1,0:T(8,128)}, u32[]{:S(2)}, u32[]{:S(2)}) async-start(f32[4,2,64,512]{3,2,1,0:T(8,128)} %shard_map.39), calls=%async_computation.3 | async-start | bytes 2097152 | tf_op jit(solution)/shard_map/all_to_all | solution.py:128
  162.0 4.5 %collective-permute-start.15 = (f32[4,64,640]{2,1,0:T(8,128)S(1)}, f32[4,64,640]{2,1,0:T(8,128)S(1)}, u32[]{:S(2)}, u32[]{:S(2)}) collective-permute-start(f32[4,64,640]{2,1,0:T(8,128)S(1)} %collective-permute-done.14.mown_ref), channel_id=1, source_target_pairs={{0,1},{1,0},{2,3},{3,2},{4,5},{5,4},{6,7},{7,6},{8,9},{9,8},{10,11... | collective-permute-start | bytes 1966088 | tf_op jit(solution)/shard_map/ppermute | solution.py:112
  169.2 18.1 %all-to-all-start.4 = ((f32[4,2,64,512]{3,2,1,0:T(8,128)}), f32[4,2,64,512]{3,2,1,0:T(8,128)S(1)}, u32[]{:S(2)}, u32[]{:S(2)}) async-start(f32[4,2,64,512]{3,2,1,0:T(8,128)} %shard_map.40), calls=%async_computation.4 | async-start | bytes 2097152 | tf_op jit(solution)/shard_map/all_to_all | solution.py:128

commit v9 on v8

--- a/solution.py
+++ b/solution.py
@@ -128,6 +128,9 @@
     return lax.all_to_all(value, "x", split_axis=0, concat_axis=0)
 
 
+Z = ("zh", "zq", "zb")
+
+
 def column_planes(z):
     half, x = z // 8, (z % 8 >> 1) ^ 1
     return half * 8 + 2 * x + half, (1 - half) * 8 + 2 * x + half
@@ -140,42 +143,39 @@
 def local(integrals, mask, coeffs):
     nslab, naux, mrows, lcols = integrals.shape
     norbit = coeffs.shape[1]
-    core, zl, zh = lax.axis_index("core"), lax.axis_index("zl"), lax.axis_index("zh")
-    low, mid, top = zl & 1, (zl >> 1) & 1, zl >> 2
+    core, zq, zh = lax.axis_index("core"), lax.axis_index("zq"), lax.axis_index("zh")
+    low, mid, top = lax.axis_index("zb"), zq & 1, zq >> 1
     parts, rows = nslab * naux, mrows // 8
     integrals = integrals.reshape(parts, mrows, lcols)
     away = half_of(integrals, mask, coeffs, 1 - core, 3 * VMEM)
     got = [swap(a, "core", 1, 2) for a in away]
     kept = half_of(integrals, mask, coeffs, core, VMEM)
-    own, before = [], None
+    own = []
     for k, g in zip(kept, got):
-        part = lax.optimization_barrier(k + g)
-        give = pick(part, 1 - low, 1)
-        if before is not None:
-            give = after(give, before)
-        before = swap(give, "zl", 1, 8)
-        part = to_x(pick(part, low, 1) + before).reshape(2, 2, rows, norbit)
-        part = pick(part, 1 - mid, 1) + swap(pick(part, mid, 1), "zl", 2, 8)
-        own.append(pick(part, top, 0) + swap(pick(part, 1 - top, 0), "zl", 4, 8))
+        part = (k + g).reshape(2 * parts, rows, norbit)
+        part = lax.all_to_all(part, ("x", "zb"), split_axis=0, concat_axis=0).reshape(2, 2, 2, rows, norbit)
+        part = part[:, :, 0] + part[:, :, 1]
+        part = pick(part, 1 - mid, 1) + swap(pick(part, mid, 1), "zq", 1, 4)
+        own.append(pick(part, top, 0) + swap(pick(part, 1 - top, 0), "zq", 2, 4))
     own = jnp.concatenate(own)
-    m = join(own, swap(own, "zl", 4, 8), top, 0)
-    first = after(lax.ppermute(own, ("zh", "zl"), FIRST), m)
-    second = after(lax.ppermute(own, ("zh", "zl"), SECOND), m)
+    m = join(own, swap(own, "zq", 2, 4), top, 0)
+    first = after(lax.ppermute(own, Z, FIRST), m)
+    second = after(lax.ppermute(own, Z, SECOND), m)
     cols = join(first, second, jnp.where(zh == low, 0, 1), 0)
     copies = jnp.broadcast_to(cols[None], (4,) + cols.shape)
     n = lax.all_to_all(copies, "y", split_axis=0, concat_axis=0)
     n = n.reshape((2, 2) + cols.shape)
     nown, noth = pick(n, core, 0), swap(pick(n, 1 - core, 0), "core", 1, 2)
-    m = join(m, swap(m, "zl", 2, 8), 1 - mid, 1).reshape(4, 2 * rows, norbit)
+    m = join(m, swap(m, "zq", 1, 4), 1 - mid, 1).reshape(4, 2 * rows, norbit)
     tiles = []
-    for m, m_swap in ((m, after(m, nown)), (swap(m, "zl", 1, 8),) * 2):
+    for m, m_swap in ((m, after(m, nown)), (swap(m, "zb", 1, 2),) * 2):
         tile = exchange_part(m, swap(m_swap, "core", 1, 2), nown, noth, core)
         tiles.append(jnp.sum(to_x(tile), axis=0))
     return join(*tiles, low, 1).reshape(mrows, lcols) * (1.0 / jnp.sqrt(jnp.float32(norbit * parts)))
 
 
 def solution(mesh):
-    fine = Mesh(mesh.devices.reshape(4, 2, 4, 8, 2), ("x", "zh", "y", "zl", "core"))
-    r, c = ("x", "zh", "y"), ("zl", "core")
+    fine = Mesh(mesh.devices.reshape(4, 2, 4, 4, 2, 2), ("x", "zh", "y", "zq", "zb", "core"))
+    r, c = ("x", "zh", "y"), ("zq", "zb", "core")
     in_specs = (P(None, None, r, c), P(None, r, c), P(c, None))
     return jax.shard_map(local, mesh=fine, in_specs=in_specs, out_specs=P(r, c), check_vma=False)

time: 189 us -> 186 us (0.984)
  starting transfers between devices: 92.2 us -> 84 us
  waiting for transfers between devices: 74.3 us -> 79.3 us
  other arithmetic: 6.42 us -> 4.5 us
    all_to_all x0 -> x2, waiting for transfers between devices: none -> 18.2 us  [local(): lax.all_to_all(part, ('x', 'zb'), split_axis=0, concat_axis=0)]
    ppermute x14 -> x12, waiting for transfers between devices: 48.8 us -> 35.3 us  [swap(): return lax.ppermute(value, axis, [(i, i ^ bit) for i in range(size)])]
    ppermute x14 -> x12, starting transfers between devices: 65.2 us -> 54.3 us  [swap(): return lax.ppermute(value, axis, [(i, i ^ bit) for i in range(size)])]
    all_to_all x4 -> x2, starting transfers between devices: 15 us -> 7.76 us  [to_x(): return lax.all_to_all(value, 'x', split_axis=0, concat_axis=0)]
    all_to_all x0 -> x2, starting transfers between devices: none -> 7.08 us  [local(): lax.all_to_all(part, ('x', 'zb'), split_axis=0, concat_axis=0)]
    all_to_all x4 -> x2, waiting for transfers between devices: 18.7 us -> 12.6 us  [to_x(): return lax.all_to_all(value, 'x', split_axis=0, concat_axis=0)]
    all_to_all x1, waiting for transfers between devices: 1.77 us -> 5.85 us  [local(): n = lax.all_to_all(copies, 'y', split_axis=0, concat_axis=0)]
    ppermute x2, starting transfers between devices: 8.49 us -> 11.1 us  [the longest x1 9.15 us: local(): second = after(lax.ppermute(own, Z, SECOND), m)]
  transfers between devices with their start and end apart: 21 -> 19, of which waited for: 13 -> 12; matrix products, arithmetic and copies ran while one was open for 3% -> 1% of each run, Pallas kernels for 4% -> 4%
where the time goes in v9:
time: 186 us; the launch traced here: 184 us
  starting transfers between devices  84 us (45%)
  waiting for transfers between devices  79.3 us (43%)
  Pallas kernels  13.4 us (7%)
  other arithmetic  4.5 us (2%)
  local copies, waits for them, and re-layouts  2.65 us (1%)
    ppermute x12, starting transfers between devices, swap(): return lax.ppermute(value, axis, [(i, i ^ bit) for i in range(size)])  54.3 us
    ppermute x12, waiting for transfers between devices, swap(): return lax.ppermute(value, axis, [(i, i ^ bit) for i in range(size)])  35.3 us
    all_to_all x2, waiting for transfers between devices, local(): lax.all_to_all(part, ('x', 'zb'), split_axis=0, concat_axis=0)  18.2 us
    all_to_all x2, waiting for transfers between devices, to_x(): return lax.all_to_all(value, 'x', split_axis=0, concat_axis=0)  12.6 us
    ppermute x1, starting transfers between devices, local(): second = after(lax.ppermute(own, Z, SECOND), m)  9.15 us
    pallas_call x2, Pallas kernels, half_of(): pl.pallas_call(half_kernel, out_shape=[jax.ShapeDtypeStruct(shape, jnp.fl...  7.87 us
    all_to_all x2, starting transfers between devices, to_x(): return lax.all_to_all(value, 'x', split_axis=0, concat_axis=0)  7.76 us
    ppermute x1, waiting for transfers between devices, local(): second = after(lax.ppermute(own, Z, SECOND), m)  7.31 us
  transfers between devices with their start and end apart: 19, of which 12 were waited for; matrix products, arithmetic and copies ran while one was open for 1% of the time, Pallas kernels for 4%

profile of v9, /device:TPU:1, one launch (start us, length us, event | category | flops | bytes accessed | tf_op | source)
XLA Modules:
  0.0 184.2 jit_solution(8999562586049275586)
XLA Ops:
  0.0 5.3 %shard_map.38 = (f32[4,2,32,640]{3,2,1,0:T(8,128)}, f32[4,2,32,640]{3,2,1,0:T(8,128)}) custom-call(s32[1]{0:T(128)} %bitcast.2.half_ref, s32[2,2,4]{2,1,0:T(2,128)} %mask_ref.3, f32[4,4,2,32,512]{4,3,2,1,0:T(8,128)} %bitcast.53, f32[512,640]{1,0:T(8,128)} %c_ref.3), custom_call_target="tpu_custom_call" | custom-call | flops 1006632960 | bytes 3670016 | tf_op jit(solution)/shard_map/pallas_call | solution.py:49
  5.3 8.8 %collective-permute-start.3 = (f32[4,2,32,640]{3,2,1,0:T(8,128)}, f32[4,2,32,640]{3,2,1,0:T(8,128)S(1)}, u32[]{:S(2)}, u32[]{:S(2)}) collective-permute-start(f32[4,2,32,640]{3,2,1,0:T(8,128)} %get-tuple-element.15), channel_id=1, source_target_pairs={{0,1},{1,0},{2,3},{3,2},{4,5},{5,4},{6,7},{7,6},{8,9},{9,8},{10,11... | collective-permute-start | bytes 1966088 | tf_op jit(solution)/shard_map/ppermute | solution.py:112
  15.4 2.6 %shard_map.37 = (f32[4,2,32,640]{3,2,1,0:T(8,128)S(1)}, f32[4,2,32,640]{3,2,1,0:T(8,128)S(1)}) custom-call(s32[1]{0:T(128)} %bitcast.half_ref.core_ref, s32[2,2,4]{2,1,0:T(2,128)S(1)} %copy-done.2, f32[4,4,2,32,512]{4,3,2,1,0:T(8,128)S(1)} %bitcast.54, f32[512,640]{1,0:T(8,128)S(1)} %copy-done.1), custom_call_target="tpu_custom_call" | custom-call | flops 1006632960 | bytes 3670016 | tf_op jit(solution)/shard_map/pallas_call | solution.py:49
  19.0 3.5 %all-to-all-start.1 = ((f32[8,32,640]{2,1,0:T(8,128)}), f32[8,32,640]{2,1,0:T(8,128)S(1)}, u32[]{:S(2)}, u32[]{:S(2)}) async-start(f32[8,32,640]{2,1,0:T(8,128)} %bitcast.9), calls=%async_computation.1 | async-start | bytes 1310720 | tf_op jit(solution)/shard_map/all_to_all | solution.py:156
  22.5 1.9 %collective-permute-start = (f32[4,2,32,640]{3,2,1,0:T(8,128)S(1)}, f32[4,2,32,640]{3,2,1,0:T(8,128)S(1)}, u32[]{:S(2)}, u32[]{:S(2)}) collective-permute-start(f32[4,2,32,640]{3,2,1,0:T(8,128)S(1)} %copy-done.3), channel_id=1, source_target_pairs={{0,1},{1,0},{2,3},{3,2},{4,5},{5,4},{6,7},{7,6},{8,9},{9,8},{10,11... | collective-permute-start | bytes 1966088 | tf_op jit(solution)/shard_map/ppermute | solution.py:112
  24.5 2.1 %collective-permute-done = f32[4,2,32,640]{3,2,1,0:T(8,128)S(1)} collective-permute-done((f32[4,2,32,640]{3,2,1,0:T(8,128)S(1)}, f32[4,2,32,640]{3,2,1,0:T(8,128)S(1)}, u32[]{:S(2)}, u32[]{:S(2)}) %collective-permute-start) | collective-permute-done | bytes 655392 | tf_op jit(solution)/shard_map/ppermute | solution.py:112
  27.4 6.7 %all-to-all-done.1 = f32[8,32,640]{2,1,0:T(8,128)S(1)} async-done(((f32[8,32,640]{2,1,0:T(8,128)}), f32[8,32,640]{2,1,0:T(8,128)S(1)}, u32[]{:S(2)}, u32[]{:S(2)}) %all-to-all-start.1) | async-done | bytes 655392 | tf_op jit(solution)/shard_map/all_to_all | solution.py:156
  34.2 3.5 %all-to-all-start = ((f32[8,32,640]{2,1,0:T(8,128)}), f32[8,32,640]{2,1,0:T(8,128)S(1)}, u32[]{:S(2)}, u32[]{:S(2)}) async-start(f32[8,32,640]{2,1,0:T(8,128)} %bitcast.3), calls=%async_computation | async-start | bytes 1310720 | tf_op jit(solution)/shard_map/all_to_all | solution.py:156
  37.8 1.9 %collective-permute-start.4 = (f32[2,32,640]{2,1,0:T(8,128)S(1)}, f32[2,32,640]{2,1,0:T(8,128)S(1)}, u32[]{:S(2)}, u32[]{:S(2)}) collective-permute-start(f32[2,32,640]{2,1,0:T(8,128)S(1)} %dynamic-slice_bitcast_fusion.2), channel_id=1, source_target_pairs={{0,4},{4,0},{8,12},{12,8},{1,5},{5,1},{9,13},{13,9},{2,6},{6,2},{1... | collective-permute-start | bytes 491528 | tf_op jit(solution)/shard_map/ppermute | solution.py:112
  39.7 11.4 %all-to-all-done = f32[8,32,640]{2,1,0:T(8,128)S(1)} async-done(((f32[8,32,640]{2,1,0:T(8,128)}), f32[8,32,640]{2,1,0:T(8,128)S(1)}, u32[]{:S(2)}, u32[]{:S(2)}) %all-to-all-start) | async-done | bytes 655392 | tf_op jit(solution)/shard_map/all_to_all | solution.py:156
  51.2 1.9 %collective-permute-start.1 = (f32[2,32,640]{2,1,0:T(8,128)S(1)}, f32[2,32,640]{2,1,0:T(8,128)S(1)}, u32[]{:S(2)}, u32[]{:S(2)}) collective-permute-start(f32[2,32,640]{2,1,0:T(8,128)S(1)} %dynamic-slice_bitcast_fusion.3), channel_id=1, source_target_pairs={{0,4},{4,0},{8,12},{12,8},{1,5},{5,1},{9,13},{13,9},{2,6},{6,2},{1... | collective-permute-start | bytes 491528 | tf_op jit(solution)/shard_map/ppermute | solution.py:112
  53.2 5.4 %collective-permute-start.5 = (f32[32,640]{1,0:T(8,128)S(1)}, f32[32,640]{1,0:T(8,128)S(1)}, u32[]{:S(2)}, u32[]{:S(2)}) collective-permute-start(f32[32,640]{1,0:T(8,128)S(1)} %dynamic-slice_bitcast_fusion.4), channel_id=1, source_target_pairs={{0,8},{4,12},{8,0},{12,4},{1,9},{5,13},{9,1},{13,5},{2,10},{6,14},... | collective-permute-start | bytes 245768 | tf_op jit(solution)/shard_map/ppermute | solution.py:112
  58.6 2.6 %collective-permute-done.1 = f32[2,32,640]{2,1,0:T(8,128)S(1)} collective-permute-done((f32[2,32,640]{2,1,0:T(8,128)S(1)}, f32[2,32,640]{2,1,0:T(8,128)S(1)}, u32[]{:S(2)}, u32[]{:S(2)}) %collective-permute-start.1) | collective-permute-done | bytes 163872 | tf_op jit(solution)/shard_map/ppermute | solution.py:112
  61.3 6.8 %collective-permute-start.2 = (f32[32,640]{1,0:T(8,128)S(1)}, f32[32,640]{1,0:T(8,128)S(1)}, u32[]{:S(2)}, u32[]{:S(2)}) collective-permute-start(f32[32,640]{1,0:T(8,128)S(1)} %dynamic-slice_bitcast_fusion.5), channel_id=1, source_target_pairs={{0,8},{4,12},{8,0},{12,4},{1,9},{5,13},{9,1},{13,5},{2,10},{6,14},... | collective-permute-start | bytes 245768 | tf_op jit(solution)/shard_map/ppermute | solution.py:112
  68.1 8.4 %collective-permute-done.2 = f32[32,640]{1,0:T(8,128)S(1)} collective-permute-done((f32[32,640]{1,0:T(8,128)S(1)}, f32[32,640]{1,0:T(8,128)S(1)}, u32[]{:S(2)}, u32[]{:S(2)}) %collective-permute-start.2) | collective-permute-done | bytes 81952 | tf_op jit(solution)/shard_map/ppermute | solution.py:112
  76.5 1.9 %collective-permute-start.6 = (f32[64,640]{1,0:T(8,128)S(1)}, f32[64,640]{1,0:T(8,128)S(1)}, u32[]{:S(2)}, u32[]{:S(2)}) collective-permute-start(f32[64,640]{1,0:T(8,128)S(1)} %pad_maximum_fusion.3), channel_id=1, source_target_pairs={{0,8},{4,12},{8,0},{12,4},{1,9},{5,13},{9,1},{13,5},{2,10},{6,14},... | collective-permute-start | bytes 491528 | tf_op jit(solution)/shard_map/ppermute | solution.py:112
  80.4 9.1 %collective-permute-start.9 = (f32[64,640]{1,0:T(8,128)S(1)}, f32[64,640]{1,0:T(8,128)S(1)}, u32[]{:S(2)}, u32[]{:S(2)}) collective-permute-start(f32[64,640]{1,0:T(8,128)S(1)} %pad_maximum_fusion.3), channel_id=1, source_target_pairs={{0,68},{2,4},{4,64},{6,0},{8,76},{10,12},{12,72},{14,8},{64,6},{66... | collective-permute-start | bytes 491528 | tf_op jit(solution)/shard_map/ppermute | solution.py:163
  89.5 4.7 %collective-permute-done.6 = f32[64,640]{1,0:T(8,128)S(1)} collective-permute-done((f32[64,640]{1,0:T(8,128)S(1)}, f32[64,640]{1,0:T(8,128)S(1)}, u32[]{:S(2)}, u32[]{:S(2)}) %collective-permute-start.6) | collective-permute-done | bytes 163872 | tf_op jit(solution)/shard_map/ppermute | solution.py:112
  94.3 7.3 %collective-permute-done.9 = f32[64,640]{1,0:T(8,128)S(1)} collective-permute-done((f32[64,640]{1,0:T(8,128)S(1)}, f32[64,640]{1,0:T(8,128)S(1)}, u32[]{:S(2)}, u32[]{:S(2)}) %collective-permute-start.9) | collective-permute-done | bytes 163872 | tf_op jit(solution)/shard_map/ppermute | solution.py:163
  102.9 3.8 %all-to-all-start.2 = ((f32[4,2,64,640]{3,2,1,0:T(8,128)}), f32[4,2,64,640]{3,2,1,0:T(8,128)S(1)}, u32[]{:S(2)}, u32[]{:S(2)}) async-start(f32[4,2,64,640]{3,2,1,0:T(8,128)} %broadcast_in_dim.2), calls=%async_computation.2 | async-start | bytes 2621440 | tf_op jit(solution)/shard_map/all_to_all | solution.py:166
  108.6 8.2 %collective-permute-done.7 = f32[2,64,640]{2,1,0:T(8,128)S(1)} collective-permute-done((f32[2,64,640]{2,1,0:T(8,128)S(1)}, f32[2,64,640]{2,1,0:T(8,128)S(1)}, u32[]{:S(2)}, u32[]{:S(2)}) %collective-permute-start.7) | collective-permute-done | bytes 327712 | tf_op jit(solution)/shard_map/ppermute | solution.py:112
  116.8 5.9 %all-to-all-done.2 = f32[4,2,64,640]{3,2,1,0:T(8,128)S(1)} async-done(((f32[4,2,64,640]{3,2,1,0:T(8,128)}), f32[4,2,64,640]{3,2,1,0:T(8,128)S(1)}, u32[]{:S(2)}, u32[]{:S(2)}) %all-to-all-start.2) | async-done | bytes 1310752 | tf_op jit(solution)/shard_map/all_to_all | solution.py:166
  122.8 4.7 %collective-permute-start.10 = (f32[4,64,640]{2,1,0:T(8,128)S(1)}, f32[4,64,640]{2,1,0:T(8,128)S(1)}, u32[]{:S(2)}, u32[]{:S(2)}) collective-permute-start(f32[4,64,640]{2,1,0:T(8,128)S(1)} %bitcast.50), channel_id=1, source_target_pairs={{0,1},{1,0},{2,3},{3,2},{4,5},{5,4},{6,7},{7,6},{8,9},{9,8},{10,11... | collective-permute-start | bytes 1966088 | tf_op jit(solution)/shard_map/ppermute | solution.py:112
  127.5 1.9 %collective-permute-start.11 = (f32[2,2,64,640]{3,2,1,0:T(8,128)S(1)}, f32[2,2,64,640]{3,2,1,0:T(8,128)S(1)}, u32[]{:S(2)}, u32[]{:S(2)}) collective-permute-start(f32[2,2,64,640]{3,2,1,0:T(8,128)S(1)} %get-tuple-element.19), channel_id=1, source_target_pairs={{0,1},{1,0},{2,3},{3,2},{4,5},{5,4},{6,7},{7,6},{8,9},{9,8},{10,11... | collective-permute-start | bytes 1966088 | tf_op jit(solution)/shard_map/ppermute | solution.py:112
  129.4 14.3 %collective-permute-start.12 = (f32[4,64,640]{2,1,0:T(8,128)S(1)}, f32[4,64,640]{2,1,0:T(8,128)S(1)}, u32[]{:S(2)}, u32[]{:S(2)}) collective-permute-start(f32[4,64,640]{2,1,0:T(8,128)S(1)} %bitcast.51), channel_id=1, source_target_pairs={{0,2},{2,0},{1,3},{3,1},{4,6},{6,4},{5,7},{7,5},{8,10},{10,8},{9,1... | collective-permute-start | bytes 1966088 | tf_op jit(solution)/shard_map/ppermute | solution.py:112
  143.7 2.8 %shard_map.39 = f32[4,2,64,512]{3,2,1,0:T(8,128)} custom-call(s32[1]{0:T(128)} %bitcast.half_ref.core_ref, f32[4,64,640]{2,1,0:T(8,128)S(1)} %bitcast.52, f32[4,64,640]{2,1,0:T(8,128)S(1)} %collective-permute-done.10.moth_ref, f32[2,2,64,640]{3,2,1,0:T(8,128)S(1)} %get-tuple-element.20.nown_ref, f32[2,2,64,640]{3,2,1,0:T(8,128)S(1)} %collective-permute-done.11.noth_ref), custom_call_target="tpu_custom_call" | custom-call | flops 1006632960 | bytes 3670016 | tf_op jit(solution)/shard_map/pallas_call | solution.py:96
  146.5 4.2 %all-to-all-start.3 = ((f32[4,2,64,512]{3,2,1,0:T(8,128)}), f32[4,2,64,512]{3,2,1,0:T(8,128)}, u32[]{:S(2)}, u32[]{:S(2)}) async-start(f32[4,2,64,512]{3,2,1,0:T(8,128)} %shard_map.39), calls=%async_computation.3 | async-start | bytes 2097152 | tf_op jit(solution)/shard_map/all_to_all | solution.py:128
  150.8 7.7 %collective-permute-done.12.mown_ref = f32[4,64,640]{2,1,0:T(8,128)S(1)} collective-permute-done((f32[4,64,640]{2,1,0:T(8,128)S(1)}, f32[4,64,640]{2,1,0:T(8,128)S(1)}, u32[]{:S(2)}, u32[]{:S(2)}) %collective-permute-start.12) | collective-permute-done | bytes 655392 | tf_op jit(solution)/shard_map/ppermute | solution.py:112
  158.5 2.8 %collective-permute-start.13 = (f32[4,64,640]{2,1,0:T(8,128)S(1)}, f32[4,64,640]{2,1,0:T(8,128)S(1)}, u32[]{:S(2)}, u32[]{:S(2)}) collective-permute-start(f32[4,64,640]{2,1,0:T(8,128)S(1)} %collective-permute-done.12.mown_ref), channel_id=1, source_target_pairs={{0,1},{1,0},{2,3},{3,2},{4,5},{5,4},{6,7},{7,6},{8,9},{9,8},{10,11... | collective-permute-start | bytes 1966088 | tf_op jit(solution)/shard_map/ppermute | solution.py:112
  163.0 2.8 %shard_map.40 = f32[4,2,64,512]{3,2,1,0:T(8,128)} custom-call(s32[1]{0:T(128)} %bitcast.half_ref.core_ref, f32[4,64,640]{2,1,0:T(8,128)S(1)} %collective-permute-done.12.mown_ref, f32[4,64,640]{2,1,0:T(8,128)S(1)} %collective-permute-done.13.moth_ref, f32[2,2,64,640]{3,2,1,0:T(8,128)S(1)} %get-tuple-element.20.nown_ref, ...), custom_call_target="tpu_custom_call" | custom-call | flops 1006632960 | bytes 3670016 | tf_op jit(solution)/shard_map/pallas_call | solution.py:96
  165.8 3.5 %all-to-all-start.4 = ((f32[4,2,64,512]{3,2,1,0:T(8,128)}), f32[4,2,64,512]{3,2,1,0:T(8,128)S(1)}, u32[]{:S(2)}, u32[]{:S(2)}) async-start(f32[4,2,64,512]{3,2,1,0:T(8,128)} %shard_map.40), calls=%async_computation.4 | async-start | bytes 2097152 | tf_op jit(solution)/shard_map/all_to_all | solution.py:128
  170.6 12.6 %all-to-all-done.4 = f32[4,2,64,512]{3,2,1,0:T(8,128)S(1)} async-done(((f32[4,2,64,512]{3,2,1,0:T(8,128)}), f32[4,2,64,512]{3,2,1,0:T(8,128)S(1)}, u32[]{:S(2)}, u32[]{:S(2)}) %all-to-all-start.4) | async-done | bytes 1048608 | tf_op jit(solution)/shard_map/all_to_all | solution.py:128
  (43 shorter events, 12.7 us)
Async XLA Ops:
  0.0 14.1 %copy-start = (f32[2,2,256,512]{3,2,1,0:T(8,128)S(1)}, f32[2,2,256,512]{3,2,1,0:T(8,128)}, u32[]{:S(2)}) copy-start(f32[2,2,256,512]{3,2,1,0:T(8,128)} %param.3) | copy-start | bytes 6291460
  0.0 14.1 %copy-start.2 = (s32[2,2,4]{2,1,0:T(2,128)S(1)}, s32[2,2,4]{2,1,0:T(2,128)}, u32[]{:S(2)}) copy-start(s32[2,2,4]{2,1,0:T(2,128)} %mask_ref.3) | copy-start | bytes 196
  5.3 12.7 %collective-permute-start.3 = (f32[4,2,32,640]{3,2,1,0:T(8,128)}, f32[4,2,32,640]{3,2,1,0:T(8,128)S(1)}, u32[]{:S(2)}, u32[]{:S(2)}) collective-permute-start(f32[4,2,32,640]{3,2,1,0:T(8,128)} %get-tuple-element.15), channel_id=1, source_target_pairs={{0,1},{1,0},{2,3},{3,2},{4,5},{5,4},{6,7},{7,6},{8,9},{9,8},{10,11... | collective-permute-start | bytes 1966088 | tf_op jit(solution)/shard_map/ppermute | solution.py:112
  14.1 1.3 copy-start.1
  18.0 4.5 %copy-start.3 = (f32[4,2,32,640]{3,2,1,0:T(8,128)S(1)}, f32[4,2,32,640]{3,2,1,0:T(8,128)}, u32[]{:S(2)}) copy-start(f32[4,2,32,640]{3,2,1,0:T(8,128)} %get-tuple-element.13) | copy-start | bytes 1966084
  19.0 15.2 %all-to-all-start.1 = ((f32[8,32,640]{2,1,0:T(8,128)}), f32[8,32,640]{2,1,0:T(8,128)S(1)}, u32[]{:S(2)}, u32[]{:S(2)}) async-start(f32[8,32,640]{2,1,0:T(8,128)} %bitcast.9), calls=%async_computation.1 | async-start | bytes 1310720 | tf_op jit(solution)/shard_map/all_to_all | solution.py:156
  22.5 4.0 %collective-permute-start = (f32[4,2,32,640]{3,2,1,0:T(8,128)S(1)}, f32[4,2,32,640]{3,2,1,0:T(8,128)S(1)}, u32[]{:S(2)}, u32[]{:S(2)}) collective-permute-start(f32[4,2,32,640]{3,2,1,0:T(8,128)S(1)} %copy-done.3), channel_id=1, source_target_pairs={{0,1},{1,0},{2,3},{3,2},{4,5},{5,4},{6,7},{7,6},{8,9},{9,8},{10,11... | collective-permute-start | bytes 1966088 | tf_op jit(solution)/shard_map/ppermute | solution.py:112
  34.2 17.0 %all-to-all-start = ((f32[8,32,640]{2,1,0:T(8,128)}), f32[8,32,640]{2,1,0:T(8,128)S(1)}, u32[]{:S(2)}, u32[]{:S(2)}) async-start(f32[8,32,640]{2,1,0:T(8,128)} %bitcast.3), calls=%async_computation | async-start | bytes 1310720 | tf_op jit(solution)/shard_map/all_to_all | solution.py:156
  37.8 15.4 %collective-permute-start.4 = (f32[2,32,640]{2,1,0:T(8,128)S(1)}, f32[2,32,640]{2,1,0:T(8,128)S(1)}, u32[]{:S(2)}, u32[]{:S(2)}) collective-permute-start(f32[2,32,640]{2,1,0:T(8,128)S(1)} %dynamic-slice_bitcast_fusion.2), channel_id=1, source_target_pairs={{0,4},{4,0},{8,12},{12,8},{1,5},{5,1},{9,13},{13,9},{2,6},{6,2},{1... | collective-permute-start | bytes 491528 | tf_op jit(solution)/shard_map/ppermute | solution.py:112
  51.2 10.0 %collective-permute-start.1 = (f32[2,32,640]{2,1,0:T(8,128)S(1)}, f32[2,32,640]{2,1,0:T(8,128)S(1)}, u32[]{:S(2)}, u32[]{:S(2)}) collective-permute-start(f32[2,32,640]{2,1,0:T(8,128)S(1)} %dynamic-slice_bitcast_fusion.3), channel_id=1, source_target_pairs={{0,4},{4,0},{8,12},{12,8},{1,5},{5,1},{9,13},{13,9},{2,6},{6,2},{1... | collective-permute-start | bytes 491528 | tf_op jit(solution)/shard_map/ppermute | solution.py:112
  53.2 14.9 %collective-permute-start.5 = (f32[32,640]{1,0:T(8,128)S(1)}, f32[32,640]{1,0:T(8,128)S(1)}, u32[]{:S(2)}, u32[]{:S(2)}) collective-permute-start(f32[32,640]{1,0:T(8,128)S(1)} %dynamic-slice_bitcast_fusion.4), channel_id=1, source_target_pairs={{0,8},{4,12},{8,0},{12,4},{1,9},{5,13},{9,1},{13,5},{2,10},{6,14},... | collective-permute-start | bytes 245768 | tf_op jit(solution)/shard_map/ppermute | solution.py:112
  61.3 15.2 %collective-permute-start.2 = (f32[32,640]{1,0:T(8,128)S(1)}, f32[32,640]{1,0:T(8,128)S(1)}, u32[]{:S(2)}, u32[]{:S(2)}) collective-permute-start(f32[32,640]{1,0:T(8,128)S(1)} %dynamic-slice_bitcast_fusion.5), channel_id=1, source_target_pairs={{0,8},{4,12},{8,0},{12,4},{1,9},{5,13},{9,1},{13,5},{2,10},{6,14},... | collective-permute-start | bytes 245768 | tf_op jit(solution)/shard_map/ppermute | solution.py:112
  76.5 17.8 %collective-permute-start.6 = (f32[64,640]{1,0:T(8,128)S(1)}, f32[64,640]{1,0:T(8,128)S(1)}, u32[]{:S(2)}, u32[]{:S(2)}) collective-permute-start(f32[64,640]{1,0:T(8,128)S(1)} %pad_maximum_fusion.3), channel_id=1, source_target_pairs={{0,8},{4,12},{8,0},{12,4},{1,9},{5,13},{9,1},{13,5},{2,10},{6,14},... | collective-permute-start | bytes 491528 | tf_op jit(solution)/shard_map/ppermute | solution.py:112
  78.5 15.9 %collective-permute-start.8 = (f32[64,640]{1,0:T(8,128)S(1)}, f32[64,640]{1,0:T(8,128)S(1)}, u32[]{:S(2)}, u32[]{:S(2)}) collective-permute-start(f32[64,640]{1,0:T(8,128)S(1)} %pad_maximum_fusion.3), channel_id=1, source_target_pairs={{0,4},{2,68},{4,0},{6,64},{8,12},{10,76},{12,8},{14,72},{64,70},{6... | collective-permute-start | bytes 491528 | tf_op jit(solution)/shard_map/ppermute | solution.py:162
  80.4 21.3 %collective-permute-start.9 = (f32[64,640]{1,0:T(8,128)S(1)}, f32[64,640]{1,0:T(8,128)S(1)}, u32[]{:S(2)}, u32[]{:S(2)}) collective-permute-start(f32[64,640]{1,0:T(8,128)S(1)} %pad_maximum_fusion.3), channel_id=1, source_target_pairs={{0,68},{2,4},{4,64},{6,0},{8,76},{10,12},{12,72},{14,8},{64,6},{66... | collective-permute-start | bytes 491528 | tf_op jit(solution)/shard_map/ppermute | solution.py:163
  102.9 19.8 %all-to-all-start.2 = ((f32[4,2,64,640]{3,2,1,0:T(8,128)}), f32[4,2,64,640]{3,2,1,0:T(8,128)S(1)}, u32[]{:S(2)}, u32[]{:S(2)}) async-start(f32[4,2,64,640]{3,2,1,0:T(8,128)} %broadcast_in_dim.2), calls=%async_computation.2 | async-start | bytes 2621440 | tf_op jit(solution)/shard_map/all_to_all | solution.py:166
  106.6 10.1 %collective-permute-start.7 = (f32[2,64,640]{2,1,0:T(8,128)S(1)}, f32[2,64,640]{2,1,0:T(8,128)S(1)}, u32[]{:S(2)}, u32[]{:S(2)}) collective-permute-start(f32[2,64,640]{2,1,0:T(8,128)S(1)} %pad_maximum_fusion.1), channel_id=1, source_target_pairs={{0,4},{4,0},{8,12},{12,8},{1,5},{5,1},{9,13},{13,9},{2,6},{6,2},{1... | collective-permute-start | bytes 983048 | tf_op jit(solution)/shard_map/ppermute | solution.py:112
  122.8 21.0 %collective-permute-start.10 = (f32[4,64,640]{2,1,0:T(8,128)S(1)}, f32[4,64,640]{2,1,0:T(8,128)S(1)}, u32[]{:S(2)}, u32[]{:S(2)}) collective-permute-start(f32[4,64,640]{2,1,0:T(8,128)S(1)} %bitcast.50), channel_id=1, source_target_pairs={{0,1},{1,0},{2,3},{3,2},{4,5},{5,4},{6,7},{7,6},{8,9},{9,8},{10,11... | collective-permute-start | bytes 1966088 | tf_op jit(solution)/shard_map/ppermute | solution.py:112
  127.5 16.2 %collective-permute-start.11 = (f32[2,2,64,640]{3,2,1,0:T(8,128)S(1)}, f32[2,2,64,640]{3,2,1,0:T(8,128)S(1)}, u32[]{:S(2)}, u32[]{:S(2)}) collective-permute-start(f32[2,2,64,640]{3,2,1,0:T(8,128)S(1)} %get-tuple-element.19), channel_id=1, source_target_pairs={{0,1},{1,0},{2,3},{3,2},{4,5},{5,4},{6,7},{7,6},{8,9},{9,8},{10,11... | collective-permute-start | bytes 1966088 | tf_op jit(solution)/shard_map/ppermute | solution.py:112
  129.4 29.0 %collective-permute-start.12 = (f32[4,64,640]{2,1,0:T(8,128)S(1)}, f32[4,64,640]{2,1,0:T(8,128)S(1)}, u32[]{:S(2)}, u32[]{:S(2)}) collective-permute-start(f32[4,64,640]{2,1,0:T(8,128)S(1)} %bitcast.51), channel_id=1, source_target_pairs={{0,2},{2,0},{1,3},{3,1},{4,6},{6,4},{5,7},{7,5},{8,10},{10,8},{9,1... | collective-permute-start | bytes 1966088 | tf_op jit(solution)/shard_map/ppermute | solution.py:112
  146.5 19.2 %all-to-all-start.3 = ((f32[4,2,64,512]{3,2,1,0:T(8,128)}), f32[4,2,64,512]{3,2,1,0:T(8,128)}, u32[]{:S(2)}, u32[]{:S(2)}) async-start(f32[4,2,64,512]{3,2,1,0:T(8,128)} %shard_map.39), calls=%async_computation.3 | async-start | bytes 2097152 | tf_op jit(solution)/shard_map/all_to_all | solution.py:128
  158.5 4.5 %collective-permute-start.13 = (f32[4,64,640]{2,1,0:T(8,128)S(1)}, f32[4,64,640]{2,1,0:T(8,128)S(1)}, u32[]{:S(2)}, u32[]{:S(2)}) collective-permute-start(f32[4,64,640]{2,1,0:T(8,128)S(1)} %collective-permute-done.12.mown_ref), channel_id=1, source_target_pairs={{0,1},{1,0},{2,3},{3,2},{4,5},{5,4},{6,7},{7,6},{8,9},{9,8},{10,11... | collective-permute-start | bytes 1966088 | tf_op jit(solution)/shard_map/ppermute | solution.py:112
  165.8 17.5 %all-to-all-start.4 = ((f32[4,2,64,512]{3,2,1,0:T(8,128)}), f32[4,2,64,512]{3,2,1,0:T(8,128)S(1)}, u32[]{:S(2)}, u32[]{:S(2)}) async-start(f32[4,2,64,512]{3,2,1,0:T(8,128)} %shard_map.40), calls=%async_computation.4 | async-start | bytes 2097152 | tf_op jit(solution)/shard_map/all_to_all | solution.py:128

commit v10 on v9

--- a/solution.py
+++ b/solution.py
@@ -65,47 +65,48 @@
     )(half.reshape(1), mask, integrals.reshape(parts, 4, 2, rows, lcols), coeffs)
 
 
-def exchange_kernel(core_ref, mown_ref, moth_ref, nown_ref, noth_ref, o_ref, mhigh, mlow, nhigh, nlow):
+def exchange_kernel(place_ref, mown_ref, moth_ref, fown_ref, foth_ref, nown_ref, noth_ref, o_ref, mhigh, mlow, nhigh, nlow):
     count, rows, norbit = mown_ref.shape
     blocks, bits, nrows, _ = nown_ref.shape
-    core = core_ref[0]
-    both = ((core, mown_ref, nown_ref), (1 - core, moth_ref, noth_ref))
+    core, low = place_ref[0], place_ref[1]
 
     @pl.when(pl.program_id(0) == 0)
     def _():
         for y in range(blocks):
-            for c, _, ref in both:
+            for c, ref in ((core, nown_ref), (1 - core, noth_ref)):
                 for b in range(bits):
                     at = pl.ds(pl.multiple_of(((y * 2 + c) * bits + b) * nrows, nrows), nrows)
                     nhigh[at, :], nlow[at, :] = halves(ref[y, b])
 
     for x in range(count):
-        for c, ref, _ in both:
-            at = pl.ds(pl.multiple_of((x * 2 + c) * rows, rows), rows)
-            mhigh[at, :], mlow[at, :] = halves(ref[x])
+        for b, own_ref, oth_ref in ((low, mown_ref, moth_ref), (1 - low, fown_ref, foth_ref)):
+            for c, ref in ((core, own_ref), (1 - core, oth_ref)):
+                at = pl.ds(pl.multiple_of(((x * 2 + c) * 2 + b) * rows, rows), rows)
+                mhigh[at, :], mlow[at, :] = halves(ref[x])
     total = dot(mhigh[...], nhigh[...], NT) + (dot(mhigh[...], nlow[...], NT) + dot(mlow[...], nhigh[...], NT))
     o_ref[...] = total.reshape(o_ref.shape)
 
 
-def exchange_part(mown, moth, nown, noth, core):
-    parts, rows, norbit = mown.shape
-    ncols = 2 * nown.shape[0] * nown.shape[1] * nown.shape[2]
+def exchange_part(near, far, cols, place):
+    parts, rows, norbit = near[0].shape
+    blocks, bits, nrows, _ = cols[0].shape
+    ncols = 2 * blocks * bits * nrows
     step = parts // 2
-    mspec = pl.BlockSpec((step, rows, norbit), lambda x, core: (x, 0, 0))
-    nspec = pl.BlockSpec(nown.shape, lambda x, core: (0, 0, 0, 0))
+    mspec = pl.BlockSpec((step, rows, norbit), lambda x, place: (x, 0, 0))
+    nspec = pl.BlockSpec(cols[0].shape, lambda x, place: (0, 0, 0, 0))
     return pl.pallas_call(
         exchange_kernel,
-        out_shape=jax.ShapeDtypeStruct((parts, 2, rows, ncols), jnp.float32),
+        out_shape=jax.ShapeDtypeStruct((parts, 4 * rows, ncols), jnp.float32),
         grid_spec=pltpu.PrefetchScalarGridSpec(
             num_scalar_prefetch=1,
             grid=(2,),
-            in_specs=[mspec, mspec, nspec, nspec],
-            out_specs=pl.BlockSpec((step, 2, rows, ncols), lambda x, core: (x, 0, 0, 0)),
-            scratch_shapes=[pltpu.VMEM((step * 2 * rows, norbit), jnp.bfloat16)] * 2 + [pltpu.VMEM((ncols, norbit), jnp.bfloat16)] * 2,
+            in_specs=[mspec] * 4 + [nspec] * 2,
+            out_specs=pl.BlockSpec((step, 4 * rows, ncols), lambda x, place: (x, 0, 0)),
+            scratch_shapes=[pltpu.VMEM((step * 4 * rows, norbit), jnp.bfloat16)] * 2 + [pltpu.VMEM((ncols, norbit), jnp.bfloat16)] * 2,
         ),
         compiler_params=pltpu.CompilerParams(vmem_limit_bytes=VMEM),
-        cost_estimate=pl.CostEstimate(flops=12 * parts * rows * ncols * norbit, bytes_accessed=4 * norbit * (2 * parts * rows + ncols) + 8 * parts * rows * ncols, transcendentals=0),
-    )(core.reshape(1), mown, moth, nown, noth)
+        cost_estimate=pl.CostEstimate(flops=24 * parts * rows * ncols * norbit, bytes_accessed=4 * norbit * (4 * parts * rows + ncols) + 16 * parts * rows * ncols, transcendentals=0),
+    )(place, *near, *far, *cols)
 
 
 def swap(value, axis, bit, size):
@@ -158,20 +159,18 @@
         part = pick(part, 1 - mid, 1) + swap(pick(part, mid, 1), "zq", 1, 4)
         own.append(pick(part, top, 0) + swap(pick(part, 1 - top, 0), "zq", 2, 4))
     own = jnp.concatenate(own)
+    first = lax.ppermute(own, Z, FIRST)
+    second = lax.ppermute(own, Z, SECOND)
     m = join(own, swap(own, "zq", 2, 4), top, 0)
-    first = after(lax.ppermute(own, Z, FIRST), m)
-    second = after(lax.ppermute(own, Z, SECOND), m)
+    m = join(m, swap(m, "zq", 1, 4), 1 - mid, 1).reshape(4, 2 * rows, norbit)
+    far = swap(m, "zb", 1, 2)
     cols = join(first, second, jnp.where(zh == low, 0, 1), 0)
-    copies = jnp.broadcast_to(cols[None], (4,) + cols.shape)
-    n = lax.all_to_all(copies, "y", split_axis=0, concat_axis=0)
-    n = n.reshape((2, 2) + cols.shape)
-    nown, noth = pick(n, core, 0), swap(pick(n, 1 - core, 0), "core", 1, 2)
-    m = join(m, swap(m, "zq", 1, 4), 1 - mid, 1).reshape(4, 2 * rows, norbit)
-    tiles = []
-    for m, m_swap in ((m, after(m, nown)), (swap(m, "zb", 1, 2),) * 2):
-        tile = exchange_part(m, swap(m_swap, "core", 1, 2), nown, noth, core)
-        tiles.append(jnp.sum(to_x(tile), axis=0))
-    return join(*tiles, low, 1).reshape(mrows, lcols) * (1.0 / jnp.sqrt(jnp.float32(norbit * parts)))
+    n = lax.all_to_all(jnp.broadcast_to(cols[None], (4,) + cols.shape), "y", split_axis=0, concat_axis=0)
+    n = after(n, far).reshape((2, 2) + cols.shape)
+    cols = pick(n, core, 0), swap(pick(n, 1 - core, 0), "core", 1, 2)
+    near, far = (m, swap(m, "core", 1, 2)), (far, swap(far, "core", 1, 2))
+    partial = to_x(exchange_part(near, far, cols, jnp.stack([core, low])))
+    return jnp.sum(partial, axis=0) * (1.0 / jnp.sqrt(jnp.float32(norbit * parts)))
 
 
 def solution(mesh):

time: 186 us -> 185 us (level)
  blocking collectives: 0 us -> 29.3 us
  waiting for transfers between devices: 79.3 us -> 56.6 us
  starting transfers between devices: 84 us -> 79.9 us
    all_to_all x0 -> x1, blocking collectives: none -> 29.3 us  [to_x(): return lax.all_to_all(value, 'x', split_axis=0, concat_axis=0)]
    all_to_all x3 -> x1, waiting for transfers between devices: 18.5 us -> 0.01 us  [local(): lax.all_to_all(jnp.broadcast_to(cols[None], (4,) + cols.shape), 'y', spli...]
    ppermute x12, starting transfers between devices: 54.3 us -> 45.6 us  [swap(): return lax.ppermute(value, axis, [(i, i ^ bit) for i in range(size)])]
    ppermute x2, waiting for transfers between devices: 7.31 us -> 0.01 us  [the longest x1 0.01 us: local(): second = lax.ppermute(own, Z, SECOND)]
    all_to_all x3 -> x1, starting transfers between devices: 11.5 us -> 15.1 us  [local(): lax.all_to_all(jnp.broadcast_to(cols[None], (4,) + cols.shape), 'y', spli...]
    ppermute x12, waiting for transfers between devices: 35.3 us -> 38.5 us  [swap(): return lax.ppermute(value, axis, [(i, i ^ bit) for i in range(size)])]
    pallas_call x2 -> x1, Pallas kernels: 5.56 us -> 3.97 us  [exchange_part(): pl.pallas_call(exchange_kernel, out_shape=jax.ShapeDtypeStruct((parts, 4...]
  transfers between devices with their start and end apart: 19 -> 17, of which waited for: 12 -> 9; matrix products, arithmetic and copies ran while one was open for 1% -> 1% of each run, Pallas kernels for 4% -> 1%
where the time goes in v10:
time: 185 us; the launch traced here: 184 us
  starting transfers between devices  79.9 us (43%)
  waiting for transfers between devices  56.6 us (31%)
  blocking collectives  29.3 us (16%)
  Pallas kernels  11.8 us (6%)
  other arithmetic  3.36 us (2%)
  local copies, waits for them, and re-layouts  2.64 us (1%)
    ppermute x12, starting transfers between devices, swap(): return lax.ppermute(value, axis, [(i, i ^ bit) for i in range(size)])  45.6 us
    ppermute x12, waiting for transfers between devices, swap(): return lax.ppermute(value, axis, [(i, i ^ bit) for i in range(size)])  38.5 us
    all_to_all x1, blocking collectives, to_x(): return lax.all_to_all(value, 'x', split_axis=0, concat_axis=0)  29.3 us
    all_to_all x2, waiting for transfers between devices, local(): lax.all_to_all(part, ('x', 'zb'), split_axis=0, concat_axis=0)  18.1 us
    all_to_all x1, starting transfers between devices, local(): lax.all_to_all(jnp.broadcast_to(cols[None], (4,) + cols.shape), 'y', spli...  15.1 us
    ppermute x1, starting transfers between devices, local(): second = lax.ppermute(own, Z, SECOND)  9.15 us
    pallas_call x2, Pallas kernels, half_of(): pl.pallas_call(half_kernel, out_shape=[jax.ShapeDtypeStruct(shape, jnp.fl...  7.86 us
    all_to_all x2, starting transfers between devices, local(): lax.all_to_all(part, ('x', 'zb'), split_axis=0, concat_axis=0)  7.08 us
  transfers between devices with their start and end apart: 17, of which 9 were waited for; matrix products, arithmetic and copies ran while one was open for 1% of the time, Pallas kernels for 1%

profile of v10, /device:TPU:1, one launch (start us, length us, event | category | flops | bytes accessed | tf_op | source)
XLA Modules:
  0.0 184.0 jit_solution(8202760933312435552)
XLA Ops:
  0.0 5.3 %shard_map.38 = (f32[4,2,32,640]{3,2,1,0:T(8,128)}, f32[4,2,32,640]{3,2,1,0:T(8,128)}) custom-call(s32[1]{0:T(128)} %bitcast.3.half_ref, s32[2,2,4]{2,1,0:T(2,128)} %mask_ref.3, f32[4,4,2,32,512]{4,3,2,1,0:T(8,128)} %bitcast.47, f32[512,640]{1,0:T(8,128)} %c_ref.3), custom_call_target="tpu_custom_call" | custom-call | flops 1006632960 | bytes 3670016 | tf_op jit(solution)/shard_map/pallas_call | solution.py:49
  5.3 8.8 %collective-permute-start.3 = (f32[4,2,32,640]{3,2,1,0:T(8,128)}, f32[4,2,32,640]{3,2,1,0:T(8,128)S(1)}, u32[]{:S(2)}, u32[]{:S(2)}) collective-permute-start(f32[4,2,32,640]{3,2,1,0:T(8,128)} %get-tuple-element.13), channel_id=1, source_target_pairs={{0,1},{1,0},{2,3},{3,2},{4,5},{5,4},{6,7},{7,6},{8,9},{9,8},{10,11... | collective-permute-start | bytes 1966088 | tf_op jit(solution)/shard_map/ppermute | solution.py:113
  14.1 1.3 copy-done.1
  15.4 2.6 %shard_map.37 = (f32[4,2,32,640]{3,2,1,0:T(8,128)S(1)}, f32[4,2,32,640]{3,2,1,0:T(8,128)S(1)}) custom-call(s32[1]{0:T(128)} %bitcast.half_ref, s32[2,2,4]{2,1,0:T(2,128)S(1)} %copy-done.2, f32[4,4,2,32,512]{4,3,2,1,0:T(8,128)S(1)} %bitcast.48, f32[512,640]{1,0:T(8,128)S(1)} %copy-done.1), custom_call_target="tpu_custom_call" | custom-call | flops 1006632960 | bytes 3670016 | tf_op jit(solution)/shard_map/pallas_call | solution.py:49
  19.0 3.5 %all-to-all-start.1 = ((f32[8,32,640]{2,1,0:T(8,128)}), f32[8,32,640]{2,1,0:T(8,128)S(1)}, u32[]{:S(2)}, u32[]{:S(2)}) async-start(f32[8,32,640]{2,1,0:T(8,128)} %bitcast.10), calls=%async_computation.1 | async-start | bytes 1310720 | tf_op jit(solution)/shard_map/all_to_all | solution.py:157
  22.5 1.9 %collective-permute-start = (f32[4,2,32,640]{3,2,1,0:T(8,128)S(1)}, f32[4,2,32,640]{3,2,1,0:T(8,128)S(1)}, u32[]{:S(2)}, u32[]{:S(2)}) collective-permute-start(f32[4,2,32,640]{3,2,1,0:T(8,128)S(1)} %copy-done.3), channel_id=1, source_target_pairs={{0,1},{1,0},{2,3},{3,2},{4,5},{5,4},{6,7},{7,6},{8,9},{9,8},{10,11... | collective-permute-start | bytes 1966088 | tf_op jit(solution)/shard_map/ppermute | solution.py:113
  24.4 2.1 %collective-permute-done = f32[4,2,32,640]{3,2,1,0:T(8,128)S(1)} collective-permute-done((f32[4,2,32,640]{3,2,1,0:T(8,128)S(1)}, f32[4,2,32,640]{3,2,1,0:T(8,128)S(1)}, u32[]{:S(2)}, u32[]{:S(2)}) %collective-permute-start) | collective-permute-done | bytes 655392 | tf_op jit(solution)/shard_map/ppermute | solution.py:113
  27.4 6.7 %all-to-all-done.1 = f32[8,32,640]{2,1,0:T(8,128)S(1)} async-done(((f32[8,32,640]{2,1,0:T(8,128)}), f32[8,32,640]{2,1,0:T(8,128)S(1)}, u32[]{:S(2)}, u32[]{:S(2)}) %all-to-all-start.1) | async-done | bytes 655392 | tf_op jit(solution)/shard_map/all_to_all | solution.py:157
  34.1 3.5 %all-to-all-start = ((f32[8,32,640]{2,1,0:T(8,128)}), f32[8,32,640]{2,1,0:T(8,128)S(1)}, u32[]{:S(2)}, u32[]{:S(2)}) async-start(f32[8,32,640]{2,1,0:T(8,128)} %bitcast.4), calls=%async_computation | async-start | bytes 1310720 | tf_op jit(solution)/shard_map/all_to_all | solution.py:157
  37.8 1.9 %collective-permute-start.4 = (f32[2,32,640]{2,1,0:T(8,128)S(1)}, f32[2,32,640]{2,1,0:T(8,128)S(1)}, u32[]{:S(2)}, u32[]{:S(2)}) collective-permute-start(f32[2,32,640]{2,1,0:T(8,128)S(1)} %dynamic-slice_bitcast_fusion.2), channel_id=1, source_target_pairs={{0,4},{4,0},{8,12},{12,8},{1,5},{5,1},{9,13},{13,9},{2,6},{6,2},{1... | collective-permute-start | bytes 491528 | tf_op jit(solution)/shard_map/ppermute | solution.py:113
  39.7 11.4 %all-to-all-done = f32[8,32,640]{2,1,0:T(8,128)S(1)} async-done(((f32[8,32,640]{2,1,0:T(8,128)}), f32[8,32,640]{2,1,0:T(8,128)S(1)}, u32[]{:S(2)}, u32[]{:S(2)}) %all-to-all-start) | async-done | bytes 655392 | tf_op jit(solution)/shard_map/all_to_all | solution.py:157
  51.2 1.9 %collective-permute-start.1 = (f32[2,32,640]{2,1,0:T(8,128)S(1)}, f32[2,32,640]{2,1,0:T(8,128)S(1)}, u32[]{:S(2)}, u32[]{:S(2)}) collective-permute-start(f32[2,32,640]{2,1,0:T(8,128)S(1)} %dynamic-slice_bitcast_fusion.3), channel_id=1, source_target_pairs={{0,4},{4,0},{8,12},{12,8},{1,5},{5,1},{9,13},{13,9},{2,6},{6,2},{1... | collective-permute-start | bytes 491528 | tf_op jit(solution)/shard_map/ppermute | solution.py:113
  53.2 5.4 %collective-permute-start.5 = (f32[32,640]{1,0:T(8,128)S(1)}, f32[32,640]{1,0:T(8,128)S(1)}, u32[]{:S(2)}, u32[]{:S(2)}) collective-permute-start(f32[32,640]{1,0:T(8,128)S(1)} %dynamic-slice_bitcast_fusion.4), channel_id=1, source_target_pairs={{0,8},{4,12},{8,0},{12,4},{1,9},{5,13},{9,1},{13,5},{2,10},{6,14},... | collective-permute-start | bytes 245768 | tf_op jit(solution)/shard_map/ppermute | solution.py:113
  58.6 2.6 %collective-permute-done.1 = f32[2,32,640]{2,1,0:T(8,128)S(1)} collective-permute-done((f32[2,32,640]{2,1,0:T(8,128)S(1)}, f32[2,32,640]{2,1,0:T(8,128)S(1)}, u32[]{:S(2)}, u32[]{:S(2)}) %collective-permute-start.1) | collective-permute-done | bytes 163872 | tf_op jit(solution)/shard_map/ppermute | solution.py:113
  61.3 6.8 %collective-permute-start.2 = (f32[32,640]{1,0:T(8,128)S(1)}, f32[32,640]{1,0:T(8,128)S(1)}, u32[]{:S(2)}, u32[]{:S(2)}) collective-permute-start(f32[32,640]{1,0:T(8,128)S(1)} %dynamic-slice_bitcast_fusion.5), channel_id=1, source_target_pairs={{0,8},{4,12},{8,0},{12,4},{1,9},{5,13},{9,1},{13,5},{2,10},{6,14},... | collective-permute-start | bytes 245768 | tf_op jit(solution)/shard_map/ppermute | solution.py:113
  68.1 8.4 %collective-permute-done.2 = f32[32,640]{1,0:T(8,128)S(1)} collective-permute-done((f32[32,640]{1,0:T(8,128)S(1)}, f32[32,640]{1,0:T(8,128)S(1)}, u32[]{:S(2)}, u32[]{:S(2)}) %collective-permute-start.2) | collective-permute-done | bytes 81952 | tf_op jit(solution)/shard_map/ppermute | solution.py:113
  76.5 1.9 %collective-permute-start.6 = (f32[64,640]{1,0:T(8,128)S(1)}, f32[64,640]{1,0:T(8,128)S(1)}, u32[]{:S(2)}, u32[]{:S(2)}) collective-permute-start(f32[64,640]{1,0:T(8,128)S(1)} %pad_maximum_fusion.3), channel_id=1, source_target_pairs={{0,8},{4,12},{8,0},{12,4},{1,9},{5,13},{9,1},{13,5},{2,10},{6,14},... | collective-permute-start | bytes 491528 | tf_op jit(solution)/shard_map/ppermute | solution.py:113
  78.4 9.1 %collective-permute-start.12 = (f32[64,640]{1,0:T(8,128)S(1)}, f32[64,640]{1,0:T(8,128)S(1)}, u32[]{:S(2)}, u32[]{:S(2)}) collective-permute-start(f32[64,640]{1,0:T(8,128)S(1)} %pad_maximum_fusion.3), channel_id=1, source_target_pairs={{0,68},{2,4},{4,64},{6,0},{8,76},{10,12},{12,72},{14,8},{64,6},{66... | collective-permute-start | bytes 491528 | tf_op jit(solution)/shard_map/ppermute | solution.py:163
  87.6 3.0 %collective-permute-start.11 = (f32[64,640]{1,0:T(8,128)S(1)}, f32[64,640]{1,0:T(8,128)S(1)}, u32[]{:S(2)}, u32[]{:S(2)}) collective-permute-start(f32[64,640]{1,0:T(8,128)S(1)} %pad_maximum_fusion.3), channel_id=1, source_target_pairs={{0,4},{2,68},{4,0},{6,64},{8,12},{10,76},{12,8},{14,72},{64,70},{6... | collective-permute-start | bytes 491528 | tf_op jit(solution)/shard_map/ppermute | solution.py:162
  90.6 7.7 %collective-permute-done.6 = f32[64,640]{1,0:T(8,128)S(1)} collective-permute-done((f32[64,640]{1,0:T(8,128)S(1)}, f32[64,640]{1,0:T(8,128)S(1)}, u32[]{:S(2)}, u32[]{:S(2)}) %collective-permute-start.6) | collective-permute-done | bytes 163872 | tf_op jit(solution)/shard_map/ppermute | solution.py:113
  98.3 1.9 %collective-permute-start.7 = (f32[2,64,640]{2,1,0:T(8,128)S(1)}, f32[2,64,640]{2,1,0:T(8,128)S(1)}, u32[]{:S(2)}, u32[]{:S(2)}) collective-permute-start(f32[2,64,640]{2,1,0:T(8,128)S(1)} %pad_maximum_fusion.1), channel_id=1, source_target_pairs={{0,4},{4,0},{8,12},{12,8},{1,5},{5,1},{9,13},{13,9},{2,6},{6,2},{1... | collective-permute-start | bytes 983048 | tf_op jit(solution)/shard_map/ppermute | solution.py:113
  100.4 1.2 broadcast_in_dim.2
  101.5 15.1 %all-to-all-start.2 = ((f32[4,2,64,640]{3,2,1,0:T(8,128)}), f32[4,2,64,640]{3,2,1,0:T(8,128)S(1)}, u32[]{:S(2)}, u32[]{:S(2)}) async-start(f32[4,2,64,640]{3,2,1,0:T(8,128)} %broadcast_in_dim.2), calls=%async_computation.2 | async-start | bytes 2621440 | tf_op jit(solution)/shard_map/all_to_all | solution.py:168
  116.6 4.4 %collective-permute-done.7 = f32[2,64,640]{2,1,0:T(8,128)S(1)} collective-permute-done((f32[2,64,640]{2,1,0:T(8,128)S(1)}, f32[2,64,640]{2,1,0:T(8,128)S(1)}, u32[]{:S(2)}, u32[]{:S(2)}) %collective-permute-start.7) | collective-permute-done | bytes 327712 | tf_op jit(solution)/shard_map/ppermute | solution.py:113
  121.1 6.9 %collective-permute-start.9 = (f32[4,64,640]{2,1,0:T(8,128)S(1)}, f32[4,64,640]{2,1,0:T(8,128)S(1)}, u32[]{:S(2)}, u32[]{:S(2)}) collective-permute-start(f32[4,64,640]{2,1,0:T(8,128)S(1)} %bitcast.44), channel_id=1, source_target_pairs={{0,2},{2,0},{1,3},{3,1},{4,6},{6,4},{5,7},{7,5},{8,10},{10,8},{9,1... | collective-permute-start | bytes 1966088 | tf_op jit(solution)/shard_map/ppermute | solution.py:113
  128.0 3.0 %collective-permute-start.8 = (f32[4,64,640]{2,1,0:T(8,128)S(1)}, f32[4,64,640]{2,1,0:T(8,128)S(1)}, u32[]{:S(2)}, u32[]{:S(2)}) collective-permute-start(f32[4,64,640]{2,1,0:T(8,128)S(1)} %bitcast.45), channel_id=1, source_target_pairs={{0,1},{1,0},{2,3},{3,2},{4,5},{5,4},{6,7},{7,6},{8,9},{9,8},{10,11... | collective-permute-start | bytes 1966088 | tf_op jit(solution)/shard_map/ppermute | solution.py:113
  131.0 11.4 %collective-permute-done.9.fown_ref = f32[4,64,640]{2,1,0:T(8,128)S(1)} collective-permute-done((f32[4,64,640]{2,1,0:T(8,128)S(1)}, f32[4,64,640]{2,1,0:T(8,128)S(1)}, u32[]{:S(2)}, u32[]{:S(2)}) %collective-permute-start.9) | collective-permute-done | bytes 655392 | tf_op jit(solution)/shard_map/ppermute | solution.py:113
  142.5 3.2 %collective-permute-start.10 = (f32[4,64,640]{2,1,0:T(8,128)S(1)}, f32[4,64,640]{2,1,0:T(8,128)S(1)}, u32[]{:S(2)}, u32[]{:S(2)}) collective-permute-start(f32[4,64,640]{2,1,0:T(8,128)S(1)} %collective-permute-done.9.fown_ref), channel_id=1, source_target_pairs={{0,1},{1,0},{2,3},{3,2},{4,5},{5,4},{6,7},{7,6},{8,9},{9,8},{10,11... | collective-permute-start | bytes 1966088 | tf_op jit(solution)/shard_map/ppermute | solution.py:113
  145.7 1.9 %collective-permute-start.13 = (f32[2,2,64,640]{3,2,1,0:T(8,128)S(1)}, f32[2,2,64,640]{3,2,1,0:T(8,128)S(1)}, u32[]{:S(2)}, u32[]{:S(2)}) collective-permute-start(f32[2,2,64,640]{3,2,1,0:T(8,128)S(1)} %get-tuple-element.15), channel_id=1, source_target_pairs={{0,1},{1,0},{2,3},{3,2},{4,5},{5,4},{6,7},{7,6},{8,9},{9,8},{10,11... | collective-permute-start | bytes 1966088 | tf_op jit(solution)/shard_map/ppermute | solution.py:113
  147.7 2.0 %collective-permute-done.13.noth_ref = f32[2,2,64,640]{3,2,1,0:T(8,128)S(1)} collective-permute-done((f32[2,2,64,640]{3,2,1,0:T(8,128)S(1)}, f32[2,2,64,640]{3,2,1,0:T(8,128)S(1)}, u32[]{:S(2)}, u32[]{:S(2)}) %collective-permute-start.13) | collective-permute-done | bytes 655392 | tf_op jit(solution)/shard_map/ppermute | solution.py:113
  149.7 4.0 %shard_map.39 = f32[4,256,512]{2,1,0:T(8,128)S(1)} custom-call(s32[2]{0:T(128)S(1)} %pad_add_fusion.place_ref, f32[4,64,640]{2,1,0:T(8,128)S(1)} %bitcast.46, f32[4,64,640]{2,1,0:T(8,128)S(1)} %collective-permute-done.8.moth_ref, f32[4,64,640]{2,1,0:T(8,128)S(1)} %collective-permute-done.9.fown_ref, f32[4,64,640]{2,1,0:T(8,128)S(1)} %collective-permute-done.10.foth_ref, ...), custom_call_target="tpu_custom_call" | custom-call | flops 2013265920 | bytes 6029312 | tf_op jit(solution)/shard_map/pallas_call | solution.py:97
  153.7 29.3 %all_to_all.20 = f32[4,256,512]{2,1,0:T(8,128)S(1)} all-to-all(f32[4,256,512]{2,1,0:T(8,128)S(1)} %shard_map.39), channel_id=1, replica_groups=mesh['x'=4,'zh'=2,'y'=4,'zq'=4,'zb'=2,'core'=2] {'x'}, dimensions={0} | all-to-all | bytes 4194304 | tf_op jit(solution)/shard_map/all_to_all | solution.py:129
  (38 shorter events, 3.6 us)
Async XLA Ops:
  0.0 14.1 %copy-start = (f32[2,2,256,512]{3,2,1,0:T(8,128)S(1)}, f32[2,2,256,512]{3,2,1,0:T(8,128)}, u32[]{:S(2)}) copy-start(f32[2,2,256,512]{3,2,1,0:T(8,128)} %param.3) | copy-start | bytes 6291460
  0.0 14.1 %copy-start.2 = (s32[2,2,4]{2,1,0:T(2,128)S(1)}, s32[2,2,4]{2,1,0:T(2,128)}, u32[]{:S(2)}) copy-start(s32[2,2,4]{2,1,0:T(2,128)} %mask_ref.3) | copy-start | bytes 196
  5.3 12.7 %collective-permute-start.3 = (f32[4,2,32,640]{3,2,1,0:T(8,128)}, f32[4,2,32,640]{3,2,1,0:T(8,128)S(1)}, u32[]{:S(2)}, u32[]{:S(2)}) collective-permute-start(f32[4,2,32,640]{3,2,1,0:T(8,128)} %get-tuple-element.13), channel_id=1, source_target_pairs={{0,1},{1,0},{2,3},{3,2},{4,5},{5,4},{6,7},{7,6},{8,9},{9,8},{10,11... | collective-permute-start | bytes 1966088 | tf_op jit(solution)/shard_map/ppermute | solution.py:113
  14.1 1.3 copy-start.1
  18.0 4.5 %copy-start.3 = (f32[4,2,32,640]{3,2,1,0:T(8,128)S(1)}, f32[4,2,32,640]{3,2,1,0:T(8,128)}, u32[]{:S(2)}) copy-start(f32[4,2,32,640]{3,2,1,0:T(8,128)} %get-tuple-element.11) | copy-start | bytes 1966084
  19.0 15.2 %all-to-all-start.1 = ((f32[8,32,640]{2,1,0:T(8,128)}), f32[8,32,640]{2,1,0:T(8,128)S(1)}, u32[]{:S(2)}, u32[]{:S(2)}) async-start(f32[8,32,640]{2,1,0:T(8,128)} %bitcast.10), calls=%async_computation.1 | async-start | bytes 1310720 | tf_op jit(solution)/shard_map/all_to_all | solution.py:157
  22.5 4.0 %collective-permute-start = (f32[4,2,32,640]{3,2,1,0:T(8,128)S(1)}, f32[4,2,32,640]{3,2,1,0:T(8,128)S(1)}, u32[]{:S(2)}, u32[]{:S(2)}) collective-permute-start(f32[4,2,32,640]{3,2,1,0:T(8,128)S(1)} %copy-done.3), channel_id=1, source_target_pairs={{0,1},{1,0},{2,3},{3,2},{4,5},{5,4},{6,7},{7,6},{8,9},{9,8},{10,11... | collective-permute-start | bytes 1966088 | tf_op jit(solution)/shard_map/ppermute | solution.py:113
  34.1 17.0 %all-to-all-start = ((f32[8,32,640]{2,1,0:T(8,128)}), f32[8,32,640]{2,1,0:T(8,128)S(1)}, u32[]{:S(2)}, u32[]{:S(2)}) async-start(f32[8,32,640]{2,1,0:T(8,128)} %bitcast.4), calls=%async_computation | async-start | bytes 1310720 | tf_op jit(solution)/shard_map/all_to_all | solution.py:157
  37.8 15.4 %collective-permute-start.4 = (f32[2,32,640]{2,1,0:T(8,128)S(1)}, f32[2,32,640]{2,1,0:T(8,128)S(1)}, u32[]{:S(2)}, u32[]{:S(2)}) collective-permute-start(f32[2,32,640]{2,1,0:T(8,128)S(1)} %dynamic-slice_bitcast_fusion.2), channel_id=1, source_target_pairs={{0,4},{4,0},{8,12},{12,8},{1,5},{5,1},{9,13},{13,9},{2,6},{6,2},{1... | collective-permute-start | bytes 491528 | tf_op jit(solution)/shard_map/ppermute | solution.py:113
  51.2 10.0 %collective-permute-start.1 = (f32[2,32,640]{2,1,0:T(8,128)S(1)}, f32[2,32,640]{2,1,0:T(8,128)S(1)}, u32[]{:S(2)}, u32[]{:S(2)}) collective-permute-start(f32[2,32,640]{2,1,0:T(8,128)S(1)} %dynamic-slice_bitcast_fusion.3), channel_id=1, source_target_pairs={{0,4},{4,0},{8,12},{12,8},{1,5},{5,1},{9,13},{13,9},{2,6},{6,2},{1... | collective-permute-start | bytes 491528 | tf_op jit(solution)/shard_map/ppermute | solution.py:113
  53.2 14.9 %collective-permute-start.5 = (f32[32,640]{1,0:T(8,128)S(1)}, f32[32,640]{1,0:T(8,128)S(1)}, u32[]{:S(2)}, u32[]{:S(2)}) collective-permute-start(f32[32,640]{1,0:T(8,128)S(1)} %dynamic-slice_bitcast_fusion.4), channel_id=1, source_target_pairs={{0,8},{4,12},{8,0},{12,4},{1,9},{5,13},{9,1},{13,5},{2,10},{6,14},... | collective-permute-start | bytes 245768 | tf_op jit(solution)/shard_map/ppermute | solution.py:113
  61.3 15.2 %collective-permute-start.2 = (f32[32,640]{1,0:T(8,128)S(1)}, f32[32,640]{1,0:T(8,128)S(1)}, u32[]{:S(2)}, u32[]{:S(2)}) collective-permute-start(f32[32,640]{1,0:T(8,128)S(1)} %dynamic-slice_bitcast_fusion.5), channel_id=1, source_target_pairs={{0,8},{4,12},{8,0},{12,4},{1,9},{5,13},{9,1},{13,5},{2,10},{6,14},... | collective-permute-start | bytes 245768 | tf_op jit(solution)/shard_map/ppermute | solution.py:113
  76.5 21.8 %collective-permute-start.6 = (f32[64,640]{1,0:T(8,128)S(1)}, f32[64,640]{1,0:T(8,128)S(1)}, u32[]{:S(2)}, u32[]{:S(2)}) collective-permute-start(f32[64,640]{1,0:T(8,128)S(1)} %pad_maximum_fusion.3), channel_id=1, source_target_pairs={{0,8},{4,12},{8,0},{12,4},{1,9},{5,13},{9,1},{13,5},{2,10},{6,14},... | collective-permute-start | bytes 491528 | tf_op jit(solution)/shard_map/ppermute | solution.py:113
  78.4 21.8 %collective-permute-start.12 = (f32[64,640]{1,0:T(8,128)S(1)}, f32[64,640]{1,0:T(8,128)S(1)}, u32[]{:S(2)}, u32[]{:S(2)}) collective-permute-start(f32[64,640]{1,0:T(8,128)S(1)} %pad_maximum_fusion.3), channel_id=1, source_target_pairs={{0,68},{2,4},{4,64},{6,0},{8,76},{10,12},{12,72},{14,8},{64,6},{66... | collective-permute-start | bytes 491528 | tf_op jit(solution)/shard_map/ppermute | solution.py:163
  87.6 12.7 %collective-permute-start.11 = (f32[64,640]{1,0:T(8,128)S(1)}, f32[64,640]{1,0:T(8,128)S(1)}, u32[]{:S(2)}, u32[]{:S(2)}) collective-permute-start(f32[64,640]{1,0:T(8,128)S(1)} %pad_maximum_fusion.3), channel_id=1, source_target_pairs={{0,4},{2,68},{4,0},{6,64},{8,12},{10,76},{12,8},{14,72},{64,70},{6... | collective-permute-start | bytes 491528 | tf_op jit(solution)/shard_map/ppermute | solution.py:162
  98.3 22.7 %collective-permute-start.7 = (f32[2,64,640]{2,1,0:T(8,128)S(1)}, f32[2,64,640]{2,1,0:T(8,128)S(1)}, u32[]{:S(2)}, u32[]{:S(2)}) collective-permute-start(f32[2,64,640]{2,1,0:T(8,128)S(1)} %pad_maximum_fusion.1), channel_id=1, source_target_pairs={{0,4},{4,0},{8,12},{12,8},{1,5},{5,1},{9,13},{13,9},{2,6},{6,2},{1... | collective-permute-start | bytes 983048 | tf_op jit(solution)/shard_map/ppermute | solution.py:113
  101.5 40.9 %all-to-all-start.2 = ((f32[4,2,64,640]{3,2,1,0:T(8,128)}), f32[4,2,64,640]{3,2,1,0:T(8,128)S(1)}, u32[]{:S(2)}, u32[]{:S(2)}) async-start(f32[4,2,64,640]{3,2,1,0:T(8,128)} %broadcast_in_dim.2), calls=%async_computation.2 | async-start | bytes 2621440 | tf_op jit(solution)/shard_map/all_to_all | solution.py:168
  121.1 21.2 %collective-permute-start.9 = (f32[4,64,640]{2,1,0:T(8,128)S(1)}, f32[4,64,640]{2,1,0:T(8,128)S(1)}, u32[]{:S(2)}, u32[]{:S(2)}) collective-permute-start(f32[4,64,640]{2,1,0:T(8,128)S(1)} %bitcast.44), channel_id=1, source_target_pairs={{0,2},{2,0},{1,3},{3,1},{4,6},{6,4},{5,7},{7,5},{8,10},{10,8},{9,1... | collective-permute-start | bytes 1966088 | tf_op jit(solution)/shard_map/ppermute | solution.py:113
  128.0 19.7 %collective-permute-start.8 = (f32[4,64,640]{2,1,0:T(8,128)S(1)}, f32[4,64,640]{2,1,0:T(8,128)S(1)}, u32[]{:S(2)}, u32[]{:S(2)}) collective-permute-start(f32[4,64,640]{2,1,0:T(8,128)S(1)} %bitcast.45), channel_id=1, source_target_pairs={{0,1},{1,0},{2,3},{3,2},{4,5},{5,4},{6,7},{7,6},{8,9},{9,8},{10,11... | collective-permute-start | bytes 1966088 | tf_op jit(solution)/shard_map/ppermute | solution.py:113
  142.5 5.3 %collective-permute-start.10 = (f32[4,64,640]{2,1,0:T(8,128)S(1)}, f32[4,64,640]{2,1,0:T(8,128)S(1)}, u32[]{:S(2)}, u32[]{:S(2)}) collective-permute-start(f32[4,64,640]{2,1,0:T(8,128)S(1)} %collective-permute-done.9.fown_ref), channel_id=1, source_target_pairs={{0,1},{1,0},{2,3},{3,2},{4,5},{5,4},{6,7},{7,6},{8,9},{9,8},{10,11... | collective-permute-start | bytes 1966088 | tf_op jit(solution)/shard_map/ppermute | solution.py:113
  145.7 4.0 %collective-permute-start.13 = (f32[2,2,64,640]{3,2,1,0:T(8,128)S(1)}, f32[2,2,64,640]{3,2,1,0:T(8,128)S(1)}, u32[]{:S(2)}, u32[]{:S(2)}) collective-permute-start(f32[2,2,64,640]{3,2,1,0:T(8,128)S(1)} %get-tuple-element.15), channel_id=1, source_target_pairs={{0,1},{1,0},{2,3},{3,2},{4,5},{5,4},{6,7},{7,6},{8,9},{9,8},{10,11... | collective-permute-start | bytes 1966088 | tf_op jit(solution)/shard_map/ppermute | solution.py:113

commit v11 on v10

--- a/solution.py
+++ b/solution.py
@@ -87,25 +87,26 @@
     o_ref[...] = total.reshape(o_ref.shape)
 
 
-def exchange_part(near, far, cols, place):
-    parts, rows, norbit = near[0].shape
+def exchange_part(near, far, cols, place, shifts):
+    _, rows, norbit = near[0].shape
     blocks, bits, nrows, _ = cols[0].shape
-    ncols = 2 * blocks * bits * nrows
-    step = parts // 2
-    mspec = pl.BlockSpec((step, rows, norbit), lambda x, place: (x, 0, 0))
-    nspec = pl.BlockSpec(cols[0].shape, lambda x, place: (0, 0, 0, 0))
+    ncols, count = 2 * blocks * bits * nrows, len(shifts)
+    here = lax.axis_index("x")
+    place = jnp.stack(place + [(here + shift) % 4 for shift in shifts])
+    mspec = pl.BlockSpec((1, rows, norbit), lambda g, place: (place[2 + g], 0, 0))
+    nspec = pl.BlockSpec(cols[0].shape, lambda g, place: (0, 0, 0, 0))
     return pl.pallas_call(
         exchange_kernel,
-        out_shape=jax.ShapeDtypeStruct((parts, 4 * rows, ncols), jnp.float32),
+        out_shape=jax.ShapeDtypeStruct((count, 4 * rows, ncols), jnp.float32),
         grid_spec=pltpu.PrefetchScalarGridSpec(
             num_scalar_prefetch=1,
-            grid=(2,),
+            grid=(count,),
             in_specs=[mspec] * 4 + [nspec] * 2,
-            out_specs=pl.BlockSpec((step, 4 * rows, ncols), lambda x, place: (x, 0, 0)),
-            scratch_shapes=[pltpu.VMEM((step * 4 * rows, norbit), jnp.bfloat16)] * 2 + [pltpu.VMEM((ncols, norbit), jnp.bfloat16)] * 2,
+            out_specs=pl.BlockSpec((1, 4 * rows, ncols), lambda g, place: (g, 0, 0)),
+            scratch_shapes=[pltpu.VMEM((4 * rows, norbit), jnp.bfloat16)] * 2 + [pltpu.VMEM((ncols, norbit), jnp.bfloat16)] * 2,
         ),
         compiler_params=pltpu.CompilerParams(vmem_limit_bytes=VMEM),
-        cost_estimate=pl.CostEstimate(flops=24 * parts * rows * ncols * norbit, bytes_accessed=4 * norbit * (4 * parts * rows + ncols) + 16 * parts * rows * ncols, transcendentals=0),
+        cost_estimate=pl.CostEstimate(flops=24 * count * rows * ncols * norbit, bytes_accessed=4 * norbit * (4 * count * rows + ncols) + 16 * count * rows * ncols, transcendentals=0),
     )(place, *near, *far, *cols)
 
 
@@ -125,8 +126,8 @@
     return lax.optimization_barrier((value, other))[0]
 
 
-def to_x(value):
-    return lax.all_to_all(value, "x", split_axis=0, concat_axis=0)
+def turn(value, by):
+    return lax.ppermute(value, "x", [(i, (i + by) % 4) for i in range(4)])
 
 
 Z = ("zh", "zq", "zb")
@@ -169,8 +170,13 @@
     n = after(n, far).reshape((2, 2) + cols.shape)
     cols = pick(n, core, 0), swap(pick(n, 1 - core, 0), "core", 1, 2)
     near, far = (m, swap(m, "core", 1, 2)), (far, swap(far, "core", 1, 2))
-    partial = to_x(exchange_part(near, far, cols, jnp.stack([core, low])))
-    return jnp.sum(partial, axis=0) * (1.0 / jnp.sqrt(jnp.float32(norbit * parts)))
+    across = exchange_part(near, far, cols, [core, low], (2,))[0]
+    half = mrows // 2
+    up, down = turn(across[:half], 1), turn(across[half:], 3)
+    right, left, here = exchange_part(near, far, cols, [core, low], (1, 3, 0))
+    right = turn(jnp.concatenate([right[:half] + up, right[half:]]), 1)
+    left = turn(jnp.concatenate([left[:half], left[half:] + down]), 3)
+    return (here + right + left) * (1.0 / jnp.sqrt(jnp.float32(norbit * parts)))
 
 
 def solution(mesh):

time: 185 us -> 190 us (1.027)
  blocking collectives: 29.3 us -> 0 us
  waiting for transfers between devices: 56.6 us -> 71 us
  starting transfers between devices: 79.9 us -> 93.3 us
  Pallas kernels: 11.8 us -> 15 us
  local copies, waits for them, and re-layouts: 2.64 us -> 4.92 us
    all_to_all x1 -> x0, blocking collectives: 29.3 us -> none  [to_x(): return lax.all_to_all(value, 'x', split_axis=0, concat_axis=0)]
    ppermute x0 -> x4, waiting for transfers between devices: none -> 14 us  [turn(): return lax.ppermute(value, 'x', [(i, (i + by) % 4) for i in range(4)])]
    ppermute x0 -> x4, starting transfers between devices: none -> 13.5 us  [turn(): return lax.ppermute(value, 'x', [(i, (i + by) % 4) for i in range(4)])]
    pallas_call x1 -> x2, Pallas kernels: 3.97 us -> 7.14 us  [exchange_part(): pl.pallas_call(exchange_kernel, out_shape=jax.ShapeDtypeStruct((count, 4...]
    squeeze x5, local copies, waits for them, and re-layouts: 0.16 us -> 2.28 us  [pick(): return lax.dynamic_index_in_dim(value, index, axis, keepdims=False)]
  transfers between devices with their start and end apart: 17 -> 21, of which waited for: 9 -> 12; matrix products, arithmetic and copies ran while one was open for 1% -> 3% of each run, Pallas kernels for 1% -> 4%
where the time goes in v11:
time: 190 us; the launch traced here: 188 us
  starting transfers between devices  93.3 us (49%)
  waiting for transfers between devices  71 us (37%)
  Pallas kernels  15 us (8%)
  local copies, waits for them, and re-layouts  4.92 us (3%)
  other arithmetic  3.38 us (2%)
    ppermute x12, starting transfers between devices, swap(): return lax.ppermute(value, axis, [(i, i ^ bit) for i in range(size)])  45.5 us
    ppermute x12, waiting for transfers between devices, swap(): return lax.ppermute(value, axis, [(i, i ^ bit) for i in range(size)])  38.9 us
    all_to_all x2, waiting for transfers between devices, local(): lax.all_to_all(part, ('x', 'zb'), split_axis=0, concat_axis=0)  18.1 us
    all_to_all x1, starting transfers between devices, local(): lax.all_to_all(jnp.broadcast_to(cols[None], (4,) + cols.shape), 'y', spli...  15.1 us
    ppermute x4, waiting for transfers between devices, turn(): return lax.ppermute(value, 'x', [(i, (i + by) % 4) for i in range(4)])  14 us
    ppermute x4, starting transfers between devices, turn(): return lax.ppermute(value, 'x', [(i, (i + by) % 4) for i in range(4)])  13.5 us
    ppermute x1, starting transfers between devices, local(): second = lax.ppermute(own, Z, SECOND)  9.15 us
    pallas_call x2, Pallas kernels, half_of(): pl.pallas_call(half_kernel, out_shape=[jax.ShapeDtypeStruct(shape, jnp.fl...  7.87 us
  transfers between devices with their start and end apart: 21, of which 12 were waited for; matrix products, arithmetic and copies ran while one was open for 3% of the time, Pallas kernels for 4%

profile of v11, /device:TPU:1, one launch (start us, length us, event | category | flops | bytes accessed | tf_op | source)
XLA Modules:
  0.0 188.2 jit_solution(11904385874780833365)
XLA Ops:
  0.0 5.3 %shard_map.38 = (f32[4,2,32,640]{3,2,1,0:T(8,128)}, f32[4,2,32,640]{3,2,1,0:T(8,128)}) custom-call(s32[1]{0:T(128)} %bitcast.6.half_ref, s32[2,2,4]{2,1,0:T(2,128)} %mask_ref.3, f32[4,4,2,32,512]{4,3,2,1,0:T(8,128)} %bitcast.76, f32[512,640]{1,0:T(8,128)} %c_ref.3), custom_call_target="tpu_custom_call" | custom-call | flops 1006632960 | bytes 3670016 | tf_op jit(solution)/shard_map/pallas_call | solution.py:49
  5.3 8.8 %collective-permute-start.3 = (f32[4,2,32,640]{3,2,1,0:T(8,128)}, f32[4,2,32,640]{3,2,1,0:T(8,128)S(1)}, u32[]{:S(2)}, u32[]{:S(2)}) collective-permute-start(f32[4,2,32,640]{3,2,1,0:T(8,128)} %get-tuple-element.13), channel_id=1, source_target_pairs={{0,1},{1,0},{2,3},{3,2},{4,5},{5,4},{6,7},{7,6},{8,9},{9,8},{10,11... | collective-permute-start | bytes 1966088 | tf_op jit(solution)/shard_map/ppermute | solution.py:114
  15.4 2.6 %shard_map.37 = (f32[4,2,32,640]{3,2,1,0:T(8,128)S(1)}, f32[4,2,32,640]{3,2,1,0:T(8,128)S(1)}) custom-call(s32[1]{0:T(128)} %bitcast.half_ref, s32[2,2,4]{2,1,0:T(2,128)S(1)} %copy-done.2, f32[4,4,2,32,512]{4,3,2,1,0:T(8,128)S(1)} %bitcast.77, f32[512,640]{1,0:T(8,128)S(1)} %copy-done.1), custom_call_target="tpu_custom_call" | custom-call | flops 1006632960 | bytes 3670016 | tf_op jit(solution)/shard_map/pallas_call | solution.py:49
  19.0 3.5 %all-to-all-start.1 = ((f32[8,32,640]{2,1,0:T(8,128)}), f32[8,32,640]{2,1,0:T(8,128)S(1)}, u32[]{:S(2)}, u32[]{:S(2)}) async-start(f32[8,32,640]{2,1,0:T(8,128)} %bitcast.13), calls=%async_computation.1 | async-start | bytes 1310720 | tf_op jit(solution)/shard_map/all_to_all | solution.py:158
  22.5 1.9 %collective-permute-start = (f32[4,2,32,640]{3,2,1,0:T(8,128)S(1)}, f32[4,2,32,640]{3,2,1,0:T(8,128)S(1)}, u32[]{:S(2)}, u32[]{:S(2)}) collective-permute-start(f32[4,2,32,640]{3,2,1,0:T(8,128)S(1)} %copy-done.3), channel_id=1, source_target_pairs={{0,1},{1,0},{2,3},{3,2},{4,5},{5,4},{6,7},{7,6},{8,9},{9,8},{10,11... | collective-permute-start | bytes 1966088 | tf_op jit(solution)/shard_map/ppermute | solution.py:114
  24.5 2.1 %collective-permute-done = f32[4,2,32,640]{3,2,1,0:T(8,128)S(1)} collective-permute-done((f32[4,2,32,640]{3,2,1,0:T(8,128)S(1)}, f32[4,2,32,640]{3,2,1,0:T(8,128)S(1)}, u32[]{:S(2)}, u32[]{:S(2)}) %collective-permute-start) | collective-permute-done | bytes 655392 | tf_op jit(solution)/shard_map/ppermute | solution.py:114
  27.4 6.7 %all-to-all-done.1 = f32[8,32,640]{2,1,0:T(8,128)S(1)} async-done(((f32[8,32,640]{2,1,0:T(8,128)}), f32[8,32,640]{2,1,0:T(8,128)S(1)}, u32[]{:S(2)}, u32[]{:S(2)}) %all-to-all-start.1) | async-done | bytes 655392 | tf_op jit(solution)/shard_map/all_to_all | solution.py:158
  34.1 3.5 %all-to-all-start = ((f32[8,32,640]{2,1,0:T(8,128)}), f32[8,32,640]{2,1,0:T(8,128)S(1)}, u32[]{:S(2)}, u32[]{:S(2)}) async-start(f32[8,32,640]{2,1,0:T(8,128)} %bitcast.7), calls=%async_computation | async-start | bytes 1310720 | tf_op jit(solution)/shard_map/all_to_all | solution.py:158
  39.7 11.4 %all-to-all-done = f32[8,32,640]{2,1,0:T(8,128)S(1)} async-done(((f32[8,32,640]{2,1,0:T(8,128)}), f32[8,32,640]{2,1,0:T(8,128)S(1)}, u32[]{:S(2)}, u32[]{:S(2)}) %all-to-all-start) | async-done | bytes 655392 | tf_op jit(solution)/shard_map/all_to_all | solution.py:158
  51.2 1.9 %collective-permute-start.1 = (f32[2,32,640]{2,1,0:T(8,128)S(1)}, f32[2,32,640]{2,1,0:T(8,128)S(1)}, u32[]{:S(2)}, u32[]{:S(2)}) collective-permute-start(f32[2,32,640]{2,1,0:T(8,128)S(1)} %dynamic-slice_bitcast_fusion.3), channel_id=1, source_target_pairs={{0,4},{4,0},{8,12},{12,8},{1,5},{5,1},{9,13},{13,9},{2,6},{6,2},{1... | collective-permute-start | bytes 491528 | tf_op jit(solution)/shard_map/ppermute | solution.py:114
  53.2 5.4 %collective-permute-start.5 = (f32[32,640]{1,0:T(8,128)S(1)}, f32[32,640]{1,0:T(8,128)S(1)}, u32[]{:S(2)}, u32[]{:S(2)}) collective-permute-start(f32[32,640]{1,0:T(8,128)S(1)} %dynamic-slice_bitcast_fusion.4), channel_id=1, source_target_pairs={{0,8},{4,12},{8,0},{12,4},{1,9},{5,13},{9,1},{13,5},{2,10},{6,14},... | collective-permute-start | bytes 245768 | tf_op jit(solution)/shard_map/ppermute | solution.py:114
  58.6 2.6 %collective-permute-done.1 = f32[2,32,640]{2,1,0:T(8,128)S(1)} collective-permute-done((f32[2,32,640]{2,1,0:T(8,128)S(1)}, f32[2,32,640]{2,1,0:T(8,128)S(1)}, u32[]{:S(2)}, u32[]{:S(2)}) %collective-permute-start.1) | collective-permute-done | bytes 163872 | tf_op jit(solution)/shard_map/ppermute | solution.py:114
  61.3 6.8 %collective-permute-start.2 = (f32[32,640]{1,0:T(8,128)S(1)}, f32[32,640]{1,0:T(8,128)S(1)}, u32[]{:S(2)}, u32[]{:S(2)}) collective-permute-start(f32[32,640]{1,0:T(8,128)S(1)} %dynamic-slice_bitcast_fusion.5), channel_id=1, source_target_pairs={{0,8},{4,12},{8,0},{12,4},{1,9},{5,13},{9,1},{13,5},{2,10},{6,14},... | collective-permute-start | bytes 245768 | tf_op jit(solution)/shard_map/ppermute | solution.py:114
  68.1 8.4 %collective-permute-done.2 = f32[32,640]{1,0:T(8,128)S(1)} collective-permute-done((f32[32,640]{1,0:T(8,128)S(1)}, f32[32,640]{1,0:T(8,128)S(1)}, u32[]{:S(2)}, u32[]{:S(2)}) %collective-permute-start.2) | collective-permute-done | bytes 81952 | tf_op jit(solution)/shard_map/ppermute | solution.py:114
  78.4 9.1 %collective-permute-start.12 = (f32[64,640]{1,0:T(8,128)S(1)}, f32[64,640]{1,0:T(8,128)S(1)}, u32[]{:S(2)}, u32[]{:S(2)}) collective-permute-start(f32[64,640]{1,0:T(8,128)S(1)} %pad_maximum_fusion.5), channel_id=1, source_target_pairs={{0,68},{2,4},{4,64},{6,0},{8,76},{10,12},{12,72},{14,8},{64,6},{66... | collective-permute-start | bytes 491528 | tf_op jit(solution)/shard_map/ppermute | solution.py:164
  87.6 3.0 %collective-permute-start.11 = (f32[64,640]{1,0:T(8,128)S(1)}, f32[64,640]{1,0:T(8,128)S(1)}, u32[]{:S(2)}, u32[]{:S(2)}) collective-permute-start(f32[64,640]{1,0:T(8,128)S(1)} %pad_maximum_fusion.5), channel_id=1, source_target_pairs={{0,4},{2,68},{4,0},{6,64},{8,12},{10,76},{12,8},{14,72},{64,70},{6... | collective-permute-start | bytes 491528 | tf_op jit(solution)/shard_map/ppermute | solution.py:163
  90.6 7.7 %collective-permute-done.6 = f32[64,640]{1,0:T(8,128)S(1)} collective-permute-done((f32[64,640]{1,0:T(8,128)S(1)}, f32[64,640]{1,0:T(8,128)S(1)}, u32[]{:S(2)}, u32[]{:S(2)}) %collective-permute-start.6) | collective-permute-done | bytes 163872 | tf_op jit(solution)/shard_map/ppermute | solution.py:114
  101.5 15.1 %all-to-all-start.2 = ((f32[4,2,64,640]{3,2,1,0:T(8,128)}), f32[4,2,64,640]{3,2,1,0:T(8,128)}, u32[]{:S(2)}, u32[]{:S(2)}) async-start(f32[4,2,64,640]{3,2,1,0:T(8,128)} %broadcast_in_dim.2), calls=%async_computation.2 | async-start | bytes 2621440 | tf_op jit(solution)/shard_map/all_to_all | solution.py:169
  116.7 4.4 %collective-permute-done.7 = f32[2,64,640]{2,1,0:T(8,128)S(1)} collective-permute-done((f32[2,64,640]{2,1,0:T(8,128)S(1)}, f32[2,64,640]{2,1,0:T(8,128)S(1)}, u32[]{:S(2)}, u32[]{:S(2)}) %collective-permute-start.7) | collective-permute-done | bytes 327712 | tf_op jit(solution)/shard_map/ppermute | solution.py:114
  121.1 7.0 %collective-permute-start.9 = (f32[4,64,640]{2,1,0:T(8,128)S(1)}, f32[4,64,640]{2,1,0:T(8,128)S(1)}, u32[]{:S(2)}, u32[]{:S(2)}) collective-permute-start(f32[4,64,640]{2,1,0:T(8,128)S(1)} %bitcast.72), channel_id=1, source_target_pairs={{0,2},{2,0},{1,3},{3,1},{4,6},{6,4},{5,7},{7,5},{8,10},{10,8},{9,1... | collective-permute-start | bytes 1966088 | tf_op jit(solution)/shard_map/ppermute | solution.py:114
  128.2 2.9 %collective-permute-start.8 = (f32[4,64,640]{2,1,0:T(8,128)S(1)}, f32[4,64,640]{2,1,0:T(8,128)S(1)}, u32[]{:S(2)}, u32[]{:S(2)}) collective-permute-start(f32[4,64,640]{2,1,0:T(8,128)S(1)} %bitcast.73), channel_id=1, source_target_pairs={{0,1},{1,0},{2,3},{3,2},{4,5},{5,4},{6,7},{7,6},{8,9},{9,8},{10,11... | collective-permute-start | bytes 1966088 | tf_op jit(solution)/shard_map/ppermute | solution.py:114
  131.0 11.6 %collective-permute-done.9.fown_ref = f32[4,64,640]{2,1,0:T(8,128)S(1)} collective-permute-done((f32[4,64,640]{2,1,0:T(8,128)S(1)}, f32[4,64,640]{2,1,0:T(8,128)S(1)}, u32[]{:S(2)}, u32[]{:S(2)}) %collective-permute-start.9) | collective-permute-done | bytes 655392 | tf_op jit(solution)/shard_map/ppermute | solution.py:114
  142.6 2.2 %dynamic-slice_bitcast_fusion = (f32[2,2,64,640]{3,2,1,0:T(8,128)}, f32[2,2,64,640]{3,2,1,0:T(8,128)S(1)}) fusion(f32[2,2,2,64,640]{4,3,2,1,0:T(8,128)} %bitcast.27, s32[]{:T(128)S(6)} %select_n.102, s32[]{:T(128)S(6)} %select_n.101), kind=kLoop, calls=%fused_computation.1 | loop fusion | bytes 2621448 | tf_op jit(solution)/shard_map/jit(dynamic_index_in_dim)/squeeze | solution.py:118
  144.8 3.1 %collective-permute-start.10 = (f32[4,64,640]{2,1,0:T(8,128)S(1)}, f32[4,64,640]{2,1,0:T(8,128)S(1)}, u32[]{:S(2)}, u32[]{:S(2)}) collective-permute-start(f32[4,64,640]{2,1,0:T(8,128)S(1)} %collective-permute-done.9.fown_ref), channel_id=1, source_target_pairs={{0,1},{1,0},{2,3},{3,2},{4,5},{5,4},{6,7},{7,6},{8,9},{9,8},{10,11... | collective-permute-start | bytes 1966088 | tf_op jit(solution)/shard_map/ppermute | solution.py:114
  148.0 1.9 %collective-permute-start.13 = (f32[2,2,64,640]{3,2,1,0:T(8,128)}, f32[2,2,64,640]{3,2,1,0:T(8,128)}, u32[]{:S(2)}, u32[]{:S(2)}) collective-permute-start(f32[2,2,64,640]{3,2,1,0:T(8,128)} %get-tuple-element.19), channel_id=1, source_target_pairs={{0,1},{1,0},{2,3},{3,2},{4,5},{5,4},{6,7},{7,6},{8,9},{9,8},{10,11... | collective-permute-start | bytes 1966088 | tf_op jit(solution)/shard_map/ppermute | solution.py:114
  150.1 2.2 %collective-permute-done.13.noth_ref = f32[2,2,64,640]{3,2,1,0:T(8,128)} collective-permute-done((f32[2,2,64,640]{3,2,1,0:T(8,128)}, f32[2,2,64,640]{3,2,1,0:T(8,128)}, u32[]{:S(2)}, u32[]{:S(2)}) %collective-permute-start.13) | collective-permute-done | bytes 655392 | tf_op jit(solution)/shard_map/ppermute | solution.py:114
  152.3 2.7 %shard_map.40 = f32[1,256,512]{2,1,0:T(8,128)S(1)} custom-call(s32[3]{0:T(128)S(1)} %pad_add_fusion.place_ref, f32[4,64,640]{2,1,0:T(8,128)S(1)} %bitcast.74, f32[4,64,640]{2,1,0:T(8,128)S(1)} %collective-permute-done.8.moth_ref, f32[4,64,640]{2,1,0:T(8,128)S(1)} %collective-permute-done.9.fown_ref, f32[4,64,640]{2,1,0:T(8,128)S(1)} %collective-permute-done.10.foth_ref, ...), custom_call_target="tpu_custom_call" | custom-call | flops 503316480 | bytes 2490368 | tf_op jit(solution)/shard_map/pallas_call | solution.py:98
  156.9 4.6 %collective-permute-start.16 = (f32[128,512]{1,0:T(8,128)S(1)}, f32[128,512]{1,0:T(8,128)S(1)}, u32[]{:S(2)}, u32[]{:S(2)}) collective-permute-start(f32[128,512]{1,0:T(8,128)S(1)} %get-tuple-element.24), channel_id=1, source_target_pairs={{0,384},{128,0},{256,128},{384,256},{1,385},{129,1},{257,129},{385... | collective-permute-start | bytes 786440 | tf_op jit(solution)/shard_map/ppermute | solution.py:130
  161.5 4.5 %shard_map.39 = f32[3,256,512]{2,1,0:T(8,128)S(1)} custom-call(s32[5]{0:T(128)S(1)} %stack.58.place_ref, f32[4,64,640]{2,1,0:T(8,128)S(1)} %bitcast.75, f32[4,64,640]{2,1,0:T(8,128)S(1)} %collective-permute-done.8.moth_ref, f32[4,64,640]{2,1,0:T(8,128)S(1)} %collective-permute-done.9.fown_ref, f32[4,64,640]{2,1,0:T(8,128)S(1)} %collective-permute-done.10.foth_ref, ...), custom_call_target="tpu_custom_call" | custom-call | flops 1509949440 | bytes 4849664 | tf_op jit(solution)/shard_map/pallas_call | solution.py:98
  167.1 5.1 %collective-permute-start.17 = (f32[256,512]{1,0:T(8,128)S(1)}, f32[256,512]{1,0:T(8,128)S(1)}, u32[]{:S(2)}, u32[]{:S(2)}) collective-permute-start(f32[256,512]{1,0:T(8,128)S(1)} %pad_maximum_fusion.2), channel_id=1, source_target_pairs={{0,384},{128,0},{256,128},{384,256},{1,385},{129,1},{257,129},{385... | collective-permute-start | bytes 1572872 | tf_op jit(solution)/shard_map/ppermute | solution.py:130
  174.2 7.9 %collective-permute-done.17 = f32[256,512]{1,0:T(8,128)S(1)} collective-permute-done((f32[256,512]{1,0:T(8,128)S(1)}, f32[256,512]{1,0:T(8,128)S(1)}, u32[]{:S(2)}, u32[]{:S(2)}) %collective-permute-start.17) | collective-permute-done | bytes 524320 | tf_op jit(solution)/shard_map/ppermute | solution.py:130
  182.1 5.1 %collective-permute-done.15 = f32[256,512]{1,0:T(8,128)S(1)} collective-permute-done((f32[256,512]{1,0:T(8,128)S(1)}, f32[256,512]{1,0:T(8,128)S(1)}, u32[]{:S(2)}, u32[]{:S(2)}) %collective-permute-start.15) | collective-permute-done | bytes 524320 | tf_op jit(solution)/shard_map/ppermute | solution.py:130
  (51 shorter events, 16.7 us)
Async XLA Ops:
  0.0 14.1 %copy-start = (f32[2,2,256,512]{3,2,1,0:T(8,128)S(1)}, f32[2,2,256,512]{3,2,1,0:T(8,128)}, u32[]{:S(2)}) copy-start(f32[2,2,256,512]{3,2,1,0:T(8,128)} %param.3) | copy-start | bytes 6291460
  0.0 14.1 %copy-start.2 = (s32[2,2,4]{2,1,0:T(2,128)S(1)}, s32[2,2,4]{2,1,0:T(2,128)}, u32[]{:S(2)}) copy-start(s32[2,2,4]{2,1,0:T(2,128)} %mask_ref.3) | copy-start | bytes 196
  5.3 12.7 %collective-permute-start.3 = (f32[4,2,32,640]{3,2,1,0:T(8,128)}, f32[4,2,32,640]{3,2,1,0:T(8,128)S(1)}, u32[]{:S(2)}, u32[]{:S(2)}) collective-permute-start(f32[4,2,32,640]{3,2,1,0:T(8,128)} %get-tuple-element.13), channel_id=1, source_target_pairs={{0,1},{1,0},{2,3},{3,2},{4,5},{5,4},{6,7},{7,6},{8,9},{9,8},{10,11... | collective-permute-start | bytes 1966088 | tf_op jit(solution)/shard_map/ppermute | solution.py:114
  14.1 1.3 copy-start.1
  18.0 4.5 %copy-start.3 = (f32[4,2,32,640]{3,2,1,0:T(8,128)S(1)}, f32[4,2,32,640]{3,2,1,0:T(8,128)}, u32[]{:S(2)}) copy-start(f32[4,2,32,640]{3,2,1,0:T(8,128)} %get-tuple-element.11) | copy-start | bytes 1966084
  19.0 15.2 %all-to-all-start.1 = ((f32[8,32,640]{2,1,0:T(8,128)}), f32[8,32,640]{2,1,0:T(8,128)S(1)}, u32[]{:S(2)}, u32[]{:S(2)}) async-start(f32[8,32,640]{2,1,0:T(8,128)} %bitcast.13), calls=%async_computation.1 | async-start | bytes 1310720 | tf_op jit(solution)/shard_map/all_to_all | solution.py:158
  22.5 4.0 %collective-permute-start = (f32[4,2,32,640]{3,2,1,0:T(8,128)S(1)}, f32[4,2,32,640]{3,2,1,0:T(8,128)S(1)}, u32[]{:S(2)}, u32[]{:S(2)}) collective-permute-start(f32[4,2,32,640]{3,2,1,0:T(8,128)S(1)} %copy-done.3), channel_id=1, source_target_pairs={{0,1},{1,0},{2,3},{3,2},{4,5},{5,4},{6,7},{7,6},{8,9},{9,8},{10,11... | collective-permute-start | bytes 1966088 | tf_op jit(solution)/shard_map/ppermute | solution.py:114
  34.1 17.0 %all-to-all-start = ((f32[8,32,640]{2,1,0:T(8,128)}), f32[8,32,640]{2,1,0:T(8,128)S(1)}, u32[]{:S(2)}, u32[]{:S(2)}) async-start(f32[8,32,640]{2,1,0:T(8,128)} %bitcast.7), calls=%async_computation | async-start | bytes 1310720 | tf_op jit(solution)/shard_map/all_to_all | solution.py:158
  37.8 15.4 %collective-permute-start.4 = (f32[2,32,640]{2,1,0:T(8,128)S(1)}, f32[2,32,640]{2,1,0:T(8,128)S(1)}, u32[]{:S(2)}, u32[]{:S(2)}) collective-permute-start(f32[2,32,640]{2,1,0:T(8,128)S(1)} %dynamic-slice_bitcast_fusion.2), channel_id=1, source_target_pairs={{0,4},{4,0},{8,12},{12,8},{1,5},{5,1},{9,13},{13,9},{2,6},{6,2},{1... | collective-permute-start | bytes 491528 | tf_op jit(solution)/shard_map/ppermute | solution.py:114
  51.2 10.0 %collective-permute-start.1 = (f32[2,32,640]{2,1,0:T(8,128)S(1)}, f32[2,32,640]{2,1,0:T(8,128)S(1)}, u32[]{:S(2)}, u32[]{:S(2)}) collective-permute-start(f32[2,32,640]{2,1,0:T(8,128)S(1)} %dynamic-slice_bitcast_fusion.3), channel_id=1, source_target_pairs={{0,4},{4,0},{8,12},{12,8},{1,5},{5,1},{9,13},{13,9},{2,6},{6,2},{1... | collective-permute-start | bytes 491528 | tf_op jit(solution)/shard_map/ppermute | solution.py:114
  53.2 14.9 %collective-permute-start.5 = (f32[32,640]{1,0:T(8,128)S(1)}, f32[32,640]{1,0:T(8,128)S(1)}, u32[]{:S(2)}, u32[]{:S(2)}) collective-permute-start(f32[32,640]{1,0:T(8,128)S(1)} %dynamic-slice_bitcast_fusion.4), channel_id=1, source_target_pairs={{0,8},{4,12},{8,0},{12,4},{1,9},{5,13},{9,1},{13,5},{2,10},{6,14},... | collective-permute-start | bytes 245768 | tf_op jit(solution)/shard_map/ppermute | solution.py:114
  61.3 15.2 %collective-permute-start.2 = (f32[32,640]{1,0:T(8,128)S(1)}, f32[32,640]{1,0:T(8,128)S(1)}, u32[]{:S(2)}, u32[]{:S(2)}) collective-permute-start(f32[32,640]{1,0:T(8,128)S(1)} %dynamic-slice_bitcast_fusion.5), channel_id=1, source_target_pairs={{0,8},{4,12},{8,0},{12,4},{1,9},{5,13},{9,1},{13,5},{2,10},{6,14},... | collective-permute-start | bytes 245768 | tf_op jit(solution)/shard_map/ppermute | solution.py:114
  76.5 21.8 %collective-permute-start.6 = (f32[64,640]{1,0:T(8,128)S(1)}, f32[64,640]{1,0:T(8,128)S(1)}, u32[]{:S(2)}, u32[]{:S(2)}) collective-permute-start(f32[64,640]{1,0:T(8,128)S(1)} %pad_maximum_fusion.5), channel_id=1, source_target_pairs={{0,8},{4,12},{8,0},{12,4},{1,9},{5,13},{9,1},{13,5},{2,10},{6,14},... | collective-permute-start | bytes 491528 | tf_op jit(solution)/shard_map/ppermute | solution.py:114
  78.4 21.8 %collective-permute-start.12 = (f32[64,640]{1,0:T(8,128)S(1)}, f32[64,640]{1,0:T(8,128)S(1)}, u32[]{:S(2)}, u32[]{:S(2)}) collective-permute-start(f32[64,640]{1,0:T(8,128)S(1)} %pad_maximum_fusion.5), channel_id=1, source_target_pairs={{0,68},{2,4},{4,64},{6,0},{8,76},{10,12},{12,72},{14,8},{64,6},{66... | collective-permute-start | bytes 491528 | tf_op jit(solution)/shard_map/ppermute | solution.py:164
  87.6 12.7 %collective-permute-start.11 = (f32[64,640]{1,0:T(8,128)S(1)}, f32[64,640]{1,0:T(8,128)S(1)}, u32[]{:S(2)}, u32[]{:S(2)}) collective-permute-start(f32[64,640]{1,0:T(8,128)S(1)} %pad_maximum_fusion.5), channel_id=1, source_target_pairs={{0,4},{2,68},{4,0},{6,64},{8,12},{10,76},{12,8},{14,72},{64,70},{6... | collective-permute-start | bytes 491528 | tf_op jit(solution)/shard_map/ppermute | solution.py:163
  98.3 22.7 %collective-permute-start.7 = (f32[2,64,640]{2,1,0:T(8,128)S(1)}, f32[2,64,640]{2,1,0:T(8,128)S(1)}, u32[]{:S(2)}, u32[]{:S(2)}) collective-permute-start(f32[2,64,640]{2,1,0:T(8,128)S(1)} %pad_maximum_fusion.3), channel_id=1, source_target_pairs={{0,4},{4,0},{8,12},{12,8},{1,5},{5,1},{9,13},{13,9},{2,6},{6,2},{1... | collective-permute-start | bytes 983048 | tf_op jit(solution)/shard_map/ppermute | solution.py:114
  101.5 41.1 %all-to-all-start.2 = ((f32[4,2,64,640]{3,2,1,0:T(8,128)}), f32[4,2,64,640]{3,2,1,0:T(8,128)}, u32[]{:S(2)}, u32[]{:S(2)}) async-start(f32[4,2,64,640]{3,2,1,0:T(8,128)} %broadcast_in_dim.2), calls=%async_computation.2 | async-start | bytes 2621440 | tf_op jit(solution)/shard_map/all_to_all | solution.py:169
  121.1 21.5 %collective-permute-start.9 = (f32[4,64,640]{2,1,0:T(8,128)S(1)}, f32[4,64,640]{2,1,0:T(8,128)S(1)}, u32[]{:S(2)}, u32[]{:S(2)}) collective-permute-start(f32[4,64,640]{2,1,0:T(8,128)S(1)} %bitcast.72), channel_id=1, source_target_pairs={{0,2},{2,0},{1,3},{3,1},{4,6},{6,4},{5,7},{7,5},{8,10},{10,8},{9,1... | collective-permute-start | bytes 1966088 | tf_op jit(solution)/shard_map/ppermute | solution.py:114
  128.2 21.9 %collective-permute-start.8 = (f32[4,64,640]{2,1,0:T(8,128)S(1)}, f32[4,64,640]{2,1,0:T(8,128)S(1)}, u32[]{:S(2)}, u32[]{:S(2)}) collective-permute-start(f32[4,64,640]{2,1,0:T(8,128)S(1)} %bitcast.73), channel_id=1, source_target_pairs={{0,1},{1,0},{2,3},{3,2},{4,5},{5,4},{6,7},{7,6},{8,9},{9,8},{10,11... | collective-permute-start | bytes 1966088 | tf_op jit(solution)/shard_map/ppermute | solution.py:114
  144.8 5.3 %collective-permute-start.10 = (f32[4,64,640]{2,1,0:T(8,128)S(1)}, f32[4,64,640]{2,1,0:T(8,128)S(1)}, u32[]{:S(2)}, u32[]{:S(2)}) collective-permute-start(f32[4,64,640]{2,1,0:T(8,128)S(1)} %collective-permute-done.9.fown_ref), channel_id=1, source_target_pairs={{0,1},{1,0},{2,3},{3,2},{4,5},{5,4},{6,7},{7,6},{8,9},{9,8},{10,11... | collective-permute-start | bytes 1966088 | tf_op jit(solution)/shard_map/ppermute | solution.py:114
  148.0 4.3 %collective-permute-start.13 = (f32[2,2,64,640]{3,2,1,0:T(8,128)}, f32[2,2,64,640]{3,2,1,0:T(8,128)}, u32[]{:S(2)}, u32[]{:S(2)}) collective-permute-start(f32[2,2,64,640]{3,2,1,0:T(8,128)} %get-tuple-element.19), channel_id=1, source_target_pairs={{0,1},{1,0},{2,3},{3,2},{4,5},{5,4},{6,7},{7,6},{8,9},{9,8},{10,11... | collective-permute-start | bytes 1966088 | tf_op jit(solution)/shard_map/ppermute | solution.py:114
  155.0 11.0 %collective-permute-start.14 = (f32[128,512]{1,0:T(8,128)S(1)}, f32[128,512]{1,0:T(8,128)S(1)}, u32[]{:S(2)}, u32[]{:S(2)}) collective-permute-start(f32[128,512]{1,0:T(8,128)S(1)} %get-tuple-element.23), channel_id=1, source_target_pairs={{0,128},{128,256},{256,384},{384,0},{1,129},{129,257},{257,385},{3... | collective-permute-start | bytes 786440 | tf_op jit(solution)/shard_map/ppermute | solution.py:130
  156.9 10.0 %collective-permute-start.16 = (f32[128,512]{1,0:T(8,128)S(1)}, f32[128,512]{1,0:T(8,128)S(1)}, u32[]{:S(2)}, u32[]{:S(2)}) collective-permute-start(f32[128,512]{1,0:T(8,128)S(1)} %get-tuple-element.24), channel_id=1, source_target_pairs={{0,384},{128,0},{256,128},{384,256},{1,385},{129,1},{257,129},{385... | collective-permute-start | bytes 786440 | tf_op jit(solution)/shard_map/ppermute | solution.py:130
  167.1 15.0 %collective-permute-start.17 = (f32[256,512]{1,0:T(8,128)S(1)}, f32[256,512]{1,0:T(8,128)S(1)}, u32[]{:S(2)}, u32[]{:S(2)}) collective-permute-start(f32[256,512]{1,0:T(8,128)S(1)} %pad_maximum_fusion.2), channel_id=1, source_target_pairs={{0,384},{128,0},{256,128},{384,256},{1,385},{129,1},{257,129},{385... | collective-permute-start | bytes 1572872 | tf_op jit(solution)/shard_map/ppermute | solution.py:130
  172.2 15.0 %collective-permute-start.15 = (f32[256,512]{1,0:T(8,128)S(1)}, f32[256,512]{1,0:T(8,128)S(1)}, u32[]{:S(2)}, u32[]{:S(2)}) collective-permute-start(f32[256,512]{1,0:T(8,128)S(1)} %pad_maximum_fusion.1), channel_id=1, source_target_pairs={{0,128},{128,256},{256,384},{384,0},{1,129},{129,257},{257,385},{3... | collective-permute-start | bytes 1572872 | tf_op jit(solution)/shard_map/ppermute | solution.py:130

commit v12 on v10

--- a/solution.py
+++ b/solution.py
@@ -166,7 +166,7 @@
     far = swap(m, "zb", 1, 2)
     cols = join(first, second, jnp.where(zh == low, 0, 1), 0)
     n = lax.all_to_all(jnp.broadcast_to(cols[None], (4,) + cols.shape), "y", split_axis=0, concat_axis=0)
-    n = after(n, far).reshape((2, 2) + cols.shape)
+    n = n.reshape((2, 2) + cols.shape)
     cols = pick(n, core, 0), swap(pick(n, 1 - core, 0), "core", 1, 2)
     near, far = (m, swap(m, "core", 1, 2)), (far, swap(far, "core", 1, 2))
     partial = to_x(exchange_part(near, far, cols, jnp.stack([core, low])))

time: 185 us -> 185 us (level)
  no operation moved by 1% of the time
where the time goes in v12:
time: 185 us; the launch traced here: 184 us
  starting transfers between devices  79.9 us (43%)
  waiting for transfers between devices  56.5 us (31%)
  blocking collectives  29.2 us (16%)
  Pallas kernels  11.8 us (6%)
  other arithmetic  3.36 us (2%)
  local copies, waits for them, and re-layouts  2.65 us (1%)
    ppermute x12, starting transfers between devices, swap(): return lax.ppermute(value, axis, [(i, i ^ bit) for i in range(size)])  45.6 us
    ppermute x12, waiting for transfers between devices, swap(): return lax.ppermute(value, axis, [(i, i ^ bit) for i in range(size)])  38.4 us
    all_to_all x1, blocking collectives, to_x(): return lax.all_to_all(value, 'x', split_axis=0, concat_axis=0)  29.2 us
    all_to_all x2, waiting for transfers between devices, local(): lax.all_to_all(part, ('x', 'zb'), split_axis=0, concat_axis=0)  18.1 us
    all_to_all x1, starting transfers between devices, local(): lax.all_to_all(jnp.broadcast_to(cols[None], (4,) + cols.shape), 'y', spli...  15.1 us
    ppermute x1, starting transfers between devices, local(): second = lax.ppermute(own, Z, SECOND)  9.15 us
    pallas_call x2, Pallas kernels, half_of(): pl.pallas_call(half_kernel, out_shape=[jax.ShapeDtypeStruct(shape, jnp.fl...  7.86 us
    all_to_all x2, starting transfers between devices, local(): lax.all_to_all(part, ('x', 'zb'), split_axis=0, concat_axis=0)  7.08 us
  transfers between devices with their start and end apart: 17, of which 9 were waited for; matrix products, arithmetic and copies ran while one was open for 1% of the time, Pallas kernels for 1%

profile of v12, /device:TPU:1, one launch (start us, length us, event | category | flops | bytes accessed | tf_op | source)
XLA Modules:
  0.0 183.9 jit_solution(8305079440396822839)
XLA Ops:
  0.0 5.3 %shard_map.38 = (f32[4,2,32,640]{3,2,1,0:T(8,128)}, f32[4,2,32,640]{3,2,1,0:T(8,128)}) custom-call(s32[1]{0:T(128)} %bitcast.3.half_ref, s32[2,2,4]{2,1,0:T(2,128)} %mask_ref.3, f32[4,4,2,32,512]{4,3,2,1,0:T(8,128)} %bitcast.47, f32[512,640]{1,0:T(8,128)} %c_ref.3), custom_call_target="tpu_custom_call" | custom-call | flops 1006632960 | bytes 3670016 | tf_op jit(solution)/shard_map/pallas_call | solution.py:49
  5.3 8.8 %collective-permute-start.3 = (f32[4,2,32,640]{3,2,1,0:T(8,128)}, f32[4,2,32,640]{3,2,1,0:T(8,128)S(1)}, u32[]{:S(2)}, u32[]{:S(2)}) collective-permute-start(f32[4,2,32,640]{3,2,1,0:T(8,128)} %get-tuple-element.12), channel_id=1, source_target_pairs={{0,1},{1,0},{2,3},{3,2},{4,5},{5,4},{6,7},{7,6},{8,9},{9,8},{10,11... | collective-permute-start | bytes 1966088 | tf_op jit(solution)/shard_map/ppermute | solution.py:113
  14.1 1.3 copy-done.1
  15.4 2.6 %shard_map.37 = (f32[4,2,32,640]{3,2,1,0:T(8,128)S(1)}, f32[4,2,32,640]{3,2,1,0:T(8,128)S(1)}) custom-call(s32[1]{0:T(128)} %bitcast.half_ref, s32[2,2,4]{2,1,0:T(2,128)S(1)} %copy-done.2, f32[4,4,2,32,512]{4,3,2,1,0:T(8,128)S(1)} %bitcast.48, f32[512,640]{1,0:T(8,128)S(1)} %copy-done.1), custom_call_target="tpu_custom_call" | custom-call | flops 1006632960 | bytes 3670016 | tf_op jit(solution)/shard_map/pallas_call | solution.py:49
  19.0 3.5 %all-to-all-start.1 = ((f32[8,32,640]{2,1,0:T(8,128)}), f32[8,32,640]{2,1,0:T(8,128)S(1)}, u32[]{:S(2)}, u32[]{:S(2)}) async-start(f32[8,32,640]{2,1,0:T(8,128)} %bitcast.10), calls=%async_computation.1 | async-start | bytes 1310720 | tf_op jit(solution)/shard_map/all_to_all | solution.py:157
  22.5 1.9 %collective-permute-start = (f32[4,2,32,640]{3,2,1,0:T(8,128)S(1)}, f32[4,2,32,640]{3,2,1,0:T(8,128)S(1)}, u32[]{:S(2)}, u32[]{:S(2)}) collective-permute-start(f32[4,2,32,640]{3,2,1,0:T(8,128)S(1)} %copy-done.3), channel_id=1, source_target_pairs={{0,1},{1,0},{2,3},{3,2},{4,5},{5,4},{6,7},{7,6},{8,9},{9,8},{10,11... | collective-permute-start | bytes 1966088 | tf_op jit(solution)/shard_map/ppermute | solution.py:113
  24.4 2.1 %collective-permute-done = f32[4,2,32,640]{3,2,1,0:T(8,128)S(1)} collective-permute-done((f32[4,2,32,640]{3,2,1,0:T(8,128)S(1)}, f32[4,2,32,640]{3,2,1,0:T(8,128)S(1)}, u32[]{:S(2)}, u32[]{:S(2)}) %collective-permute-start) | collective-permute-done | bytes 655392 | tf_op jit(solution)/shard_map/ppermute | solution.py:113
  27.4 6.7 %all-to-all-done.1 = f32[8,32,640]{2,1,0:T(8,128)S(1)} async-done(((f32[8,32,640]{2,1,0:T(8,128)}), f32[8,32,640]{2,1,0:T(8,128)S(1)}, u32[]{:S(2)}, u32[]{:S(2)}) %all-to-all-start.1) | async-done | bytes 655392 | tf_op jit(solution)/shard_map/all_to_all | solution.py:157
  34.1 3.5 %all-to-all-start = ((f32[8,32,640]{2,1,0:T(8,128)}), f32[8,32,640]{2,1,0:T(8,128)S(1)}, u32[]{:S(2)}, u32[]{:S(2)}) async-start(f32[8,32,640]{2,1,0:T(8,128)} %bitcast.4), calls=%async_computation | async-start | bytes 1310720 | tf_op jit(solution)/shard_map/all_to_all | solution.py:157
  37.8 1.9 %collective-permute-start.4 = (f32[2,32,640]{2,1,0:T(8,128)S(1)}, f32[2,32,640]{2,1,0:T(8,128)S(1)}, u32[]{:S(2)}, u32[]{:S(2)}) collective-permute-start(f32[2,32,640]{2,1,0:T(8,128)S(1)} %dynamic-slice_bitcast_fusion.2), channel_id=1, source_target_pairs={{0,4},{4,0},{8,12},{12,8},{1,5},{5,1},{9,13},{13,9},{2,6},{6,2},{1... | collective-permute-start | bytes 491528 | tf_op jit(solution)/shard_map/ppermute | solution.py:113
  39.7 11.4 %all-to-all-done = f32[8,32,640]{2,1,0:T(8,128)S(1)} async-done(((f32[8,32,640]{2,1,0:T(8,128)}), f32[8,32,640]{2,1,0:T(8,128)S(1)}, u32[]{:S(2)}, u32[]{:S(2)}) %all-to-all-start) | async-done | bytes 655392 | tf_op jit(solution)/shard_map/all_to_all | solution.py:157
  51.2 1.9 %collective-permute-start.1 = (f32[2,32,640]{2,1,0:T(8,128)S(1)}, f32[2,32,640]{2,1,0:T(8,128)S(1)}, u32[]{:S(2)}, u32[]{:S(2)}) collective-permute-start(f32[2,32,640]{2,1,0:T(8,128)S(1)} %dynamic-slice_bitcast_fusion.3), channel_id=1, source_target_pairs={{0,4},{4,0},{8,12},{12,8},{1,5},{5,1},{9,13},{13,9},{2,6},{6,2},{1... | collective-permute-start | bytes 491528 | tf_op jit(solution)/shard_map/ppermute | solution.py:113
  53.2 5.4 %collective-permute-start.5 = (f32[32,640]{1,0:T(8,128)S(1)}, f32[32,640]{1,0:T(8,128)S(1)}, u32[]{:S(2)}, u32[]{:S(2)}) collective-permute-start(f32[32,640]{1,0:T(8,128)S(1)} %dynamic-slice_bitcast_fusion.4), channel_id=1, source_target_pairs={{0,8},{4,12},{8,0},{12,4},{1,9},{5,13},{9,1},{13,5},{2,10},{6,14},... | collective-permute-start | bytes 245768 | tf_op jit(solution)/shard_map/ppermute | solution.py:113
  58.6 2.6 %collective-permute-done.1 = f32[2,32,640]{2,1,0:T(8,128)S(1)} collective-permute-done((f32[2,32,640]{2,1,0:T(8,128)S(1)}, f32[2,32,640]{2,1,0:T(8,128)S(1)}, u32[]{:S(2)}, u32[]{:S(2)}) %collective-permute-start.1) | collective-permute-done | bytes 163872 | tf_op jit(solution)/shard_map/ppermute | solution.py:113
  61.3 6.8 %collective-permute-start.2 = (f32[32,640]{1,0:T(8,128)S(1)}, f32[32,640]{1,0:T(8,128)S(1)}, u32[]{:S(2)}, u32[]{:S(2)}) collective-permute-start(f32[32,640]{1,0:T(8,128)S(1)} %dynamic-slice_bitcast_fusion.5), channel_id=1, source_target_pairs={{0,8},{4,12},{8,0},{12,4},{1,9},{5,13},{9,1},{13,5},{2,10},{6,14},... | collective-permute-start | bytes 245768 | tf_op jit(solution)/shard_map/ppermute | solution.py:113
  68.1 8.4 %collective-permute-done.2 = f32[32,640]{1,0:T(8,128)S(1)} collective-permute-done((f32[32,640]{1,0:T(8,128)S(1)}, f32[32,640]{1,0:T(8,128)S(1)}, u32[]{:S(2)}, u32[]{:S(2)}) %collective-permute-start.2) | collective-permute-done | bytes 81952 | tf_op jit(solution)/shard_map/ppermute | solution.py:113
  76.5 1.9 %collective-permute-start.6 = (f32[64,640]{1,0:T(8,128)S(1)}, f32[64,640]{1,0:T(8,128)S(1)}, u32[]{:S(2)}, u32[]{:S(2)}) collective-permute-start(f32[64,640]{1,0:T(8,128)S(1)} %pad_maximum_fusion.3), channel_id=1, source_target_pairs={{0,8},{4,12},{8,0},{12,4},{1,9},{5,13},{9,1},{13,5},{2,10},{6,14},... | collective-permute-start | bytes 491528 | tf_op jit(solution)/shard_map/ppermute | solution.py:113
  78.4 9.1 %collective-permute-start.12 = (f32[64,640]{1,0:T(8,128)S(1)}, f32[64,640]{1,0:T(8,128)S(1)}, u32[]{:S(2)}, u32[]{:S(2)}) collective-permute-start(f32[64,640]{1,0:T(8,128)S(1)} %pad_maximum_fusion.3), channel_id=1, source_target_pairs={{0,68},{2,4},{4,64},{6,0},{8,76},{10,12},{12,72},{14,8},{64,6},{66... | collective-permute-start | bytes 491528 | tf_op jit(solution)/shard_map/ppermute | solution.py:163
  87.6 3.0 %collective-permute-start.11 = (f32[64,640]{1,0:T(8,128)S(1)}, f32[64,640]{1,0:T(8,128)S(1)}, u32[]{:S(2)}, u32[]{:S(2)}) collective-permute-start(f32[64,640]{1,0:T(8,128)S(1)} %pad_maximum_fusion.3), channel_id=1, source_target_pairs={{0,4},{2,68},{4,0},{6,64},{8,12},{10,76},{12,8},{14,72},{64,70},{6... | collective-permute-start | bytes 491528 | tf_op jit(solution)/shard_map/ppermute | solution.py:162
  90.6 7.7 %collective-permute-done.6 = f32[64,640]{1,0:T(8,128)S(1)} collective-permute-done((f32[64,640]{1,0:T(8,128)S(1)}, f32[64,640]{1,0:T(8,128)S(1)}, u32[]{:S(2)}, u32[]{:S(2)}) %collective-permute-start.6) | collective-permute-done | bytes 163872 | tf_op jit(solution)/shard_map/ppermute | solution.py:113
  98.3 1.9 %collective-permute-start.7 = (f32[2,64,640]{2,1,0:T(8,128)S(1)}, f32[2,64,640]{2,1,0:T(8,128)S(1)}, u32[]{:S(2)}, u32[]{:S(2)}) collective-permute-start(f32[2,64,640]{2,1,0:T(8,128)S(1)} %pad_maximum_fusion.1), channel_id=1, source_target_pairs={{0,4},{4,0},{8,12},{12,8},{1,5},{5,1},{9,13},{13,9},{2,6},{6,2},{1... | collective-permute-start | bytes 983048 | tf_op jit(solution)/shard_map/ppermute | solution.py:113
  100.4 1.2 broadcast_in_dim.2
  101.5 15.1 %all-to-all-start.2 = ((f32[4,2,64,640]{3,2,1,0:T(8,128)}), f32[4,2,64,640]{3,2,1,0:T(8,128)S(1)}, u32[]{:S(2)}, u32[]{:S(2)}) async-start(f32[4,2,64,640]{3,2,1,0:T(8,128)} %broadcast_in_dim.2), calls=%async_computation.2 | async-start | bytes 2621440 | tf_op jit(solution)/shard_map/all_to_all | solution.py:168
  116.6 4.4 %collective-permute-done.7 = f32[2,64,640]{2,1,0:T(8,128)S(1)} collective-permute-done((f32[2,64,640]{2,1,0:T(8,128)S(1)}, f32[2,64,640]{2,1,0:T(8,128)S(1)}, u32[]{:S(2)}, u32[]{:S(2)}) %collective-permute-start.7) | collective-permute-done | bytes 327712 | tf_op jit(solution)/shard_map/ppermute | solution.py:113
  121.1 6.9 %collective-permute-start.9 = (f32[4,64,640]{2,1,0:T(8,128)S(1)}, f32[4,64,640]{2,1,0:T(8,128)S(1)}, u32[]{:S(2)}, u32[]{:S(2)}) collective-permute-start(f32[4,64,640]{2,1,0:T(8,128)S(1)} %bitcast.44), channel_id=1, source_target_pairs={{0,2},{2,0},{1,3},{3,1},{4,6},{6,4},{5,7},{7,5},{8,10},{10,8},{9,1... | collective-permute-start | bytes 1966088 | tf_op jit(solution)/shard_map/ppermute | solution.py:113
  128.0 3.0 %collective-permute-start.8 = (f32[4,64,640]{2,1,0:T(8,128)S(1)}, f32[4,64,640]{2,1,0:T(8,128)S(1)}, u32[]{:S(2)}, u32[]{:S(2)}) collective-permute-start(f32[4,64,640]{2,1,0:T(8,128)S(1)} %bitcast.45), channel_id=1, source_target_pairs={{0,1},{1,0},{2,3},{3,2},{4,5},{5,4},{6,7},{7,6},{8,9},{9,8},{10,11... | collective-permute-start | bytes 1966088 | tf_op jit(solution)/shard_map/ppermute | solution.py:113
  131.1 11.2 %collective-permute-done.9.fown_ref = f32[4,64,640]{2,1,0:T(8,128)S(1)} collective-permute-done((f32[4,64,640]{2,1,0:T(8,128)S(1)}, f32[4,64,640]{2,1,0:T(8,128)S(1)}, u32[]{:S(2)}, u32[]{:S(2)}) %collective-permute-start.9) | collective-permute-done | bytes 655392 | tf_op jit(solution)/shard_map/ppermute | solution.py:113
  142.4 3.2 %collective-permute-start.10 = (f32[4,64,640]{2,1,0:T(8,128)S(1)}, f32[4,64,640]{2,1,0:T(8,128)S(1)}, u32[]{:S(2)}, u32[]{:S(2)}) collective-permute-start(f32[4,64,640]{2,1,0:T(8,128)S(1)} %collective-permute-done.9.fown_ref), channel_id=1, source_target_pairs={{0,1},{1,0},{2,3},{3,2},{4,5},{5,4},{6,7},{7,6},{8,9},{9,8},{10,11... | collective-permute-start | bytes 1966088 | tf_op jit(solution)/shard_map/ppermute | solution.py:113
  145.6 1.9 %collective-permute-start.13 = (f32[2,2,64,640]{3,2,1,0:T(8,128)S(1)}, f32[2,2,64,640]{3,2,1,0:T(8,128)S(1)}, u32[]{:S(2)}, u32[]{:S(2)}) collective-permute-start(f32[2,2,64,640]{3,2,1,0:T(8,128)S(1)} %get-tuple-element.13), channel_id=1, source_target_pairs={{0,1},{1,0},{2,3},{3,2},{4,5},{5,4},{6,7},{7,6},{8,9},{9,8},{10,11... | collective-permute-start | bytes 1966088 | tf_op jit(solution)/shard_map/ppermute | solution.py:113
  147.6 2.0 %collective-permute-done.13.noth_ref = f32[2,2,64,640]{3,2,1,0:T(8,128)S(1)} collective-permute-done((f32[2,2,64,640]{3,2,1,0:T(8,128)S(1)}, f32[2,2,64,640]{3,2,1,0:T(8,128)S(1)}, u32[]{:S(2)}, u32[]{:S(2)}) %collective-permute-start.13) | collective-permute-done | bytes 655392 | tf_op jit(solution)/shard_map/ppermute | solution.py:113
  149.6 4.0 %shard_map.39 = f32[4,256,512]{2,1,0:T(8,128)S(1)} custom-call(s32[2]{0:T(128)S(1)} %pad_add_fusion.place_ref, f32[4,64,640]{2,1,0:T(8,128)S(1)} %bitcast.46, f32[4,64,640]{2,1,0:T(8,128)S(1)} %collective-permute-done.8.moth_ref, f32[4,64,640]{2,1,0:T(8,128)S(1)} %collective-permute-done.9.fown_ref, f32[4,64,640]{2,1,0:T(8,128)S(1)} %collective-permute-done.10.foth_ref, ...), custom_call_target="tpu_custom_call" | custom-call | flops 2013265920 | bytes 6029312 | tf_op jit(solution)/shard_map/pallas_call | solution.py:97
  153.6 29.2 %all_to_all.20 = f32[4,256,512]{2,1,0:T(8,128)S(1)} all-to-all(f32[4,256,512]{2,1,0:T(8,128)S(1)} %shard_map.39), channel_id=1, replica_groups=mesh['x'=4,'zh'=2,'y'=4,'zq'=4,'zb'=2,'core'=2] {'x'}, dimensions={0} | all-to-all | bytes 4194304 | tf_op jit(solution)/shard_map/all_to_all | solution.py:129
  (38 shorter events, 3.6 us)
Async XLA Ops:
  0.0 14.1 %copy-start = (f32[2,2,256,512]{3,2,1,0:T(8,128)S(1)}, f32[2,2,256,512]{3,2,1,0:T(8,128)}, u32[]{:S(2)}) copy-start(f32[2,2,256,512]{3,2,1,0:T(8,128)} %param.3) | copy-start | bytes 6291460
  0.0 14.1 %copy-start.2 = (s32[2,2,4]{2,1,0:T(2,128)S(1)}, s32[2,2,4]{2,1,0:T(2,128)}, u32[]{:S(2)}) copy-start(s32[2,2,4]{2,1,0:T(2,128)} %mask_ref.3) | copy-start | bytes 196
  5.3 12.7 %collective-permute-start.3 = (f32[4,2,32,640]{3,2,1,0:T(8,128)}, f32[4,2,32,640]{3,2,1,0:T(8,128)S(1)}, u32[]{:S(2)}, u32[]{:S(2)}) collective-permute-start(f32[4,2,32,640]{3,2,1,0:T(8,128)} %get-tuple-element.12), channel_id=1, source_target_pairs={{0,1},{1,0},{2,3},{3,2},{4,5},{5,4},{6,7},{7,6},{8,9},{9,8},{10,11... | collective-permute-start | bytes 1966088 | tf_op jit(solution)/shard_map/ppermute | solution.py:113
  14.1 1.3 copy-start.1
  18.0 4.5 %copy-start.3 = (f32[4,2,32,640]{3,2,1,0:T(8,128)S(1)}, f32[4,2,32,640]{3,2,1,0:T(8,128)}, u32[]{:S(2)}) copy-start(f32[4,2,32,640]{3,2,1,0:T(8,128)} %get-tuple-element.10) | copy-start | bytes 1966084
  19.0 15.2 %all-to-all-start.1 = ((f32[8,32,640]{2,1,0:T(8,128)}), f32[8,32,640]{2,1,0:T(8,128)S(1)}, u32[]{:S(2)}, u32[]{:S(2)}) async-start(f32[8,32,640]{2,1,0:T(8,128)} %bitcast.10), calls=%async_computation.1 | async-start | bytes 1310720 | tf_op jit(solution)/shard_map/all_to_all | solution.py:157
  22.5 4.0 %collective-permute-start = (f32[4,2,32,640]{3,2,1,0:T(8,128)S(1)}, f32[4,2,32,640]{3,2,1,0:T(8,128)S(1)}, u32[]{:S(2)}, u32[]{:S(2)}) collective-permute-start(f32[4,2,32,640]{3,2,1,0:T(8,128)S(1)} %copy-done.3), channel_id=1, source_target_pairs={{0,1},{1,0},{2,3},{3,2},{4,5},{5,4},{6,7},{7,6},{8,9},{9,8},{10,11... | collective-permute-start | bytes 1966088 | tf_op jit(solution)/shard_map/ppermute | solution.py:113
  34.1 17.0 %all-to-all-start = ((f32[8,32,640]{2,1,0:T(8,128)}), f32[8,32,640]{2,1,0:T(8,128)S(1)}, u32[]{:S(2)}, u32[]{:S(2)}) async-start(f32[8,32,640]{2,1,0:T(8,128)} %bitcast.4), calls=%async_computation | async-start | bytes 1310720 | tf_op jit(solution)/shard_map/all_to_all | solution.py:157
  37.8 15.4 %collective-permute-start.4 = (f32[2,32,640]{2,1,0:T(8,128)S(1)}, f32[2,32,640]{2,1,0:T(8,128)S(1)}, u32[]{:S(2)}, u32[]{:S(2)}) collective-permute-start(f32[2,32,640]{2,1,0:T(8,128)S(1)} %dynamic-slice_bitcast_fusion.2), channel_id=1, source_target_pairs={{0,4},{4,0},{8,12},{12,8},{1,5},{5,1},{9,13},{13,9},{2,6},{6,2},{1... | collective-permute-start | bytes 491528 | tf_op jit(solution)/shard_map/ppermute | solution.py:113
  51.2 10.0 %collective-permute-start.1 = (f32[2,32,640]{2,1,0:T(8,128)S(1)}, f32[2,32,640]{2,1,0:T(8,128)S(1)}, u32[]{:S(2)}, u32[]{:S(2)}) collective-permute-start(f32[2,32,640]{2,1,0:T(8,128)S(1)} %dynamic-slice_bitcast_fusion.3), channel_id=1, source_target_pairs={{0,4},{4,0},{8,12},{12,8},{1,5},{5,1},{9,13},{13,9},{2,6},{6,2},{1... | collective-permute-start | bytes 491528 | tf_op jit(solution)/shard_map/ppermute | solution.py:113
  53.2 14.9 %collective-permute-start.5 = (f32[32,640]{1,0:T(8,128)S(1)}, f32[32,640]{1,0:T(8,128)S(1)}, u32[]{:S(2)}, u32[]{:S(2)}) collective-permute-start(f32[32,640]{1,0:T(8,128)S(1)} %dynamic-slice_bitcast_fusion.4), channel_id=1, source_target_pairs={{0,8},{4,12},{8,0},{12,4},{1,9},{5,13},{9,1},{13,5},{2,10},{6,14},... | collective-permute-start | bytes 245768 | tf_op jit(solution)/shard_map/ppermute | solution.py:113
  61.3 15.2 %collective-permute-start.2 = (f32[32,640]{1,0:T(8,128)S(1)}, f32[32,640]{1,0:T(8,128)S(1)}, u32[]{:S(2)}, u32[]{:S(2)}) collective-permute-start(f32[32,640]{1,0:T(8,128)S(1)} %dynamic-slice_bitcast_fusion.5), channel_id=1, source_target_pairs={{0,8},{4,12},{8,0},{12,4},{1,9},{5,13},{9,1},{13,5},{2,10},{6,14},... | collective-permute-start | bytes 245768 | tf_op jit(solution)/shard_map/ppermute | solution.py:113
  76.5 21.8 %collective-permute-start.6 = (f32[64,640]{1,0:T(8,128)S(1)}, f32[64,640]{1,0:T(8,128)S(1)}, u32[]{:S(2)}, u32[]{:S(2)}) collective-permute-start(f32[64,640]{1,0:T(8,128)S(1)} %pad_maximum_fusion.3), channel_id=1, source_target_pairs={{0,8},{4,12},{8,0},{12,4},{1,9},{5,13},{9,1},{13,5},{2,10},{6,14},... | collective-permute-start | bytes 491528 | tf_op jit(solution)/shard_map/ppermute | solution.py:113
  78.4 21.8 %collective-permute-start.12 = (f32[64,640]{1,0:T(8,128)S(1)}, f32[64,640]{1,0:T(8,128)S(1)}, u32[]{:S(2)}, u32[]{:S(2)}) collective-permute-start(f32[64,640]{1,0:T(8,128)S(1)} %pad_maximum_fusion.3), channel_id=1, source_target_pairs={{0,68},{2,4},{4,64},{6,0},{8,76},{10,12},{12,72},{14,8},{64,6},{66... | collective-permute-start | bytes 491528 | tf_op jit(solution)/shard_map/ppermute | solution.py:163
  87.6 12.7 %collective-permute-start.11 = (f32[64,640]{1,0:T(8,128)S(1)}, f32[64,640]{1,0:T(8,128)S(1)}, u32[]{:S(2)}, u32[]{:S(2)}) collective-permute-start(f32[64,640]{1,0:T(8,128)S(1)} %pad_maximum_fusion.3), channel_id=1, source_target_pairs={{0,4},{2,68},{4,0},{6,64},{8,12},{10,76},{12,8},{14,72},{64,70},{6... | collective-permute-start | bytes 491528 | tf_op jit(solution)/shard_map/ppermute | solution.py:162
  98.3 22.7 %collective-permute-start.7 = (f32[2,64,640]{2,1,0:T(8,128)S(1)}, f32[2,64,640]{2,1,0:T(8,128)S(1)}, u32[]{:S(2)}, u32[]{:S(2)}) collective-permute-start(f32[2,64,640]{2,1,0:T(8,128)S(1)} %pad_maximum_fusion.1), channel_id=1, source_target_pairs={{0,4},{4,0},{8,12},{12,8},{1,5},{5,1},{9,13},{13,9},{2,6},{6,2},{1... | collective-permute-start | bytes 983048 | tf_op jit(solution)/shard_map/ppermute | solution.py:113
  101.5 29.5 %all-to-all-start.2 = ((f32[4,2,64,640]{3,2,1,0:T(8,128)}), f32[4,2,64,640]{3,2,1,0:T(8,128)S(1)}, u32[]{:S(2)}, u32[]{:S(2)}) async-start(f32[4,2,64,640]{3,2,1,0:T(8,128)} %broadcast_in_dim.2), calls=%async_computation.2 | async-start | bytes 2621440 | tf_op jit(solution)/shard_map/all_to_all | solution.py:168
  121.1 21.2 %collective-permute-start.9 = (f32[4,64,640]{2,1,0:T(8,128)S(1)}, f32[4,64,640]{2,1,0:T(8,128)S(1)}, u32[]{:S(2)}, u32[]{:S(2)}) collective-permute-start(f32[4,64,640]{2,1,0:T(8,128)S(1)} %bitcast.44), channel_id=1, source_target_pairs={{0,2},{2,0},{1,3},{3,1},{4,6},{6,4},{5,7},{7,5},{8,10},{10,8},{9,1... | collective-permute-start | bytes 1966088 | tf_op jit(solution)/shard_map/ppermute | solution.py:113
  128.0 19.6 %collective-permute-start.8 = (f32[4,64,640]{2,1,0:T(8,128)S(1)}, f32[4,64,640]{2,1,0:T(8,128)S(1)}, u32[]{:S(2)}, u32[]{:S(2)}) collective-permute-start(f32[4,64,640]{2,1,0:T(8,128)S(1)} %bitcast.45), channel_id=1, source_target_pairs={{0,1},{1,0},{2,3},{3,2},{4,5},{5,4},{6,7},{7,6},{8,9},{9,8},{10,11... | collective-permute-start | bytes 1966088 | tf_op jit(solution)/shard_map/ppermute | solution.py:113
  142.4 5.3 %collective-permute-start.10 = (f32[4,64,640]{2,1,0:T(8,128)S(1)}, f32[4,64,640]{2,1,0:T(8,128)S(1)}, u32[]{:S(2)}, u32[]{:S(2)}) collective-permute-start(f32[4,64,640]{2,1,0:T(8,128)S(1)} %collective-permute-done.9.fown_ref), channel_id=1, source_target_pairs={{0,1},{1,0},{2,3},{3,2},{4,5},{5,4},{6,7},{7,6},{8,9},{9,8},{10,11... | collective-permute-start | bytes 1966088 | tf_op jit(solution)/shard_map/ppermute | solution.py:113
  145.6 4.0 %collective-permute-start.13 = (f32[2,2,64,640]{3,2,1,0:T(8,128)S(1)}, f32[2,2,64,640]{3,2,1,0:T(8,128)S(1)}, u32[]{:S(2)}, u32[]{:S(2)}) collective-permute-start(f32[2,2,64,640]{3,2,1,0:T(8,128)S(1)} %get-tuple-element.13), channel_id=1, source_target_pairs={{0,1},{1,0},{2,3},{3,2},{4,5},{5,4},{6,7},{7,6},{8,9},{9,8},{10,11... | collective-permute-start | bytes 1966088 | tf_op jit(solution)/shard_map/ppermute | solution.py:113

commit v13 on v9

--- a/solution.py
+++ b/solution.py
@@ -65,10 +65,11 @@
     )(half.reshape(1), mask, integrals.reshape(parts, 4, 2, rows, lcols), coeffs)
 
 
-def exchange_kernel(core_ref, mown_ref, moth_ref, nown_ref, noth_ref, o_ref, mhigh, mlow, nhigh, nlow):
+def exchange_kernel(place_ref, mown_ref, moth_ref, nown_ref, noth_ref, *rest):
+    *_, o_ref, mhigh, mlow, nhigh, nlow = rest
     count, rows, norbit = mown_ref.shape
     blocks, bits, nrows, _ = nown_ref.shape
-    core = core_ref[0]
+    core = place_ref[0]
     both = ((core, mown_ref, nown_ref), (1 - core, moth_ref, noth_ref))
 
     @pl.when(pl.program_id(0) == 0)
@@ -87,25 +88,26 @@
     o_ref[...] = total.reshape(o_ref.shape)
 
 
-def exchange_part(mown, moth, nown, noth, core):
+def exchange_part(mown, moth, nown, noth, core, bit, before):
     parts, rows, norbit = mown.shape
     ncols = 2 * nown.shape[0] * nown.shape[1] * nown.shape[2]
     step = parts // 2
-    mspec = pl.BlockSpec((step, rows, norbit), lambda x, core: (x, 0, 0))
-    nspec = pl.BlockSpec(nown.shape, lambda x, core: (0, 0, 0, 0))
+    mspec = pl.BlockSpec((step, rows, norbit), lambda x, place: (x, 0, 0))
+    nspec = pl.BlockSpec(nown.shape, lambda x, place: (0, 0, 0, 0))
     return pl.pallas_call(
         exchange_kernel,
-        out_shape=jax.ShapeDtypeStruct((parts, 2, rows, ncols), jnp.float32),
+        out_shape=jax.ShapeDtypeStruct((parts, 2, 2, rows, ncols), jnp.float32),
         grid_spec=pltpu.PrefetchScalarGridSpec(
             num_scalar_prefetch=1,
             grid=(2,),
-            in_specs=[mspec, mspec, nspec, nspec],
-            out_specs=pl.BlockSpec((step, 2, rows, ncols), lambda x, core: (x, 0, 0, 0)),
+            in_specs=[mspec, mspec, nspec, nspec] + [pl.BlockSpec(memory_space=pl.ANY)] * len(before),
+            out_specs=pl.BlockSpec((step, 2, 1, rows, ncols), lambda x, place: (x, 0, place[1], 0, 0)),
             scratch_shapes=[pltpu.VMEM((step * 2 * rows, norbit), jnp.bfloat16)] * 2 + [pltpu.VMEM((ncols, norbit), jnp.bfloat16)] * 2,
         ),
+        input_output_aliases={5: 0} if before else {},
         compiler_params=pltpu.CompilerParams(vmem_limit_bytes=VMEM),
         cost_estimate=pl.CostEstimate(flops=12 * parts * rows * ncols * norbit, bytes_accessed=4 * norbit * (2 * parts * rows + ncols) + 8 * parts * rows * ncols, transcendentals=0),
-    )(core.reshape(1), mown, moth, nown, noth)
+    )(jnp.stack([core, bit]), mown, moth, nown, noth, *before)
 
 
 def swap(value, axis, bit, size):
@@ -158,20 +160,19 @@
         part = pick(part, 1 - mid, 1) + swap(pick(part, mid, 1), "zq", 1, 4)
         own.append(pick(part, top, 0) + swap(pick(part, 1 - top, 0), "zq", 2, 4))
     own = jnp.concatenate(own)
+    first = lax.ppermute(own, Z, FIRST)
+    second = lax.ppermute(own, Z, SECOND)
     m = join(own, swap(own, "zq", 2, 4), top, 0)
-    first = after(lax.ppermute(own, Z, FIRST), m)
-    second = after(lax.ppermute(own, Z, SECOND), m)
+    m = join(m, swap(m, "zq", 1, 4), 1 - mid, 1).reshape(4, 2 * rows, norbit)
+    far = swap(m, "zb", 1, 2)
     cols = join(first, second, jnp.where(zh == low, 0, 1), 0)
-    copies = jnp.broadcast_to(cols[None], (4,) + cols.shape)
-    n = lax.all_to_all(copies, "y", split_axis=0, concat_axis=0)
+    n = lax.all_to_all(jnp.broadcast_to(cols[None], (4,) + cols.shape), "y", split_axis=0, concat_axis=0)
     n = n.reshape((2, 2) + cols.shape)
-    nown, noth = pick(n, core, 0), swap(pick(n, 1 - core, 0), "core", 1, 2)
-    m = join(m, swap(m, "zq", 1, 4), 1 - mid, 1).reshape(4, 2 * rows, norbit)
-    tiles = []
-    for m, m_swap in ((m, after(m, nown)), (swap(m, "zb", 1, 2),) * 2):
-        tile = exchange_part(m, swap(m_swap, "core", 1, 2), nown, noth, core)
-        tiles.append(jnp.sum(to_x(tile), axis=0))
-    return join(*tiles, low, 1).reshape(mrows, lcols) * (1.0 / jnp.sqrt(jnp.float32(norbit * parts)))
+    cols = pick(n, core, 0), swap(pick(n, 1 - core, 0), "core", 1, 2)
+    tile = exchange_part(m, swap(m, "core", 1, 2), *cols, core, low, ())
+    tile = exchange_part(far, swap(far, "core", 1, 2), *cols, core, 1 - low, (tile,))
+    partial = to_x(tile.reshape(4, mrows, lcols))
+    return jnp.sum(partial, axis=0) * (1.0 / jnp.sqrt(jnp.float32(norbit * parts)))
 
 
 def solution(mesh):

time: 186 us -> 187 us (level)
  the two profiles are of different devices: /device:TPU:1 before, /device:TPU:32 now
where the time goes in v13:
time: 187 us; the launch traced here: 186 us
  starting transfers between devices  79.3 us (42%)
  waiting for transfers between devices  54 us (29%)
  blocking collectives  30.1 us (16%)
  Pallas kernels  14 us (7%)
  local copies, waits for them, and re-layouts  4.8 us (3%)
  other arithmetic  3.46 us (2%)
    ppermute x12, starting transfers between devices, swap(): return lax.ppermute(value, axis, [(i, i ^ bit) for i in range(size)])  47.4 us
    all_to_all x1, blocking collectives, to_x(): return lax.all_to_all(value, 'x', split_axis=0, concat_axis=0)  30.1 us
    ppermute x1, waiting for transfers between devices, local(): second = lax.ppermute(own, Z, SECOND)  15.6 us
    all_to_all x2, waiting for transfers between devices, local(): lax.all_to_all(part, ('x', 'zb'), split_axis=0, concat_axis=0)  15.1 us
    all_to_all x1, waiting for transfers between devices, local(): lax.all_to_all(jnp.broadcast_to(cols[None], (4,) + cols.shape), 'y', spli...  14.3 us
    all_to_all x2, starting transfers between devices, local(): lax.all_to_all(part, ('x', 'zb'), split_axis=0, concat_axis=0)  13.6 us
    ppermute x12, waiting for transfers between devices, swap(): return lax.ppermute(value, axis, [(i, i ^ bit) for i in range(size)])  9.09 us
    ppermute x1, starting transfers between devices, local(): first = lax.ppermute(own, Z, FIRST)  8.48 us
  transfers between devices with their start and end apart: 17, of which 7 were waited for; matrix products, arithmetic and copies ran while one was open for 3% of the time, Pallas kernels for 3%

profile of v13, /device:TPU:32, one launch (start us, length us, event | category | flops | bytes accessed | tf_op | source)
XLA Modules:
  0.0 185.9 jit_solution(1551400970195487290)
XLA Ops:
  0.0 5.3 %shard_map.38 = (f32[4,2,32,640]{3,2,1,0:T(8,128)}, f32[4,2,32,640]{3,2,1,0:T(8,128)}) custom-call(s32[1]{0:T(128)} %bitcast.3.half_ref, s32[2,2,4]{2,1,0:T(2,128)} %mask_ref.3, f32[4,4,2,32,512]{4,3,2,1,0:T(8,128)} %bitcast.50, f32[512,640]{1,0:T(8,128)} %c_ref.3), custom_call_target="tpu_custom_call" | custom-call | flops 1006632960 | bytes 3670016 | tf_op jit(solution)/shard_map/pallas_call | solution.py:49
  5.3 1.9 %collective-permute-start.3 = (f32[4,2,32,640]{3,2,1,0:T(8,128)}, f32[4,2,32,640]{3,2,1,0:T(8,128)S(1)}, u32[]{:S(2)}, u32[]{:S(2)}) collective-permute-start(f32[4,2,32,640]{3,2,1,0:T(8,128)} %get-tuple-element.12), channel_id=1, source_target_pairs={{0,1},{1,0},{2,3},{3,2},{4,5},{5,4},{6,7},{7,6},{8,9},{9,8},{10,11... | collective-permute-start | bytes 1966088 | tf_op jit(solution)/shard_map/ppermute | solution.py:114
  7.2 1.3 copy-done.1
  8.6 2.6 %shard_map.37 = (f32[4,2,32,640]{3,2,1,0:T(8,128)S(1)}, f32[4,2,32,640]{3,2,1,0:T(8,128)S(1)}) custom-call(s32[1]{0:T(128)} %bitcast.half_ref, s32[2,2,4]{2,1,0:T(2,128)S(1)} %copy-done.2, f32[4,4,2,32,512]{4,3,2,1,0:T(8,128)S(1)} %bitcast.51, f32[512,640]{1,0:T(8,128)S(1)} %copy-done.1), custom_call_target="tpu_custom_call" | custom-call | flops 1006632960 | bytes 3670016 | tf_op jit(solution)/shard_map/pallas_call | solution.py:49
  12.1 8.9 %all-to-all-start.1 = ((f32[8,32,640]{2,1,0:T(8,128)}), f32[8,32,640]{2,1,0:T(8,128)S(1)}, u32[]{:S(2)}, u32[]{:S(2)}) async-start(f32[8,32,640]{2,1,0:T(8,128)} %bitcast.10), calls=%async_computation.1 | async-start | bytes 1310720 | tf_op jit(solution)/shard_map/all_to_all | solution.py:158
  21.0 2.1 %collective-permute-start = (f32[4,2,32,640]{3,2,1,0:T(8,128)S(1)}, f32[4,2,32,640]{3,2,1,0:T(8,128)S(1)}, u32[]{:S(2)}, u32[]{:S(2)}) collective-permute-start(f32[4,2,32,640]{3,2,1,0:T(8,128)S(1)} %copy-done.3), channel_id=1, source_target_pairs={{0,1},{1,0},{2,3},{3,2},{4,5},{5,4},{6,7},{7,6},{8,9},{9,8},{10,11... | collective-permute-start | bytes 1966088 | tf_op jit(solution)/shard_map/ppermute | solution.py:114
  23.1 1.9 %collective-permute-done = f32[4,2,32,640]{3,2,1,0:T(8,128)S(1)} collective-permute-done((f32[4,2,32,640]{3,2,1,0:T(8,128)S(1)}, f32[4,2,32,640]{3,2,1,0:T(8,128)S(1)}, u32[]{:S(2)}, u32[]{:S(2)}) %collective-permute-start) | collective-permute-done | bytes 655392 | tf_op jit(solution)/shard_map/ppermute | solution.py:114
  25.9 6.4 %all-to-all-done.1 = f32[8,32,640]{2,1,0:T(8,128)S(1)} async-done(((f32[8,32,640]{2,1,0:T(8,128)}), f32[8,32,640]{2,1,0:T(8,128)S(1)}, u32[]{:S(2)}, u32[]{:S(2)}) %all-to-all-start.1) | async-done | bytes 655392 | tf_op jit(solution)/shard_map/all_to_all | solution.py:158
  32.3 4.7 %all-to-all-start = ((f32[8,32,640]{2,1,0:T(8,128)}), f32[8,32,640]{2,1,0:T(8,128)S(1)}, u32[]{:S(2)}, u32[]{:S(2)}) async-start(f32[8,32,640]{2,1,0:T(8,128)} %bitcast.4), calls=%async_computation | async-start | bytes 1310720 | tf_op jit(solution)/shard_map/all_to_all | solution.py:158
  37.0 1.9 %collective-permute-start.4 = (f32[2,32,640]{2,1,0:T(8,128)S(1)}, f32[2,32,640]{2,1,0:T(8,128)S(1)}, u32[]{:S(2)}, u32[]{:S(2)}) collective-permute-start(f32[2,32,640]{2,1,0:T(8,128)S(1)} %dynamic-slice_bitcast_fusion.2), channel_id=1, source_target_pairs={{0,4},{4,0},{8,12},{12,8},{1,5},{5,1},{9,13},{13,9},{2,6},{6,2},{1... | collective-permute-start | bytes 491528 | tf_op jit(solution)/shard_map/ppermute | solution.py:114
  39.0 8.7 %all-to-all-done = f32[8,32,640]{2,1,0:T(8,128)S(1)} async-done(((f32[8,32,640]{2,1,0:T(8,128)}), f32[8,32,640]{2,1,0:T(8,128)S(1)}, u32[]{:S(2)}, u32[]{:S(2)}) %all-to-all-start) | async-done | bytes 655392 | tf_op jit(solution)/shard_map/all_to_all | solution.py:158
  47.7 3.8 %collective-permute-start.1 = (f32[2,32,640]{2,1,0:T(8,128)S(1)}, f32[2,32,640]{2,1,0:T(8,128)S(1)}, u32[]{:S(2)}, u32[]{:S(2)}) collective-permute-start(f32[2,32,640]{2,1,0:T(8,128)S(1)} %dynamic-slice_bitcast_fusion.3), channel_id=1, source_target_pairs={{0,4},{4,0},{8,12},{12,8},{1,5},{5,1},{9,13},{13,9},{2,6},{6,2},{1... | collective-permute-start | bytes 491528 | tf_op jit(solution)/shard_map/ppermute | solution.py:114
  51.6 8.0 %collective-permute-start.5 = (f32[32,640]{1,0:T(8,128)S(1)}, f32[32,640]{1,0:T(8,128)S(1)}, u32[]{:S(2)}, u32[]{:S(2)}) collective-permute-start(f32[32,640]{1,0:T(8,128)S(1)} %dynamic-slice_bitcast_fusion.4), channel_id=1, source_target_pairs={{0,8},{4,12},{8,0},{12,4},{1,9},{5,13},{9,1},{13,5},{2,10},{6,14},... | collective-permute-start | bytes 245768 | tf_op jit(solution)/shard_map/ppermute | solution.py:114
  59.7 5.4 %collective-permute-start.2 = (f32[32,640]{1,0:T(8,128)S(1)}, f32[32,640]{1,0:T(8,128)S(1)}, u32[]{:S(2)}, u32[]{:S(2)}) collective-permute-start(f32[32,640]{1,0:T(8,128)S(1)} %dynamic-slice_bitcast_fusion.5), channel_id=1, source_target_pairs={{0,8},{4,12},{8,0},{12,4},{1,9},{5,13},{9,1},{13,5},{2,10},{6,14},... | collective-permute-start | bytes 245768 | tf_op jit(solution)/shard_map/ppermute | solution.py:114
  65.0 4.3 %collective-permute-done.5 = f32[32,640]{1,0:T(8,128)S(1)} collective-permute-done((f32[32,640]{1,0:T(8,128)S(1)}, f32[32,640]{1,0:T(8,128)S(1)}, u32[]{:S(2)}, u32[]{:S(2)}) %collective-permute-start.5) | collective-permute-done | bytes 81952 | tf_op jit(solution)/shard_map/ppermute | solution.py:114
  69.3 2.9 %collective-permute-done.2 = f32[32,640]{1,0:T(8,128)S(1)} collective-permute-done((f32[32,640]{1,0:T(8,128)S(1)}, f32[32,640]{1,0:T(8,128)S(1)}, u32[]{:S(2)}, u32[]{:S(2)}) %collective-permute-start.2) | collective-permute-done | bytes 81952 | tf_op jit(solution)/shard_map/ppermute | solution.py:114
  72.3 3.0 %collective-permute-start.6 = (f32[64,640]{1,0:T(8,128)S(1)}, f32[64,640]{1,0:T(8,128)S(1)}, u32[]{:S(2)}, u32[]{:S(2)}) collective-permute-start(f32[64,640]{1,0:T(8,128)S(1)} %pad_maximum_fusion.3), channel_id=1, source_target_pairs={{0,8},{4,12},{8,0},{12,4},{1,9},{5,13},{9,1},{13,5},{2,10},{6,14},... | collective-permute-start | bytes 491528 | tf_op jit(solution)/shard_map/ppermute | solution.py:114
  75.3 5.3 %collective-permute-start.11 = (f32[64,640]{1,0:T(8,128)S(1)}, f32[64,640]{1,0:T(8,128)S(1)}, u32[]{:S(2)}, u32[]{:S(2)}) collective-permute-start(f32[64,640]{1,0:T(8,128)S(1)} %pad_maximum_fusion.3), channel_id=1, source_target_pairs={{0,68},{2,4},{4,64},{6,0},{8,76},{10,12},{12,72},{14,8},{64,6},{66... | collective-permute-start | bytes 491528 | tf_op jit(solution)/shard_map/ppermute | solution.py:164
  80.6 8.5 %collective-permute-start.10 = (f32[64,640]{1,0:T(8,128)S(1)}, f32[64,640]{1,0:T(8,128)S(1)}, u32[]{:S(2)}, u32[]{:S(2)}) collective-permute-start(f32[64,640]{1,0:T(8,128)S(1)} %pad_maximum_fusion.3), channel_id=1, source_target_pairs={{0,4},{2,68},{4,0},{6,64},{8,12},{10,76},{12,8},{14,72},{64,70},{6... | collective-permute-start | bytes 491528 | tf_op jit(solution)/shard_map/ppermute | solution.py:163
  89.2 13.2 %collective-permute-start.7 = (f32[2,64,640]{2,1,0:T(8,128)S(1)}, f32[2,64,640]{2,1,0:T(8,128)S(1)}, u32[]{:S(2)}, u32[]{:S(2)}) collective-permute-start(f32[2,64,640]{2,1,0:T(8,128)S(1)} %pad_maximum_fusion.1), channel_id=1, source_target_pairs={{0,4},{4,0},{8,12},{12,8},{1,5},{5,1},{9,13},{13,9},{2,6},{6,2},{1... | collective-permute-start | bytes 983048 | tf_op jit(solution)/shard_map/ppermute | solution.py:114
  102.4 15.6 %collective-permute-done.11 = f32[64,640]{1,0:T(8,128)S(1)} collective-permute-done((f32[64,640]{1,0:T(8,128)S(1)}, f32[64,640]{1,0:T(8,128)S(1)}, u32[]{:S(2)}, u32[]{:S(2)}) %collective-permute-start.11) | collective-permute-done | bytes 163872 | tf_op jit(solution)/shard_map/ppermute | solution.py:164
  118.0 1.2 broadcast_in_dim.2
  119.2 4.5 %all-to-all-start.2 = ((f32[4,2,64,640]{3,2,1,0:T(8,128)}), f32[4,2,64,640]{3,2,1,0:T(8,128)}, u32[]{:S(2)}, u32[]{:S(2)}) async-start(f32[4,2,64,640]{3,2,1,0:T(8,128)} %broadcast_in_dim.2), calls=%async_computation.2 | async-start | bytes 2621440 | tf_op jit(solution)/shard_map/all_to_all | solution.py:169
  123.8 1.9 %collective-permute-start.8 = (f32[4,64,640]{2,1,0:T(8,128)S(1)}, f32[4,64,640]{2,1,0:T(8,128)S(1)}, u32[]{:S(2)}, u32[]{:S(2)}) collective-permute-start(f32[4,64,640]{2,1,0:T(8,128)S(1)} %bitcast.47), channel_id=1, source_target_pairs={{0,2},{2,0},{1,3},{3,1},{4,6},{6,4},{5,7},{7,5},{8,10},{10,8},{9,1... | collective-permute-start | bytes 1966088 | tf_op jit(solution)/shard_map/ppermute | solution.py:114
  125.7 1.9 %collective-permute-start.13 = (f32[4,64,640]{2,1,0:T(8,128)S(1)}, f32[4,64,640]{2,1,0:T(8,128)S(1)}, u32[]{:S(2)}, u32[]{:S(2)}) collective-permute-start(f32[4,64,640]{2,1,0:T(8,128)S(1)} %bitcast.48), channel_id=1, source_target_pairs={{0,1},{1,0},{2,3},{3,2},{4,5},{5,4},{6,7},{7,6},{8,9},{9,8},{10,11... | collective-permute-start | bytes 1966088 | tf_op jit(solution)/shard_map/ppermute | solution.py:114
  127.6 14.3 %all-to-all-done.2 = f32[4,2,64,640]{3,2,1,0:T(8,128)} async-done(((f32[4,2,64,640]{3,2,1,0:T(8,128)}), f32[4,2,64,640]{3,2,1,0:T(8,128)}, u32[]{:S(2)}, u32[]{:S(2)}) %all-to-all-start.2) | async-done | bytes 1310752 | tf_op jit(solution)/shard_map/all_to_all | solution.py:169
  141.9 2.2 %dynamic-slice_bitcast_fusion = (f32[2,2,64,640]{3,2,1,0:T(8,128)}, f32[2,2,64,640]{3,2,1,0:T(8,128)S(1)}) fusion(f32[2,2,2,64,640]{4,3,2,1,0:T(8,128)} %bitcast.24, s32[]{:T(128)S(6)} %select_n.80, s32[]{:T(128)S(6)} %select_n.79), kind=kLoop, calls=%fused_computation.1 | loop fusion | bytes 2621448 | tf_op jit(solution)/shard_map/jit(dynamic_index_in_dim)/squeeze | solution.py:118
  144.1 1.9 %collective-permute-start.12 = (f32[2,2,64,640]{3,2,1,0:T(8,128)}, f32[2,2,64,640]{3,2,1,0:T(8,128)S(1)}, u32[]{:S(2)}, u32[]{:S(2)}) collective-permute-start(f32[2,2,64,640]{3,2,1,0:T(8,128)} %get-tuple-element.13), channel_id=1, source_target_pairs={{0,1},{1,0},{2,3},{3,2},{4,5},{5,4},{6,7},{7,6},{8,9},{9,8},{10,11... | collective-permute-start | bytes 1966088 | tf_op jit(solution)/shard_map/ppermute | solution.py:114
  146.1 2.4 %collective-permute-start.9 = (f32[4,64,640]{2,1,0:T(8,128)S(1)}, f32[4,64,640]{2,1,0:T(8,128)}, u32[]{:S(2)}, u32[]{:S(2)}) collective-permute-start(f32[4,64,640]{2,1,0:T(8,128)S(1)} %collective-permute-done.8.mown_ref), channel_id=1, source_target_pairs={{0,1},{1,0},{2,3},{3,2},{4,5},{5,4},{6,7},{7,6},{8,9},{9,8},{10,11... | collective-permute-start | bytes 1966088 | tf_op jit(solution)/shard_map/ppermute | solution.py:114
  148.6 2.6 %shard_map.39.rest_0_ = f32[4,2,2,64,512]{4,3,2,1,0:T(8,128)S(1)} custom-call(s32[2]{0:T(128)S(1)} %pad_add_fusion.1.place_ref, f32[4,64,640]{2,1,0:T(8,128)S(1)} %bitcast.49, f32[4,64,640]{2,1,0:T(8,128)S(1)} %collective-permute-done.13.moth_ref, f32[2,2,64,640]{3,2,1,0:T(8,128)S(1)} %get-tuple-element.14.nown_ref, ...), custom_call_target="tpu_custom_call" | custom-call | flops 1006632960 | bytes 3670016 | tf_op jit(solution)/shard_map/pallas_call | solution.py:97
  151.2 3.5 %shard_map.40 = f32[4,2,2,64,512]{4,3,2,1,0:T(8,128)S(1)} custom-call(s32[2]{0:T(128)S(1)} %pad_add_fusion.place_ref, f32[4,64,640]{2,1,0:T(8,128)S(1)} %collective-permute-done.8.mown_ref, f32[4,64,640]{2,1,0:T(8,128)} %collective-permute-done.9.moth_ref, f32[2,2,64,640]{3,2,1,0:T(8,128)S(1)} %get-tuple-element.14.nown_ref, ...), custom_call_target="tpu_custom_call", output_to_operand_aliasing={{}: (5, {})} | custom-call | flops 1006632960 | bytes 3670016 | tf_op jit(solution)/shard_map/pallas_call | solution.py:97
  154.8 30.1 %all_to_all.20 = f32[4,256,512]{2,1,0:T(8,128)S(1)} all-to-all(f32[4,256,512]{2,1,0:T(8,128)S(1)} %bitcast.46), channel_id=1, replica_groups=mesh['x'=4,'zh'=2,'y'=4,'zq'=4,'zb'=2,'core'=2] {'x'}, dimensions={0} | all-to-all | bytes 4194304 | tf_op jit(solution)/shard_map/all_to_all | solution.py:130
  (40 shorter events, 3.6 us)
Async XLA Ops:
  0.0 7.2 %copy-start.2 = (s32[2,2,4]{2,1,0:T(2,128)S(1)}, s32[2,2,4]{2,1,0:T(2,128)}, u32[]{:S(2)}) copy-start(s32[2,2,4]{2,1,0:T(2,128)} %mask_ref.3) | copy-start | bytes 196
  0.0 7.2 %copy-start = (f32[2,2,256,512]{3,2,1,0:T(8,128)S(1)}, f32[2,2,256,512]{3,2,1,0:T(8,128)}, u32[]{:S(2)}) copy-start(f32[2,2,256,512]{3,2,1,0:T(8,128)} %param.3) | copy-start | bytes 6291460
  5.3 5.9 %collective-permute-start.3 = (f32[4,2,32,640]{3,2,1,0:T(8,128)}, f32[4,2,32,640]{3,2,1,0:T(8,128)S(1)}, u32[]{:S(2)}, u32[]{:S(2)}) collective-permute-start(f32[4,2,32,640]{3,2,1,0:T(8,128)} %get-tuple-element.12), channel_id=1, source_target_pairs={{0,1},{1,0},{2,3},{3,2},{4,5},{5,4},{6,7},{7,6},{8,9},{9,8},{10,11... | collective-permute-start | bytes 1966088 | tf_op jit(solution)/shard_map/ppermute | solution.py:114
  7.2 1.3 copy-start.1
  11.1 9.9 %copy-start.3 = (f32[4,2,32,640]{3,2,1,0:T(8,128)S(1)}, f32[4,2,32,640]{3,2,1,0:T(8,128)}, u32[]{:S(2)}) copy-start(f32[4,2,32,640]{3,2,1,0:T(8,128)} %get-tuple-element.10) | copy-start | bytes 1966084
  12.1 20.2 %all-to-all-start.1 = ((f32[8,32,640]{2,1,0:T(8,128)}), f32[8,32,640]{2,1,0:T(8,128)S(1)}, u32[]{:S(2)}, u32[]{:S(2)}) async-start(f32[8,32,640]{2,1,0:T(8,128)} %bitcast.10), calls=%async_computation.1 | async-start | bytes 1310720 | tf_op jit(solution)/shard_map/all_to_all | solution.py:158
  21.0 4.0 %collective-permute-start = (f32[4,2,32,640]{3,2,1,0:T(8,128)S(1)}, f32[4,2,32,640]{3,2,1,0:T(8,128)S(1)}, u32[]{:S(2)}, u32[]{:S(2)}) collective-permute-start(f32[4,2,32,640]{3,2,1,0:T(8,128)S(1)} %copy-done.3), channel_id=1, source_target_pairs={{0,1},{1,0},{2,3},{3,2},{4,5},{5,4},{6,7},{7,6},{8,9},{9,8},{10,11... | collective-permute-start | bytes 1966088 | tf_op jit(solution)/shard_map/ppermute | solution.py:114
  32.3 15.4 %all-to-all-start = ((f32[8,32,640]{2,1,0:T(8,128)}), f32[8,32,640]{2,1,0:T(8,128)S(1)}, u32[]{:S(2)}, u32[]{:S(2)}) async-start(f32[8,32,640]{2,1,0:T(8,128)} %bitcast.4), calls=%async_computation | async-start | bytes 1310720 | tf_op jit(solution)/shard_map/all_to_all | solution.py:158
  37.0 14.5 %collective-permute-start.4 = (f32[2,32,640]{2,1,0:T(8,128)S(1)}, f32[2,32,640]{2,1,0:T(8,128)S(1)}, u32[]{:S(2)}, u32[]{:S(2)}) collective-permute-start(f32[2,32,640]{2,1,0:T(8,128)S(1)} %dynamic-slice_bitcast_fusion.2), channel_id=1, source_target_pairs={{0,4},{4,0},{8,12},{12,8},{1,5},{5,1},{9,13},{13,9},{2,6},{6,2},{1... | collective-permute-start | bytes 491528 | tf_op jit(solution)/shard_map/ppermute | solution.py:114
  47.7 11.8 %collective-permute-start.1 = (f32[2,32,640]{2,1,0:T(8,128)S(1)}, f32[2,32,640]{2,1,0:T(8,128)S(1)}, u32[]{:S(2)}, u32[]{:S(2)}) collective-permute-start(f32[2,32,640]{2,1,0:T(8,128)S(1)} %dynamic-slice_bitcast_fusion.3), channel_id=1, source_target_pairs={{0,4},{4,0},{8,12},{12,8},{1,5},{5,1},{9,13},{13,9},{2,6},{6,2},{1... | collective-permute-start | bytes 491528 | tf_op jit(solution)/shard_map/ppermute | solution.py:114
  51.6 17.7 %collective-permute-start.5 = (f32[32,640]{1,0:T(8,128)S(1)}, f32[32,640]{1,0:T(8,128)S(1)}, u32[]{:S(2)}, u32[]{:S(2)}) collective-permute-start(f32[32,640]{1,0:T(8,128)S(1)} %dynamic-slice_bitcast_fusion.4), channel_id=1, source_target_pairs={{0,8},{4,12},{8,0},{12,4},{1,9},{5,13},{9,1},{13,5},{2,10},{6,14},... | collective-permute-start | bytes 245768 | tf_op jit(solution)/shard_map/ppermute | solution.py:114
  59.7 12.6 %collective-permute-start.2 = (f32[32,640]{1,0:T(8,128)S(1)}, f32[32,640]{1,0:T(8,128)S(1)}, u32[]{:S(2)}, u32[]{:S(2)}) collective-permute-start(f32[32,640]{1,0:T(8,128)S(1)} %dynamic-slice_bitcast_fusion.5), channel_id=1, source_target_pairs={{0,8},{4,12},{8,0},{12,4},{1,9},{5,13},{9,1},{13,5},{2,10},{6,14},... | collective-permute-start | bytes 245768 | tf_op jit(solution)/shard_map/ppermute | solution.py:114
  72.3 16.8 %collective-permute-start.6 = (f32[64,640]{1,0:T(8,128)S(1)}, f32[64,640]{1,0:T(8,128)S(1)}, u32[]{:S(2)}, u32[]{:S(2)}) collective-permute-start(f32[64,640]{1,0:T(8,128)S(1)} %pad_maximum_fusion.3), channel_id=1, source_target_pairs={{0,8},{4,12},{8,0},{12,4},{1,9},{5,13},{9,1},{13,5},{2,10},{6,14},... | collective-permute-start | bytes 491528 | tf_op jit(solution)/shard_map/ppermute | solution.py:114
  75.3 42.6 %collective-permute-start.11 = (f32[64,640]{1,0:T(8,128)S(1)}, f32[64,640]{1,0:T(8,128)S(1)}, u32[]{:S(2)}, u32[]{:S(2)}) collective-permute-start(f32[64,640]{1,0:T(8,128)S(1)} %pad_maximum_fusion.3), channel_id=1, source_target_pairs={{0,68},{2,4},{4,64},{6,0},{8,76},{10,12},{12,72},{14,8},{64,6},{66... | collective-permute-start | bytes 491528 | tf_op jit(solution)/shard_map/ppermute | solution.py:164
  80.6 37.3 %collective-permute-start.10 = (f32[64,640]{1,0:T(8,128)S(1)}, f32[64,640]{1,0:T(8,128)S(1)}, u32[]{:S(2)}, u32[]{:S(2)}) collective-permute-start(f32[64,640]{1,0:T(8,128)S(1)} %pad_maximum_fusion.3), channel_id=1, source_target_pairs={{0,4},{2,68},{4,0},{6,64},{8,12},{10,76},{12,8},{14,72},{64,70},{6... | collective-permute-start | bytes 491528 | tf_op jit(solution)/shard_map/ppermute | solution.py:163
  89.2 34.5 %collective-permute-start.7 = (f32[2,64,640]{2,1,0:T(8,128)S(1)}, f32[2,64,640]{2,1,0:T(8,128)S(1)}, u32[]{:S(2)}, u32[]{:S(2)}) collective-permute-start(f32[2,64,640]{2,1,0:T(8,128)S(1)} %pad_maximum_fusion.1), channel_id=1, source_target_pairs={{0,4},{4,0},{8,12},{12,8},{1,5},{5,1},{9,13},{13,9},{2,6},{6,2},{1... | collective-permute-start | bytes 983048 | tf_op jit(solution)/shard_map/ppermute | solution.py:114
  119.2 22.7 %all-to-all-start.2 = ((f32[4,2,64,640]{3,2,1,0:T(8,128)}), f32[4,2,64,640]{3,2,1,0:T(8,128)}, u32[]{:S(2)}, u32[]{:S(2)}) async-start(f32[4,2,64,640]{3,2,1,0:T(8,128)} %broadcast_in_dim.2), calls=%async_computation.2 | async-start | bytes 2621440 | tf_op jit(solution)/shard_map/all_to_all | solution.py:169
  123.8 22.3 %collective-permute-start.8 = (f32[4,64,640]{2,1,0:T(8,128)S(1)}, f32[4,64,640]{2,1,0:T(8,128)S(1)}, u32[]{:S(2)}, u32[]{:S(2)}) collective-permute-start(f32[4,64,640]{2,1,0:T(8,128)S(1)} %bitcast.47), channel_id=1, source_target_pairs={{0,2},{2,0},{1,3},{3,1},{4,6},{6,4},{5,7},{7,5},{8,10},{10,8},{9,1... | collective-permute-start | bytes 1966088 | tf_op jit(solution)/shard_map/ppermute | solution.py:114
  125.7 23.0 %collective-permute-start.13 = (f32[4,64,640]{2,1,0:T(8,128)S(1)}, f32[4,64,640]{2,1,0:T(8,128)S(1)}, u32[]{:S(2)}, u32[]{:S(2)}) collective-permute-start(f32[4,64,640]{2,1,0:T(8,128)S(1)} %bitcast.48), channel_id=1, source_target_pairs={{0,1},{1,0},{2,3},{3,2},{4,5},{5,4},{6,7},{7,6},{8,9},{9,8},{10,11... | collective-permute-start | bytes 1966088 | tf_op jit(solution)/shard_map/ppermute | solution.py:114
  144.1 4.5 %collective-permute-start.12 = (f32[2,2,64,640]{3,2,1,0:T(8,128)}, f32[2,2,64,640]{3,2,1,0:T(8,128)S(1)}, u32[]{:S(2)}, u32[]{:S(2)}) collective-permute-start(f32[2,2,64,640]{3,2,1,0:T(8,128)} %get-tuple-element.13), channel_id=1, source_target_pairs={{0,1},{1,0},{2,3},{3,2},{4,5},{5,4},{6,7},{7,6},{8,9},{9,8},{10,11... | collective-permute-start | bytes 1966088 | tf_op jit(solution)/shard_map/ppermute | solution.py:114
  146.1 5.1 %collective-permute-start.9 = (f32[4,64,640]{2,1,0:T(8,128)S(1)}, f32[4,64,640]{2,1,0:T(8,128)}, u32[]{:S(2)}, u32[]{:S(2)}) collective-permute-start(f32[4,64,640]{2,1,0:T(8,128)S(1)} %collective-permute-done.8.mown_ref), channel_id=1, source_target_pairs={{0,1},{1,0},{2,3},{3,2},{4,5},{5,4},{6,7},{7,6},{8,9},{9,8},{10,11... | collective-permute-start | bytes 1966088 | tf_op jit(solution)/shard_map/ppermute | solution.py:114

commit v14 on v9

--- a/solution.py
+++ b/solution.py
@@ -168,7 +168,7 @@
     nown, noth = pick(n, core, 0), swap(pick(n, 1 - core, 0), "core", 1, 2)
     m = join(m, swap(m, "zq", 1, 4), 1 - mid, 1).reshape(4, 2 * rows, norbit)
     tiles = []
-    for m, m_swap in ((m, after(m, nown)), (swap(m, "zb", 1, 2),) * 2):
+    for m, m_swap in ((m, m), (swap(m, "zb", 1, 2),) * 2):
         tile = exchange_part(m, swap(m_swap, "core", 1, 2), nown, noth, core)
         tiles.append(jnp.sum(to_x(tile), axis=0))
     return join(*tiles, low, 1).reshape(mrows, lcols) * (1.0 / jnp.sqrt(jnp.float32(norbit * parts)))

time: 186 us -> 184 us (0.989)
  waiting for transfers between devices: 79.3 us -> 75 us
  starting transfers between devices: 84 us -> 86.4 us
    all_to_all x1, waiting for transfers between devices: 5.85 us -> 1.1 us  [local(): n = lax.all_to_all(copies, 'y', split_axis=0, concat_axis=0)]
    ppermute x12, starting transfers between devices: 54.3 us -> 56.7 us  [swap(): return lax.ppermute(value, axis, [(i, i ^ bit) for i in range(size)])]
where the time goes in v14:
time: 184 us; the launch traced here: 182 us
  starting transfers between devices  86.4 us (47%)
  waiting for transfers between devices  75 us (41%)
  Pallas kernels  13.4 us (7%)
  other arithmetic  4.5 us (2%)
  local copies, waits for them, and re-layouts  2.65 us (1%)
    ppermute x12, starting transfers between devices, swap(): return lax.ppermute(value, axis, [(i, i ^ bit) for i in range(size)])  56.7 us
    ppermute x12, waiting for transfers between devices, swap(): return lax.ppermute(value, axis, [(i, i ^ bit) for i in range(size)])  35.8 us
    all_to_all x2, waiting for transfers between devices, local(): lax.all_to_all(part, ('x', 'zb'), split_axis=0, concat_axis=0)  18.2 us
    all_to_all x2, waiting for transfers between devices, to_x(): return lax.all_to_all(value, 'x', split_axis=0, concat_axis=0)  12.7 us
    ppermute x1, starting transfers between devices, local(): second = after(lax.ppermute(own, Z, SECOND), m)  9.15 us
    pallas_call x2, Pallas kernels, half_of(): pl.pallas_call(half_kernel, out_shape=[jax.ShapeDtypeStruct(shape, jnp.fl...  7.87 us
    all_to_all x2, starting transfers between devices, to_x(): return lax.all_to_all(value, 'x', split_axis=0, concat_axis=0)  7.76 us
    ppermute x1, waiting for transfers between devices, local(): second = after(lax.ppermute(own, Z, SECOND), m)  7.31 us
  transfers between devices with their start and end apart: 19, of which 12 were waited for; matrix products, arithmetic and copies ran while one was open for 1% of the time, Pallas kernels for 4%

profile of v14, /device:TPU:1, one launch (start us, length us, event | category | flops | bytes accessed | tf_op | source)
XLA Modules:
  0.0 182.4 jit_solution(9368180625316235017)
XLA Ops:
  0.0 5.3 %shard_map.38 = (f32[4,2,32,640]{3,2,1,0:T(8,128)}, f32[4,2,32,640]{3,2,1,0:T(8,128)}) custom-call(s32[1]{0:T(128)} %bitcast.2.half_ref, s32[2,2,4]{2,1,0:T(2,128)} %mask_ref.3, f32[4,4,2,32,512]{4,3,2,1,0:T(8,128)} %bitcast.53, f32[512,640]{1,0:T(8,128)} %c_ref.3), custom_call_target="tpu_custom_call" | custom-call | flops 1006632960 | bytes 3670016 | tf_op jit(solution)/shard_map/pallas_call | solution.py:49
  5.3 8.8 %collective-permute-start.3 = (f32[4,2,32,640]{3,2,1,0:T(8,128)}, f32[4,2,32,640]{3,2,1,0:T(8,128)S(1)}, u32[]{:S(2)}, u32[]{:S(2)}) collective-permute-start(f32[4,2,32,640]{3,2,1,0:T(8,128)} %get-tuple-element.14), channel_id=1, source_target_pairs={{0,1},{1,0},{2,3},{3,2},{4,5},{5,4},{6,7},{7,6},{8,9},{9,8},{10,11... | collective-permute-start | bytes 1966088 | tf_op jit(solution)/shard_map/ppermute | solution.py:112
  15.4 2.6 %shard_map.37 = (f32[4,2,32,640]{3,2,1,0:T(8,128)S(1)}, f32[4,2,32,640]{3,2,1,0:T(8,128)S(1)}) custom-call(s32[1]{0:T(128)} %bitcast.half_ref.core_ref, s32[2,2,4]{2,1,0:T(2,128)S(1)} %copy-done.2, f32[4,4,2,32,512]{4,3,2,1,0:T(8,128)S(1)} %bitcast.54, f32[512,640]{1,0:T(8,128)S(1)} %copy-done.1), custom_call_target="tpu_custom_call" | custom-call | flops 1006632960 | bytes 3670016 | tf_op jit(solution)/shard_map/pallas_call | solution.py:49
  19.0 3.5 %all-to-all-start.1 = ((f32[8,32,640]{2,1,0:T(8,128)}), f32[8,32,640]{2,1,0:T(8,128)S(1)}, u32[]{:S(2)}, u32[]{:S(2)}) async-start(f32[8,32,640]{2,1,0:T(8,128)} %bitcast.9), calls=%async_computation.1 | async-start | bytes 1310720 | tf_op jit(solution)/shard_map/all_to_all | solution.py:156
  22.5 1.9 %collective-permute-start = (f32[4,2,32,640]{3,2,1,0:T(8,128)S(1)}, f32[4,2,32,640]{3,2,1,0:T(8,128)S(1)}, u32[]{:S(2)}, u32[]{:S(2)}) collective-permute-start(f32[4,2,32,640]{3,2,1,0:T(8,128)S(1)} %copy-done.3), channel_id=1, source_target_pairs={{0,1},{1,0},{2,3},{3,2},{4,5},{5,4},{6,7},{7,6},{8,9},{9,8},{10,11... | collective-permute-start | bytes 1966088 | tf_op jit(solution)/shard_map/ppermute | solution.py:112
  24.5 2.1 %collective-permute-done = f32[4,2,32,640]{3,2,1,0:T(8,128)S(1)} collective-permute-done((f32[4,2,32,640]{3,2,1,0:T(8,128)S(1)}, f32[4,2,32,640]{3,2,1,0:T(8,128)S(1)}, u32[]{:S(2)}, u32[]{:S(2)}) %collective-permute-start) | collective-permute-done | bytes 655392 | tf_op jit(solution)/shard_map/ppermute | solution.py:112
  27.4 6.7 %all-to-all-done.1 = f32[8,32,640]{2,1,0:T(8,128)S(1)} async-done(((f32[8,32,640]{2,1,0:T(8,128)}), f32[8,32,640]{2,1,0:T(8,128)S(1)}, u32[]{:S(2)}, u32[]{:S(2)}) %all-to-all-start.1) | async-done | bytes 655392 | tf_op jit(solution)/shard_map/all_to_all | solution.py:156
  34.2 3.5 %all-to-all-start = ((f32[8,32,640]{2,1,0:T(8,128)}), f32[8,32,640]{2,1,0:T(8,128)S(1)}, u32[]{:S(2)}, u32[]{:S(2)}) async-start(f32[8,32,640]{2,1,0:T(8,128)} %bitcast.3), calls=%async_computation | async-start | bytes 1310720 | tf_op jit(solution)/shard_map/all_to_all | solution.py:156
  37.8 1.9 %collective-permute-start.4 = (f32[2,32,640]{2,1,0:T(8,128)S(1)}, f32[2,32,640]{2,1,0:T(8,128)S(1)}, u32[]{:S(2)}, u32[]{:S(2)}) collective-permute-start(f32[2,32,640]{2,1,0:T(8,128)S(1)} %dynamic-slice_bitcast_fusion.2), channel_id=1, source_target_pairs={{0,4},{4,0},{8,12},{12,8},{1,5},{5,1},{9,13},{13,9},{2,6},{6,2},{1... | collective-permute-start | bytes 491528 | tf_op jit(solution)/shard_map/ppermute | solution.py:112
  39.7 11.4 %all-to-all-done = f32[8,32,640]{2,1,0:T(8,128)S(1)} async-done(((f32[8,32,640]{2,1,0:T(8,128)}), f32[8,32,640]{2,1,0:T(8,128)S(1)}, u32[]{:S(2)}, u32[]{:S(2)}) %all-to-all-start) | async-done | bytes 655392 | tf_op jit(solution)/shard_map/all_to_all | solution.py:156
  51.2 1.9 %collective-permute-start.1 = (f32[2,32,640]{2,1,0:T(8,128)S(1)}, f32[2,32,640]{2,1,0:T(8,128)S(1)}, u32[]{:S(2)}, u32[]{:S(2)}) collective-permute-start(f32[2,32,640]{2,1,0:T(8,128)S(1)} %dynamic-slice_bitcast_fusion.3), channel_id=1, source_target_pairs={{0,4},{4,0},{8,12},{12,8},{1,5},{5,1},{9,13},{13,9},{2,6},{6,2},{1... | collective-permute-start | bytes 491528 | tf_op jit(solution)/shard_map/ppermute | solution.py:112
  53.2 5.4 %collective-permute-start.5 = (f32[32,640]{1,0:T(8,128)S(1)}, f32[32,640]{1,0:T(8,128)S(1)}, u32[]{:S(2)}, u32[]{:S(2)}) collective-permute-start(f32[32,640]{1,0:T(8,128)S(1)} %dynamic-slice_bitcast_fusion.4), channel_id=1, source_target_pairs={{0,8},{4,12},{8,0},{12,4},{1,9},{5,13},{9,1},{13,5},{2,10},{6,14},... | collective-permute-start | bytes 245768 | tf_op jit(solution)/shard_map/ppermute | solution.py:112
  58.6 2.6 %collective-permute-done.1 = f32[2,32,640]{2,1,0:T(8,128)S(1)} collective-permute-done((f32[2,32,640]{2,1,0:T(8,128)S(1)}, f32[2,32,640]{2,1,0:T(8,128)S(1)}, u32[]{:S(2)}, u32[]{:S(2)}) %collective-permute-start.1) | collective-permute-done | bytes 163872 | tf_op jit(solution)/shard_map/ppermute | solution.py:112
  61.3 6.8 %collective-permute-start.2 = (f32[32,640]{1,0:T(8,128)S(1)}, f32[32,640]{1,0:T(8,128)S(1)}, u32[]{:S(2)}, u32[]{:S(2)}) collective-permute-start(f32[32,640]{1,0:T(8,128)S(1)} %dynamic-slice_bitcast_fusion.5), channel_id=1, source_target_pairs={{0,8},{4,12},{8,0},{12,4},{1,9},{5,13},{9,1},{13,5},{2,10},{6,14},... | collective-permute-start | bytes 245768 | tf_op jit(solution)/shard_map/ppermute | solution.py:112
  68.1 8.4 %collective-permute-done.2 = f32[32,640]{1,0:T(8,128)S(1)} collective-permute-done((f32[32,640]{1,0:T(8,128)S(1)}, f32[32,640]{1,0:T(8,128)S(1)}, u32[]{:S(2)}, u32[]{:S(2)}) %collective-permute-start.2) | collective-permute-done | bytes 81952 | tf_op jit(solution)/shard_map/ppermute | solution.py:112
  76.5 1.9 %collective-permute-start.6 = (f32[64,640]{1,0:T(8,128)S(1)}, f32[64,640]{1,0:T(8,128)S(1)}, u32[]{:S(2)}, u32[]{:S(2)}) collective-permute-start(f32[64,640]{1,0:T(8,128)S(1)} %pad_maximum_fusion.3), channel_id=1, source_target_pairs={{0,8},{4,12},{8,0},{12,4},{1,9},{5,13},{9,1},{13,5},{2,10},{6,14},... | collective-permute-start | bytes 491528 | tf_op jit(solution)/shard_map/ppermute | solution.py:112
  78.5 1.9 %collective-permute-start.9 = (f32[64,640]{1,0:T(8,128)S(1)}, f32[64,640]{1,0:T(8,128)S(1)}, u32[]{:S(2)}, u32[]{:S(2)}) collective-permute-start(f32[64,640]{1,0:T(8,128)S(1)} %pad_maximum_fusion.3), channel_id=1, source_target_pairs={{0,4},{2,68},{4,0},{6,64},{8,12},{10,76},{12,8},{14,72},{64,70},{6... | collective-permute-start | bytes 491528 | tf_op jit(solution)/shard_map/ppermute | solution.py:162
  80.4 9.1 %collective-permute-start.10 = (f32[64,640]{1,0:T(8,128)S(1)}, f32[64,640]{1,0:T(8,128)S(1)}, u32[]{:S(2)}, u32[]{:S(2)}) collective-permute-start(f32[64,640]{1,0:T(8,128)S(1)} %pad_maximum_fusion.3), channel_id=1, source_target_pairs={{0,68},{2,4},{4,64},{6,0},{8,76},{10,12},{12,72},{14,8},{64,6},{66... | collective-permute-start | bytes 491528 | tf_op jit(solution)/shard_map/ppermute | solution.py:163
  89.5 4.7 %collective-permute-done.6 = f32[64,640]{1,0:T(8,128)S(1)} collective-permute-done((f32[64,640]{1,0:T(8,128)S(1)}, f32[64,640]{1,0:T(8,128)S(1)}, u32[]{:S(2)}, u32[]{:S(2)}) %collective-permute-start.6) | collective-permute-done | bytes 163872 | tf_op jit(solution)/shard_map/ppermute | solution.py:112
  94.3 7.3 %collective-permute-done.10 = f32[64,640]{1,0:T(8,128)S(1)} collective-permute-done((f32[64,640]{1,0:T(8,128)S(1)}, f32[64,640]{1,0:T(8,128)S(1)}, u32[]{:S(2)}, u32[]{:S(2)}) %collective-permute-start.10) | collective-permute-done | bytes 163872 | tf_op jit(solution)/shard_map/ppermute | solution.py:163
  102.9 3.8 %all-to-all-start.2 = ((f32[4,2,64,640]{3,2,1,0:T(8,128)}), f32[4,2,64,640]{3,2,1,0:T(8,128)S(1)}, u32[]{:S(2)}, u32[]{:S(2)}) async-start(f32[4,2,64,640]{3,2,1,0:T(8,128)} %broadcast_in_dim.2), calls=%async_computation.2 | async-start | bytes 2621440 | tf_op jit(solution)/shard_map/all_to_all | solution.py:166
  108.6 8.2 %collective-permute-done.7 = f32[2,64,640]{2,1,0:T(8,128)S(1)} collective-permute-done((f32[2,64,640]{2,1,0:T(8,128)S(1)}, f32[2,64,640]{2,1,0:T(8,128)S(1)}, u32[]{:S(2)}, u32[]{:S(2)}) %collective-permute-start.7) | collective-permute-done | bytes 327712 | tf_op jit(solution)/shard_map/ppermute | solution.py:112
  116.8 4.7 %collective-permute-start.8 = (f32[4,64,640]{2,1,0:T(8,128)S(1)}, f32[4,64,640]{2,1,0:T(8,128)S(1)}, u32[]{:S(2)}, u32[]{:S(2)}) collective-permute-start(f32[4,64,640]{2,1,0:T(8,128)S(1)} %bitcast.50), channel_id=1, source_target_pairs={{0,1},{1,0},{2,3},{3,2},{4,5},{5,4},{6,7},{7,6},{8,9},{9,8},{10,11... | collective-permute-start | bytes 1966088 | tf_op jit(solution)/shard_map/ppermute | solution.py:112
  122.8 4.7 %collective-permute-start.11 = (f32[2,2,64,640]{3,2,1,0:T(8,128)S(1)}, f32[2,2,64,640]{3,2,1,0:T(8,128)S(1)}, u32[]{:S(2)}, u32[]{:S(2)}) collective-permute-start(f32[2,2,64,640]{3,2,1,0:T(8,128)S(1)} %get-tuple-element.17), channel_id=1, source_target_pairs={{0,1},{1,0},{2,3},{3,2},{4,5},{5,4},{6,7},{7,6},{8,9},{9,8},{10,11... | collective-permute-start | bytes 1966088 | tf_op jit(solution)/shard_map/ppermute | solution.py:112
  127.5 14.3 %collective-permute-start.12 = (f32[4,64,640]{2,1,0:T(8,128)S(1)}, f32[4,64,640]{2,1,0:T(8,128)S(1)}, u32[]{:S(2)}, u32[]{:S(2)}) collective-permute-start(f32[4,64,640]{2,1,0:T(8,128)S(1)} %bitcast.51), channel_id=1, source_target_pairs={{0,2},{2,0},{1,3},{3,1},{4,6},{6,4},{5,7},{7,5},{8,10},{10,8},{9,1... | collective-permute-start | bytes 1966088 | tf_op jit(solution)/shard_map/ppermute | solution.py:112
  141.8 2.8 %shard_map.39 = f32[4,2,64,512]{3,2,1,0:T(8,128)} custom-call(s32[1]{0:T(128)} %bitcast.half_ref.core_ref, f32[4,64,640]{2,1,0:T(8,128)S(1)} %bitcast.52, f32[4,64,640]{2,1,0:T(8,128)S(1)} %collective-permute-done.8.moth_ref, f32[2,2,64,640]{3,2,1,0:T(8,128)S(1)} %get-tuple-element.18.nown_ref, f32[2,2,64,640]{3,2,1,0:T(8,128)S(1)} %collective-permute-done.11.noth_ref), custom_call_target="tpu_custom_call" | custom-call | flops 1006632960 | bytes 3670016 | tf_op jit(solution)/shard_map/pallas_call | solution.py:96
  144.6 4.2 %all-to-all-start.3 = ((f32[4,2,64,512]{3,2,1,0:T(8,128)}), f32[4,2,64,512]{3,2,1,0:T(8,128)}, u32[]{:S(2)}, u32[]{:S(2)}) async-start(f32[4,2,64,512]{3,2,1,0:T(8,128)} %shard_map.39), calls=%async_computation.3 | async-start | bytes 2097152 | tf_op jit(solution)/shard_map/all_to_all | solution.py:128
  148.8 8.2 %collective-permute-done.12.mown_ref = f32[4,64,640]{2,1,0:T(8,128)S(1)} collective-permute-done((f32[4,64,640]{2,1,0:T(8,128)S(1)}, f32[4,64,640]{2,1,0:T(8,128)S(1)}, u32[]{:S(2)}, u32[]{:S(2)}) %collective-permute-start.12) | collective-permute-done | bytes 655392 | tf_op jit(solution)/shard_map/ppermute | solution.py:112
  157.0 2.4 %collective-permute-start.13 = (f32[4,64,640]{2,1,0:T(8,128)S(1)}, f32[4,64,640]{2,1,0:T(8,128)S(1)}, u32[]{:S(2)}, u32[]{:S(2)}) collective-permute-start(f32[4,64,640]{2,1,0:T(8,128)S(1)} %collective-permute-done.12.mown_ref), channel_id=1, source_target_pairs={{0,1},{1,0},{2,3},{3,2},{4,5},{5,4},{6,7},{7,6},{8,9},{9,8},{10,11... | collective-permute-start | bytes 1966088 | tf_op jit(solution)/shard_map/ppermute | solution.py:112
  161.1 2.8 %shard_map.40 = f32[4,2,64,512]{3,2,1,0:T(8,128)} custom-call(s32[1]{0:T(128)} %bitcast.half_ref.core_ref, f32[4,64,640]{2,1,0:T(8,128)S(1)} %collective-permute-done.12.mown_ref, f32[4,64,640]{2,1,0:T(8,128)S(1)} %collective-permute-done.13.moth_ref, f32[2,2,64,640]{3,2,1,0:T(8,128)S(1)} %get-tuple-element.18.nown_ref, ...), custom_call_target="tpu_custom_call" | custom-call | flops 1006632960 | bytes 3670016 | tf_op jit(solution)/shard_map/pallas_call | solution.py:96
  163.8 3.5 %all-to-all-start.4 = ((f32[4,2,64,512]{3,2,1,0:T(8,128)}), f32[4,2,64,512]{3,2,1,0:T(8,128)S(1)}, u32[]{:S(2)}, u32[]{:S(2)}) async-start(f32[4,2,64,512]{3,2,1,0:T(8,128)} %shard_map.40), calls=%async_computation.4 | async-start | bytes 2097152 | tf_op jit(solution)/shard_map/all_to_all | solution.py:128
  168.7 12.7 %all-to-all-done.4 = f32[4,2,64,512]{3,2,1,0:T(8,128)S(1)} async-done(((f32[4,2,64,512]{3,2,1,0:T(8,128)}), f32[4,2,64,512]{3,2,1,0:T(8,128)S(1)}, u32[]{:S(2)}, u32[]{:S(2)}) %all-to-all-start.4) | async-done | bytes 1048608 | tf_op jit(solution)/shard_map/all_to_all | solution.py:128
  (43 shorter events, 11.9 us)
Async XLA Ops:
  0.0 14.1 %copy-start = (f32[2,2,256,512]{3,2,1,0:T(8,128)S(1)}, f32[2,2,256,512]{3,2,1,0:T(8,128)}, u32[]{:S(2)}) copy-start(f32[2,2,256,512]{3,2,1,0:T(8,128)} %param.3) | copy-start | bytes 6291460
  0.0 14.1 %copy-start.2 = (s32[2,2,4]{2,1,0:T(2,128)S(1)}, s32[2,2,4]{2,1,0:T(2,128)}, u32[]{:S(2)}) copy-start(s32[2,2,4]{2,1,0:T(2,128)} %mask_ref.3) | copy-start | bytes 196
  5.3 12.7 %collective-permute-start.3 = (f32[4,2,32,640]{3,2,1,0:T(8,128)}, f32[4,2,32,640]{3,2,1,0:T(8,128)S(1)}, u32[]{:S(2)}, u32[]{:S(2)}) collective-permute-start(f32[4,2,32,640]{3,2,1,0:T(8,128)} %get-tuple-element.14), channel_id=1, source_target_pairs={{0,1},{1,0},{2,3},{3,2},{4,5},{5,4},{6,7},{7,6},{8,9},{9,8},{10,11... | collective-permute-start | bytes 1966088 | tf_op jit(solution)/shard_map/ppermute | solution.py:112
  14.1 1.3 copy-start.1
  18.0 4.5 %copy-start.3 = (f32[4,2,32,640]{3,2,1,0:T(8,128)S(1)}, f32[4,2,32,640]{3,2,1,0:T(8,128)}, u32[]{:S(2)}) copy-start(f32[4,2,32,640]{3,2,1,0:T(8,128)} %get-tuple-element.12) | copy-start | bytes 1966084
  19.0 15.2 %all-to-all-start.1 = ((f32[8,32,640]{2,1,0:T(8,128)}), f32[8,32,640]{2,1,0:T(8,128)S(1)}, u32[]{:S(2)}, u32[]{:S(2)}) async-start(f32[8,32,640]{2,1,0:T(8,128)} %bitcast.9), calls=%async_computation.1 | async-start | bytes 1310720 | tf_op jit(solution)/shard_map/all_to_all | solution.py:156
  22.5 4.0 %collective-permute-start = (f32[4,2,32,640]{3,2,1,0:T(8,128)S(1)}, f32[4,2,32,640]{3,2,1,0:T(8,128)S(1)}, u32[]{:S(2)}, u32[]{:S(2)}) collective-permute-start(f32[4,2,32,640]{3,2,1,0:T(8,128)S(1)} %copy-done.3), channel_id=1, source_target_pairs={{0,1},{1,0},{2,3},{3,2},{4,5},{5,4},{6,7},{7,6},{8,9},{9,8},{10,11... | collective-permute-start | bytes 1966088 | tf_op jit(solution)/shard_map/ppermute | solution.py:112
  34.2 17.0 %all-to-all-start = ((f32[8,32,640]{2,1,0:T(8,128)}), f32[8,32,640]{2,1,0:T(8,128)S(1)}, u32[]{:S(2)}, u32[]{:S(2)}) async-start(f32[8,32,640]{2,1,0:T(8,128)} %bitcast.3), calls=%async_computation | async-start | bytes 1310720 | tf_op jit(solution)/shard_map/all_to_all | solution.py:156
  37.8 15.4 %collective-permute-start.4 = (f32[2,32,640]{2,1,0:T(8,128)S(1)}, f32[2,32,640]{2,1,0:T(8,128)S(1)}, u32[]{:S(2)}, u32[]{:S(2)}) collective-permute-start(f32[2,32,640]{2,1,0:T(8,128)S(1)} %dynamic-slice_bitcast_fusion.2), channel_id=1, source_target_pairs={{0,4},{4,0},{8,12},{12,8},{1,5},{5,1},{9,13},{13,9},{2,6},{6,2},{1... | collective-permute-start | bytes 491528 | tf_op jit(solution)/shard_map/ppermute | solution.py:112
  51.2 10.0 %collective-permute-start.1 = (f32[2,32,640]{2,1,0:T(8,128)S(1)}, f32[2,32,640]{2,1,0:T(8,128)S(1)}, u32[]{:S(2)}, u32[]{:S(2)}) collective-permute-start(f32[2,32,640]{2,1,0:T(8,128)S(1)} %dynamic-slice_bitcast_fusion.3), channel_id=1, source_target_pairs={{0,4},{4,0},{8,12},{12,8},{1,5},{5,1},{9,13},{13,9},{2,6},{6,2},{1... | collective-permute-start | bytes 491528 | tf_op jit(solution)/shard_map/ppermute | solution.py:112
  53.2 14.9 %collective-permute-start.5 = (f32[32,640]{1,0:T(8,128)S(1)}, f32[32,640]{1,0:T(8,128)S(1)}, u32[]{:S(2)}, u32[]{:S(2)}) collective-permute-start(f32[32,640]{1,0:T(8,128)S(1)} %dynamic-slice_bitcast_fusion.4), channel_id=1, source_target_pairs={{0,8},{4,12},{8,0},{12,4},{1,9},{5,13},{9,1},{13,5},{2,10},{6,14},... | collective-permute-start | bytes 245768 | tf_op jit(solution)/shard_map/ppermute | solution.py:112
  61.3 15.2 %collective-permute-start.2 = (f32[32,640]{1,0:T(8,128)S(1)}, f32[32,640]{1,0:T(8,128)S(1)}, u32[]{:S(2)}, u32[]{:S(2)}) collective-permute-start(f32[32,640]{1,0:T(8,128)S(1)} %dynamic-slice_bitcast_fusion.5), channel_id=1, source_target_pairs={{0,8},{4,12},{8,0},{12,4},{1,9},{5,13},{9,1},{13,5},{2,10},{6,14},... | collective-permute-start | bytes 245768 | tf_op jit(solution)/shard_map/ppermute | solution.py:112
  76.5 17.8 %collective-permute-start.6 = (f32[64,640]{1,0:T(8,128)S(1)}, f32[64,640]{1,0:T(8,128)S(1)}, u32[]{:S(2)}, u32[]{:S(2)}) collective-permute-start(f32[64,640]{1,0:T(8,128)S(1)} %pad_maximum_fusion.3), channel_id=1, source_target_pairs={{0,8},{4,12},{8,0},{12,4},{1,9},{5,13},{9,1},{13,5},{2,10},{6,14},... | collective-permute-start | bytes 491528 | tf_op jit(solution)/shard_map/ppermute | solution.py:112
  78.5 15.9 %collective-permute-start.9 = (f32[64,640]{1,0:T(8,128)S(1)}, f32[64,640]{1,0:T(8,128)S(1)}, u32[]{:S(2)}, u32[]{:S(2)}) collective-permute-start(f32[64,640]{1,0:T(8,128)S(1)} %pad_maximum_fusion.3), channel_id=1, source_target_pairs={{0,4},{2,68},{4,0},{6,64},{8,12},{10,76},{12,8},{14,72},{64,70},{6... | collective-permute-start | bytes 491528 | tf_op jit(solution)/shard_map/ppermute | solution.py:162
  80.4 21.3 %collective-permute-start.10 = (f32[64,640]{1,0:T(8,128)S(1)}, f32[64,640]{1,0:T(8,128)S(1)}, u32[]{:S(2)}, u32[]{:S(2)}) collective-permute-start(f32[64,640]{1,0:T(8,128)S(1)} %pad_maximum_fusion.3), channel_id=1, source_target_pairs={{0,68},{2,4},{4,64},{6,0},{8,76},{10,12},{12,72},{14,8},{64,6},{66... | collective-permute-start | bytes 491528 | tf_op jit(solution)/shard_map/ppermute | solution.py:163
  102.9 19.8 %all-to-all-start.2 = ((f32[4,2,64,640]{3,2,1,0:T(8,128)}), f32[4,2,64,640]{3,2,1,0:T(8,128)S(1)}, u32[]{:S(2)}, u32[]{:S(2)}) async-start(f32[4,2,64,640]{3,2,1,0:T(8,128)} %broadcast_in_dim.2), calls=%async_computation.2 | async-start | bytes 2621440 | tf_op jit(solution)/shard_map/all_to_all | solution.py:166
  106.6 10.1 %collective-permute-start.7 = (f32[2,64,640]{2,1,0:T(8,128)S(1)}, f32[2,64,640]{2,1,0:T(8,128)S(1)}, u32[]{:S(2)}, u32[]{:S(2)}) collective-permute-start(f32[2,64,640]{2,1,0:T(8,128)S(1)} %pad_maximum_fusion.1), channel_id=1, source_target_pairs={{0,4},{4,0},{8,12},{12,8},{1,5},{5,1},{9,13},{13,9},{2,6},{6,2},{1... | collective-permute-start | bytes 983048 | tf_op jit(solution)/shard_map/ppermute | solution.py:112
  116.8 25.0 %collective-permute-start.8 = (f32[4,64,640]{2,1,0:T(8,128)S(1)}, f32[4,64,640]{2,1,0:T(8,128)S(1)}, u32[]{:S(2)}, u32[]{:S(2)}) collective-permute-start(f32[4,64,640]{2,1,0:T(8,128)S(1)} %bitcast.50), channel_id=1, source_target_pairs={{0,1},{1,0},{2,3},{3,2},{4,5},{5,4},{6,7},{7,6},{8,9},{9,8},{10,11... | collective-permute-start | bytes 1966088 | tf_op jit(solution)/shard_map/ppermute | solution.py:112
  122.8 19.0 %collective-permute-start.11 = (f32[2,2,64,640]{3,2,1,0:T(8,128)S(1)}, f32[2,2,64,640]{3,2,1,0:T(8,128)S(1)}, u32[]{:S(2)}, u32[]{:S(2)}) collective-permute-start(f32[2,2,64,640]{3,2,1,0:T(8,128)S(1)} %get-tuple-element.17), channel_id=1, source_target_pairs={{0,1},{1,0},{2,3},{3,2},{4,5},{5,4},{6,7},{7,6},{8,9},{9,8},{10,11... | collective-permute-start | bytes 1966088 | tf_op jit(solution)/shard_map/ppermute | solution.py:112
  127.5 29.5 %collective-permute-start.12 = (f32[4,64,640]{2,1,0:T(8,128)S(1)}, f32[4,64,640]{2,1,0:T(8,128)S(1)}, u32[]{:S(2)}, u32[]{:S(2)}) collective-permute-start(f32[4,64,640]{2,1,0:T(8,128)S(1)} %bitcast.51), channel_id=1, source_target_pairs={{0,2},{2,0},{1,3},{3,1},{4,6},{6,4},{5,7},{7,5},{8,10},{10,8},{9,1... | collective-permute-start | bytes 1966088 | tf_op jit(solution)/shard_map/ppermute | solution.py:112
  144.6 19.3 %all-to-all-start.3 = ((f32[4,2,64,512]{3,2,1,0:T(8,128)}), f32[4,2,64,512]{3,2,1,0:T(8,128)}, u32[]{:S(2)}, u32[]{:S(2)}) async-start(f32[4,2,64,512]{3,2,1,0:T(8,128)} %shard_map.39), calls=%async_computation.3 | async-start | bytes 2097152 | tf_op jit(solution)/shard_map/all_to_all | solution.py:128
  157.0 4.1 %collective-permute-start.13 = (f32[4,64,640]{2,1,0:T(8,128)S(1)}, f32[4,64,640]{2,1,0:T(8,128)S(1)}, u32[]{:S(2)}, u32[]{:S(2)}) collective-permute-start(f32[4,64,640]{2,1,0:T(8,128)S(1)} %collective-permute-done.12.mown_ref), channel_id=1, source_target_pairs={{0,1},{1,0},{2,3},{3,2},{4,5},{5,4},{6,7},{7,6},{8,9},{9,8},{10,11... | collective-permute-start | bytes 1966088 | tf_op jit(solution)/shard_map/ppermute | solution.py:112
  163.8 17.5 %all-to-all-start.4 = ((f32[4,2,64,512]{3,2,1,0:T(8,128)}), f32[4,2,64,512]{3,2,1,0:T(8,128)S(1)}, u32[]{:S(2)}, u32[]{:S(2)}) async-start(f32[4,2,64,512]{3,2,1,0:T(8,128)} %shard_map.40), calls=%async_computation.4 | async-start | bytes 2097152 | tf_op jit(solution)/shard_map/all_to_all | solution.py:128
